TPU v7x, 32 devices: a whole 2x2x4 slice. The times are simulated.
32 devices in a mesh: rows: 8 (over z, x), far: 4 (over y, core).
Axes of the slice: x: 2, y: 2, z: 4, core: 2. Of those that a mesh axis runs over, the one named last changes fastest.
Arguments:
- right_side: float32 [16384, 256], P('rows'), may hold values from -24 to 24
- near_blocks: float32 [128, 24, 128, 128], P('rows', 'far'), may hold values from -0.03125 to 0.03125
- near_cols: int32 [128, 24], P('rows', 'far'), may hold values from 0 to 127, as said below
- far_src: int32 [8, 8, 4], P('rows', None, 'far'), may hold values from 0 to 15
- far_tgt: int32 [8, 8, 4], P('rows', None, 'far'), may hold values from 0 to 15
- far_left: float32 [8, 8, 4, 128, 64], P('rows', None, 'far'), may hold values from -0.15625 to 0.15625
- far_right: float32 [8, 8, 4, 128, 64], P('rows', None, 'far'), may hold values from -0.5 to 0.5
Outputs:
- solution: float32 [16384, 256], P('rows', 'far')
- residual: float32 [16384, 256], P('rows', 'far')
Inputs may be any that keep to these rules, and one draw needn't show every extreme that they name: `near_cols`: each near-field column lies within 8 clusters of its row; slot 0 of row i names i itself, slot 1 names min(i + 8, 127) and slot 2 names max(i - 8, 0).
All inputs are finite; a program needn't handle non-finite values.
Results may differ from a plain program's by a relative error of at most 0.0003.
Values sent between devices are 32-bit elements; how exact they have to be, the bound alone decides.
No kernel may reach another device: no remote copies, remote signals or barrier semaphores. Data moves between devices by JAX's collectives and lax.ppermute only.
A program may use at most 128 MiB of HBM per device.

v0:
```python
import jax
import jax.numpy as jnp
from jax import lax
from jax.sharding import PartitionSpec as P

B = 128
CL_DEV = 16
REACH = 8


TOP_PRECISION = lax.Precision.HIGHEST
EPS = 1e-06


def with_halo(cells, sides, width):
    for axis, dim in sides:
        count = lax.axis_size(axis)
        ends = count - 1
        head = lax.slice_in_dim(cells, 0, width, axis=dim)
        tail = lax.slice_in_dim(cells, cells.shape[dim] - width, cells.shape[dim], axis=dim)
        cells = jnp.concatenate(
            [
                lax.ppermute(tail, axis, [(i, (i + 1) % count) for i in range(ends)]),
                cells,
                lax.ppermute(head, axis, [((i + 1) % count, i) for i in range(ends)]),
            ],
            axis=dim,
        )
    return cells


def column_dots(left_vec, right_vector):
    return jnp.sum(left_vec * right_vector, axis=0)


def near_term(vector_in, near_blocks, near_cols):
    rhs_count = vector_in.shape[1]
    padded = with_halo(vector_in, (("rows", 0),), REACH * B)
    clusters = padded.reshape(-1, B, rhs_count)
    offset = lax.axis_index("rows") * CL_DEV - REACH
    picked = jnp.take(clusters, near_cols - offset, axis=0)
    return jnp.einsum("cspq,csqn->cpn", near_blocks, picked, precision=TOP_PRECISION)


def far_term(vector_in, far_src, far_tgt, far_left, far_right):
    clusters = vector_in.reshape(CL_DEV, B, vector_in.shape[1])
    picked = jnp.take(clusters, far_src[0], axis=0)
    coefficients = jnp.einsum("tsbr,tsbn->tsrn", far_right[0], picked, precision=TOP_PRECISION)
    owning_devices = (far_tgt[0][:, :, None] == jnp.arange(CL_DEV, dtype=jnp.int32)).astype(
        jnp.float32
    )
    contribution_part = jnp.einsum(
        "asbr,asrn->asbn",
        far_left[0],
        lax.all_to_all(coefficients, "rows", split_axis=0, concat_axis=0, tiled=True),
        precision=TOP_PRECISION,
    )
    return jnp.einsum("hyo,hyze->oze", owning_devices, contribution_part, precision=TOP_PRECISION)


def own_columns(vector_in):
    share_width = vector_in.shape[-1] // lax.axis_size("far")
    return lax.dynamic_slice_in_dim(
        vector_in, lax.axis_index("far") * share_width, share_width, vector_in.ndim - 1
    )


def least_squares(rhs_length, upper_left, lower_left, column_two, lower_right):
    radius_one = jnp.sqrt(upper_left * upper_left + lower_left * lower_left)
    cosine_one = upper_left / radius_one
    sine_one = lower_left / radius_one
    rotated_top = cosine_one * rhs_length
    rotated_mid = -sine_one * rhs_length
    coupled = cosine_one * column_two[0] + sine_one * column_two[1]
    diagonal_two = cosine_one * column_two[1] - sine_one * column_two[0]
    radius_two = jnp.sqrt(diagonal_two * diagonal_two + lower_right * lower_right)
    weight_two = diagonal_two * rotated_mid / (radius_two * radius_two)
    weight_one = (rotated_top - coupled * weight_two) / radius_one
    return (weight_one, weight_two)


def shards(right_side, near_blocks, near_cols, far_src, far_tgt, far_left, far_right):

    def partial_image(vector_in):
        near_part = near_term(vector_in, near_blocks, near_cols)
        far_part = far_term(vector_in, far_src, far_tgt, far_left, far_right)
        return (near_part + far_part).reshape(vector_in.shape)

    def finish(vector_in):
        return own_columns(vector_in)

    def apply_op(vector_in):
        return 0.5 * vector_in + lax.psum(partial_image(vector_in), "far")

    def orthogonal(vectors, candidate):
        heights = lax.psum(jnp.stack([column_dots(item, candidate) for item in vectors]), "rows")
        for slot_id in range(len(vectors)):
            candidate = candidate - heights[slot_id] * vectors[slot_id]
        length = jnp.sqrt(lax.psum(column_dots(candidate, candidate), "rows") + EPS)
        return (heights, candidate, length)

    rhs_length = jnp.sqrt(lax.psum(column_dots(right_side, right_side), "rows") + EPS)
    first_full = right_side / rhs_length
    image_one = apply_op(first_full)
    heights_one, candidate, lower_left = orthogonal((first_full,), image_one)
    second_vec = candidate / lower_left
    image_two = apply_op(second_vec)
    heights_two, candidate, lower_right = orthogonal((first_full, second_vec), image_two)
    weight_one, weight_two = least_squares(
        rhs_length, heights_one[0], lower_left, heights_two, lower_right
    )
    own_solution = weight_one * first_full + weight_two * second_vec
    own_residual = right_side - weight_one * image_one - weight_two * image_two
    return (finish(own_solution), finish(own_residual))


def solution(mesh):
    return jax.shard_map(
        shards,
        mesh=mesh,
        in_specs=(
            P("rows", None),
            P("rows", "far", None, None),
            P("rows", "far"),
            P("rows", None, "far"),
            P("rows", None, "far"),
            P("rows", None, "far", None, None),
            P("rows", None, "far", None, None),
        ),
        out_specs=(P("rows", "far"), P("rows", "far")),
        check_vma=False,
    )
```

profile of v0, /device:TPU:0, one launch (start us, length us, event | category | flops | bytes accessed | tf_op | source)
XLA Modules:
  0.0 454.4 jit_solution(17679893587616139320)
XLA Ops:
  7.2 0.0 copy-start
  7.2 2.0 copy.35
  9.2 0.0 copy-start.6
  9.2 1.9 multiply_reduce_fusion.5
  11.1 23.1 %psum.49 = f32[256]{0:T(256)S(1)} all-reduce(f32[256]{0:T(256)S(1)} %multiply_reduce_fusion.5), channel_id=1, replica_groups=mesh['rows'=8,'far'=4] {'rows'}, use_global_device_ids=true, to_apply=%region_1.0 | all-reduce | flops 256 | bytes 2048 | tf_op jit(solution)/shard_map/psum | solution.py:102
  34.2 1.7 broadcast_divide_fusion.1
  35.9 2.9 copy.39
  38.8 2.2 gather_fusion.1
  41.0 2.6 convolution_bitcast_fusion.3
  43.6 4.1 all-to-all-start
  47.7 0.0 copy-start.4
  47.7 0.0 all-reduce.3.cloned.1.call-start
  47.8 3.1 fusion.41
  50.9 4.9 %collective-permute-start = (f32[1024,256]{0,1:T(8,128)}, f32[1024,256]{0,1:T(8,128)}, u32[]{:S(2)}, u32[]{:S(2)}) collective-permute-start(f32[1024,256]{0,1:T(8,128)} %get-tuple-element.15), channel_id=1, source_target_pairs={{0,4},{4,8},{8,12},{12,16},{16,20},{20,24},{24,28},{1,5},{5,9},{9,... | collective-permute-start | bytes 3145736 | tf_op jit(solution)/shard_map/ppermute | solution.py:23
  55.8 1.3 collective-permute-start.1
  57.2 0.1 copy.38
  57.2 0.1 reshape.164
  57.3 0.1 copy.36
  57.4 2.4 all-to-all-done
  59.8 3.0 convolution_bitcast_fusion.1
  62.8 1.4 copy.41
  64.2 3.8 fusion.29
  67.9 29.6 %collective-permute-done = f32[1024,256]{0,1:T(8,128)} collective-permute-done((f32[1024,256]{0,1:T(8,128)}, f32[1024,256]{0,1:T(8,128)}, u32[]{:S(2)}, u32[]{:S(2)}) %collective-permute-start) | collective-permute-done | bytes 1048608 | tf_op jit(solution)/shard_map/ppermute | solution.py:23
  97.5 0.0 collective-permute-done.1
  97.5 3.8 pad_maximum_fusion
  101.4 5.6 %copy.37 = f32[4096,256]{1,0:T(8,128)} copy(f32[4096,256]{0,1:T(8,128)} %pad_maximum_fusion) | data formatting | bytes 8388608 | tf_op jit(solution)/shard_map/concatenate | solution.py:21
  107.0 10.9 %gather_fusion = f32[96,128,256]{2,1,0:T(8,128)} fusion(f32[32,128,256]{2,1,0:T(8,128)} %bitcast.92, s32[1024]{0:T(1024)S(1)} %pad_clamp_fusion.1), kind=kCustom, calls=%fused_computation.clone | custom fusion | bytes 25166208 | tf_op jit(solution)/shard_map/jit(_take)/gather | solution.py:41
  117.9 20.4 %bitcast_add_fusion.1 = f32[16,128,256]{2,1,0:T(8,128)} fusion(f32[16,128,256]{2,0,1:T(8,128)} %fusion.29, f32[16,6,128,128]{3,2,1,0:T(8,128)} %param.12, f32[16,6,128,256]{3,2,1,0:T(8,128)} %bitcast.94, pred[16,6]{1,0:T(8,128)(4,1)S(1)} %copy.36), kind=kOutput, calls=%fused_computation.15 | convolution fusion | flops 4835508224 | bytes 23068768 | tf_op jit(solution)/shard_map/cspq,csqn->cpn/dot_general | solution.py:42
  138.3 2.9 copy.43
  141.2 0.0 all-reduce.3.cloned.1.call-update
  141.2 54.7 %all-reduce.3.cloned.1.call-done = f32[2048,256]{0,1:T(8,128)} async-done(((f32[2048,256]{0,1:T(8,128)}), f32[2048,256]{0,1:T(8,128)}) %all-reduce.3.cloned.1.call-update) | async-done | bytes 2097168 | tf_op jit(solution)/shard_map/psum | solution.py:93
  195.9 3.3 multiply_add_fusion.1
  199.2 21.3 %psum.51 = f32[256]{0:T(256)S(1)} all-reduce(f32[256]{0:T(256)S(1)} %get-tuple-element.12), channel_id=1, replica_groups=mesh['rows'=8,'far'=4] {'rows'}, use_global_device_ids=true, to_apply=%region_4.7 | all-reduce | flops 256 | bytes 2048 | tf_op jit(solution)/shard_map/psum | solution.py:96
  220.6 2.2 multiply_reduce_fusion.3
  222.8 17.4 %psum.52 = f32[256]{0:T(256)S(1)} all-reduce(f32[256]{0:T(256)S(1)} %multiply_reduce_fusion.3), channel_id=1, replica_groups=mesh['rows'=8,'far'=4] {'rows'}, use_global_device_ids=true, to_apply=%region_6.9 | all-reduce | flops 256 | bytes 2048 | tf_op jit(solution)/shard_map/psum | solution.py:99
  240.1 3.4 broadcast_divide_fusion
  243.6 2.9 copy.47
  246.5 2.2 gather_fusion.3
  248.7 2.6 convolution_bitcast_fusion.2
  251.3 4.1 all-to-all-start.1
  255.4 0.0 all-reduce.5.cloned.1.call-start
  255.5 3.1 fusion.40
  258.6 4.8 %collective-permute-start.2 = (f32[1024,256]{0,1:T(8,128)}, f32[1024,256]{0,1:T(8,128)}, u32[]{:S(2)}, u32[]{:S(2)}) collective-permute-start(f32[1024,256]{0,1:T(8,128)} %get-tuple-element.13), channel_id=1, source_target_pairs={{0,4},{4,8},{8,12},{12,16},{16,20},{20,24},{24,28},{1,5},{5,9},{9,... | collective-permute-start | bytes 3145736 | tf_op jit(solution)/shard_map/ppermute | solution.py:23
  263.4 1.3 collective-permute-start.3
  264.7 2.1 all-to-all-done.1
  266.8 3.0 convolution_bitcast_fusion
  269.7 1.4 copy.49
  271.1 3.8 fusion.27
  274.9 27.8 %collective-permute-done.2 = f32[1024,256]{0,1:T(8,128)} collective-permute-done((f32[1024,256]{0,1:T(8,128)}, f32[1024,256]{0,1:T(8,128)}, u32[]{:S(2)}, u32[]{:S(2)}) %collective-permute-start.2) | collective-permute-done | bytes 1048608 | tf_op jit(solution)/shard_map/ppermute | solution.py:23
  302.8 0.0 collective-permute-done.3
  302.8 3.8 pad_maximum_fusion.1
  306.6 5.6 %copy.45 = f32[4096,256]{1,0:T(8,128)} copy(f32[4096,256]{0,1:T(8,128)} %pad_maximum_fusion.1) | data formatting | bytes 8388608 | tf_op jit(solution)/shard_map/concatenate | solution.py:21
  312.3 10.9 %gather_fusion.2 = f32[96,128,256]{2,1,0:T(8,128)} fusion(f32[32,128,256]{2,1,0:T(8,128)} %bitcast.91, s32[1024]{0:T(1024)S(1)} %pad_clamp_fusion.1), kind=kCustom, calls=%fused_computation.2.clone | custom fusion | bytes 25166208 | tf_op jit(solution)/shard_map/jit(_take)/gather | solution.py:41
  323.2 20.4 %bitcast_add_fusion = f32[16,128,256]{2,1,0:T(8,128)} fusion(f32[16,128,256]{2,0,1:T(8,128)} %fusion.27, f32[16,6,128,128]{3,2,1,0:T(8,128)} %param.12, f32[16,6,128,256]{3,2,1,0:T(8,128)} %bitcast.93, pred[16,6]{1,0:T(8,128)(4,1)S(1)} %copy.36), kind=kOutput, calls=%fused_computation.14 | convolution fusion | flops 4835508224 | bytes 23068768 | tf_op jit(solution)/shard_map/cspq,csqn->cpn/dot_general | solution.py:42
  343.6 2.9 copy.51
  346.5 0.0 all-reduce.5.cloned.1.call-update
  346.6 52.7 %all-reduce.5.cloned.1.call-done = f32[2048,256]{0,1:T(8,128)} async-done(((f32[2048,256]{0,1:T(8,128)}), f32[2048,256]{0,1:T(8,128)}) %all-reduce.5.cloned.1.call-update) | async-done | bytes 2097168 | tf_op jit(solution)/shard_map/psum | solution.py:93
  399.3 4.0 multiply_reduce_fusion.2
  403.2 21.4 %psum.54 = f32[2,256]{1,0:T(2,128)S(1)} all-reduce(f32[2,256]{1,0:T(2,128)S(1)} %pad_maximum_fusion.2), channel_id=1, replica_groups=mesh['rows'=8,'far'=4] {'rows'}, use_global_device_ids=true, to_apply=%region_10.13 | all-reduce | flops 512 | bytes 4096 | tf_op jit(solution)/shard_map/psum | solution.py:96
  424.6 2.9 multiply_reduce_fusion
  427.5 17.1 %psum.55 = f32[256]{0:T(256)S(1)} all-reduce(f32[256]{0:T(256)S(1)} %multiply_reduce_fusion), channel_id=1, replica_groups=mesh['rows'=8,'far'=4] {'rows'}, use_global_device_ids=true, to_apply=%region_12.15 | all-reduce | flops 256 | bytes 2048 | tf_op jit(solution)/shard_map/psum | solution.py:99
  444.7 0.1 dynamic-slice
  444.8 0.1 dynamic-slice.1
  444.8 2.8 fusion.14
  (21 shorter events, 0.1 us)
Async XLA Ops:
  7.2 52.6 %copy-start = (f32[1,8,1,128,64]{3,4,2,1,0:T(8,128)S(1)}, f32[1,8,1,128,64]{3,4,2,1,0:T(8,128)}, u32[]{:S(2)}) copy-start(f32[1,8,1,128,64]{3,4,2,1,0:T(8,128)} %param.16) | copy-start | bytes 786436
  9.2 1.9 copy-start.6
  43.6 16.2 %all-to-all-start = ((f32[8,1,64,256]{3,2,1,0:T(8,128)}), f32[8,1,64,256]{3,2,1,0:T(8,128)}, u32[]{:S(2)}, u32[]{:S(2)}) async-start(f32[8,1,64,256]{3,2,1,0:T(8,128)} %convolution_bitcast_fusion.3), calls=%async_computation | async-start | bytes 1048576 | tf_op jit(solution)/shard_map/all_to_all | solution.py:55
  47.7 9.4 %copy-start.4 = (s32[16,6]{0,1:T(8,128)S(1)}, s32[16,6]{0,1:T(8,128)}, u32[]{:S(2)}) copy-start(s32[16,6]{0,1:T(8,128)} %param.13) | copy-start | bytes 1156
  47.7 148.2 %all-reduce.3.cloned.1.call-start = ((), (), s32[]{:S(2)}) async-start(), calls=%async_computation.2 | async-start | bytes 4194304 | tf_op jit(solution)/shard_map/psum | solution.py:93
  50.9 13.2 %copy-start.5 = (s32[1,8,1]{1,2,0:T(1,128)S(1)}, s32[1,8,1]{1,2,0:T(1,128)}, u32[]{:S(2)}) copy-start(s32[1,8,1]{1,2,0:T(1,128)} %param.15) | copy-start | bytes 100
  50.9 46.6 %collective-permute-start = (f32[1024,256]{0,1:T(8,128)}, f32[1024,256]{0,1:T(8,128)}, u32[]{:S(2)}, u32[]{:S(2)}) collective-permute-start(f32[1024,256]{0,1:T(8,128)} %get-tuple-element.15), channel_id=1, source_target_pairs={{0,4},{4,8},{8,12},{12,16},{16,20},{20,24},{24,28},{1,5},{5,9},{9,... | collective-permute-start | bytes 3145736 | tf_op jit(solution)/shard_map/ppermute | solution.py:23
  55.8 41.7 %collective-permute-start.1 = (f32[1024,256]{0,1:T(8,128)}, f32[1024,256]{0,1:T(8,128)}, u32[]{:S(2)}, u32[]{:S(2)}) collective-permute-start(f32[1024,256]{0,1:T(8,128)} %get-tuple-element.16), channel_id=1, source_target_pairs={{4,0},{8,4},{12,8},{16,12},{20,16},{24,20},{28,24},{5,1},{9,5},{13... | collective-permute-start | bytes 3145736 | tf_op jit(solution)/shard_map/ppermute | solution.py:25
  64.2 33.3 %copy-start.3 = (f32[2048,256]{0,1:T(8,128)S(1)}, f32[2048,256]{0,1:T(8,128)}, u32[]{:S(2)}) copy-start(f32[2048,256]{0,1:T(8,128)} %broadcast_divide_fusion.1) | copy-start | bytes 6291460
  251.3 15.5 %all-to-all-start.1 = ((f32[8,1,64,256]{3,2,1,0:T(8,128)}), f32[8,1,64,256]{3,2,1,0:T(8,128)}, u32[]{:S(2)}, u32[]{:S(2)}) async-start(f32[8,1,64,256]{3,2,1,0:T(8,128)} %convolution_bitcast_fusion.2), calls=%async_computation.1 | async-start | bytes 1048576 | tf_op jit(solution)/shard_map/all_to_all | solution.py:55
  255.4 143.8 %all-reduce.5.cloned.1.call-start = ((), (), s32[]{:S(2)}) async-start(), calls=%async_computation.3 | async-start | bytes 4194304 | tf_op jit(solution)/shard_map/psum | solution.py:93
  258.6 44.2 %collective-permute-start.2 = (f32[1024,256]{0,1:T(8,128)}, f32[1024,256]{0,1:T(8,128)}, u32[]{:S(2)}, u32[]{:S(2)}) collective-permute-start(f32[1024,256]{0,1:T(8,128)} %get-tuple-element.13), channel_id=1, source_target_pairs={{0,4},{4,8},{8,12},{12,16},{16,20},{20,24},{24,28},{1,5},{5,9},{9,... | collective-permute-start | bytes 3145736 | tf_op jit(solution)/shard_map/ppermute | solution.py:23
  263.4 39.4 %collective-permute-start.3 = (f32[1024,256]{0,1:T(8,128)}, f32[1024,256]{0,1:T(8,128)}, u32[]{:S(2)}, u32[]{:S(2)}) collective-permute-start(f32[1024,256]{0,1:T(8,128)} %get-tuple-element.14), channel_id=1, source_target_pairs={{4,0},{8,4},{12,8},{16,12},{20,16},{24,20},{28,24},{5,1},{9,5},{13... | collective-permute-start | bytes 3145736 | tf_op jit(solution)/shard_map/ppermute | solution.py:25
  271.1 31.7 %copy-start.2 = (f32[2048,256]{0,1:T(8,128)S(1)}, f32[2048,256]{0,1:T(8,128)}, u32[]{:S(2)}) copy-start(f32[2048,256]{0,1:T(8,128)} %broadcast_divide_fusion) | copy-start | bytes 6291460
  424.6 23.0 %copy-start.1 = (f32[1,8,1,128,64]{3,4,2,1,0:T(8,128)S(1)}, f32[1,8,1,128,64]{3,4,2,1,0:T(8,128)}, u32[]{:S(2)}) copy-start(f32[1,8,1,128,64]{3,4,2,1,0:T(8,128)} %param.16) | copy-start | bytes 786436
Sparse Core Ops, SparseCore 0:
  141.4 54.5 all-reduce.2
  346.7 52.5 all-reduce.4
where the time goes:
time: 456 us; the launch traced here: 454 us
  waiting for transfers between devices  169 us (37%)
  blocking collectives  100 us (22%)
  local copies, waits for them, and re-layouts  60.7 us (13%)
  matrix products  59.5 us (13%)
  other arithmetic  29.9 us (7%)
  starting transfers between devices  20.6 us (5%)
  between operations  14.2 us (3%)
    psum x2, waiting for transfers between devices, apply_op(): return 0.5 * vector_in + lax.psum(partial_image(vector_in), 'far')  107 us
    ppermute x2, waiting for transfers between devices, with_halo(): lax.ppermute(tail, axis, [(i, (i + 1) % count) for i in range(ends)])  57.4 us
    psum x2, blocking collectives, orthogonal(): lax.psum(jnp.stack([column_dots(item, candidate) for item in vectors]), '...  42.7 us
    dot_general x2, matrix products, near_term(): jnp.einsum('cspq,csqn->cpn', near_blocks, picked, precision=TOP_PRECISION)  40.8 us
    psum x2, blocking collectives, orthogonal(): length = jnp.sqrt(lax.psum(column_dots(candidate, candidate), 'rows') + EPS)  34.5 us
    psum x1, blocking collectives, shards(): lax.psum(column_dots(right_side, right_side), 'rows') + EPS  23.1 us
    gather x2, local copies, waits for them, and re-layouts, near_term(): picked = jnp.take(clusters, near_cols - offset, axis=0)  21.8 us
    concatenate x2, local copies, waits for them, and re-layouts, with_halo(): jnp.concatenate([lax.ppermute(tail, axis, [(i, (i + 1) % count) for i in...  11.3 us
  transfers between devices with their start and end apart: 8, of which 6 were waited for; matrix products, arithmetic and copies ran while one was open for 5% of the time, Pallas kernels for 0%

commit v1 on v0

v1 whole, which is shorter than its diff:
```python
import functools

import jax
import jax.numpy as jnp
from jax import lax
from jax.experimental import pallas as pl
from jax.experimental.pallas import tpu as pltpu
from jax.sharding import PartitionSpec as P

B = 128
R = 64
CL_DEV = 16
REACH = 8
CORES = 2
LANES = 128
EPS = 1e-06
F32 = jnp.float32
BF16 = jnp.bfloat16
VMEM_LIMIT = 48 * 1024 * 1024

VMEM_SPEC = pl.BlockSpec(memory_space=pltpu.VMEM)
SMEM_SPEC = pl.BlockSpec(memory_space=pltpu.SMEM)


def split(value):
    high = value.astype(BF16)
    low = (value - high.astype(F32)).astype(BF16)
    return high, low


def dot3(left, right, dims):
    (lh, ll), (rh, rl) = left, right
    dot = functools.partial(lax.dot_general, dimension_numbers=(dims, ((), ())), preferred_element_type=F32)
    return dot(lh, rh) + (dot(ll, rh) + dot(lh, rl))


def far_place(far_size):
    index = lax.axis_index("far")
    return index // CORES, index % CORES, far_size // CORES


def owner_at(shift, other_core, far_size):
    y, core, ys = far_place(far_size)
    return lax.rem(y - shift + ys, ys) * CORES + (1 - core if other_core else core)


def place_own(pieces, far_size, store):
    q = REACH // far_size
    ys = far_size // CORES
    for n, piece in enumerate(pieces):
        owner = owner_at(n % ys, n >= ys, far_size)
        for half in range(2):
            for j in range(q):
                store(half * REACH + owner * q + j, piece[half * q + j])


def coefficient_kernel(far_size, whole, src_ref, right_ref, *refs):
    pieces, (out_ref, held) = refs[:-2], refs[-2:]
    if whole:
        field = pieces[0]
    else:
        field = held

        def store(cluster, value):
            held[cluster] = value

        place_own(pieces, far_size, store)
    for t in range(right_ref.shape[0]):
        factor = split(right_ref[t])
        source = split(field[src_ref[t]])
        out_ref[t] = dot3(factor, source, (((0,), (0,))))


def coefficients(pieces, src, right, far_size):
    whole = len(pieces) == 1
    groups, _, rank = right.shape
    cols = pieces[0].shape[-1]
    held = (8, LANES) if whole else (CL_DEV, B, cols)
    return pl.pallas_call(
        functools.partial(coefficient_kernel, far_size, whole),
        out_shape=jax.ShapeDtypeStruct((groups, rank, cols), F32),
        in_specs=[SMEM_SPEC, VMEM_SPEC] + [VMEM_SPEC] * len(pieces),
        out_specs=VMEM_SPEC,
        scratch_shapes=[pltpu.VMEM(held, F32)],
        compiler_params=pltpu.CompilerParams(vmem_limit_bytes=VMEM_LIMIT),
        cost_estimate=pl.CostEstimate(
            flops=6 * groups * rank * B * cols, bytes_accessed=4 * CL_DEV * B * cols, transcendentals=0
        ),
        name="coefficients",
    )(src, right, *pieces)


def operator_kernel(
    far_size, last, n_pieces, cols_ref, tgt_ref, blocks_ref, coef_ref, left_ref, *refs
):
    pieces = refs[:n_pieces]
    keep_ref, send_ref, high, low, far_acc = refs[n_pieces:]
    step = pl.program_id(0)
    y, core, ys = far_place(far_size)
    q = REACH // far_size
    groups = blocks_ref.shape[0]
    slots = blocks_ref.shape[2]
    per = CL_DEV // groups
    base = lax.axis_index("rows") * CL_DEV - REACH

    def put(position, value):
        h, l = split(value)
        high[position] = h
        low[position] = l

    @pl.when(step == 0)
    def _():
        if not last:
            own, left_mine, right_mine, left_other, right_other = pieces
            for c in range(CL_DEV):
                put(REACH + c, own[c])
            part = REACH // CORES
            for c, lefts, rights in ((core, left_mine, right_mine), (1 - core, left_other, right_other)):
                for j in range(part):
                    put(c * part + j, lefts[j])
                    put(REACH + CL_DEV + c * part + j, rights[j])
        else:
            n_own = CORES * ys
            place_own(pieces[:n_own], far_size, lambda c, v: put(REACH + c, v))
            for n in range(n_own):
                owner = owner_at(n % ys, n >= ys, far_size)
                lefts, rights = pieces[n_own + 2 * n], pieces[n_own + 2 * n + 1]
                for j in range(q):
                    put(owner * q + j, lefts[j])
                    put(REACH + CL_DEV + owner * q + j, rights[j])
        far_acc[...] = jnp.zeros_like(far_acc)
        for a in range(left_ref.shape[0]):
            target = tgt_ref[a]
            far_acc[target] += dot3(split(left_ref[a]), split(coef_ref[a]), (((1,), (0,))))

    def image(group):
        cluster = group * per + step
        at = [cols_ref[cluster * slots + s] - base for s in range(slots)]
        left = split(jnp.concatenate([blocks_ref[group, 0, s] for s in range(slots)], axis=1))
        right = tuple(jnp.concatenate([ref[p] for p in at], axis=0) for ref in (high, low))
        return far_acc[cluster] + dot3(left, right, (((1,), (0,))))

    images = [image(g) for g in range(groups)]
    if not last:
        owner = step // q
        behind = lax.rem(owner // CORES - y + ys, ys)
        mine = owner % CORES == core

        for half in range(2):
            slot = half * q + step % q

            @pl.when(mine)
            def _():
                keep_ref[behind, slot] = images[half]

            @pl.when(jnp.logical_not(mine))
            def _():
                send_ref[behind, slot] = images[half]
    else:
        width = LANES // groups
        for owner in range(far_size):
            packed = jnp.concatenate(
                [im[:, owner * width : (owner + 1) * width] for im in images], axis=1
            )
            behind = lax.rem(owner // CORES - y + ys, ys)
            mine = owner % CORES == core

            @pl.when(mine)
            def _():
                keep_ref[behind, step] = packed

            @pl.when(jnp.logical_not(mine))
            def _():
                send_ref[behind, step] = packed


def operator(pieces, cols, tgt, blocks, coef, left, far_size, last):
    width = pieces[0].shape[-1]
    slots = blocks.shape[1]
    ys = far_size // CORES
    if last:
        groups = LANES * far_size // width
        part = (ys, CL_DEV // groups, B, LANES)
    else:
        groups = 2
        part = (ys, 2 * REACH // far_size, B, width)
    steps = CL_DEV // groups
    blocks = blocks.reshape(groups, steps, slots, B, B)
    return pl.pallas_call(
        functools.partial(operator_kernel, far_size, last, len(pieces)),
        out_shape=[jax.ShapeDtypeStruct(part, F32)] * 2,
        grid=(steps,),
        in_specs=[
            SMEM_SPEC,
            SMEM_SPEC,
            pl.BlockSpec((groups, 1, slots, B, B), lambda i: (0, i, 0, 0, 0)),
            VMEM_SPEC,
            VMEM_SPEC,
        ]
        + [VMEM_SPEC] * len(pieces),
        out_specs=[VMEM_SPEC] * 2,
        scratch_shapes=[
            pltpu.VMEM((CL_DEV + 2 * REACH, B, width), BF16),
            pltpu.VMEM((CL_DEV + 2 * REACH, B, width), BF16),
            pltpu.VMEM((CL_DEV, B, width), F32),
        ],
        compiler_params=pltpu.CompilerParams(vmem_limit_bytes=VMEM_LIMIT),
        cost_estimate=pl.CostEstimate(
            flops=6 * CL_DEV * slots * B * B * width, bytes_accessed=4 * blocks.size, transcendentals=0
        ),
        name="operator",
    )(cols, tgt, blocks, coef, left, *pieces)


def pack_kernel(far_size, own_ref, *refs):
    pieces, (b_out, g_out, held) = refs[:-3], refs[-3:]
    index = lax.axis_index("far")
    groups = CL_DEV // b_out.shape[0]
    width = LANES // groups
    per = CL_DEV // groups

    def store(cluster, value):
        held[cluster] = value

    place_own(pieces, far_size, store)
    for owner in range(far_size):

        @pl.when(index == owner)
        def _():
            for k in range(per):
                for source, out in ((own_ref, b_out), (held, g_out)):
                    out[k] = jnp.concatenate(
                        [
                            source[g * per + k][:, owner * width : (owner + 1) * width]
                            for g in range(groups)
                        ],
                        axis=1,
                    )


def pack(own, pieces, far_size):
    width = own.shape[-1]
    groups = LANES * far_size // width
    part = jax.ShapeDtypeStruct((CL_DEV // groups, B, LANES), F32)
    return pl.pallas_call(
        functools.partial(pack_kernel, far_size),
        out_shape=[part] * 2,
        in_specs=[VMEM_SPEC] * (1 + len(pieces)),
        out_specs=[VMEM_SPEC] * 2,
        scratch_shapes=[pltpu.VMEM((CL_DEV, B, width), F32)],
        compiler_params=pltpu.CompilerParams(vmem_limit_bytes=VMEM_LIMIT),
        cost_estimate=pl.CostEstimate(flops=0, bytes_accessed=8 * own.size, transcendentals=0),
        name="pack",
    )(own, *pieces)


def dots_kernel(groups, n_parts, b_ref, g_ref, *refs):
    parts, (out_ref, image_ref) = refs[:n_parts], refs[n_parts:]
    image = parts[0][...]
    for part in parts[1:]:
        image = image + part[...]
    image_ref[...] = image
    vectors = (b_ref[...], g_ref[...], image)
    width = LANES // groups
    rows = []
    for left, right in ((0, 0), (0, 1), (0, 2), (1, 1), (1, 2), (2, 2)):
        total = jnp.sum(vectors[left] * vectors[right], axis=0)
        total = jnp.sum(total, axis=0, keepdims=True)
        folded = total
        for g in range(1, groups):
            folded = folded + pltpu.roll(total, g * width, 1)
        rows.append(folded)
    rows.append(jnp.zeros((2, LANES), F32))
    out_ref[...] = jnp.concatenate(rows, axis=0)


def dots(b_own, g_own, parts, groups):
    return pl.pallas_call(
        functools.partial(dots_kernel, groups, len(parts)),
        out_shape=[
            jax.ShapeDtypeStruct((8, LANES), F32),
            jax.ShapeDtypeStruct(b_own.shape, F32),
        ],
        in_specs=[VMEM_SPEC] * (2 + len(parts)),
        out_specs=[VMEM_SPEC] * 2,
        compiler_params=pltpu.CompilerParams(vmem_limit_bytes=VMEM_LIMIT),
        cost_estimate=pl.CostEstimate(
            flops=14 * b_own.size, bytes_accessed=20 * b_own.size, transcendentals=0
        ),
        name="dots",
    )(b_own, g_own, *parts)


def least_squares(rhs_length, upper_left, lower_left, top_two, mid_two, lower_right):
    radius_one = jnp.sqrt(upper_left * upper_left + lower_left * lower_left)
    cosine_one = upper_left / radius_one
    sine_one = lower_left / radius_one
    rotated_top = cosine_one * rhs_length
    rotated_mid = -sine_one * rhs_length
    coupled = cosine_one * top_two + sine_one * mid_two
    diagonal_two = cosine_one * mid_two - sine_one * top_two
    radius_two = jnp.sqrt(diagonal_two * diagonal_two + lower_right * lower_right)
    weight_two = diagonal_two * rotated_mid / (radius_two * radius_two)
    weight_one = (rotated_top - coupled * weight_two) / radius_one
    return (weight_one, weight_two)


def finish_kernel(groups, dots_ref, b_ref, g_ref, image_ref, solution_ref, residual_ref):
    bb, b1, b2, s11, s12, s22 = [dots_ref[i : i + 1, :] for i in range(6)]
    square = bb + EPS
    rhs_length = jnp.sqrt(square)
    upper_left = (0.5 * bb + b1) / square
    shift = (0.5 * EPS - b1) / square
    one = jnp.maximum(shift * shift * bb + 2.0 * shift * b1 + s11, 0.0) / square
    lower_square = one + EPS
    lower_left = jnp.sqrt(lower_square)
    f_s = (shift * bb + b1) / (square * lower_left)
    f_gs = (shift * b1 + b2) / (square * lower_left)
    s_s = one / lower_square
    s_gs = (shift * shift * b1 + shift * b2 + shift * s11 + s12) / (square * lower_square)
    gs_gs = (shift * shift * s11 + 2.0 * shift * s12 + s22) / (square * lower_square)
    top_two = 0.5 * f_s + f_gs
    mid_two = 0.5 * s_s + s_gs
    rest = 0.5 * (EPS / lower_square) - s_gs
    two = (
        gs_gs
        + top_two * top_two * (bb / square)
        + rest * rest * s_s
        - 2.0 * top_two * f_gs
        + 2.0 * rest * s_gs
        - 2.0 * top_two * rest * f_s
    )
    lower_right = jnp.sqrt(jnp.maximum(two, 0.0) + EPS)
    weight_one, weight_two = least_squares(
        rhs_length, upper_left, lower_left, top_two, mid_two, lower_right
    )
    one_scale = weight_one / rhs_length
    two_scale = weight_two / (rhs_length * lower_left)
    sol_b = one_scale + two_scale * shift
    res_b = 1.0 - 0.5 * one_scale - 0.5 * two_scale * shift
    res_1 = one_scale + two_scale * (0.5 + shift)
    width = LANES // groups
    per = b_ref.shape[0]
    for k in range(per):
        b, g, image = b_ref[k], g_ref[k], image_ref[k]
        answer = sol_b * b + two_scale * g
        left = res_b * b - res_1 * g - two_scale * image
        for j in range(groups):
            cut = slice(j * width, (j + 1) * width)
            solution_ref[j * per + k] = answer[:, cut]
            residual_ref[j * per + k] = left[:, cut]


def finish(total, b_own, g_own, image, groups):
    part = jax.ShapeDtypeStruct((CL_DEV, B, LANES // groups), F32)
    return pl.pallas_call(
        functools.partial(finish_kernel, groups),
        out_shape=[part] * 2,
        in_specs=[VMEM_SPEC] * 4,
        out_specs=[VMEM_SPEC] * 2,
        compiler_params=pltpu.CompilerParams(vmem_limit_bytes=VMEM_LIMIT),
        cost_estimate=pl.CostEstimate(
            flops=8 * b_own.size, bytes_accessed=28 * b_own.size, transcendentals=0
        ),
        name="finish",
    )(total, b_own, g_own, image)


def swap_cores(value):
    size = lax.axis_size("far")
    return lax.ppermute(value, "far", [(i, i ^ 1) for i in range(size)])


def along_y(value, shift):
    size = lax.axis_size("far")
    return lax.ppermute(value, "far", [(i, (i + CORES * shift) % size) for i in range(size)])


def to_next(value):
    return lax.ppermute(value, "rows", [(i, i + 1) for i in range(lax.axis_size("rows") - 1)])


def to_previous(value):
    return lax.ppermute(value, "rows", [(i + 1, i) for i in range(lax.axis_size("rows") - 1)])


def sum_rows(value):
    size = lax.axis_size("rows")
    step = 1
    while step < size:
        value = value + lax.ppermute(value, "rows", [(i, i ^ step) for i in range(size)])
        step *= 2
    return value


def sum_far(keep, send):
    ys = lax.axis_size("far") // CORES
    got = swap_cores(send)
    mine = [keep[0], got[0]]
    for shift in range(1, ys):
        mine.append(along_y(keep[shift] + got[shift], shift))
    return mine


def shards(right_side, near_blocks, near_cols, far_src, far_tgt, far_left, far_right):
    far_size = lax.axis_size("far")
    ys = far_size // CORES
    q = REACH // far_size
    width = right_side.shape[1]
    groups = LANES * far_size // width
    core = lax.axis_index("far") % CORES
    cols = near_cols.reshape(-1)
    src, tgt = far_src.reshape(-1), far_tgt.reshape(-1)
    left = far_left.reshape(far_left.shape[1], B, R)
    right = far_right.reshape(far_right.shape[1], B, R)

    def exchange(coef):
        return lax.all_to_all(coef, "rows", split_axis=0, concat_axis=0, tiled=True)

    own = right_side.reshape(CL_DEV, B, width)
    part = REACH // CORES
    tail = lax.dynamic_slice_in_dim(own, CL_DEV - REACH + core * part, part, 0)
    head = lax.dynamic_slice_in_dim(own, core * part, part, 0)
    from_left, from_right = to_next(tail), to_previous(head)
    coef = exchange(coefficients([own], src, right, far_size))
    pieces = [own, from_left, from_right, swap_cores(from_left), swap_cores(from_right)]
    keep, send = operator(pieces, cols, tgt, near_blocks, coef, left, far_size, False)
    mine = sum(sum_far(keep, send))

    from_left, from_right = to_next(mine[q:]), to_previous(mine[:q])
    owns = [mine] + [along_y(mine, s) for s in range(1, ys)]
    owns += [swap_cores(item) for item in owns]
    coef = exchange(coefficients(owns, src, right, far_size))
    halos = [(from_left, from_right)]
    halos += [(along_y(from_left, s), along_y(from_right, s)) for s in range(1, ys)]
    halos += [(swap_cores(a), swap_cores(b)) for a, b in halos]
    pieces = owns + [item for pair in halos for item in pair]
    keep, send = operator(pieces, cols, tgt, near_blocks, coef, left, far_size, True)
    b_own, g_own = pack(own, owns, far_size)
    part_dots, image = dots(b_own, g_own, sum_far(keep, send), groups)
    answer, residual = finish(sum_rows(part_dots), b_own, g_own, image, groups)
    shape = (CL_DEV * B, width // far_size)
    return answer.reshape(shape), residual.reshape(shape)


def solution(mesh):
    return jax.shard_map(
        shards,
        mesh=mesh,
        in_specs=(
            P("rows", None),
            P("rows", "far", None, None),
            P("rows", "far"),
            P("rows", None, "far"),
            P("rows", None, "far"),
            P("rows", None, "far", None, None),
            P("rows", None, "far", None, None),
        ),
        out_specs=(P("rows", "far"), P("rows", "far")),
        check_vma=False,
    )
```

time: 456 us -> 181 us (0.40)
  blocking collectives: 100 us -> 0 us
  waiting for transfers between devices: 169 us -> 83.6 us
  matrix products: 59.5 us -> 0 us
  local copies, waits for them, and re-layouts: 60.7 us -> 22.3 us
  other arithmetic: 29.9 us -> 1.71 us
  Pallas kernels: 0 us -> 25.8 us
  starting transfers between devices: 20.6 us -> 45.6 us
  between operations: 14.2 us -> 0.85 us
    psum x2 -> x0, waiting for transfers between devices: 107 us -> none  [apply_op(): return 0.5 * vector_in + lax.psum(partial_image(vector_in), 'far')]
    psum x5 -> x0, blocking collectives: 100 us -> none  [the longest x2 42.7 us: orthogonal(): lax.psum(jnp.stack([column_dots(item, candidate) for item in vectors]), '...]
    dot_general x8 -> x0, matrix products: 59.5 us -> none  [the longest x2 40.8 us: near_term(): jnp.einsum('cspq,csqn->cpn', near_blocks, picked, precision=TOP_PRECISION)]
    gather x4 -> x0, local copies, waits for them, and re-layouts: 26.2 us -> none  [the longest x2 21.8 us: near_term(): picked = jnp.take(clusters, near_cols - offset, axis=0)]
    pallas_call x0 -> x7, Pallas kernels: none -> 25.8 us  [the longest x2 21.5 us: operator(): pl.pallas_call(functools.partial(operator_kernel, far_size, last, len(pie...]
    ppermute x4 -> x22, waiting for transfers between devices: 57.4 us -> 82.7 us  [the longest x5 42.3 us: along_y(): lax.ppermute(value, 'far', [(i, (i + CORES * shift) % size) for i in rang...]
    ppermute x4 -> x22, starting transfers between devices: 12.2 us -> 33.5 us  [the longest x3 10.9 us: sum_rows(): lax.ppermute(value, 'rows', [(i, i ^ step) for i in range(size)])]
    unnamed x15 -> x55, local copies, waits for them, and re-layouts: 2.01 us -> 19.7 us
  transfers between devices with their start and end apart: 8 -> 24, of which waited for: 6 -> 16; matrix products, arithmetic and copies ran while one was open for 5% -> 1% of each run, Pallas kernels for 0% -> 1%
where the time goes in v1:
time: 181 us; the launch traced here: 180 us
  waiting for transfers between devices  83.6 us (46%)
  starting transfers between devices  45.6 us (25%)
  Pallas kernels  25.8 us (14%)
  local copies, waits for them, and re-layouts  22.3 us (12%)
    ppermute x5, waiting for transfers between devices, along_y(): lax.ppermute(value, 'far', [(i, (i + CORES * shift) % size) for i in rang...  42.3 us
    pallas_call x2, Pallas kernels, operator(): pl.pallas_call(functools.partial(operator_kernel, far_size, last, len(pie...  21.5 us
    unnamed x55, local copies, waits for them, and re-layouts  19.7 us
    ppermute x2, waiting for transfers between devices, to_next(): lax.ppermute(value, 'rows', [(i, i + 1) for i in range(lax.axis_size('row...  18.4 us
    all_to_all x2, starting transfers between devices, exchange(): return lax.all_to_all(coef, 'rows', split_axis=0, concat_axis=0, tiled=True)  12.1 us
    ppermute x3, starting transfers between devices, sum_rows(): lax.ppermute(value, 'rows', [(i, i ^ step) for i in range(size)])  10.9 us
    ppermute x2, starting transfers between devices, to_next(): lax.ppermute(value, 'rows', [(i, i + 1) for i in range(lax.axis_size('row...  10.9 us
    ppermute x2, waiting for transfers between devices, to_previous(): lax.ppermute(value, 'rows', [(i + 1, i) for i in range(lax.axis_size('row...  9.38 us
  transfers between devices with their start and end apart: 24, of which 16 were waited for; matrix products, arithmetic and copies ran while one was open for 1% of the time, Pallas kernels for 1%

profile of v1, /device:TPU:0, one launch (start us, length us, event | category | flops | bytes accessed | tf_op | source)
XLA Modules:
  0.0 179.8 jit_solution(11116397834955370420)
XLA Ops:
  0.7 2.4 %constant_dynamic-slice_fusion = (f32[4,128,256]{2,1,0:T(8,128)}, f32[4,128,256]{2,1,0:T(8,128)}) fusion(f32[16,128,256]{2,1,0:T(8,128)} %bitcast.20, s32[]{:T(128)S(6)} %select_n.15, s32[]{:T(128)S(6)} %select_n.14), kind=kLoop, calls=%fused_computation.9 | loop fusion | bytes 2097160 | tf_op jit(solution)/shard_map/dynamic_slice | solution.py:423
  3.1 1.3 collective-permute-start.1
  4.4 6.3 %collective-permute-start = (f32[4,128,256]{2,1,0:T(8,128)}, f32[4,128,256]{2,1,0:T(8,128)}, u32[]{:S(2)}, u32[]{:S(2)}) collective-permute-start(f32[4,128,256]{2,1,0:T(8,128)} %get-tuple-element.27), channel_id=1, source_target_pairs={{0,4},{4,8},{8,12},{12,16},{16,20},{20,24},{24,28},{1,5},{5,9},{9,... | collective-permute-start | bytes 1572872 | tf_op jit(solution)/shard_map/ppermute | solution.py:380
  10.7 1.1 copy.15
  11.9 1.8 coefficients.2
  13.6 5.4 %all-to-all-start = ((f32[8,64,256]{2,1,0:T(8,128)}), f32[8,64,256]{2,1,0:T(8,128)S(1)}, u32[]{:S(2)}, u32[]{:S(2)}) async-start(f32[8,64,256]{2,1,0:T(8,128)} %coefficients.2), calls=%async_computation | async-start | bytes 1048576 | tf_op jit(solution)/shard_map/all_to_all | solution.py:418
  19.0 1.0 collective-permute-done.1.refs_2_
  20.0 15.8 %collective-permute-done.refs_1_ = f32[4,128,256]{2,1,0:T(8,128)} collective-permute-done((f32[4,128,256]{2,1,0:T(8,128)}, f32[4,128,256]{2,1,0:T(8,128)}, u32[]{:S(2)}, u32[]{:S(2)}) %collective-permute-start) | collective-permute-done | bytes 524320 | tf_op jit(solution)/shard_map/ppermute | solution.py:380
  36.0 0.2 copy.16
  36.2 0.9 all-to-all-done.coef_ref
  37.1 0.8 copy-done.3
  37.9 0.8 copy-done.5
  38.7 1.0 copy-done.4
  39.8 1.0 copy-done.6
  40.8 9.7 %operator.2 = (f32[2,4,128,256]{3,2,1,0:T(8,128)S(1)}, f32[2,4,128,256]{3,2,1,0:T(8,128)S(1)}) custom-call(s32[96]{0:T(128)S(1)} %reshape.36.cols_ref, s32[8]{0:T(128)S(1)} %bitcast.30, f32[2,8,6,128,128]{4,3,2,1,0:T(8,128)} %bitcast.34, f32[8,64,256]{2,1,0:T(8,128)S(1)} %all-to-all-done.coef_ref, f32[8,128,64]{2,1,0:T(8,128)S(1)} %bitcast.24, ...), custom_call_target="tpu_custom_call" | custom-call | flops 2415919104 | bytes 6291456 | tf_op jit(solution)/shard_map/operator/pallas_call | solution.py:189
  50.8 2.5 %collective-permute-done.4 = f32[2,4,128,256]{3,2,1,0:T(8,128)S(1)} collective-permute-done((f32[2,4,128,256]{3,2,1,0:T(8,128)S(1)}, f32[2,4,128,256]{3,2,1,0:T(8,128)S(1)}, u32[]{:S(2)}, u32[]{:S(2)}) %collective-permute-start.4) | collective-permute-done | bytes 1048608 | tf_op jit(solution)/shard_map/ppermute | solution.py:371
  53.4 1.6 collective-permute-start.5
  55.0 12.4 %collective-permute-done.5 = f32[4,128,256]{2,1,0:T(8,128)S(1)} collective-permute-done((f32[4,128,256]{2,1,0:T(8,128)S(1)}, f32[4,128,256]{2,1,0:T(8,128)S(1)}, u32[]{:S(2)}, u32[]{:S(2)}) %collective-permute-start.5) | collective-permute-done | bytes 524320 | tf_op jit(solution)/shard_map/ppermute | solution.py:376
  67.5 1.6 collective-permute-start.6
  69.1 11.6 %collective-permute-done.6.refs_1_ = f32[4,128,256]{2,1,0:T(8,128)S(1)} collective-permute-done((f32[4,128,256]{2,1,0:T(8,128)S(1)}, f32[4,128,256]{2,1,0:T(8,128)S(1)}, u32[]{:S(2)}, u32[]{:S(2)}) %collective-permute-start.6) | collective-permute-done | bytes 524320 | tf_op jit(solution)/shard_map/ppermute | solution.py:376
  80.7 1.9 %collective-permute-done.8.refs_3_ = f32[4,128,256]{2,1,0:T(8,128)S(1)} collective-permute-done((f32[4,128,256]{2,1,0:T(8,128)S(1)}, f32[4,128,256]{2,1,0:T(8,128)S(1)}, u32[]{:S(2)}, u32[]{:S(2)}) %collective-permute-start.8) | collective-permute-done | bytes 524320 | tf_op jit(solution)/shard_map/ppermute | solution.py:371
  82.7 1.1 coefficients.3
  83.8 0.8 copy-done.2
  84.5 6.7 %all-to-all-start.1 = ((f32[8,64,256]{2,1,0:T(8,128)}), f32[8,64,256]{2,1,0:T(8,128)S(1)}, u32[]{:S(2)}, u32[]{:S(2)}) async-start(f32[8,64,256]{2,1,0:T(8,128)} %copy-done.2), calls=%async_computation.1 | async-start | bytes 1048576 | tf_op jit(solution)/shard_map/all_to_all | solution.py:418
  91.3 1.3 collective-permute-start.10
  92.6 4.6 %collective-permute-start.9 = (f32[2,128,256]{2,1,0:T(8,128)S(1)}, f32[2,128,256]{2,1,0:T(8,128)S(1)}, u32[]{:S(2)}, u32[]{:S(2)}) collective-permute-start(f32[2,128,256]{2,1,0:T(8,128)S(1)} %get-tuple-element.32), channel_id=1, source_target_pairs={{0,4},{4,8},{8,12},{12,16},{16,20},{20,24},{24,28},{1,5},{5,9},{9,... | collective-permute-start | bytes 786440 | tf_op jit(solution)/shard_map/ppermute | solution.py:380
  97.2 8.4 %collective-permute-done.10.refs_5_ = f32[2,128,256]{2,1,0:T(8,128)S(1)} collective-permute-done((f32[2,128,256]{2,1,0:T(8,128)S(1)}, f32[2,128,256]{2,1,0:T(8,128)S(1)}, u32[]{:S(2)}, u32[]{:S(2)}) %collective-permute-start.10) | collective-permute-done | bytes 262176 | tf_op jit(solution)/shard_map/ppermute | solution.py:384
  105.6 1.5 collective-permute-start.12
  107.1 2.6 %collective-permute-done.9.refs_4_ = f32[2,128,256]{2,1,0:T(8,128)S(1)} collective-permute-done((f32[2,128,256]{2,1,0:T(8,128)S(1)}, f32[2,128,256]{2,1,0:T(8,128)S(1)}, u32[]{:S(2)}, u32[]{:S(2)}) %collective-permute-start.9) | collective-permute-done | bytes 262176 | tf_op jit(solution)/shard_map/ppermute | solution.py:380
  109.8 1.5 collective-permute-start.11
  111.3 0.5 collective-permute-start.13
  111.8 0.7 copy-done.7
  112.5 2.2 %collective-permute-done.12.refs_7_ = f32[2,128,256]{2,1,0:T(8,128)S(1)} collective-permute-done((f32[2,128,256]{2,1,0:T(8,128)S(1)}, f32[2,128,256]{2,1,0:T(8,128)S(1)}, u32[]{:S(2)}, u32[]{:S(2)}) %collective-permute-start.12) | collective-permute-done | bytes 262176 | tf_op jit(solution)/shard_map/ppermute | solution.py:376
  114.8 0.7 copy-done.9
  115.5 3.9 %collective-permute-done.11.refs_6_ = f32[2,128,256]{2,1,0:T(8,128)S(1)} collective-permute-done((f32[2,128,256]{2,1,0:T(8,128)S(1)}, f32[2,128,256]{2,1,0:T(8,128)S(1)}, u32[]{:S(2)}, u32[]{:S(2)}) %collective-permute-start.11) | collective-permute-done | bytes 262176 | tf_op jit(solution)/shard_map/ppermute | solution.py:376
  119.4 0.7 copy-done.11
  120.1 0.7 copy-done.13
  120.8 0.7 copy-done.15
  121.5 0.7 copy-done.17
  122.2 0.7 copy-done.19
  122.9 0.9 copy-done.8
  123.9 0.9 copy-done.10
  124.8 0.9 copy-done.12
  125.8 0.9 copy-done.14
  126.7 0.9 copy-done.16
  127.7 0.9 copy-done.18
  128.6 0.9 copy-done.20
  129.6 11.8 %operator.3 = (f32[2,8,128,128]{3,2,1,0:T(8,128)}, f32[2,8,128,128]{3,2,1,0:T(8,128)}) custom-call(s32[96]{0:T(128)S(1)} %reshape.36.cols_ref, s32[8]{0:T(128)S(1)} %bitcast.31, f32[2,8,6,128,128]{4,3,2,1,0:T(8,128)} %bitcast.35, f32[8,64,256]{2,1,0:T(8,128)S(1)} %all-to-all-done.1.coef_ref, f32[8,128,64]{2,1,0:T(8,128)S(1)} %bitcast.25, ...), custom_call_target="tpu_custom_call" | custom-call | flops 2415919104 | bytes 6291456 | tf_op jit(solution)/shard_map/operator/pallas_call | solution.py:189
  141.3 0.5 collective-permute-start.17
  141.9 2.5 %collective-permute-done.17 = f32[2,8,128,128]{3,2,1,0:T(8,128)S(1)} collective-permute-done((f32[2,8,128,128]{3,2,1,0:T(8,128)}, f32[2,8,128,128]{3,2,1,0:T(8,128)S(1)}, u32[]{:S(2)}, u32[]{:S(2)}) %collective-permute-start.17) | collective-permute-done | bytes 1048608 | tf_op jit(solution)/shard_map/ppermute | solution.py:371
  144.4 1.5 fusion
  145.9 1.6 collective-permute-start.18
  147.5 0.5 pack.1
  148.0 12.2 %collective-permute-done.18.refs_2_ = f32[8,128,128]{2,1,0:T(8,128)S(1)} collective-permute-done((f32[8,128,128]{2,1,0:T(8,128)S(1)}, f32[8,128,128]{2,1,0:T(8,128)S(1)}, u32[]{:S(2)}, u32[]{:S(2)}) %collective-permute-start.18) | collective-permute-done | bytes 524320 | tf_op jit(solution)/shard_map/ppermute | solution.py:376
  160.1 0.5 dots.1
  160.7 3.8 %collective-permute-start.19 = (f32[8,128]{1,0:T(8,128)S(1)}, f32[8,128]{1,0:T(8,128)S(1)}, u32[]{:S(2)}, u32[]{:S(2)}) collective-permute-start(f32[8,128]{1,0:T(8,128)S(1)} %get-tuple-element.18), channel_id=1, source_target_pairs={{0,4},{4,0},{8,12},{12,8},{16,20},{20,16},{24,28},{28,24},{1,5},{5... | collective-permute-start | bytes 12296 | tf_op jit(solution)/shard_map/ppermute | solution.py:391
  164.4 1.6 collective-permute-done.19
  166.0 5.0 %collective-permute-start.20 = (f32[8,128]{1,0:T(8,128)S(1)}, f32[8,128]{1,0:T(8,128)S(1)}, u32[]{:S(2)}, u32[]{:S(2)}) collective-permute-start(f32[8,128]{1,0:T(8,128)S(1)} %add.52), channel_id=1, source_target_pairs={{0,8},{4,12},{8,0},{12,4},{16,24},{20,28},{24,16},{28,20},{1,9},{5... | collective-permute-start | bytes 12296 | tf_op jit(solution)/shard_map/ppermute | solution.py:391
  171.0 1.6 collective-permute-done.20
  172.6 2.1 %collective-permute-start.21 = (f32[8,128]{1,0:T(8,128)S(1)}, f32[8,128]{1,0:T(8,128)S(1)}, u32[]{:S(2)}, u32[]{:S(2)}) collective-permute-start(f32[8,128]{1,0:T(8,128)S(1)} %add.53), channel_id=1, source_target_pairs={{0,16},{4,20},{8,24},{12,28},{16,0},{20,4},{24,8},{28,12},{1,17},{... | collective-permute-start | bytes 12296 | tf_op jit(solution)/shard_map/ppermute | solution.py:391
  174.7 2.4 %collective-permute-done.21 = f32[8,128]{1,0:T(8,128)S(1)} collective-permute-done((f32[8,128]{1,0:T(8,128)S(1)}, f32[8,128]{1,0:T(8,128)S(1)}, u32[]{:S(2)}, u32[]{:S(2)}) %collective-permute-start.21) | collective-permute-done | bytes 4128 | tf_op jit(solution)/shard_map/ppermute | solution.py:391
  177.1 0.4 finish.1
  177.6 1.1 copy.17
  178.7 1.1 copy.18
  (55 shorter events, 0.7 us)
Async XLA Ops:
  0.6 11.2 %copy-start = (f32[2048,256]{1,0:T(8,128)S(1)}, f32[2048,256]{1,0:T(8,128)}, u32[]{:S(2)}) copy-start(f32[2048,256]{1,0:T(8,128)} %param.7) | copy-start | bytes 6291460
  0.6 11.2 %copy-start.22 = (s32[1,8,1]{1,2,0:T(1,128)S(1)}, s32[1,8,1]{1,2,0:T(1,128)}, u32[]{:S(2)}) copy-start(s32[1,8,1]{1,2,0:T(1,128)} %param.10) | copy-start | bytes 100
  3.1 17.0 %collective-permute-start.1 = (f32[4,128,256]{2,1,0:T(8,128)}, f32[4,128,256]{2,1,0:T(8,128)S(1)}, u32[]{:S(2)}, u32[]{:S(2)}) collective-permute-start(f32[4,128,256]{2,1,0:T(8,128)} %get-tuple-element.26), channel_id=1, source_target_pairs={{4,0},{8,4},{12,8},{16,12},{20,16},{24,20},{28,24},{5,1},{9,5},{13... | collective-permute-start | bytes 1572872 | tf_op jit(solution)/shard_map/ppermute | solution.py:384
  4.4 31.5 %collective-permute-start = (f32[4,128,256]{2,1,0:T(8,128)}, f32[4,128,256]{2,1,0:T(8,128)}, u32[]{:S(2)}, u32[]{:S(2)}) collective-permute-start(f32[4,128,256]{2,1,0:T(8,128)} %get-tuple-element.27), channel_id=1, source_target_pairs={{0,4},{4,8},{8,12},{12,16},{16,20},{20,24},{24,28},{1,5},{5,9},{9,... | collective-permute-start | bytes 1572872 | tf_op jit(solution)/shard_map/ppermute | solution.py:380
  11.8 24.0 %copy-start.24 = (s32[16,6]{0,1:T(8,128)S(1)}, s32[16,6]{0,1:T(8,128)}, u32[]{:S(2)}) copy-start(s32[16,6]{0,1:T(8,128)} %param.9) | copy-start | bytes 1156
  11.8 24.2 %copy-start.23 = (f32[1,8,1,128,64]{3,4,2,1,0:T(8,128)S(1)}, f32[1,8,1,128,64]{3,4,2,1,0:T(8,128)}, u32[]{:S(2)}) copy-start(f32[1,8,1,128,64]{3,4,2,1,0:T(8,128)} %param.12) | copy-start | bytes 786436
  11.9 26.9 %copy-start.21 = (s32[1,8,1]{1,2,0:T(1,128)S(1)}, s32[1,8,1]{1,2,0:T(1,128)}, u32[]{:S(2)}) copy-start(s32[1,8,1]{1,2,0:T(1,128)} %param.11) | copy-start | bytes 100
  13.6 23.5 %all-to-all-start = ((f32[8,64,256]{2,1,0:T(8,128)}), f32[8,64,256]{2,1,0:T(8,128)S(1)}, u32[]{:S(2)}, u32[]{:S(2)}) async-start(f32[8,64,256]{2,1,0:T(8,128)} %coefficients.2), calls=%async_computation | async-start | bytes 1048576 | tf_op jit(solution)/shard_map/all_to_all | solution.py:418
  20.0 17.1 %collective-permute-start.3 = (f32[4,128,256]{2,1,0:T(8,128)S(1)}, f32[4,128,256]{2,1,0:T(8,128)S(1)}, u32[]{:S(2)}, u32[]{:S(2)}) collective-permute-start(f32[4,128,256]{2,1,0:T(8,128)S(1)} %collective-permute-done.1.refs_2_), channel_id=1, source_target_pairs={{0,1},{1,0},{2,3},{3,2},{4,5},{5,4},{6,7},{7,6},{8,9},{9,8},{10,11... | collective-permute-start | bytes 1572872 | tf_op jit(solution)/shard_map/ppermute | solution.py:371
  35.8 2.1 %collective-permute-start.2 = (f32[4,128,256]{2,1,0:T(8,128)}, f32[4,128,256]{2,1,0:T(8,128)S(1)}, u32[]{:S(2)}, u32[]{:S(2)}) collective-permute-start(f32[4,128,256]{2,1,0:T(8,128)} %collective-permute-done.refs_1_), channel_id=1, source_target_pairs={{0,1},{1,0},{2,3},{3,2},{4,5},{5,4},{6,7},{7,6},{8,9},{9,8},{10,11... | collective-permute-start | bytes 1572872 | tf_op jit(solution)/shard_map/ppermute | solution.py:371
  37.1 0.8 copy-start.3
  37.9 0.8 copy-start.5
  38.7 1.0 copy-start.4
  39.8 1.0 copy-start.6
  50.6 2.7 %collective-permute-start.4 = (f32[2,4,128,256]{3,2,1,0:T(8,128)S(1)}, f32[2,4,128,256]{3,2,1,0:T(8,128)S(1)}, u32[]{:S(2)}, u32[]{:S(2)}) collective-permute-start(f32[2,4,128,256]{3,2,1,0:T(8,128)S(1)} %get-tuple-element.13), channel_id=1, source_target_pairs={{0,1},{1,0},{2,3},{3,2},{4,5},{5,4},{6,7},{7,6},{8,9},{9,8},{10,11... | collective-permute-start | bytes 3145736 | tf_op jit(solution)/shard_map/ppermute | solution.py:371
  53.4 14.0 %collective-permute-start.5 = (f32[4,128,256]{2,1,0:T(8,128)S(1)}, f32[4,128,256]{2,1,0:T(8,128)S(1)}, u32[]{:S(2)}, u32[]{:S(2)}) collective-permute-start(f32[4,128,256]{2,1,0:T(8,128)S(1)} %fusion.1), channel_id=1, source_target_pairs={{0,2},{1,3},{2,0},{3,1},{4,6},{5,7},{6,4},{7,5},{8,10},{9,11},{10,... | collective-permute-start | bytes 1572872 | tf_op jit(solution)/shard_map/ppermute | solution.py:376
  67.5 13.2 %collective-permute-start.6 = (f32[4,128,256]{2,1,0:T(8,128)S(1)}, f32[4,128,256]{2,1,0:T(8,128)S(1)}, u32[]{:S(2)}, u32[]{:S(2)}) collective-permute-start(f32[4,128,256]{2,1,0:T(8,128)S(1)} %fusion.3.refs_0_), channel_id=1, source_target_pairs={{0,2},{1,3},{2,0},{3,1},{4,6},{5,7},{6,4},{7,5},{8,10},{9,11},{10,... | collective-permute-start | bytes 1572872 | tf_op jit(solution)/shard_map/ppermute | solution.py:376
  69.1 11.6 %collective-permute-start.7 = (f32[4,128,256]{2,1,0:T(8,128)S(1)}, f32[4,128,256]{2,1,0:T(8,128)S(1)}, u32[]{:S(2)}, u32[]{:S(2)}) collective-permute-start(f32[4,128,256]{2,1,0:T(8,128)S(1)} %fusion.3.refs_0_), channel_id=1, source_target_pairs={{0,1},{1,0},{2,3},{3,2},{4,5},{5,4},{6,7},{7,6},{8,9},{9,8},{10,11... | collective-permute-start | bytes 1572872 | tf_op jit(solution)/shard_map/ppermute | solution.py:371
  80.7 1.9 %collective-permute-start.8 = (f32[4,128,256]{2,1,0:T(8,128)S(1)}, f32[4,128,256]{2,1,0:T(8,128)S(1)}, u32[]{:S(2)}, u32[]{:S(2)}) collective-permute-start(f32[4,128,256]{2,1,0:T(8,128)S(1)} %collective-permute-done.6.refs_1_), channel_id=1, source_target_pairs={{0,1},{1,0},{2,3},{3,2},{4,5},{5,4},{6,7},{7,6},{8,9},{9,8},{10,11... | collective-permute-start | bytes 1572872 | tf_op jit(solution)/shard_map/ppermute | solution.py:371
  83.8 0.8 copy-start.2
  84.5 38.4 %all-to-all-start.1 = ((f32[8,64,256]{2,1,0:T(8,128)}), f32[8,64,256]{2,1,0:T(8,128)S(1)}, u32[]{:S(2)}, u32[]{:S(2)}) async-start(f32[8,64,256]{2,1,0:T(8,128)} %copy-done.2), calls=%async_computation.1 | async-start | bytes 1048576 | tf_op jit(solution)/shard_map/all_to_all | solution.py:418
  91.3 14.3 %collective-permute-start.10 = (f32[2,128,256]{2,1,0:T(8,128)S(1)}, f32[2,128,256]{2,1,0:T(8,128)S(1)}, u32[]{:S(2)}, u32[]{:S(2)}) collective-permute-start(f32[2,128,256]{2,1,0:T(8,128)S(1)} %get-tuple-element.31), channel_id=1, source_target_pairs={{4,0},{8,4},{12,8},{16,12},{20,16},{24,20},{28,24},{5,1},{9,5},{13... | collective-permute-start | bytes 786440 | tf_op jit(solution)/shard_map/ppermute | solution.py:384
  92.6 17.2 %collective-permute-start.9 = (f32[2,128,256]{2,1,0:T(8,128)S(1)}, f32[2,128,256]{2,1,0:T(8,128)S(1)}, u32[]{:S(2)}, u32[]{:S(2)}) collective-permute-start(f32[2,128,256]{2,1,0:T(8,128)S(1)} %get-tuple-element.32), channel_id=1, source_target_pairs={{0,4},{4,8},{8,12},{12,16},{16,20},{20,24},{24,28},{1,5},{5,9},{9,... | collective-permute-start | bytes 786440 | tf_op jit(solution)/shard_map/ppermute | solution.py:380
  105.6 9.2 %collective-permute-start.12 = (f32[2,128,256]{2,1,0:T(8,128)S(1)}, f32[2,128,256]{2,1,0:T(8,128)S(1)}, u32[]{:S(2)}, u32[]{:S(2)}) collective-permute-start(f32[2,128,256]{2,1,0:T(8,128)S(1)} %collective-permute-done.10.refs_5_), channel_id=1, source_target_pairs={{0,2},{1,3},{2,0},{3,1},{4,6},{5,7},{6,4},{7,5},{8,10},{9,11},{10,... | collective-permute-start | bytes 786440 | tf_op jit(solution)/shard_map/ppermute | solution.py:376
  109.8 9.6 %collective-permute-start.11 = (f32[2,128,256]{2,1,0:T(8,128)S(1)}, f32[2,128,256]{2,1,0:T(8,128)S(1)}, u32[]{:S(2)}, u32[]{:S(2)}) collective-permute-start(f32[2,128,256]{2,1,0:T(8,128)S(1)} %collective-permute-done.9.refs_4_), channel_id=1, source_target_pairs={{0,2},{1,3},{2,0},{3,1},{4,6},{5,7},{6,4},{7,5},{8,10},{9,11},{10,... | collective-permute-start | bytes 786440 | tf_op jit(solution)/shard_map/ppermute | solution.py:376
  111.3 8.8 %collective-permute-start.14 = (f32[2,128,256]{2,1,0:T(8,128)S(1)}, f32[2,128,256]{2,1,0:T(8,128)S(1)}, u32[]{:S(2)}, u32[]{:S(2)}) collective-permute-start(f32[2,128,256]{2,1,0:T(8,128)S(1)} %collective-permute-done.10.refs_5_), channel_id=1, source_target_pairs={{0,1},{1,0},{2,3},{3,2},{4,5},{5,4},{6,7},{7,6},{8,9},{9,8},{10,11... | collective-permute-start | bytes 786440 | tf_op jit(solution)/shard_map/ppermute | solution.py:371
  111.3 9.5 %collective-permute-start.13 = (f32[2,128,256]{2,1,0:T(8,128)S(1)}, f32[2,128,256]{2,1,0:T(8,128)S(1)}, u32[]{:S(2)}, u32[]{:S(2)}) collective-permute-start(f32[2,128,256]{2,1,0:T(8,128)S(1)} %collective-permute-done.9.refs_4_), channel_id=1, source_target_pairs={{0,1},{1,0},{2,3},{3,2},{4,5},{5,4},{6,7},{7,6},{8,9},{9,8},{10,11... | collective-permute-start | bytes 786440 | tf_op jit(solution)/shard_map/ppermute | solution.py:371
  111.8 0.7 copy-start.7
  114.8 6.7 %collective-permute-start.16 = (f32[2,128,256]{2,1,0:T(8,128)S(1)}, f32[2,128,256]{2,1,0:T(8,128)S(1)}, u32[]{:S(2)}, u32[]{:S(2)}) collective-permute-start(f32[2,128,256]{2,1,0:T(8,128)S(1)} %collective-permute-done.12.refs_7_), channel_id=1, source_target_pairs={{0,1},{1,0},{2,3},{3,2},{4,5},{5,4},{6,7},{7,6},{8,9},{9,8},{10,11... | collective-permute-start | bytes 786440 | tf_op jit(solution)/shard_map/ppermute | solution.py:371
  114.8 0.7 copy-start.9
  119.4 2.8 %collective-permute-start.15 = (f32[2,128,256]{2,1,0:T(8,128)S(1)}, f32[2,128,256]{2,1,0:T(8,128)S(1)}, u32[]{:S(2)}, u32[]{:S(2)}) collective-permute-start(f32[2,128,256]{2,1,0:T(8,128)S(1)} %collective-permute-done.11.refs_6_), channel_id=1, source_target_pairs={{0,1},{1,0},{2,3},{3,2},{4,5},{5,4},{6,7},{7,6},{8,9},{9,8},{10,11... | collective-permute-start | bytes 786440 | tf_op jit(solution)/shard_map/ppermute | solution.py:371
  119.4 0.7 copy-start.11
  120.1 0.7 copy-start.13
  120.8 0.7 copy-start.15
  121.5 0.7 copy-start.17
  122.2 0.7 copy-start.19
  122.9 1.0 copy-start.8
  123.9 0.9 copy-start.10
  124.8 0.9 copy-start.12
  125.8 0.9 copy-start.14
  126.7 0.9 copy-start.16
  127.7 0.9 copy-start.18
  128.6 0.9 copy-start.20
  141.3 6.2 %copy-start.1 = (f32[2048,256]{1,0:T(8,128)S(1)}, f32[2048,256]{1,0:T(8,128)}, u32[]{:S(2)}) copy-start(f32[2048,256]{1,0:T(8,128)} %param.7) | copy-start | bytes 6291460
  141.3 3.0 %collective-permute-start.17 = (f32[2,8,128,128]{3,2,1,0:T(8,128)}, f32[2,8,128,128]{3,2,1,0:T(8,128)S(1)}, u32[]{:S(2)}, u32[]{:S(2)}) collective-permute-start(f32[2,8,128,128]{3,2,1,0:T(8,128)} %get-tuple-element.17), channel_id=1, source_target_pairs={{0,1},{1,0},{2,3},{3,2},{4,5},{5,4},{6,7},{7,6},{8,9},{9,8},{10,11... | collective-permute-start | bytes 3145736 | tf_op jit(solution)/shard_map/ppermute | solution.py:371
  145.9 14.3 %collective-permute-start.18 = (f32[8,128,128]{2,1,0:T(8,128)S(1)}, f32[8,128,128]{2,1,0:T(8,128)S(1)}, u32[]{:S(2)}, u32[]{:S(2)}) collective-permute-start(f32[8,128,128]{2,1,0:T(8,128)S(1)} %get-tuple-element.28), channel_id=1, source_target_pairs={{0,2},{1,3},{2,0},{3,1},{4,6},{5,7},{6,4},{7,5},{8,10},{9,11},{10,... | collective-permute-start | bytes 1572872 | tf_op jit(solution)/shard_map/ppermute | solution.py:376
  160.7 5.3 %collective-permute-start.19 = (f32[8,128]{1,0:T(8,128)S(1)}, f32[8,128]{1,0:T(8,128)S(1)}, u32[]{:S(2)}, u32[]{:S(2)}) collective-permute-start(f32[8,128]{1,0:T(8,128)S(1)} %get-tuple-element.18), channel_id=1, source_target_pairs={{0,4},{4,0},{8,12},{12,8},{16,20},{20,16},{24,28},{28,24},{1,5},{5... | collective-permute-start | bytes 12296 | tf_op jit(solution)/shard_map/ppermute | solution.py:391
  166.0 6.6 %collective-permute-start.20 = (f32[8,128]{1,0:T(8,128)S(1)}, f32[8,128]{1,0:T(8,128)S(1)}, u32[]{:S(2)}, u32[]{:S(2)}) collective-permute-start(f32[8,128]{1,0:T(8,128)S(1)} %add.52), channel_id=1, source_target_pairs={{0,8},{4,12},{8,0},{12,4},{16,24},{20,28},{24,16},{28,20},{1,9},{5... | collective-permute-start | bytes 12296 | tf_op jit(solution)/shard_map/ppermute | solution.py:391
  172.6 4.5 %collective-permute-start.21 = (f32[8,128]{1,0:T(8,128)S(1)}, f32[8,128]{1,0:T(8,128)S(1)}, u32[]{:S(2)}, u32[]{:S(2)}) collective-permute-start(f32[8,128]{1,0:T(8,128)S(1)} %add.53), channel_id=1, source_target_pairs={{0,16},{4,20},{8,24},{12,28},{16,0},{20,4},{24,8},{28,12},{1,17},{... | collective-permute-start | bytes 12296 | tf_op jit(solution)/shard_map/ppermute | solution.py:391

commit v2 on v0

v2 whole, which is shorter than its diff:
```python
import functools

import jax
import jax.numpy as jnp
from jax import lax
from jax.experimental import pallas as pl
from jax.experimental.pallas import tpu as pltpu
from jax.sharding import PartitionSpec as P

B = 128
R = 64
CL_DEV = 16
REACH = 8
CORES = 2
LANES = 128
ZERO = CL_DEV
EPS = 1e-06
F32 = jnp.float32
BF16 = jnp.bfloat16
VMEM_LIMIT = 48 * 1024 * 1024


VMEM_SPEC = pl.BlockSpec(memory_space=pltpu.VMEM)
SMEM_SPEC = pl.BlockSpec(memory_space=pltpu.SMEM)
ANY_SPEC = pl.BlockSpec(memory_space=pl.ANY)
PARAMS = pltpu.CompilerParams(vmem_limit_bytes=VMEM_LIMIT)


def split(value):
    high = value.astype(BF16)
    low = (value - high.astype(F32)).astype(BF16)
    return high, low


def dot3(left, right, dims=((1,), (0,))):
    (lh, ll), (rh, rl) = left, right
    dot = functools.partial(
        lax.dot_general, dimension_numbers=(dims, ((), ())), preferred_element_type=F32
    )
    return dot(lh, rh) + (dot(ll, rh) + dot(lh, rl))


def cost(flops, size):
    return pl.CostEstimate(flops=flops, bytes_accessed=size, transcendentals=0)


def place(far_size):
    index = lax.axis_index("far")
    return index // CORES, index % CORES, far_size // CORES


def owner_of(n, far_size):
    y, core, ys = place(far_size)
    shift, other = n % ys, n // ys
    return lax.rem(y - shift + ys, ys) * CORES + (1 - core if other else core)


def fetch(pairs, sems):
    copies = [pltpu.make_async_copy(a, b, sems.at[n]) for n, (a, b) in enumerate(pairs)]
    for copy in copies:
        copy.start()
    for copy in copies:
        copy.wait()


def cluster_at(half, j, k, per):
    return half * REACH + j * per + k


def prepare_kernel(far_size, right_ref, left_ref, b_ref, factors_ref, own_ref):
    for t in range(right_ref.shape[0]):
        factors_ref[0, t] = right_ref[t].T
        left = left_ref[t]
        factors_ref[1, t] = jnp.concatenate([left[: B // 2], left[B // 2 :]], axis=1)
    index = lax.axis_index("far")
    per = own_ref.shape[0] // 2
    packs = REACH // per
    width = LANES // packs
    for owner in range(far_size):

        @pl.when(index == owner)
        def _():
            for half in range(2):
                for k in range(per):
                    own_ref[half * per + k] = jnp.concatenate(
                        [
                            b_ref[cluster_at(half, j, k, per)][:, owner * width : (owner + 1) * width]
                            for j in range(packs)
                        ],
                        axis=1,
                    )


def prepare(right, left, own, far_size, per):
    groups = right.shape[0]
    return pl.pallas_call(
        functools.partial(prepare_kernel, far_size),
        grid=(1,),
        out_shape=[
            jax.ShapeDtypeStruct((2, groups, R, B), F32),
            jax.ShapeDtypeStruct((2 * per, B, LANES), F32),
        ],
        in_specs=[
            pl.BlockSpec(right.shape, lambda i: (0, 0, 0)),
            pl.BlockSpec(left.shape, lambda i: (0, 0, 0)),
            pl.BlockSpec(own.shape, lambda i: (0, 0, 0)),
        ],
        out_specs=[
            pl.BlockSpec((2, groups, R, B), lambda i: (0, 0, 0, 0)),
            pl.BlockSpec((2 * per, B, LANES), lambda i: (0, 0, 0)),
        ],
        compiler_params=PARAMS,
        cost_estimate=cost(0, 4 * own.size),
        name="prepare",
    )(right, left, own)


def coefficient_kernel(far_size, *refs):
    meta, factors = refs[:far_size], refs[far_size : 2 * far_size]
    fields = refs[2 * far_size : -5]
    out_ref, held, stage, high, low = refs[-5:]
    del held
    per = sum(f.shape[0] for f in fields) // 2
    packs = REACH // per
    width = LANES // packs
    entries = [f[k] for f in fields for k in range(f.shape[0])]
    for half in range(2):
        for k in range(per):
            entry = entries[half * per + k]
            for j in range(packs):
                h, l = split(entry[:, j * width : (j + 1) * width])
                high[cluster_at(half, j, k, per)] = h
                low[cluster_at(half, j, k, per)] = l
    depth = far_size // packs

    def group(t, carry):
        for e in range(depth):
            parts = []
            for j in range(packs):
                n = j * depth + e
                source = meta[n][0, t]
                parts.append(dot3(split(factors[n][0, t]), (high[source], low[source])))
            out_ref[t, e] = jnp.concatenate(parts, axis=1)
        return carry

    lax.fori_loop(0, out_ref.shape[0], group, 0)


def coefficients(meta, factors, fields, far_size):
    groups = factors[0].shape[1]
    per = sum(f.shape[0] for f in fields) // 2
    packs = REACH // per
    width = LANES // packs
    shape = (groups, far_size // packs, R, LANES)
    full = lambda a: pl.BlockSpec(a.shape, lambda i: (0,) * a.ndim)
    return pl.pallas_call(
        functools.partial(coefficient_kernel, far_size),
        grid=(1,),
        out_shape=jax.ShapeDtypeStruct(shape, F32),
        in_specs=[SMEM_SPEC] * far_size + [full(f) for f in factors] + [full(f) for f in fields],
        out_specs=pl.BlockSpec(shape, lambda i: (0, 0, 0, 0)),
        scratch_shapes=[
            pltpu.VMEM((8, LANES), F32),
            pltpu.VMEM((8, LANES), F32),
            pltpu.VMEM((CL_DEV, B, width), BF16),
            pltpu.VMEM((CL_DEV, B, width), BF16),
        ],
        compiler_params=PARAMS,
        cost_estimate=cost(6 * groups * far_size * R * B * width, 4 * 1024 * 1024),
        name="coefficients",
    )(*meta, *factors, *fields)


def far_kernel(far_size, *refs):
    meta, factors = refs[:far_size], refs[far_size : 2 * far_size]
    coef_ref, out_ref, total = refs[-3:]
    per = out_ref.shape[0] // 2
    packs = REACH // per
    width = LANES // packs
    depth = far_size // packs
    total[...] = jnp.zeros_like(total)

    def group(a, carry):
        for e in range(depth):
            here = coef_ref[a, e]
            for j in range(packs):
                n = j * depth + e
                dense = factors[n][1, a]
                left = jnp.concatenate([dense[:, :R], dense[:, R:]], axis=0)
                target = meta[n][1, a]
                total[target] += dot3(split(left), split(here[:, j * width : (j + 1) * width]))
        return carry

    lax.fori_loop(0, coef_ref.shape[0], group, 0)
    for half in range(2):
        for k in range(per):
            out_ref[half * per + k] = jnp.concatenate(
                [total[cluster_at(half, j, k, per)] for j in range(packs)], axis=1
            )


def far_part(meta, factors, coef, far_size, per):
    groups = coef.shape[0]
    width = LANES * per // REACH
    full = lambda a: pl.BlockSpec(a.shape, lambda i: (0,) * a.ndim)
    return pl.pallas_call(
        functools.partial(far_kernel, far_size),
        grid=(1,),
        out_shape=jax.ShapeDtypeStruct((2 * per, B, LANES), F32),
        in_specs=[SMEM_SPEC] * far_size + [full(f) for f in factors] + [full(coef)],
        out_specs=pl.BlockSpec((2 * per, B, LANES), lambda i: (0, 0, 0)),
        scratch_shapes=[pltpu.VMEM((CL_DEV, B, width), F32)],
        compiler_params=PARAMS,
        cost_estimate=cost(6 * groups * far_size * R * B * width, 4 * 1024 * 1024),
        name="far_part",
    )(*meta, *factors, coef)


def unpack(stage, per, put):
    far_size, halves = stage.shape[0], stage.shape[1]
    packs = REACH // per
    width = LANES // packs
    for half in range(halves):
        for k in range(per):
            for block in range(far_size // packs):
                entries = [stage[block * packs + i, half, k] for i in range(packs)]
                for j in range(packs):
                    value = jnp.concatenate(
                        [e[:, j * width : (j + 1) * width] for e in entries], axis=1
                    )
                    put(half, j * per + k, block * LANES, value)


def own_kernel(far_size, n_pieces, cols_ref, blocks_ref, *refs):
    pieces, (out_ref, high, low, stage, sems) = refs[:n_pieces], refs[n_pieces:]
    half, k = pl.program_id(0), pl.program_id(1)
    packs, slots = blocks_ref.shape[1], blocks_ref.shape[3]
    per = REACH // packs
    base = lax.axis_index("rows") * CL_DEV

    @pl.when((half == 0) & (k == 0))
    def _():
        if n_pieces == 1:
            fetch([(pieces[0], stage)], sems)
            for c in range(CL_DEV):
                high[c], low[c] = split(stage[c])
        else:
            pairs = []
            for n in range(far_size):
                owner = owner_of(n, far_size)
                for h in range(2):
                    pairs.append((pieces[2 * n + h], stage.at[owner, h]))
            fetch(pairs, sems)

            def put(h, c, lane, value):
                hi, lo = split(value)
                high[h * REACH + c, :, lane : lane + LANES] = hi
                low[h * REACH + c, :, lane : lane + LANES] = lo

            unpack(stage, per, put)
        high[ZERO] = jnp.zeros_like(high[ZERO])
        low[ZERO] = jnp.zeros_like(low[ZERO])

    for j in range(packs):
        cluster = cluster_at(half, j, k, per)
        at = []
        for s in range(slots):
            p = cols_ref[cluster * slots + s] - base
            at.append(jnp.where((p >= 0) & (p < CL_DEV), p, ZERO))
        left = split(jnp.concatenate([blocks_ref[0, j, 0, s] for s in range(slots)], axis=1))
        right = tuple(jnp.concatenate([ref[p] for p in at], axis=0) for ref in (high, low))
        out_ref[0, j, 0] = dot3(left, right)


def own_products(pieces, cols, blocks, far_size, width, per):
    packs = REACH // per
    slots = blocks.shape[1]
    if len(pieces) == 1:
        stage = pltpu.VMEM((CL_DEV, B, width), F32)
    else:
        stage = pltpu.VMEM((far_size, 2, per, B, LANES), F32)
    return pl.pallas_call(
        functools.partial(own_kernel, far_size, len(pieces)),
        out_shape=jax.ShapeDtypeStruct((2, packs, per, B, width), F32),
        grid=(2, per),
        in_specs=[
            SMEM_SPEC,
            pl.BlockSpec((1, packs, 1, slots, B, B), lambda h, k: (h, 0, k, 0, 0, 0)),
        ]
        + [ANY_SPEC] * len(pieces),
        out_specs=pl.BlockSpec((1, packs, 1, B, width), lambda h, k: (h, 0, k, 0, 0)),
        scratch_shapes=[
            pltpu.VMEM((CL_DEV + 1, B, width), BF16),
            pltpu.VMEM((CL_DEV + 1, B, width), BF16),
            stage,
            pltpu.SemaphoreType.DMA((len(pieces),)),
        ],
        compiler_params=PARAMS,
        cost_estimate=cost(6 * CL_DEV * slots * B * B * width, 4 * blocks.size),
        name="own_products",
    )(cols, blocks.reshape(2, packs, per, slots, B, B), *pieces)


def halo_kernel(far_size, last, n_pieces, cols_ref, blocks_ref, done_ref, *refs):
    pieces = refs[:n_pieces]
    ys = far_size // CORES
    keeps, sends = refs[n_pieces : n_pieces + ys], refs[n_pieces + ys : n_pieces + 2 * ys]
    high, low, stage, listed, sems = refs[n_pieces + 2 * ys :]
    half, k = pl.program_id(0), pl.program_id(1)
    packs, slots = blocks_ref.shape[1], blocks_ref.shape[3]
    per = REACH // packs
    y, core, _ = place(far_size)
    base = lax.axis_index("rows") * CL_DEV

    @pl.when((half == 0) & (k == 0))
    def _():
        if not last:
            part = REACH // CORES
            pairs = []
            for n, piece in enumerate(pieces):
                c = core if n < 2 else 1 - core
                pairs.append((piece, stage.at[pl.ds((n % 2) * REACH + c * part, part)]))
            fetch(pairs, sems)
            for c in range(2 * REACH):
                high[c], low[c] = split(stage[c])
        else:
            pairs = []
            for n in range(far_size):
                owner = owner_of(n, far_size)
                for h in range(2):
                    pairs.append((pieces[2 * n + h], stage.at[owner, h]))
            fetch(pairs, sems)

            def put(h, c, lane, value):
                hi, lo = split(value)
                high[h * REACH + c, :, lane : lane + LANES] = hi
                low[h * REACH + c, :, lane : lane + LANES] = lo

            unpack(stage, per, put)
        high[ZERO] = jnp.zeros_like(high[ZERO])
        low[ZERO] = jnp.zeros_like(low[ZERO])

    images = []
    for j in range(packs):
        cluster = cluster_at(half, j, k, per)
        count = jnp.int32(0)
        for s in range(slots):
            p = cols_ref[cluster * slots + s] - base
            listed[0, count] = s
            listed[1, count] = jnp.where(p < 0, p + REACH, p - CL_DEV + REACH)
            count = count + ((p < 0) | (p >= CL_DEV)).astype(jnp.int32)
        listed[0, count] = 0
        listed[1, count] = ZERO

        def two(i, total):
            s0, s1 = listed[0, 2 * i], listed[0, 2 * i + 1]
            p0, p1 = listed[1, 2 * i], listed[1, 2 * i + 1]
            left = split(jnp.concatenate([blocks_ref[0, j, 0, s0], blocks_ref[0, j, 0, s1]], axis=1))
            right = tuple(jnp.concatenate([ref[p0], ref[p1]], axis=0) for ref in (high, low))
            return total + dot3(left, right)

        images.append(lax.fori_loop(0, (count + 1) // 2, two, done_ref[0, j, 0]))

    width = LANES // packs
    for owner in range(far_size):
        packed = jnp.concatenate([im[:, owner * width : (owner + 1) * width] for im in images], axis=1)
        behind = lax.rem(owner // CORES - y + ys, ys)
        mine = owner % CORES == core
        for steps in range(ys):

            @pl.when(mine & (behind == steps))
            def _():
                keeps[steps][0] = packed

            @pl.when(jnp.logical_not(mine) & (behind == steps))
            def _():
                sends[steps][0] = packed


def with_halo(pieces, done, cols, blocks, far_size, last):
    _, packs, per, _, width = done.shape
    slots = blocks.shape[1]
    ys = far_size // CORES
    if last:
        stage = pltpu.VMEM((far_size, 2, per, B, LANES), F32)
    else:
        stage = pltpu.VMEM((2 * REACH, B, width), F32)
    outs = pl.pallas_call(
        functools.partial(halo_kernel, far_size, last, len(pieces)),
        out_shape=[jax.ShapeDtypeStruct((2 * per, B, LANES), F32)] * (2 * ys),
        grid=(2, per),
        in_specs=[
            SMEM_SPEC,
            pl.BlockSpec((1, packs, 1, slots, B, B), lambda h, k: (h, 0, k, 0, 0, 0)),
            pl.BlockSpec((1, packs, 1, B, width), lambda h, k: (h, 0, k, 0, 0)),
        ]
        + [ANY_SPEC] * len(pieces),
        out_specs=[pl.BlockSpec((1, B, LANES), lambda h, k: (h * per + k, 0, 0))] * (2 * ys),
        scratch_shapes=[
            pltpu.VMEM((CL_DEV + 1, B, width), BF16),
            pltpu.VMEM((CL_DEV + 1, B, width), BF16),
            stage,
            pltpu.SMEM((2, slots + 2), jnp.int32),
            pltpu.SemaphoreType.DMA((len(pieces),)),
        ],
        compiler_params=PARAMS,
        cost_estimate=cost(2 * CL_DEV * slots * B * B * width, 4 * blocks.size),
        name="with_halo",
    )(cols, blocks.reshape(2, packs, per, slots, B, B), done, *pieces)
    return outs[:ys], outs[ys:]


def add_kernel(n, *refs):
    parts, outs = refs[:n], refs[n:]
    total = parts[0][...]
    for part in parts[1:]:
        total = total + part[...]
    per = total.shape[0] // 2
    outs[0][...] = total[:per]
    outs[1][...] = total[per:]


def add_halves(parts):
    shape = parts[0].shape
    half = (shape[0] // 2,) + shape[1:]
    return pl.pallas_call(
        functools.partial(add_kernel, len(parts)),
        grid=(1,),
        out_shape=[jax.ShapeDtypeStruct(half, F32)] * 2,
        in_specs=[pl.BlockSpec(shape, lambda i: (0, 0, 0))] * len(parts),
        out_specs=[pl.BlockSpec(half, lambda i: (0, 0, 0))] * 2,
        compiler_params=PARAMS,
        cost_estimate=cost(4 * parts[0].size, 20 * parts[0].size),
        name="add_halves",
    )(*parts)


def dots_kernel(packs, n_parts, b_ref, gl_ref, gr_ref, *refs):
    parts, (out_ref, image_ref) = refs[:n_parts], refs[n_parts:]
    image = parts[0][...]
    for part in parts[1:]:
        image = image + part[...]
    image_ref[...] = image
    vectors = (b_ref[...], jnp.concatenate([gl_ref[...], gr_ref[...]], axis=0), image)
    width = LANES // packs
    rows = []
    for left, right in ((0, 0), (0, 1), (0, 2), (1, 1), (1, 2), (2, 2)):
        total = jnp.sum(vectors[left] * vectors[right], axis=0)
        total = jnp.sum(total, axis=0, keepdims=True)
        folded = total
        for g in range(1, packs):
            folded = folded + pltpu.roll(total, g * width, 1)
        rows.append(folded)
    rows.append(jnp.zeros((2, LANES), F32))
    out_ref[...] = jnp.concatenate(rows, axis=0)


def dots(b_own, g_own, parts, packs):
    full = lambda a: pl.BlockSpec(a.shape, lambda i: (0,) * a.ndim)
    return pl.pallas_call(
        functools.partial(dots_kernel, packs, len(parts)),
        grid=(1,),
        out_shape=[
            jax.ShapeDtypeStruct((8, LANES), F32),
            jax.ShapeDtypeStruct(b_own.shape, F32),
        ],
        in_specs=[full(a) for a in (b_own, *g_own, *parts)],
        out_specs=[pl.BlockSpec((8, LANES), lambda i: (0, 0)), full(b_own)],
        compiler_params=PARAMS,
        cost_estimate=cost(14 * b_own.size, 20 * b_own.size),
        name="dots",
    )(b_own, *g_own, *parts)


def least_squares(rhs_length, upper_left, lower_left, top_two, mid_two, lower_right):
    radius_one = jnp.sqrt(upper_left * upper_left + lower_left * lower_left)
    cosine_one = upper_left / radius_one
    sine_one = lower_left / radius_one
    rotated_top = cosine_one * rhs_length
    rotated_mid = -sine_one * rhs_length
    coupled = cosine_one * top_two + sine_one * mid_two
    diagonal_two = cosine_one * mid_two - sine_one * top_two
    radius_two = jnp.sqrt(diagonal_two * diagonal_two + lower_right * lower_right)
    weight_two = diagonal_two * rotated_mid / (radius_two * radius_two)
    weight_one = (rotated_top - coupled * weight_two) / radius_one
    return (weight_one, weight_two)


def finish_kernel(packs, dots_ref, b_ref, gl_ref, gr_ref, image_ref, solution_ref, residual_ref):
    bb, b1, b2, s11, s12, s22 = [dots_ref[i : i + 1, :] for i in range(6)]
    square = bb + EPS
    rhs_length = jnp.sqrt(square)
    upper_left = (0.5 * bb + b1) / square
    shift = (0.5 * EPS - b1) / square
    one = jnp.maximum(shift * shift * bb + 2.0 * shift * b1 + s11, 0.0) / square
    lower_square = one + EPS
    lower_left = jnp.sqrt(lower_square)
    f_s = (shift * bb + b1) / (square * lower_left)
    f_gs = (shift * b1 + b2) / (square * lower_left)
    s_s = one / lower_square
    s_gs = (shift * shift * b1 + shift * b2 + shift * s11 + s12) / (square * lower_square)
    gs_gs = (shift * shift * s11 + 2.0 * shift * s12 + s22) / (square * lower_square)
    top_two = 0.5 * f_s + f_gs
    mid_two = 0.5 * s_s + s_gs
    rest = 0.5 * (EPS / lower_square) - s_gs
    two = (
        gs_gs
        + top_two * top_two * (bb / square)
        + rest * rest * s_s
        - 2.0 * top_two * f_gs
        + 2.0 * rest * s_gs
        - 2.0 * top_two * rest * f_s
    )
    lower_right = jnp.sqrt(jnp.maximum(two, 0.0) + EPS)
    weight_one, weight_two = least_squares(
        rhs_length, upper_left, lower_left, top_two, mid_two, lower_right
    )
    one_scale = weight_one / rhs_length
    two_scale = weight_two / (rhs_length * lower_left)
    sol_b = one_scale + two_scale * shift
    res_b = 1.0 - 0.5 * one_scale - 0.5 * two_scale * shift
    res_1 = one_scale + two_scale * (0.5 + shift)
    width = LANES // packs
    per = REACH // packs
    for half, g_ref in enumerate((gl_ref, gr_ref)):
        for k in range(per):
            b, g, image = b_ref[half * per + k], g_ref[k], image_ref[half * per + k]
            answer = sol_b * b + two_scale * g
            left = res_b * b - res_1 * g - two_scale * image
            for j in range(packs):
                cut = slice(j * width, (j + 1) * width)
                solution_ref[cluster_at(half, j, k, per)] = answer[:, cut]
                residual_ref[cluster_at(half, j, k, per)] = left[:, cut]


def finish(total, b_own, g_own, image, packs):
    part = (CL_DEV, B, LANES // packs)
    full = lambda a: pl.BlockSpec(a.shape, lambda i: (0,) * a.ndim)
    return pl.pallas_call(
        functools.partial(finish_kernel, packs),
        grid=(1,),
        out_shape=[jax.ShapeDtypeStruct(part, F32)] * 2,
        in_specs=[full(a) for a in (total, b_own, *g_own, image)],
        out_specs=[pl.BlockSpec(part, lambda i: (0, 0, 0))] * 2,
        compiler_params=PARAMS,
        cost_estimate=cost(8 * b_own.size, 28 * b_own.size),
        name="finish",
    )(total, b_own, *g_own, image)


def swap_cores(value):
    size = lax.axis_size("far")
    return lax.ppermute(value, "far", [(i, i ^ 1) for i in range(size)])


def along_y(value, shift):
    size = lax.axis_size("far")
    return lax.ppermute(value, "far", [(i, (i + CORES * shift) % size) for i in range(size)])


def gather_far(value):
    ys = lax.axis_size("far") // CORES
    near = [value] + [along_y(value, s) for s in range(1, ys)]
    return near + [swap_cores(item) for item in near]


def to_next(value):
    return lax.ppermute(value, "rows", [(i, i + 1) for i in range(lax.axis_size("rows") - 1)])


def to_previous(value):
    return lax.ppermute(value, "rows", [(i + 1, i) for i in range(lax.axis_size("rows") - 1)])


def sum_rows(value):
    size = lax.axis_size("rows")
    step = 1
    while step < size:
        value = value + lax.ppermute(value, "rows", [(i, i ^ step) for i in range(size)])
        step *= 2
    return value


def exchange(coef):
    return lax.all_to_all(coef, "rows", split_axis=0, concat_axis=0, tiled=True)


def sum_far(keeps, sends):
    terms = [keeps[0]]
    for shift in range(1, len(keeps)):
        terms.append(along_y(keeps[shift] + swap_cores(sends[shift]), shift))
    return terms + [swap_cores(sends[0])]


def shards(right_side, near_blocks, near_cols, far_src, far_tgt, far_left, far_right):
    far_size = lax.axis_size("far")
    ys = far_size // CORES
    width = right_side.shape[1]
    packs = LANES * far_size // width
    per = REACH // packs
    core = lax.axis_index("far") % CORES
    cols = near_cols.reshape(-1)
    own = right_side.reshape(CL_DEV, B, width)
    groups = far_left.shape[1]

    part = REACH // CORES
    tail = lax.dynamic_slice_in_dim(own, CL_DEV - REACH + core * part, part, 0)
    head = lax.dynamic_slice_in_dim(own, core * part, part, 0)
    from_left, from_right = to_next(tail), to_previous(head)
    factors, b_own = prepare(
        far_right.reshape(groups, B, R), far_left.reshape(groups, B, R), own, far_size, per
    )
    meta = gather_far(jnp.stack([far_src.reshape(-1), far_tgt.reshape(-1)]))
    factors = gather_far(factors)
    done = own_products([own], cols, near_blocks, far_size, width, per)
    coef = exchange(coefficients(meta, factors, [b_own], far_size))
    pieces = [from_left, from_right, swap_cores(from_left), swap_cores(from_right)]
    keeps, sends = with_halo(pieces, done, cols, near_blocks, far_size, False)
    far = far_part(meta, factors, coef, far_size, per)
    g_own = add_halves(sum_far(keeps, sends) + [far])

    head, tail = g_own
    from_left, from_right = to_next(tail), to_previous(head)
    heads = [head] + [along_y(head, s) for s in range(1, ys)]
    tails = [tail] + [along_y(tail, s) for s in range(1, ys)]
    owns = [item for pair in zip(heads, tails) for item in pair]
    owns += [swap_cores(item) for item in owns]
    done = own_products(owns, cols, near_blocks, far_size, width, per)
    coef = exchange(coefficients(meta, factors, g_own, far_size))
    halos = [from_left, from_right]
    for s in range(1, ys):
        halos += [along_y(from_left, s), to_previous(heads[s])]
    halos += [swap_cores(item) for item in halos]
    keeps, sends = with_halo(halos, done, cols, near_blocks, far_size, True)
    far = far_part(meta, factors, coef, far_size, per)
    part_dots, image = dots(b_own, g_own, sum_far(keeps, sends) + [far], packs)
    answer, residual = finish(sum_rows(part_dots), b_own, g_own, image, packs)
    shape = (CL_DEV * B, width // far_size)
    return answer.reshape(shape), residual.reshape(shape)


def solution(mesh):
    return jax.shard_map(
        shards,
        mesh=mesh,
        in_specs=(
            P("rows", None),
            P("rows", "far", None, None),
            P("rows", "far"),
            P("rows", None, "far"),
            P("rows", None, "far"),
            P("rows", None, "far", None, None),
            P("rows", None, "far", None, None),
        ),
        out_specs=(P("rows", "far"), P("rows", "far")),
        check_vma=False,
    )
```

time: 456 us -> 183 us (0.40)
  waiting for transfers between devices: 169 us -> 59.9 us
  blocking collectives: 100 us -> 0 us
  Pallas kernels: 0 us -> 60.6 us
  matrix products: 59.5 us -> 0 us
  local copies, waits for them, and re-layouts: 60.7 us -> 12.3 us
  other arithmetic: 29.9 us -> 3.8 us
  starting transfers between devices: 20.6 us -> 43.2 us
  between operations: 14.2 us -> 0.97 us
    psum x2 -> x0, waiting for transfers between devices: 107 us -> none  [apply_op(): return 0.5 * vector_in + lax.psum(partial_image(vector_in), 'far')]
    psum x5 -> x0, blocking collectives: 100 us -> none  [the longest x2 42.7 us: orthogonal(): lax.psum(jnp.stack([column_dots(item, candidate) for item in vectors]), '...]
    pallas_call x0 -> x12, Pallas kernels: none -> 60.6 us  [the longest x2 22.6 us: with_halo(): pl.pallas_call(functools.partial(halo_kernel, far_size, last, len(pieces)...]
    dot_general x8 -> x0, matrix products: 59.5 us -> none  [the longest x2 40.8 us: near_term(): jnp.einsum('cspq,csqn->cpn', near_blocks, picked, precision=TOP_PRECISION)]
    gather x4 -> x0, local copies, waits for them, and re-layouts: 26.2 us -> none  [the longest x2 21.8 us: near_term(): picked = jnp.take(clusters, near_cols - offset, axis=0)]
    ppermute x4 -> x33, waiting for transfers between devices: 57.4 us -> 37 us  [the longest x2 15.3 us: to_next(): lax.ppermute(value, 'rows', [(i, i + 1) for i in range(lax.axis_size('row...]
    all_to_all x2, waiting for transfers between devices: 4.43 us -> 22.9 us  [exchange(): return lax.all_to_all(coef, 'rows', split_axis=0, concat_axis=0, tiled=True)]
    ppermute x4 -> x33, starting transfers between devices: 12.2 us -> 30.2 us  [the longest x2 10.8 us: to_next(): lax.ppermute(value, 'rows', [(i, i + 1) for i in range(lax.axis_size('row...]
  transfers between devices with their start and end apart: 8 -> 35, of which waited for: 6 -> 13; matrix products, arithmetic and copies ran while one was open for 5% -> 3% of each run, Pallas kernels for 0% -> 26%
where the time goes in v2:
time: 183 us; the launch traced here: 181 us
  Pallas kernels  60.6 us (33%)
  waiting for transfers between devices  59.9 us (33%)
  starting transfers between devices  43.2 us (24%)
  local copies, waits for them, and re-layouts  12.3 us (7%)
  other arithmetic  3.8 us (2%)
    all_to_all x2, waiting for transfers between devices, exchange(): return lax.all_to_all(coef, 'rows', split_axis=0, concat_axis=0, tiled=True)  22.9 us
    pallas_call x2, Pallas kernels, with_halo(): pl.pallas_call(functools.partial(halo_kernel, far_size, last, len(pieces)...  22.6 us
    pallas_call x2, Pallas kernels, own_products(): pl.pallas_call(functools.partial(own_kernel, far_size, len(pieces)), out_...  16.2 us
    ppermute x2, waiting for transfers between devices, to_next(): lax.ppermute(value, 'rows', [(i, i + 1) for i in range(lax.axis_size('row...  15.3 us
    all_to_all x2, starting transfers between devices, exchange(): return lax.all_to_all(coef, 'rows', split_axis=0, concat_axis=0, tiled=True)  13 us
    ppermute x2, starting transfers between devices, to_next(): lax.ppermute(value, 'rows', [(i, i + 1) for i in range(lax.axis_size('row...  10.8 us
    ppermute x7, starting transfers between devices, along_y(): lax.ppermute(value, 'far', [(i, (i + CORES * shift) % size) for i in rang...  10.5 us
    unnamed x33, local copies, waits for them, and re-layouts  9.8 us
  transfers between devices with their start and end apart: 35, of which 13 were waited for; matrix products, arithmetic and copies ran while one was open for 3% of the time, Pallas kernels for 26%

profile of v2, /device:TPU:0, one launch (start us, length us, event | category | flops | bytes accessed | tf_op | source)
XLA Modules:
  0.0 180.8 jit_solution(14934705264744432053)
XLA Ops:
  0.7 2.4 %constant_dynamic-slice_fusion = (f32[4,128,256]{2,1,0:T(8,128)}, f32[4,128,256]{2,1,0:T(8,128)}) fusion(f32[16,128,256]{2,1,0:T(8,128)} %bitcast.8, s32[]{:T(128)S(6)} %select_n.15, s32[]{:T(128)S(6)} %select_n.14), kind=kLoop, calls=%fused_computation.1 | loop fusion | bytes 2097160 | tf_op jit(solution)/shard_map/dynamic_slice | solution.py:608
  3.1 1.3 collective-permute-start.1
  4.4 6.3 %collective-permute-start = (f32[4,128,256]{2,1,0:T(8,128)}, f32[4,128,256]{2,1,0:T(8,128)}, u32[]{:S(2)}, u32[]{:S(2)}) collective-permute-start(f32[4,128,256]{2,1,0:T(8,128)} %get-tuple-element.39), channel_id=1, source_target_pairs={{0,4},{4,8},{8,12},{12,16},{16,20},{20,24},{24,28},{1,5},{5,9},{9,... | collective-permute-start | bytes 1572872 | tf_op jit(solution)/shard_map/ppermute | solution.py:568
  10.6 1.1 copy.15
  11.8 1.0 copy.14
  12.8 1.0 copy-done.5
  13.9 0.5 prepare.1
  14.3 0.8 copy-done.3
  15.1 2.1 %collective-permute-start.10 = (f32[2,8,64,128]{3,2,1,0:T(8,128)S(1)}, f32[2,8,64,128]{3,2,1,0:T(8,128)S(1)}, u32[]{:S(2)}, u32[]{:S(2)}) collective-permute-start(f32[2,8,64,128]{3,2,1,0:T(8,128)S(1)} %get-tuple-element.23.refs_4_), channel_id=1, source_target_pairs={{0,2},{1,3},{2,0},{3,1},{4,6},{5,7},{6,4},{7,5},{8,10},{9,11},{10,... | collective-permute-start | bytes 1572872 | tf_op jit(solution)/shard_map/ppermute | solution.py:558
  17.2 2.9 %collective-permute-done.1.refs_1_ = f32[4,128,256]{2,1,0:T(8,128)} collective-permute-done((f32[4,128,256]{2,1,0:T(8,128)}, f32[4,128,256]{2,1,0:T(8,128)}, u32[]{:S(2)}, u32[]{:S(2)}) %collective-permute-start.1) | collective-permute-done | bytes 524320 | tf_op jit(solution)/shard_map/ppermute | solution.py:572
  20.2 11.4 %collective-permute-done.refs_0_ = f32[4,128,256]{2,1,0:T(8,128)} collective-permute-done((f32[4,128,256]{2,1,0:T(8,128)}, f32[4,128,256]{2,1,0:T(8,128)}, u32[]{:S(2)}, u32[]{:S(2)}) %collective-permute-start) | collective-permute-done | bytes 524320 | tf_op jit(solution)/shard_map/ppermute | solution.py:568
  31.5 0.0 collective-permute-start.2
  31.6 0.5 collective-permute-start.11
  32.1 0.0 collective-permute-start.12
  32.1 0.1 copy.16
  32.2 0.1 reshape.31.cols_ref
  32.2 7.9 %own_products.2.done_ref = f32[2,2,4,128,256]{4,3,2,1,0:T(8,128)S(1)} custom-call(s32[96]{0:T(128)S(1)} %reshape.31.cols_ref, f32[2,2,4,6,128,128]{5,4,3,2,1,0:T(8,128)} %bitcast.15, f32[16,128,256]{2,1,0:T(8,128)S(1)} %bitcast.10), custom_call_target="tpu_custom_call" | custom-call | flops 2415919104 | bytes 6291456 | tf_op jit(solution)/shard_map/own_products/pallas_call | solution.py:282
  40.1 1.3 copy-done.2
  41.5 11.8 %with_halo.2 = (f32[8,128,128]{2,1,0:T(8,128)S(1)}, f32[8,128,128]{2,1,0:T(8,128)S(1)}, f32[8,128,128]{2,1,0:T(8,128)S(1)}, f32[8,128,128]{2,1,0:T(8,128)}) custom-call(s32[96]{0:T(128)S(1)} %reshape.31.cols_ref, f32[2,2,4,6,128,128]{5,4,3,2,1,0:T(8,128)} %bitcast.16, f32[2,2,4,128,256]{4,3,2,1,0:T(8,128)} %copy-done.2, ...), custom_call_target="tpu_custom_call" | custom-call | flops 805306368 | bytes 6291456 | tf_op jit(solution)/shard_map/with_halo/pallas_call | solution.py:388
  53.3 0.2 collective-permute-start.4
  53.5 1.7 collective-permute-start.7
  55.2 1.9 %collective-permute-done.7.refs_1_ = s32[2,8]{1,0:T(2,128)S(1)} collective-permute-done((s32[2,8]{1,0:T(2,128)S(1)}, s32[2,8]{1,0:T(2,128)S(1)}, u32[]{:S(2)}, u32[]{:S(2)}) %collective-permute-start.7) | collective-permute-done | bytes 96 | tf_op jit(solution)/shard_map/ppermute | solution.py:558
  57.2 1.1 collective-permute-done.9.refs_3_
  58.3 4.8 %coefficients.2 = f32[8,2,64,128]{3,2,1,0:T(8,128)} custom-call(s32[2,8]{1,0:T(2,128)S(1)} %pad_add_fusion.refs_0_, s32[2,8]{1,0:T(2,128)S(1)} %collective-permute-done.7.refs_1_, s32[2,8]{1,0:T(2,128)S(1)} %collective-permute-done.8.refs_2_, s32[2,8]{1,0:T(2,128)S(1)} %collective-permute-done.9.refs_3_, f32[2,8,64,128]{3,2,1,0:T(8,128)S(1)} %get-tuple-element.23.refs_4_, ...), custom_call_target="tpu_custom_call" | custom-call | flops 100663296 | bytes 4194304 | tf_op jit(solution)/shard_map/coefficients/pallas_call | solution.py:156
  63.2 7.3 %all-to-all-start = ((f32[8,2,64,128]{3,2,1,0:T(8,128)}), f32[8,2,64,128]{3,2,1,0:T(8,128)S(1)}, u32[]{:S(2)}, u32[]{:S(2)}) async-start(f32[8,2,64,128]{3,2,1,0:T(8,128)} %coefficients.2), calls=%async_computation | async-start | bytes 1048576 | tf_op jit(solution)/shard_map/all_to_all | solution.py:585
  70.4 1.9 %add.30 = f32[8,128,128]{2,1,0:T(8,128)} add(f32[8,128,128]{2,1,0:T(8,128)S(1)} %get-tuple-element.20, f32[8,128,128]{2,1,0:T(8,128)} %collective-permute-done.4) | non-fusion elementwise | flops 131072 | bytes 1572864 | tf_op jit(solution)/shard_map/add | solution.py:591
  72.3 1.5 collective-permute-start.5
  73.8 11.4 %all-to-all-done.refs_8_ = f32[8,2,64,128]{3,2,1,0:T(8,128)S(1)} async-done(((f32[8,2,64,128]{3,2,1,0:T(8,128)}), f32[8,2,64,128]{3,2,1,0:T(8,128)S(1)}, u32[]{:S(2)}, u32[]{:S(2)}) %all-to-all-start) | async-done | bytes 524320 | tf_op jit(solution)/shard_map/all_to_all | solution.py:585
  85.3 4.0 %far_part.2.refs_3_ = f32[8,128,128]{2,1,0:T(8,128)S(1)} custom-call(s32[2,8]{1,0:T(2,128)S(1)} %pad_add_fusion.refs_0_, s32[2,8]{1,0:T(2,128)S(1)} %collective-permute-done.7.refs_1_, s32[2,8]{1,0:T(2,128)S(1)} %collective-permute-done.8.refs_2_, s32[2,8]{1,0:T(2,128)S(1)} %collective-permute-done.9.refs_3_, ...), custom_call_target="tpu_custom_call" | custom-call | flops 100663296 | bytes 4194304 | tf_op jit(solution)/shard_map/far_part/pallas_call | solution.py:206
  89.3 1.3 add_halves.1
  90.6 1.3 collective-permute-start.20
  91.9 1.6 collective-permute-start.13
  93.5 4.6 %collective-permute-start.19 = (f32[4,128,128]{2,1,0:T(8,128)S(1)}, f32[4,128,128]{2,1,0:T(8,128)S(1)}, u32[]{:S(2)}, u32[]{:S(2)}) collective-permute-start(f32[4,128,128]{2,1,0:T(8,128)S(1)} %get-tuple-element.25.refs_1_.refs_9_.gr_ref), channel_id=1, source_target_pairs={{0,4},{4,8},{8,12},{12,16},{16,20},{20,24},{24,28},{1,5},{5,9},{9,... | collective-permute-start | bytes 786440 | tf_op jit(solution)/shard_map/ppermute | solution.py:568
  98.1 0.6 collective-permute-start.14
  98.6 0.9 collective-permute-done.20.refs_1_
  99.6 1.3 collective-permute-start.22
  100.9 0.6 collective-permute-start.17
  101.4 3.9 %collective-permute-done.19.refs_0_ = f32[4,128,128]{2,1,0:T(8,128)S(1)} collective-permute-done((f32[4,128,128]{2,1,0:T(8,128)S(1)}, f32[4,128,128]{2,1,0:T(8,128)S(1)}, u32[]{:S(2)}, u32[]{:S(2)}) %collective-permute-start.19) | collective-permute-done | bytes 262176 | tf_op jit(solution)/shard_map/ppermute | solution.py:568
  105.4 1.5 collective-permute-start.21
  106.9 0.5 collective-permute-start.23
  107.4 3.8 %collective-permute-done.22.refs_3_ = f32[4,128,128]{2,1,0:T(8,128)S(1)} collective-permute-done((f32[4,128,128]{2,1,0:T(8,128)S(1)}, f32[4,128,128]{2,1,0:T(8,128)S(1)}, u32[]{:S(2)}, u32[]{:S(2)}) %collective-permute-start.22) | collective-permute-done | bytes 262176 | tf_op jit(solution)/shard_map/ppermute | solution.py:572
  111.2 0.5 collective-permute-start.26
  111.7 1.9 %collective-permute-done.21.refs_2_ = f32[4,128,128]{2,1,0:T(8,128)S(1)} collective-permute-done((f32[4,128,128]{2,1,0:T(8,128)S(1)}, f32[4,128,128]{2,1,0:T(8,128)S(1)}, u32[]{:S(2)}, u32[]{:S(2)}) %collective-permute-start.21) | collective-permute-done | bytes 262176 | tf_op jit(solution)/shard_map/ppermute | solution.py:558
  113.6 8.3 %own_products.3.done_ref = f32[2,2,4,128,256]{4,3,2,1,0:T(8,128)S(1)} custom-call(s32[96]{0:T(128)S(1)} %reshape.31.cols_ref, f32[2,2,4,6,128,128]{5,4,3,2,1,0:T(8,128)} %bitcast.17, f32[4,128,128]{2,1,0:T(8,128)S(1)} %get-tuple-element.24.refs_0_.refs_8_.gl_ref, f32[4,128,128]{2,1,0:T(8,128)S(1)} %get-tuple-element.25.refs_1_.refs_9_.gr_ref, ...), custom_call_target="tpu_custom_call" | custom-call | flops 2415919104 | bytes 6291456 | tf_op jit(solution)/shard_map/own_products/pallas_call | solution.py:282
  122.0 1.3 copy-done.1
  123.3 10.8 %with_halo.3 = (f32[8,128,128]{2,1,0:T(8,128)S(1)}, f32[8,128,128]{2,1,0:T(8,128)S(1)}, f32[8,128,128]{2,1,0:T(8,128)S(1)}, f32[8,128,128]{2,1,0:T(8,128)}) custom-call(s32[96]{0:T(128)S(1)} %reshape.31.cols_ref, f32[2,2,4,6,128,128]{5,4,3,2,1,0:T(8,128)} %bitcast.18, f32[2,2,4,128,256]{4,3,2,1,0:T(8,128)} %copy-done.1, ...), custom_call_target="tpu_custom_call" | custom-call | flops 805306368 | bytes 6291456 | tf_op jit(solution)/shard_map/with_halo/pallas_call | solution.py:388
  134.1 0.8 copy-done.9
  134.9 0.1 collective-permute-start.27
  135.0 4.9 %coefficients.3 = f32[8,2,64,128]{3,2,1,0:T(8,128)} custom-call(s32[2,8]{1,0:T(2,128)S(1)} %pad_add_fusion.refs_0_, s32[2,8]{1,0:T(2,128)S(1)} %collective-permute-done.7.refs_1_, s32[2,8]{1,0:T(2,128)S(1)} %collective-permute-done.8.refs_2_, s32[2,8]{1,0:T(2,128)S(1)} %collective-permute-done.9.refs_3_, f32[2,8,64,128]{3,2,1,0:T(8,128)S(1)} %get-tuple-element.23.refs_4_, ...), custom_call_target="tpu_custom_call" | custom-call | flops 100663296 | bytes 4194304 | tf_op jit(solution)/shard_map/coefficients/pallas_call | solution.py:156
  139.9 5.8 %all-to-all-start.1 = ((f32[8,2,64,128]{3,2,1,0:T(8,128)}), f32[8,2,64,128]{3,2,1,0:T(8,128)S(1)}, u32[]{:S(2)}, u32[]{:S(2)}) async-start(f32[8,2,64,128]{3,2,1,0:T(8,128)} %coefficients.3), calls=%async_computation.1 | async-start | bytes 1048576 | tf_op jit(solution)/shard_map/all_to_all | solution.py:585
  145.7 1.9 %add.31 = f32[8,128,128]{2,1,0:T(8,128)} add(f32[8,128,128]{2,1,0:T(8,128)S(1)} %get-tuple-element.27, f32[8,128,128]{2,1,0:T(8,128)} %collective-permute-done.27) | non-fusion elementwise | flops 131072 | bytes 1572864 | tf_op jit(solution)/shard_map/add | solution.py:591
  147.6 1.5 collective-permute-start.28
  149.1 11.5 %all-to-all-done.1.refs_8_ = f32[8,2,64,128]{3,2,1,0:T(8,128)S(1)} async-done(((f32[8,2,64,128]{3,2,1,0:T(8,128)}), f32[8,2,64,128]{3,2,1,0:T(8,128)S(1)}, u32[]{:S(2)}, u32[]{:S(2)}) %all-to-all-start.1) | async-done | bytes 524320 | tf_op jit(solution)/shard_map/all_to_all | solution.py:585
  160.6 4.0 %far_part.3.refs_3_ = f32[8,128,128]{2,1,0:T(8,128)S(1)} custom-call(s32[2,8]{1,0:T(2,128)S(1)} %pad_add_fusion.refs_0_, s32[2,8]{1,0:T(2,128)S(1)} %collective-permute-done.7.refs_1_, s32[2,8]{1,0:T(2,128)S(1)} %collective-permute-done.8.refs_2_, s32[2,8]{1,0:T(2,128)S(1)} %collective-permute-done.9.refs_3_, ...), custom_call_target="tpu_custom_call" | custom-call | flops 100663296 | bytes 4194304 | tf_op jit(solution)/shard_map/far_part/pallas_call | solution.py:206
  164.7 1.7 dots.1
  166.4 1.5 collective-permute-start.30
  167.9 2.1 %collective-permute-done.30 = f32[8,128]{1,0:T(8,128)S(1)} collective-permute-done((f32[8,128]{1,0:T(8,128)S(1)}, f32[8,128]{1,0:T(8,128)S(1)}, u32[]{:S(2)}, u32[]{:S(2)}) %collective-permute-start.30) | collective-permute-done | bytes 4128 | tf_op jit(solution)/shard_map/ppermute | solution.py:579
  170.0 0.8 collective-permute-start.31
  170.8 2.8 %collective-permute-done.31 = f32[8,128]{1,0:T(8,128)S(1)} collective-permute-done((f32[8,128]{1,0:T(8,128)S(1)}, f32[8,128]{1,0:T(8,128)S(1)}, u32[]{:S(2)}, u32[]{:S(2)}) %collective-permute-start.31) | collective-permute-done | bytes 4128 | tf_op jit(solution)/shard_map/ppermute | solution.py:579
  173.6 0.5 collective-permute-start.32
  174.1 4.0 %collective-permute-done.32 = f32[8,128]{1,0:T(8,128)S(1)} collective-permute-done((f32[8,128]{1,0:T(8,128)S(1)}, f32[8,128]{1,0:T(8,128)S(1)}, u32[]{:S(2)}, u32[]{:S(2)}) %collective-permute-start.32) | collective-permute-done | bytes 4128 | tf_op jit(solution)/shard_map/ppermute | solution.py:579
  178.1 0.4 finish.1
  178.6 1.1 copy.17
  179.7 1.1 copy.18
  (59 shorter events, 0.2 us)
Async XLA Ops:
  0.6 12.2 %copy-start = (f32[2048,256]{1,0:T(8,128)S(1)}, f32[2048,256]{1,0:T(8,128)}, u32[]{:S(2)}) copy-start(f32[2048,256]{1,0:T(8,128)} %param.7) | copy-start | bytes 6291460
  0.6 11.2 %copy-start.10 = (f32[1,8,1,128,64]{3,4,2,1,0:T(8,128)S(1)}, f32[1,8,1,128,64]{3,4,2,1,0:T(8,128)}, u32[]{:S(2)}) copy-start(f32[1,8,1,128,64]{3,4,2,1,0:T(8,128)} %param.13) | copy-start | bytes 786436
  3.1 17.1 %collective-permute-start.1 = (f32[4,128,256]{2,1,0:T(8,128)}, f32[4,128,256]{2,1,0:T(8,128)}, u32[]{:S(2)}, u32[]{:S(2)}) collective-permute-start(f32[4,128,256]{2,1,0:T(8,128)} %get-tuple-element.38), channel_id=1, source_target_pairs={{4,0},{8,4},{12,8},{16,12},{20,16},{24,20},{28,24},{5,1},{9,5},{13... | collective-permute-start | bytes 1572872 | tf_op jit(solution)/shard_map/ppermute | solution.py:572
  4.4 27.2 %collective-permute-start = (f32[4,128,256]{2,1,0:T(8,128)}, f32[4,128,256]{2,1,0:T(8,128)}, u32[]{:S(2)}, u32[]{:S(2)}) collective-permute-start(f32[4,128,256]{2,1,0:T(8,128)} %get-tuple-element.39), channel_id=1, source_target_pairs={{0,4},{4,8},{8,12},{12,16},{16,20},{20,24},{24,28},{1,5},{5,9},{9,... | collective-permute-start | bytes 1572872 | tf_op jit(solution)/shard_map/ppermute | solution.py:568
  11.8 20.3 %copy-start.11 = (s32[16,6]{0,1:T(8,128)S(1)}, s32[16,6]{0,1:T(8,128)}, u32[]{:S(2)}) copy-start(s32[16,6]{0,1:T(8,128)} %param.9) | copy-start | bytes 1156
  12.8 1.0 copy-start.5
  14.3 0.8 copy-start.3
  15.1 16.9 %collective-permute-start.10 = (f32[2,8,64,128]{3,2,1,0:T(8,128)S(1)}, f32[2,8,64,128]{3,2,1,0:T(8,128)S(1)}, u32[]{:S(2)}, u32[]{:S(2)}) collective-permute-start(f32[2,8,64,128]{3,2,1,0:T(8,128)S(1)} %get-tuple-element.23.refs_4_), channel_id=1, source_target_pairs={{0,2},{1,3},{2,0},{3,1},{4,6},{5,7},{6,4},{7,5},{8,10},{9,11},{10,... | collective-permute-start | bytes 1572872 | tf_op jit(solution)/shard_map/ppermute | solution.py:558
  20.2 21.3 %collective-permute-start.3 = (f32[4,128,256]{2,1,0:T(8,128)}, f32[4,128,256]{2,1,0:T(8,128)}, u32[]{:S(2)}, u32[]{:S(2)}) collective-permute-start(f32[4,128,256]{2,1,0:T(8,128)} %collective-permute-done.1.refs_1_), channel_id=1, source_target_pairs={{0,1},{1,0},{2,3},{3,2},{4,5},{5,4},{6,7},{7,6},{8,9},{9,8},{10,11... | collective-permute-start | bytes 1572872 | tf_op jit(solution)/shard_map/ppermute | solution.py:553
  31.5 9.9 %collective-permute-start.2 = (f32[4,128,256]{2,1,0:T(8,128)}, f32[4,128,256]{2,1,0:T(8,128)}, u32[]{:S(2)}, u32[]{:S(2)}) collective-permute-start(f32[4,128,256]{2,1,0:T(8,128)} %collective-permute-done.refs_0_), channel_id=1, source_target_pairs={{0,1},{1,0},{2,3},{3,2},{4,5},{5,4},{6,7},{7,6},{8,9},{9,8},{10,11... | collective-permute-start | bytes 1572872 | tf_op jit(solution)/shard_map/ppermute | solution.py:553
  31.6 26.7 %collective-permute-start.11 = (f32[2,8,64,128]{3,2,1,0:T(8,128)S(1)}, f32[2,8,64,128]{3,2,1,0:T(8,128)}, u32[]{:S(2)}, u32[]{:S(2)}) collective-permute-start(f32[2,8,64,128]{3,2,1,0:T(8,128)S(1)} %get-tuple-element.23.refs_4_), channel_id=1, source_target_pairs={{0,1},{1,0},{2,3},{3,2},{4,5},{5,4},{6,7},{7,6},{8,9},{9,8},{10,11... | collective-permute-start | bytes 1572872 | tf_op jit(solution)/shard_map/ppermute | solution.py:553
  32.1 26.2 %collective-permute-start.12 = (f32[2,8,64,128]{3,2,1,0:T(8,128)S(1)}, f32[2,8,64,128]{3,2,1,0:T(8,128)}, u32[]{:S(2)}, u32[]{:S(2)}) collective-permute-start(f32[2,8,64,128]{3,2,1,0:T(8,128)S(1)} %collective-permute-done.10.refs_5_), channel_id=1, source_target_pairs={{0,1},{1,0},{2,3},{3,2},{4,5},{5,4},{6,7},{7,6},{8,9},{9,8},{10,11... | collective-permute-start | bytes 1572872 | tf_op jit(solution)/shard_map/ppermute | solution.py:553
  40.1 1.3 copy-start.2
  41.5 12.1 %copy-start.12 = (s32[1,8,1]{1,2,0:T(1,128)S(1)}, s32[1,8,1]{1,2,0:T(1,128)}, u32[]{:S(2)}) copy-start(s32[1,8,1]{1,2,0:T(1,128)} %param.11) | copy-start | bytes 100
  41.5 12.1 %copy-start.13 = (s32[1,8,1]{1,2,0:T(1,128)S(1)}, s32[1,8,1]{1,2,0:T(1,128)}, u32[]{:S(2)}) copy-start(s32[1,8,1]{1,2,0:T(1,128)} %param.10) | copy-start | bytes 100
  41.5 16.8 %copy-start.4 = (f32[8,128,128]{2,1,0:T(8,128)S(1)}, f32[8,128,128]{2,1,0:T(8,128)}, u32[]{:S(2)}) copy-start(f32[8,128,128]{2,1,0:T(8,128)} %copy-done.3) | copy-start | bytes 1572868
  53.3 9.8 %copy-start.8 = (f32[8,128,128]{2,1,0:T(8,128)}, f32[8,128,128]{2,1,0:T(8,128)S(1)}, u32[]{:S(2)}) copy-start(f32[8,128,128]{2,1,0:T(8,128)S(1)} %get-tuple-element.22) | copy-start | bytes 1572868
  53.3 17.1 %collective-permute-start.4 = (f32[8,128,128]{2,1,0:T(8,128)}, f32[8,128,128]{2,1,0:T(8,128)}, u32[]{:S(2)}, u32[]{:S(2)}) collective-permute-start(f32[8,128,128]{2,1,0:T(8,128)} %get-tuple-element.21), channel_id=1, source_target_pairs={{0,1},{1,0},{2,3},{3,2},{4,5},{5,4},{6,7},{7,6},{8,9},{9,8},{10,11... | collective-permute-start | bytes 1572872 | tf_op jit(solution)/shard_map/ppermute | solution.py:553
  53.5 3.6 %collective-permute-start.7 = (s32[2,8]{1,0:T(2,128)S(1)}, s32[2,8]{1,0:T(2,128)S(1)}, u32[]{:S(2)}, u32[]{:S(2)}) collective-permute-start(s32[2,8]{1,0:T(2,128)S(1)} %pad_add_fusion.refs_0_), channel_id=1, source_target_pairs={{0,2},{1,3},{2,0},{3,1},{4,6},{5,7},{6,4},{7,5},{8,10},{9,11},{10,... | collective-permute-start | bytes 200 | tf_op jit(solution)/shard_map/ppermute | solution.py:558
  55.2 1.9 %collective-permute-start.8 = (s32[2,8]{1,0:T(2,128)S(1)}, s32[2,8]{1,0:T(2,128)S(1)}, u32[]{:S(2)}, u32[]{:S(2)}) collective-permute-start(s32[2,8]{1,0:T(2,128)S(1)} %pad_add_fusion.refs_0_), channel_id=1, source_target_pairs={{0,1},{1,0},{2,3},{3,2},{4,5},{5,4},{6,7},{7,6},{8,9},{9,8},{10,11... | collective-permute-start | bytes 200 | tf_op jit(solution)/shard_map/ppermute | solution.py:553
  57.2 1.1 collective-permute-start.9
  63.2 22.1 %all-to-all-start = ((f32[8,2,64,128]{3,2,1,0:T(8,128)}), f32[8,2,64,128]{3,2,1,0:T(8,128)S(1)}, u32[]{:S(2)}, u32[]{:S(2)}) async-start(f32[8,2,64,128]{3,2,1,0:T(8,128)} %coefficients.2), calls=%async_computation | async-start | bytes 1048576 | tf_op jit(solution)/shard_map/all_to_all | solution.py:585
  70.4 18.9 %collective-permute-start.6 = (f32[8,128,128]{2,1,0:T(8,128)}, f32[8,128,128]{2,1,0:T(8,128)}, u32[]{:S(2)}, u32[]{:S(2)}) collective-permute-start(f32[8,128,128]{2,1,0:T(8,128)} %copy-done.8), channel_id=1, source_target_pairs={{0,1},{1,0},{2,3},{3,2},{4,5},{5,4},{6,7},{7,6},{8,9},{9,8},{10,11... | collective-permute-start | bytes 1572872 | tf_op jit(solution)/shard_map/ppermute | solution.py:553
  72.3 17.0 %collective-permute-start.5 = (f32[8,128,128]{2,1,0:T(8,128)}, f32[8,128,128]{2,1,0:T(8,128)}, u32[]{:S(2)}, u32[]{:S(2)}) collective-permute-start(f32[8,128,128]{2,1,0:T(8,128)} %add.30), channel_id=1, source_target_pairs={{0,2},{1,3},{2,0},{3,1},{4,6},{5,7},{6,4},{7,5},{8,10},{9,11},{10,... | collective-permute-start | bytes 1572872 | tf_op jit(solution)/shard_map/ppermute | solution.py:558
  90.6 8.9 %collective-permute-start.20 = (f32[4,128,128]{2,1,0:T(8,128)S(1)}, f32[4,128,128]{2,1,0:T(8,128)S(1)}, u32[]{:S(2)}, u32[]{:S(2)}) collective-permute-start(f32[4,128,128]{2,1,0:T(8,128)S(1)} %get-tuple-element.24.refs_0_.refs_8_.gl_ref), channel_id=1, source_target_pairs={{4,0},{8,4},{12,8},{16,12},{20,16},{24,20},{28,24},{5,1},{9,5},{13... | collective-permute-start | bytes 786440 | tf_op jit(solution)/shard_map/ppermute | solution.py:572
  91.9 7.6 %collective-permute-start.13 = (f32[4,128,128]{2,1,0:T(8,128)S(1)}, f32[4,128,128]{2,1,0:T(8,128)S(1)}, u32[]{:S(2)}, u32[]{:S(2)}) collective-permute-start(f32[4,128,128]{2,1,0:T(8,128)S(1)} %get-tuple-element.24.refs_0_.refs_8_.gl_ref), channel_id=1, source_target_pairs={{0,2},{1,3},{2,0},{3,1},{4,6},{5,7},{6,4},{7,5},{8,10},{9,11},{10,... | collective-permute-start | bytes 786440 | tf_op jit(solution)/shard_map/ppermute | solution.py:558
  93.5 7.4 %collective-permute-start.15 = (f32[4,128,128]{2,1,0:T(8,128)S(1)}, f32[4,128,128]{2,1,0:T(8,128)S(1)}, u32[]{:S(2)}, u32[]{:S(2)}) collective-permute-start(f32[4,128,128]{2,1,0:T(8,128)S(1)} %get-tuple-element.24.refs_0_.refs_8_.gl_ref), channel_id=1, source_target_pairs={{0,1},{1,0},{2,3},{3,2},{4,5},{5,4},{6,7},{7,6},{8,9},{9,8},{10,11... | collective-permute-start | bytes 786440 | tf_op jit(solution)/shard_map/ppermute | solution.py:553
  93.5 11.9 %collective-permute-start.19 = (f32[4,128,128]{2,1,0:T(8,128)S(1)}, f32[4,128,128]{2,1,0:T(8,128)S(1)}, u32[]{:S(2)}, u32[]{:S(2)}) collective-permute-start(f32[4,128,128]{2,1,0:T(8,128)S(1)} %get-tuple-element.25.refs_1_.refs_9_.gr_ref), channel_id=1, source_target_pairs={{0,4},{4,8},{8,12},{12,16},{16,20},{20,24},{24,28},{1,5},{5,9},{9,... | collective-permute-start | bytes 786440 | tf_op jit(solution)/shard_map/ppermute | solution.py:568
  98.1 8.8 %collective-permute-start.14 = (f32[4,128,128]{2,1,0:T(8,128)S(1)}, f32[4,128,128]{2,1,0:T(8,128)S(1)}, u32[]{:S(2)}, u32[]{:S(2)}) collective-permute-start(f32[4,128,128]{2,1,0:T(8,128)S(1)} %get-tuple-element.25.refs_1_.refs_9_.gr_ref), channel_id=1, source_target_pairs={{0,2},{1,3},{2,0},{3,1},{4,6},{5,7},{6,4},{7,5},{8,10},{9,11},{10,... | collective-permute-start | bytes 786440 | tf_op jit(solution)/shard_map/ppermute | solution.py:558
  99.6 7.3 %collective-permute-start.16 = (f32[4,128,128]{2,1,0:T(8,128)S(1)}, f32[4,128,128]{2,1,0:T(8,128)S(1)}, u32[]{:S(2)}, u32[]{:S(2)}) collective-permute-start(f32[4,128,128]{2,1,0:T(8,128)S(1)} %get-tuple-element.25.refs_1_.refs_9_.gr_ref), channel_id=1, source_target_pairs={{0,1},{1,0},{2,3},{3,2},{4,5},{5,4},{6,7},{7,6},{8,9},{9,8},{10,11... | collective-permute-start | bytes 786440 | tf_op jit(solution)/shard_map/ppermute | solution.py:553
  99.6 11.6 %collective-permute-start.22 = (f32[4,128,128]{2,1,0:T(8,128)S(1)}, f32[4,128,128]{2,1,0:T(8,128)S(1)}, u32[]{:S(2)}, u32[]{:S(2)}) collective-permute-start(f32[4,128,128]{2,1,0:T(8,128)S(1)} %collective-permute-done.13.refs_2_), channel_id=1, source_target_pairs={{4,0},{8,4},{12,8},{16,12},{20,16},{24,20},{28,24},{5,1},{9,5},{13... | collective-permute-start | bytes 786440 | tf_op jit(solution)/shard_map/ppermute | solution.py:572
  100.9 10.3 %collective-permute-start.17 = (f32[4,128,128]{2,1,0:T(8,128)S(1)}, f32[4,128,128]{2,1,0:T(8,128)S(1)}, u32[]{:S(2)}, u32[]{:S(2)}) collective-permute-start(f32[4,128,128]{2,1,0:T(8,128)S(1)} %collective-permute-done.13.refs_2_), channel_id=1, source_target_pairs={{0,1},{1,0},{2,3},{3,2},{4,5},{5,4},{6,7},{7,6},{8,9},{9,8},{10,11... | collective-permute-start | bytes 786440 | tf_op jit(solution)/shard_map/ppermute | solution.py:553
  105.4 8.3 %collective-permute-start.21 = (f32[4,128,128]{2,1,0:T(8,128)S(1)}, f32[4,128,128]{2,1,0:T(8,128)S(1)}, u32[]{:S(2)}, u32[]{:S(2)}) collective-permute-start(f32[4,128,128]{2,1,0:T(8,128)S(1)} %collective-permute-done.19.refs_0_), channel_id=1, source_target_pairs={{0,2},{1,3},{2,0},{3,1},{4,6},{5,7},{6,4},{7,5},{8,10},{9,11},{10,... | collective-permute-start | bytes 786440 | tf_op jit(solution)/shard_map/ppermute | solution.py:558
  106.9 6.7 %collective-permute-start.18 = (f32[4,128,128]{2,1,0:T(8,128)S(1)}, f32[4,128,128]{2,1,0:T(8,128)S(1)}, u32[]{:S(2)}, u32[]{:S(2)}) collective-permute-start(f32[4,128,128]{2,1,0:T(8,128)S(1)} %collective-permute-done.14.refs_3_), channel_id=1, source_target_pairs={{0,1},{1,0},{2,3},{3,2},{4,5},{5,4},{6,7},{7,6},{8,9},{9,8},{10,11... | collective-permute-start | bytes 786440 | tf_op jit(solution)/shard_map/ppermute | solution.py:553
  106.9 16.4 %collective-permute-start.23 = (f32[4,128,128]{2,1,0:T(8,128)S(1)}, f32[4,128,128]{2,1,0:T(8,128)S(1)}, u32[]{:S(2)}, u32[]{:S(2)}) collective-permute-start(f32[4,128,128]{2,1,0:T(8,128)S(1)} %collective-permute-done.19.refs_0_), channel_id=1, source_target_pairs={{0,1},{1,0},{2,3},{3,2},{4,5},{5,4},{6,7},{7,6},{8,9},{9,8},{10,11... | collective-permute-start | bytes 786440 | tf_op jit(solution)/shard_map/ppermute | solution.py:553
  111.2 12.1 %collective-permute-start.24 = (f32[4,128,128]{2,1,0:T(8,128)S(1)}, f32[4,128,128]{2,1,0:T(8,128)S(1)}, u32[]{:S(2)}, u32[]{:S(2)}) collective-permute-start(f32[4,128,128]{2,1,0:T(8,128)S(1)} %collective-permute-done.20.refs_1_), channel_id=1, source_target_pairs={{0,1},{1,0},{2,3},{3,2},{4,5},{5,4},{6,7},{7,6},{8,9},{9,8},{10,11... | collective-permute-start | bytes 786440 | tf_op jit(solution)/shard_map/ppermute | solution.py:553
  111.2 12.1 %collective-permute-start.26 = (f32[4,128,128]{2,1,0:T(8,128)S(1)}, f32[4,128,128]{2,1,0:T(8,128)S(1)}, u32[]{:S(2)}, u32[]{:S(2)}) collective-permute-start(f32[4,128,128]{2,1,0:T(8,128)S(1)} %collective-permute-done.22.refs_3_), channel_id=1, source_target_pairs={{0,1},{1,0},{2,3},{3,2},{4,5},{5,4},{6,7},{7,6},{8,9},{9,8},{10,11... | collective-permute-start | bytes 786440 | tf_op jit(solution)/shard_map/ppermute | solution.py:553
  113.6 9.7 %collective-permute-start.25 = (f32[4,128,128]{2,1,0:T(8,128)S(1)}, f32[4,128,128]{2,1,0:T(8,128)S(1)}, u32[]{:S(2)}, u32[]{:S(2)}) collective-permute-start(f32[4,128,128]{2,1,0:T(8,128)S(1)} %collective-permute-done.21.refs_2_), channel_id=1, source_target_pairs={{0,1},{1,0},{2,3},{3,2},{4,5},{5,4},{6,7},{7,6},{8,9},{9,8},{10,11... | collective-permute-start | bytes 786440 | tf_op jit(solution)/shard_map/ppermute | solution.py:553
  121.9 1.3 copy-start.1
  134.1 0.8 copy-start.9
  134.9 5.0 %copy-start.6 = (f32[8,128,128]{2,1,0:T(8,128)}, f32[8,128,128]{2,1,0:T(8,128)S(1)}, u32[]{:S(2)}) copy-start(f32[8,128,128]{2,1,0:T(8,128)S(1)} %get-tuple-element.26.refs_0_) | copy-start | bytes 1572868
  134.9 10.8 %collective-permute-start.27 = (f32[8,128,128]{2,1,0:T(8,128)}, f32[8,128,128]{2,1,0:T(8,128)}, u32[]{:S(2)}, u32[]{:S(2)}) collective-permute-start(f32[8,128,128]{2,1,0:T(8,128)} %get-tuple-element.28), channel_id=1, source_target_pairs={{0,1},{1,0},{2,3},{3,2},{4,5},{5,4},{6,7},{7,6},{8,9},{9,8},{10,11... | collective-permute-start | bytes 1572872 | tf_op jit(solution)/shard_map/ppermute | solution.py:553
  139.9 20.7 %all-to-all-start.1 = ((f32[8,2,64,128]{3,2,1,0:T(8,128)}), f32[8,2,64,128]{3,2,1,0:T(8,128)S(1)}, u32[]{:S(2)}, u32[]{:S(2)}) async-start(f32[8,2,64,128]{3,2,1,0:T(8,128)} %coefficients.3), calls=%async_computation.1 | async-start | bytes 1048576 | tf_op jit(solution)/shard_map/all_to_all | solution.py:585
  145.7 19.0 %collective-permute-start.29 = (f32[8,128,128]{2,1,0:T(8,128)}, f32[8,128,128]{2,1,0:T(8,128)}, u32[]{:S(2)}, u32[]{:S(2)}) collective-permute-start(f32[8,128,128]{2,1,0:T(8,128)} %copy-done.9), channel_id=1, source_target_pairs={{0,1},{1,0},{2,3},{3,2},{4,5},{5,4},{6,7},{7,6},{8,9},{9,8},{10,11... | collective-permute-start | bytes 1572872 | tf_op jit(solution)/shard_map/ppermute | solution.py:553
  147.6 17.1 %copy-start.7 = (f32[8,128,128]{2,1,0:T(8,128)S(1)}, f32[8,128,128]{2,1,0:T(8,128)}, u32[]{:S(2)}) copy-start(f32[8,128,128]{2,1,0:T(8,128)} %copy-done.6) | copy-start | bytes 1572868
  147.6 17.1 %collective-permute-start.28 = (f32[8,128,128]{2,1,0:T(8,128)}, f32[8,128,128]{2,1,0:T(8,128)}, u32[]{:S(2)}, u32[]{:S(2)}) collective-permute-start(f32[8,128,128]{2,1,0:T(8,128)} %add.31), channel_id=1, source_target_pairs={{0,2},{1,3},{2,0},{3,1},{4,6},{5,7},{6,4},{7,5},{8,10},{9,11},{10,... | collective-permute-start | bytes 1572872 | tf_op jit(solution)/shard_map/ppermute | solution.py:558
  166.4 3.6 %collective-permute-start.30 = (f32[8,128]{1,0:T(8,128)S(1)}, f32[8,128]{1,0:T(8,128)S(1)}, u32[]{:S(2)}, u32[]{:S(2)}) collective-permute-start(f32[8,128]{1,0:T(8,128)S(1)} %get-tuple-element.30), channel_id=1, source_target_pairs={{0,4},{4,0},{8,12},{12,8},{16,20},{20,16},{24,28},{28,24},{1,5},{5... | collective-permute-start | bytes 12296 | tf_op jit(solution)/shard_map/ppermute | solution.py:579
  170.0 3.6 %collective-permute-start.31 = (f32[8,128]{1,0:T(8,128)S(1)}, f32[8,128]{1,0:T(8,128)S(1)}, u32[]{:S(2)}, u32[]{:S(2)}) collective-permute-start(f32[8,128]{1,0:T(8,128)S(1)} %add.32), channel_id=1, source_target_pairs={{0,8},{4,12},{8,0},{12,4},{16,24},{20,28},{24,16},{28,20},{1,9},{5... | collective-permute-start | bytes 12296 | tf_op jit(solution)/shard_map/ppermute | solution.py:579
  173.6 4.5 %collective-permute-start.32 = (f32[8,128]{1,0:T(8,128)S(1)}, f32[8,128]{1,0:T(8,128)S(1)}, u32[]{:S(2)}, u32[]{:S(2)}) collective-permute-start(f32[8,128]{1,0:T(8,128)S(1)} %add.33), channel_id=1, source_target_pairs={{0,16},{4,20},{8,24},{12,28},{16,0},{20,4},{24,8},{28,12},{1,17},{... | collective-permute-start | bytes 12296 | tf_op jit(solution)/shard_map/ppermute | solution.py:579

commit v3 on v2

v3 whole, which is shorter than its diff:
```python
import functools

import jax
import jax.numpy as jnp
from jax import lax
from jax.experimental import pallas as pl
from jax.experimental.pallas import tpu as pltpu
from jax.sharding import PartitionSpec as P

B = 128
R = 64
CL_DEV = 16
REACH = 8
CORES = 2
LANES = 128
EPS = 1e-06
F32 = jnp.float32
BF16 = jnp.bfloat16
VMEM_LIMIT = 54 * 1024 * 1024


VMEM_SPEC = pl.BlockSpec(memory_space=pltpu.VMEM)
SMEM_SPEC = pl.BlockSpec(memory_space=pltpu.SMEM)
ANY_SPEC = pl.BlockSpec(memory_space=pl.ANY)
PARAMS = pltpu.CompilerParams(vmem_limit_bytes=VMEM_LIMIT)


def split(value):
    high = value.astype(BF16)
    low = (value - high.astype(F32)).astype(BF16)
    return high, low


def dot3(left, right, dims=((1,), (0,))):
    (lh, ll), (rh, rl) = left, right
    dot = functools.partial(
        lax.dot_general, dimension_numbers=(dims, ((), ())), preferred_element_type=F32
    )
    return dot(lh, rh) + (dot(ll, rh) + dot(lh, rl))


def cost(flops, size):
    return pl.CostEstimate(flops=flops, bytes_accessed=size, transcendentals=0)


def place(far_size):
    index = lax.axis_index("far")
    return index // CORES, index % CORES, far_size // CORES


def owner_of(n, far_size):
    y, core, ys = place(far_size)
    shift, other = n % ys, n // ys
    return lax.rem(y - shift + ys, ys) * CORES + (1 - core if other else core)


def begin(pairs, sems, first=0):
    copies = [pltpu.make_async_copy(a, b, sems.at[first + n]) for n, (a, b) in enumerate(pairs)]
    for copy in copies:
        copy.start()
    return copies


def fetch(pairs, sems, first=0):
    for copy in begin(pairs, sems, first):
        copy.wait()


def buffers(arrays):
    return [pltpu.VMEM(a.shape, a.dtype) for a in arrays]


def cluster_at(half, j, k, per):
    return half * REACH + j * per + k


def pack_columns(far_size, per, source, out_ref):
    index = lax.axis_index("far")
    packs = REACH // per
    width = LANES // packs
    for owner in range(far_size):

        @pl.when(index == owner)
        def _():
            for half in range(2):
                for k in range(per):
                    out_ref[half * per + k] = jnp.concatenate(
                        [
                            source(cluster_at(half, j, k, per))[:, owner * width : (owner + 1) * width]
                            for j in range(packs)
                        ],
                        axis=1,
                    )


def pack_kernel(far_size, b_ref, out, field, own, sems):
    fetch([(b_ref, field)], sems)
    pack_columns(far_size, own.shape[0] // 2, lambda c: field[c], own)
    fetch([(own, out)], sems)


def pack(field, far_size, per):
    out = jax.ShapeDtypeStruct((2 * per, B, LANES), F32)
    return pl.pallas_call(
        functools.partial(pack_kernel, far_size),
        out_shape=out,
        in_specs=[ANY_SPEC],
        out_specs=ANY_SPEC,
        scratch_shapes=buffers([field, out]) + [pltpu.SemaphoreType.DMA((1,))],
        compiler_params=PARAMS,
        cost_estimate=cost(0, 8 * field.size),
        name="pack",
    )(field)


def coefficient_kernel(far_size, n_fields, *refs):
    meta, hbm = refs[:far_size], refs[far_size : 2 * far_size + n_fields]
    out, refs = refs[2 * far_size + n_fields], refs[2 * far_size + n_fields + 1 :]
    vmem, (held, high, low, sems) = refs[: far_size + n_fields], refs[far_size + n_fields :]
    copies = begin(list(zip(hbm, vmem)), sems)
    factors, fields = vmem[:far_size], vmem[far_size:]
    per = sum(f.shape[0] for f in fields) // 2
    packs = REACH // per
    width = LANES // packs
    for copy in copies[far_size:]:
        copy.wait()
    entries = [f[k] for f in fields for k in range(f.shape[0])]
    for half in range(2):
        for k in range(per):
            entry = entries[half * per + k]
            for j in range(packs):
                h, l = split(entry[:, j * width : (j + 1) * width])
                high[cluster_at(half, j, k, per)] = h
                low[cluster_at(half, j, k, per)] = l
    for copy in copies[:far_size]:
        copy.wait()
    depth = far_size // packs

    def group(t, carry):
        for e in range(depth):
            parts = []
            for j in range(packs):
                n = j * depth + e
                source = meta[n][0, t]
                parts.append(dot3(split(factors[n][t]), (high[source], low[source])))
            held[t, e] = jnp.concatenate(parts, axis=1)
        return carry

    lax.fori_loop(0, held.shape[0], group, 0)
    fetch([(held, out)], sems)


def coefficients(meta, factors, fields, far_size):
    groups = factors[0].shape[0]
    per = sum(f.shape[0] for f in fields) // 2
    packs = REACH // per
    width = LANES // packs
    out = jax.ShapeDtypeStruct((groups, far_size // packs, R, LANES), F32)
    return pl.pallas_call(
        functools.partial(coefficient_kernel, far_size, len(fields)),
        out_shape=out,
        in_specs=[SMEM_SPEC] * far_size + [ANY_SPEC] * (far_size + len(fields)),
        out_specs=ANY_SPEC,
        scratch_shapes=buffers([*factors, *fields, out])
        + [
            pltpu.VMEM((CL_DEV, B, width), BF16),
            pltpu.VMEM((CL_DEV, B, width), BF16),
            pltpu.SemaphoreType.DMA((far_size + len(fields),)),
        ],
        compiler_params=PARAMS,
        cost_estimate=cost(6 * groups * far_size * R * B * width, 4 * 1024 * 1024),
        name="coefficients",
    )(*meta, *factors, *fields)


def far_kernel(far_size, *refs):
    meta, hbm = refs[:far_size], refs[far_size : 2 * far_size + 1]
    out, refs = refs[2 * far_size + 1], refs[2 * far_size + 2 :]
    vmem, (held, total, sems) = refs[: far_size + 1], refs[far_size + 1 :]
    copies = begin(list(zip(hbm, vmem)), sems)
    factors, coef = vmem[:far_size], vmem[far_size]
    per = held.shape[0] // 2
    packs = REACH // per
    width = LANES // packs
    depth = far_size // packs
    total[...] = jnp.zeros_like(total)
    for copy in copies:
        copy.wait()

    def group(a, carry):
        for e in range(depth):
            for j in range(packs):
                n = j * depth + e
                here = coef[a, e][:, j * width : (j + 1) * width]
                target = meta[n][1, a]
                total[target] += dot3(split(factors[n][a]), split(here), ((0,), (0,)))
        return carry

    lax.fori_loop(0, coef.shape[0], group, 0)
    for half in range(2):
        for k in range(per):
            held[half * per + k] = jnp.concatenate(
                [total[cluster_at(half, j, k, per)] for j in range(packs)], axis=1
            )
    fetch([(held, out)], sems)


def far_part(meta, factors, coef, far_size, per):
    groups = coef.shape[0]
    width = LANES * per // REACH
    out = jax.ShapeDtypeStruct((2 * per, B, LANES), F32)
    return pl.pallas_call(
        functools.partial(far_kernel, far_size),
        out_shape=out,
        in_specs=[SMEM_SPEC] * far_size + [ANY_SPEC] * (far_size + 1),
        out_specs=ANY_SPEC,
        scratch_shapes=buffers([*factors, coef, out])
        + [pltpu.VMEM((CL_DEV, B, width), F32), pltpu.SemaphoreType.DMA((far_size + 1,))],
        compiler_params=PARAMS,
        cost_estimate=cost(6 * groups * far_size * R * B * width, 4 * 1024 * 1024),
        name="far_part",
    )(*meta, *factors, coef)


def unpack(stage, per, put):
    far_size, halves = stage.shape[0], stage.shape[1]
    packs = REACH // per
    width = LANES // packs
    for half in range(halves):
        for k in range(per):
            for block in range(far_size // packs):
                entries = [stage[block * packs + i, half, k] for i in range(packs)]
                for j in range(packs):
                    value = jnp.concatenate(
                        [e[:, j * width : (j + 1) * width] for e in entries], axis=1
                    )
                    put(half, j * per + k, block * LANES, value)


def store_split(high, low, first=0, after=0):
    def put(half, c, lane, value):
        place_ = (after if half else first) + c
        hi, lo = split(value)
        high[place_, :, lane : lane + LANES] = hi
        low[place_, :, lane : lane + LANES] = lo

    return put


def packed_pairs(pieces, far_size, stage):
    pairs = []
    for n in range(far_size):
        owner = owner_of(n, far_size)
        for half in range(2):
            pairs.append((pieces[2 * n + half], stage.at[owner, half]))
    return pairs


def operator_kernel(far_size, per, last, n_pieces, cols_ref, blocks_ref, *refs):
    pieces, refs = refs[:n_pieces], refs[n_pieces:]
    ys = far_size // CORES
    outs, refs = refs[: 2 * ys], refs[2 * ys :]
    high, low, own_stage, stage, held, own_sems, in_sems, out_sems = refs
    slots = cols_ref.shape[0]
    packs = REACH // per
    width = LANES // packs
    y, core, _ = place(far_size)
    base = lax.axis_index("rows") * CL_DEV - REACH

    if last:
        own_pairs = packed_pairs(pieces[: 2 * far_size], far_size, own_stage)
        halo_pairs = packed_pairs(pieces[2 * far_size :], far_size, stage)
    else:
        part = REACH // CORES
        own_pairs = [(pieces[0], own_stage)]
        halo_pairs = []
        for n, piece in enumerate(pieces[1:]):
            c = core if n < 2 else 1 - core
            halo_pairs.append((piece, stage.at[pl.ds((n % 2) * REACH + c * part, part)]))
    own_copies = begin(own_pairs, own_sems)
    halo_copies = begin(halo_pairs, in_sems)

    for copy in own_copies:
        copy.wait()
    if last:
        unpack(own_stage, per, store_split(high, low, REACH, 2 * REACH))
    else:
        for c in range(CL_DEV):
            high[REACH + c], low[REACH + c] = split(own_stage[c])
    for copy in halo_copies:
        copy.wait()
    if last:
        unpack(stage, per, store_split(high, low, 0, REACH + CL_DEV))
    else:
        for c in range(2 * REACH):
            at = c if c < REACH else CL_DEV + c
            high[at], low[at] = split(stage[c])

    def out_copies(entry):
        copies = []
        for n, out in enumerate(outs):
            taker = core if n < ys else 1 - core
            owner = lax.rem(y + n % ys, ys) * CORES + taker
            copies.append(
                pltpu.make_async_copy(held.at[owner, entry], out.at[entry], out_sems.at[n, entry])
            )
        return copies

    def step(entry, carry):
        half, k = entry // per, entry % per
        images = []
        for j in range(packs):
            cluster = cluster_at(half, j, k, per)
            at = [cols_ref[s, cluster] - base for s in range(slots)]
            right = tuple(jnp.concatenate([ref[p] for p in at], axis=0) for ref in (high, low))
            left = split(jnp.concatenate([blocks_ref[cluster, s] for s in range(slots)], axis=1))
            images.append(dot3(left, right))
        for owner in range(far_size):
            held[owner, entry] = jnp.concatenate(
                [im[:, owner * width : (owner + 1) * width] for im in images], axis=1
            )
        for copy in out_copies(entry):
            copy.start()
        return carry

    lax.fori_loop(0, 2 * per, step, 0, unroll=2)

    def drain(entry, carry):
        for copy in out_copies(entry):
            copy.wait()
        return carry

    lax.fori_loop(0, 2 * per, drain, 0)


def operator(blocks, pieces, cols, far_size, per, width, last):
    ys = far_size // CORES
    n_own = 2 * far_size if last else 1
    if last:
        stages = [pltpu.VMEM((far_size, 2, per, B, LANES), F32)] * 2
    else:
        stages = [pltpu.VMEM((CL_DEV, B, width), F32), pltpu.VMEM((2 * REACH, B, width), F32)]
    outs = pl.pallas_call(
        functools.partial(operator_kernel, far_size, per, last, len(pieces)),
        out_shape=[jax.ShapeDtypeStruct((2 * per, B, LANES), F32)] * (2 * ys),
        in_specs=[SMEM_SPEC, VMEM_SPEC] + [ANY_SPEC] * len(pieces),
        out_specs=[ANY_SPEC] * (2 * ys),
        scratch_shapes=[
            pltpu.VMEM((CL_DEV + 2 * REACH, B, width), BF16),
            pltpu.VMEM((CL_DEV + 2 * REACH, B, width), BF16),
            *stages,
            pltpu.VMEM((far_size, 2 * per, B, LANES), F32),
            pltpu.SemaphoreType.DMA((n_own,)),
            pltpu.SemaphoreType.DMA((len(pieces) - n_own,)),
            pltpu.SemaphoreType.DMA((2 * ys, 2 * per)),
        ],
        compiler_params=PARAMS,
        cost_estimate=cost(0, 0),
        name="operator",
    )(cols, blocks, *pieces)
    return outs[:ys], outs[ys:]


def add_kernel(n, *refs):
    hbm, outs, vmem, (first, second, sems) = refs[:n], refs[n : n + 2], refs[n + 2 : -3], refs[-3:]
    fetch(list(zip(hbm, vmem)), sems)
    total = vmem[0][...]
    for part in vmem[1:]:
        total = total + part[...]
    per = total.shape[0] // 2
    first[...] = total[:per]
    second[...] = total[per:]
    fetch([(first, outs[0]), (second, outs[1])], sems)


def add_halves(parts):
    shape = parts[0].shape
    half = jax.ShapeDtypeStruct((shape[0] // 2,) + shape[1:], F32)
    return pl.pallas_call(
        functools.partial(add_kernel, len(parts)),
        out_shape=[half] * 2,
        in_specs=[ANY_SPEC] * len(parts),
        out_specs=[ANY_SPEC] * 2,
        scratch_shapes=buffers(list(parts) + [half] * 2) + [pltpu.SemaphoreType.DMA((len(parts),))],
        compiler_params=PARAMS,
        cost_estimate=cost(4 * parts[0].size, 20 * parts[0].size),
        name="add_halves",
    )(*parts)


def dots_kernel(packs, n, *refs):
    hbm, (out, image_out), vmem = refs[:n], refs[n : n + 2], refs[n + 2 : 2 * n + 2]
    held, image_held, sems = refs[2 * n + 2 :]
    fetch(list(zip(hbm, vmem)), sems)
    b_ref, gl_ref, gr_ref, *parts = vmem
    image = parts[0][...]
    for part in parts[1:]:
        image = image + part[...]
    image_held[...] = image
    (image_copy,) = begin([(image_held, image_out)], sems)
    vectors = (b_ref[...], jnp.concatenate([gl_ref[...], gr_ref[...]], axis=0), image)
    width = LANES // packs
    rows = []
    for left, right in ((0, 0), (0, 1), (0, 2), (1, 1), (1, 2), (2, 2)):
        total = jnp.sum(vectors[left] * vectors[right], axis=0)
        total = jnp.sum(total, axis=0, keepdims=True)
        folded = total
        for g in range(1, packs):
            folded = folded + pltpu.roll(total, g * width, 1)
        rows.append(folded)
    rows.append(jnp.zeros((2, LANES), F32))
    held[...] = jnp.concatenate(rows, axis=0)
    fetch([(held, out)], sems, 1)
    image_copy.wait()


def dots(b_own, g_own, parts, packs):
    operands = (b_own, *g_own, *parts)
    outs = [jax.ShapeDtypeStruct((8, LANES), F32), jax.ShapeDtypeStruct(b_own.shape, F32)]
    return pl.pallas_call(
        functools.partial(dots_kernel, packs, len(operands)),
        out_shape=outs,
        in_specs=[ANY_SPEC] * len(operands),
        out_specs=[ANY_SPEC] * 2,
        scratch_shapes=buffers([*operands, *outs]) + [pltpu.SemaphoreType.DMA((len(operands),))],
        compiler_params=PARAMS,
        cost_estimate=cost(14 * b_own.size, 20 * b_own.size),
        name="dots",
    )(*operands)


def least_squares(rhs_length, upper_left, lower_left, top_two, mid_two, lower_right):
    radius_one = jnp.sqrt(upper_left * upper_left + lower_left * lower_left)
    cosine_one = upper_left / radius_one
    sine_one = lower_left / radius_one
    rotated_top = cosine_one * rhs_length
    rotated_mid = -sine_one * rhs_length
    coupled = cosine_one * top_two + sine_one * mid_two
    diagonal_two = cosine_one * mid_two - sine_one * top_two
    radius_two = jnp.sqrt(diagonal_two * diagonal_two + lower_right * lower_right)
    weight_two = diagonal_two * rotated_mid / (radius_two * radius_two)
    weight_one = (rotated_top - coupled * weight_two) / radius_one
    return (weight_one, weight_two)


def finish_kernel(packs, *refs):
    hbm, outs, vmem, (solution_ref, residual_ref, sems) = refs[:5], refs[5:7], refs[7:12], refs[12:]
    fetch(list(zip(hbm, vmem)), sems)
    dots_ref, b_ref, gl_ref, gr_ref, image_ref = vmem
    bb, b1, b2, s11, s12, s22 = [dots_ref[i : i + 1, :] for i in range(6)]
    square = bb + EPS
    rhs_length = jnp.sqrt(square)
    upper_left = (0.5 * bb + b1) / square
    shift = (0.5 * EPS - b1) / square
    one = jnp.maximum(shift * shift * bb + 2.0 * shift * b1 + s11, 0.0) / square
    lower_square = one + EPS
    lower_left = jnp.sqrt(lower_square)
    f_s = (shift * bb + b1) / (square * lower_left)
    f_gs = (shift * b1 + b2) / (square * lower_left)
    s_s = one / lower_square
    s_gs = (shift * shift * b1 + shift * b2 + shift * s11 + s12) / (square * lower_square)
    gs_gs = (shift * shift * s11 + 2.0 * shift * s12 + s22) / (square * lower_square)
    top_two = 0.5 * f_s + f_gs
    mid_two = 0.5 * s_s + s_gs
    rest = 0.5 * (EPS / lower_square) - s_gs
    two = (
        gs_gs
        + top_two * top_two * (bb / square)
        + rest * rest * s_s
        - 2.0 * top_two * f_gs
        + 2.0 * rest * s_gs
        - 2.0 * top_two * rest * f_s
    )
    lower_right = jnp.sqrt(jnp.maximum(two, 0.0) + EPS)
    weight_one, weight_two = least_squares(
        rhs_length, upper_left, lower_left, top_two, mid_two, lower_right
    )
    one_scale = weight_one / rhs_length
    two_scale = weight_two / (rhs_length * lower_left)
    sol_b = one_scale + two_scale * shift
    res_b = 1.0 - 0.5 * one_scale - 0.5 * two_scale * shift
    res_1 = one_scale + two_scale * (0.5 + shift)
    width = LANES // packs
    per = REACH // packs
    for half, g_ref in enumerate((gl_ref, gr_ref)):
        for k in range(per):
            b, g, image = b_ref[half * per + k], g_ref[k], image_ref[half * per + k]
            answer = sol_b * b + two_scale * g
            left = res_b * b - res_1 * g - two_scale * image
            for value, out_ref in ((answer, solution_ref), (left, residual_ref)):
                turned = value.T
                for j in range(packs):
                    at = cluster_at(half, j, k, per) * B
                    out_ref[:, at : at + B] = turned[j * width : (j + 1) * width]
    fetch([(solution_ref, outs[0]), (residual_ref, outs[1])], sems)


def finish(total, b_own, g_own, image, packs):
    operands = (total, b_own, *g_own, image)
    out = jax.ShapeDtypeStruct((LANES // packs, CL_DEV * B), F32)
    return pl.pallas_call(
        functools.partial(finish_kernel, packs),
        out_shape=[out] * 2,
        in_specs=[ANY_SPEC] * len(operands),
        out_specs=[ANY_SPEC] * 2,
        scratch_shapes=buffers([*operands, out, out])
        + [pltpu.SemaphoreType.DMA((len(operands),))],
        compiler_params=PARAMS,
        cost_estimate=cost(8 * b_own.size, 28 * b_own.size),
        name="finish",
    )(*operands)


def swap_cores(value):
    size = lax.axis_size("far")
    return lax.ppermute(value, "far", [(i, i ^ 1) for i in range(size)])


def along_y(value, shift):
    size = lax.axis_size("far")
    return lax.ppermute(value, "far", [(i, (i + CORES * shift) % size) for i in range(size)])


def along_all_y(value):
    return [value] + [along_y(value, s) for s in range(1, lax.axis_size("far") // CORES)]


def after(values, *earlier):
    flat = lax.optimization_barrier((tuple(values), earlier))
    return list(flat[0])


def to_next(value):
    return lax.ppermute(value, "rows", [(i, i + 1) for i in range(lax.axis_size("rows") - 1)])


def to_previous(value):
    return lax.ppermute(value, "rows", [(i + 1, i) for i in range(lax.axis_size("rows") - 1)])


def sum_rows(value):
    size = lax.axis_size("rows")
    step = 1
    while step < size:
        value = value + lax.ppermute(value, "rows", [(i, i ^ step) for i in range(size)])
        step *= 2
    return value


def exchange(coef):
    return lax.all_to_all(coef, "rows", split_axis=0, concat_axis=0, tiled=True)


def sum_far(keeps, sends, coef):
    terms = [keeps[0]]
    for shift in range(1, len(keeps)):
        got, coef = lax.optimization_barrier((swap_cores(sends[shift]), coef))
        terms.append(along_y(keeps[shift] + got, shift))
    return terms + [swap_cores(sends[0])], coef


def shards(right_side, near_blocks, near_cols, far_src, far_tgt, far_left, far_right):
    far_size = lax.axis_size("far")
    ys = far_size // CORES
    width = right_side.shape[1]
    packs = LANES * far_size // width
    per = REACH // packs
    core = lax.axis_index("far") % CORES
    cols = near_cols.T
    own = right_side.reshape(CL_DEV, B, width)
    groups = far_left.shape[1]

    part = REACH // CORES
    tail = lax.dynamic_slice_in_dim(own, CL_DEV - REACH + core * part, part, 0)
    head = lax.dynamic_slice_in_dim(own, core * part, part, 0)
    from_left, from_right = to_next(tail), to_previous(head)
    gathered = [
        item
        for value in (
            jnp.stack([far_src.reshape(-1), far_tgt.reshape(-1)]),
            far_right.reshape(groups, B, R).transpose(0, 2, 1),
            far_left.reshape(groups, B, R).transpose(0, 2, 1),
        )
        for item in along_all_y(value)
    ]
    b_own = pack(own, far_size, per)
    gathered = after(gathered, b_own)
    meta, rights, lefts = [
        part_ + [swap_cores(item) for item in part_]
        for part_ in (gathered[:ys], gathered[ys : 2 * ys], gathered[2 * ys :])
    ]
    coef = coefficients(meta, rights, [b_own], far_size)
    pieces = after([from_left, from_right], coef)
    pieces += [swap_cores(item) for item in pieces]
    coef = exchange(coef)
    keeps, sends = operator(near_blocks, [own] + pieces, cols, far_size, per, width, False)
    terms, coef = sum_far(keeps, sends, coef)
    g_own = add_halves(terms + [far_part(meta, lefts, coef, far_size, per)])

    head, tail = g_own
    from_left, from_right = to_next(tail), to_previous(head)
    heads, tails = along_all_y(head), along_all_y(tail)
    coef = coefficients(meta, rights, g_own, far_size)
    arrived = after([from_left, from_right] + heads[1:] + tails[1:], coef)
    from_left, from_right = arrived[:2]
    heads, tails = heads[:1] + arrived[2 : 1 + ys], tails[:1] + arrived[1 + ys :]
    halos = [from_left, from_right]
    for s in range(1, ys):
        halos += [along_y(from_left, s), to_previous(heads[s])]
    owns = [item for pair in zip(heads, tails) for item in pair]
    owns += [swap_cores(item) for item in owns]
    halos += [swap_cores(item) for item in halos]
    coef = exchange(coef)
    keeps, sends = operator(near_blocks, owns + halos, cols, far_size, per, width, True)
    terms, coef = sum_far(keeps, sends, coef)
    far = far_part(meta, lefts, coef, far_size, per)
    part_dots, image = dots(b_own, g_own, terms + [far], packs)
    answer, residual = finish(sum_rows(part_dots), b_own, g_own, image, packs)
    return answer.T, residual.T


def solution(mesh):
    return jax.shard_map(
        shards,
        mesh=mesh,
        in_specs=(
            P("rows", None),
            P("rows", "far", None, None),
            P("rows", "far"),
            P("rows", None, "far"),
            P("rows", None, "far"),
            P("rows", None, "far", None, None),
            P("rows", None, "far", None, None),
        ),
        out_specs=(P("rows", "far"), P("rows", "far")),
        check_vma=False,
    )
```

time: 183 us -> 151 us (0.83)
  waiting for transfers between devices: 59.9 us -> 30.8 us
  starting transfers between devices: 43.2 us -> 52 us
  Pallas kernels: 60.6 us -> 55 us
  local copies, waits for them, and re-layouts: 12.3 us -> 7.36 us
    all_to_all x2, waiting for transfers between devices: 22.9 us -> 3.47 us  [exchange(): return lax.all_to_all(coef, 'rows', split_axis=0, concat_axis=0, tiled=True)]
    ppermute x2, waiting for transfers between devices: 15.3 us -> 6.83 us  [to_next(): lax.ppermute(value, 'rows', [(i, i + 1) for i in range(lax.axis_size('row...]
    ppermute x3, waiting for transfers between devices: 7.65 us -> 0.2 us  [to_previous(): lax.ppermute(value, 'rows', [(i + 1, i) for i in range(lax.axis_size('row...]
    ppermute x3, starting transfers between devices: 2.69 us -> 8.98 us  [sum_rows(): lax.ppermute(value, 'rows', [(i, i ^ step) for i in range(size)])]
    ppermute x18 -> x20, waiting for transfers between devices: 1.18 us -> 6.76 us  [swap_cores(): return lax.ppermute(value, 'far', [(i, i ^ 1) for i in range(size)])]
    pallas_call x12 -> x10, Pallas kernels: 60.6 us -> 55 us  [the longest x2 20.7 us: operator(): pl.pallas_call(functools.partial(operator_kernel, far_size, per, last, le...]
    ppermute x7 -> x8, waiting for transfers between devices: 3.85 us -> 8.55 us  [along_y(): lax.ppermute(value, 'far', [(i, (i + CORES * shift) % size) for i in rang...]
    ppermute x3, waiting for transfers between devices: 9.03 us -> 4.96 us  [sum_rows(): lax.ppermute(value, 'rows', [(i, i ^ step) for i in range(size)])]
  transfers between devices with their start and end apart: 35 -> 38, of which waited for: 13 -> 19; matrix products, arithmetic and copies ran while one was open for 3% -> 2% of each run, Pallas kernels for 26% -> 31%
where the time goes in v3:
time: 151 us; the launch traced here: 150 us
  Pallas kernels  55 us (36%)
  starting transfers between devices  52 us (34%)
  waiting for transfers between devices  30.8 us (20%)
  local copies, waits for them, and re-layouts  7.36 us (5%)
  other arithmetic  3.68 us (2%)
    pallas_call x2, Pallas kernels, operator(): pl.pallas_call(functools.partial(operator_kernel, far_size, per, last, le...  20.7 us
    all_to_all x2, starting transfers between devices, exchange(): return lax.all_to_all(coef, 'rows', split_axis=0, concat_axis=0, tiled=True)  14.3 us
    pallas_call x2, Pallas kernels, far_part(): pl.pallas_call(functools.partial(far_kernel, far_size), out_shape=out, in...  11.9 us
    pallas_call x2, Pallas kernels, coefficients(): pl.pallas_call(functools.partial(coefficient_kernel, far_size, len(fields...  11.6 us
    ppermute x8, starting transfers between devices, along_y(): lax.ppermute(value, 'far', [(i, (i + CORES * shift) % size) for i in rang...  11 us
    ppermute x2, starting transfers between devices, to_next(): lax.ppermute(value, 'rows', [(i, i + 1) for i in range(lax.axis_size('row...  9.13 us
    ppermute x3, starting transfers between devices, sum_rows(): lax.ppermute(value, 'rows', [(i, i ^ step) for i in range(size)])  8.98 us
    ppermute x8, waiting for transfers between devices, along_y(): lax.ppermute(value, 'far', [(i, (i + CORES * shift) % size) for i in rang...  8.55 us
  transfers between devices with their start and end apart: 38, of which 19 were waited for; matrix products, arithmetic and copies ran while one was open for 2% of the time, Pallas kernels for 31%

profile of v3, /device:TPU:0, one launch (start us, length us, event | category | flops | bytes accessed | tf_op | source)
XLA Modules:
  0.0 150.0 jit_solution(3951036944150728265)
XLA Ops:
  0.6 3.0 %collective-permute-start.4 = (f32[8,64,128]{2,1,0:T(8,128)}, f32[8,64,128]{2,1,0:T(8,128)S(1)}, u32[]{:S(2)}, u32[]{:S(2)}) collective-permute-start(f32[8,64,128]{2,1,0:T(8,128)} %bitcast.19), channel_id=1, source_target_pairs={{0,2},{1,3},{2,0},{3,1},{4,6},{5,7},{6,4},{7,5},{8,10},{9,11},{10,... | collective-permute-start | bytes 786440 | tf_op jit(solution)/shard_map/ppermute | solution.py:521
  3.8 1.3 constant_dynamic-slice_fusion
  5.1 1.3 collective-permute-start.1
  6.4 4.6 %collective-permute-start = (f32[4,128,256]{2,1,0:T(8,128)S(1)}, f32[4,128,256]{2,1,0:T(8,128)S(1)}, u32[]{:S(2)}, u32[]{:S(2)}) collective-permute-start(f32[4,128,256]{2,1,0:T(8,128)S(1)} %get-tuple-element.63), channel_id=1, source_target_pairs={{0,4},{4,8},{8,12},{12,16},{16,20},{20,24},{24,28},{1,5},{5,9},{9,... | collective-permute-start | bytes 1572872 | tf_op jit(solution)/shard_map/ppermute | solution.py:534
  11.0 2.0 %collective-permute-start.2 = (s32[2,8]{1,0:T(2,128)S(1)}, s32[2,8]{1,0:T(2,128)S(1)}, u32[]{:S(2)}, u32[]{:S(2)}) collective-permute-start(s32[2,8]{1,0:T(2,128)S(1)} %pad_add_fusion.refs_0_), channel_id=1, source_target_pairs={{0,2},{1,3},{2,0},{3,1},{4,6},{5,7},{6,4},{7,5},{8,10},{9,11},{10,... | collective-permute-start | bytes 200 | tf_op jit(solution)/shard_map/ppermute | solution.py:521
  13.0 2.6 %pack.1.refs_8_.refs_0_.refs_1_ = f32[8,128,128]{2,1,0:T(8,128)} custom-call(f32[16,128,256]{2,1,0:T(8,128)} %bitcast.13), custom_call_target="tpu_custom_call" | custom-call | bytes 4194304 | tf_op jit(solution)/shard_map/pack/pallas_call | solution.py:104
  16.0 0.5 collective-permute-start.8
  16.6 1.3 collective-permute-done.5.refs_2_
  18.0 1.0 collective-permute-done.6.refs_3_
  19.1 0.5 copy-done.36
  19.7 0.7 copy-done.10
  20.4 5.8 %coefficients.2 = f32[8,2,64,128]{3,2,1,0:T(8,128)} custom-call(s32[2,8]{1,0:T(2,128)} %copy-done.33, s32[2,8]{1,0:T(2,128)} %copy-done.34, s32[2,8]{1,0:T(2,128)} %copy-done.35, s32[2,8]{1,0:T(2,128)} %copy-done.36, f32[8,64,128]{2,1,0:T(8,128)} %bitcast.16, f32[8,64,128]{2,1,0:T(8,128)} %copy-done.6, f32[8,64,128]{2,1,0:T(8,128)} %copy-done.9, ...), custom_call_target="tpu_custom_call" | custom-call | flops 100663296 | bytes 4194304 | tf_op jit(solution)/shard_map/coefficients/pallas_call | solution.py:159
  26.2 5.4 %collective-permute-done.refs_1_ = f32[4,128,256]{2,1,0:T(8,128)S(1)} collective-permute-done((f32[4,128,256]{2,1,0:T(8,128)S(1)}, f32[4,128,256]{2,1,0:T(8,128)S(1)}, u32[]{:S(2)}, u32[]{:S(2)}) %collective-permute-start) | collective-permute-done | bytes 524320 | tf_op jit(solution)/shard_map/ppermute | solution.py:534
  31.7 0.5 collective-permute-start.10
  32.2 5.8 %all-to-all-start = ((f32[8,2,64,128]{3,2,1,0:T(8,128)}), f32[8,2,64,128]{3,2,1,0:T(8,128)S(1)}, u32[]{:S(2)}, u32[]{:S(2)}) async-start(f32[8,2,64,128]{3,2,1,0:T(8,128)} %coefficients.2), calls=%async_computation | async-start | bytes 1048576 | tf_op jit(solution)/shard_map/all_to_all | solution.py:551
  38.0 0.8 copy-done.13
  38.9 9.9 %operator.2 = (f32[8,128,128]{2,1,0:T(8,128)}, f32[8,128,128]{2,1,0:T(8,128)}, f32[8,128,128]{2,1,0:T(8,128)}, f32[8,128,128]{2,1,0:T(8,128)}) custom-call(s32[6,16]{1,0:T(8,128)} %bitcast.23, f32[16,6,128,128]{3,2,1,0:T(8,128)} %blocks_ref.3, f32[16,128,256]{2,1,0:T(8,128)} %bitcast.14, f32[4,128,256]{2,1,0:T(8,128)} %copy-done.12, ...), custom_call_target="tpu_custom_call" | custom-call | tf_op jit(solution)/shard_map/operator/pallas_call | solution.py:343
  48.9 0.5 collective-permute-start.13
  49.4 3.2 %all-to-all-done.refs_8_ = f32[8,2,64,128]{3,2,1,0:T(8,128)S(1)} async-done(((f32[8,2,64,128]{3,2,1,0:T(8,128)}), f32[8,2,64,128]{3,2,1,0:T(8,128)S(1)}, u32[]{:S(2)}, u32[]{:S(2)}) %all-to-all-start) | async-done | bytes 524320 | tf_op jit(solution)/shard_map/all_to_all | solution.py:551
  52.6 1.3 add.30
  53.9 1.6 %collective-permute-start.12 = (f32[8,128,128]{2,1,0:T(8,128)S(1)}, f32[8,128,128]{2,1,0:T(8,128)S(1)}, u32[]{:S(2)}, u32[]{:S(2)}) collective-permute-start(f32[8,128,128]{2,1,0:T(8,128)S(1)} %add.30), channel_id=1, source_target_pairs={{0,2},{1,3},{2,0},{3,1},{4,6},{5,7},{6,4},{7,5},{8,10},{9,11},{10,... | collective-permute-start | bytes 1572872 | tf_op jit(solution)/shard_map/ppermute | solution.py:521
  55.5 0.5 collective-permute-start.15
  56.0 1.0 collective-permute-done.14.refs_6_
  57.0 0.4 collective-permute-done.15.refs_7_
  57.4 0.4 copy-done.7
  57.8 0.7 copy-done.8
  58.5 6.0 %far_part.2.refs_3_ = f32[8,128,128]{2,1,0:T(8,128)} custom-call(s32[2,8]{1,0:T(2,128)} %copy-done.33, s32[2,8]{1,0:T(2,128)} %copy-done.34, s32[2,8]{1,0:T(2,128)} %copy-done.35, s32[2,8]{1,0:T(2,128)} %copy-done.36, f32[8,64,128]{2,1,0:T(8,128)} %bitcast.20, f32[8,64,128]{2,1,0:T(8,128)} %copy-done.5, f32[8,64,128]{2,1,0:T(8,128)} %copy-done.7, ...), custom_call_target="tpu_custom_call" | custom-call | flops 100663296 | bytes 4194304 | tf_op jit(solution)/shard_map/far_part/pallas_call | solution.py:212
  64.5 1.9 %collective-permute-done.12.refs_1_ = f32[8,128,128]{2,1,0:T(8,128)S(1)} collective-permute-done((f32[8,128,128]{2,1,0:T(8,128)S(1)}, f32[8,128,128]{2,1,0:T(8,128)S(1)}, u32[]{:S(2)}, u32[]{:S(2)}) %collective-permute-start.12) | collective-permute-done | bytes 524320 | tf_op jit(solution)/shard_map/ppermute | solution.py:521
  66.4 0.8 copy-done.17
  67.2 2.4 %add_halves.1 = (f32[4,128,128]{2,1,0:T(8,128)}, f32[4,128,128]{2,1,0:T(8,128)}) custom-call(f32[8,128,128]{2,1,0:T(8,128)} %get-tuple-element.38.refs_0_, f32[8,128,128]{2,1,0:T(8,128)} %copy-done.17, f32[8,128,128]{2,1,0:T(8,128)} %copy-done.15, f32[8,128,128]{2,1,0:T(8,128)} %far_part.2.refs_3_), custom_call_target="tpu_custom_call" | custom-call | flops 524288 | bytes 2621440 | tf_op jit(solution)/shard_map/add_halves/pallas_call | solution.py:379
  69.6 1.6 %collective-permute-start.18 = (f32[4,128,128]{2,1,0:T(8,128)}, f32[4,128,128]{2,1,0:T(8,128)S(1)}, u32[]{:S(2)}, u32[]{:S(2)}) collective-permute-start(f32[4,128,128]{2,1,0:T(8,128)} %get-tuple-element.46.refs_8_.refs_0_.refs_1_.refs_2_), channel_id=1, source_target_pairs={{0,2},{1,3},{2,0},{3,1},{4,6},{5,7},{6,4},{7,5},{8,10},{9,11},{10,... | collective-permute-start | bytes 786440 | tf_op jit(solution)/shard_map/ppermute | solution.py:521
  71.1 1.3 collective-permute-start.17
  72.4 0.6 collective-permute-start.19
  73.0 4.5 %collective-permute-start.16 = (f32[4,128,128]{2,1,0:T(8,128)}, f32[4,128,128]{2,1,0:T(8,128)S(1)}, u32[]{:S(2)}, u32[]{:S(2)}) collective-permute-start(f32[4,128,128]{2,1,0:T(8,128)} %get-tuple-element.47.refs_9_.refs_1_.refs_2_.refs_3_), channel_id=1, source_target_pairs={{0,4},{4,8},{8,12},{12,16},{16,20},{20,24},{24,28},{1,5},{5,9},{9,... | collective-permute-start | bytes 786440 | tf_op jit(solution)/shard_map/ppermute | solution.py:534
  77.6 5.8 %coefficients.3 = f32[8,2,64,128]{3,2,1,0:T(8,128)} custom-call(s32[2,8]{1,0:T(2,128)} %copy-done.33, s32[2,8]{1,0:T(2,128)} %copy-done.34, s32[2,8]{1,0:T(2,128)} %copy-done.35, s32[2,8]{1,0:T(2,128)} %copy-done.36, f32[8,64,128]{2,1,0:T(8,128)} %bitcast.17, f32[8,64,128]{2,1,0:T(8,128)} %copy-done.6, f32[8,64,128]{2,1,0:T(8,128)} %copy-done.9, ...), custom_call_target="tpu_custom_call" | custom-call | flops 100663296 | bytes 4194304 | tf_op jit(solution)/shard_map/coefficients/pallas_call | solution.py:159
  83.5 0.6 collective-permute-start.21
  84.0 1.4 collective-permute-done.16.refs_8_
  85.5 1.3 collective-permute-start.25
  86.8 0.6 collective-permute-start.24
  87.3 8.5 %all-to-all-start.1 = ((f32[8,2,64,128]{3,2,1,0:T(8,128)}), f32[8,2,64,128]{3,2,1,0:T(8,128)S(1)}, u32[]{:S(2)}, u32[]{:S(2)}) async-start(f32[8,2,64,128]{3,2,1,0:T(8,128)} %coefficients.3), calls=%async_computation.1 | async-start | bytes 1048576 | tf_op jit(solution)/shard_map/all_to_all | solution.py:551
  95.9 0.5 collective-permute-start.26
  97.0 0.3 collective-permute-start.28
  97.2 1.0 collective-permute-done.27.refs_13_
  98.2 0.4 collective-permute-done.29.refs_15_
  98.6 0.4 collective-permute-done.28.refs_14_
  99.3 0.7 copy-done.32
  100.0 10.8 %operator.3 = (f32[8,128,128]{2,1,0:T(8,128)}, f32[8,128,128]{2,1,0:T(8,128)}, f32[8,128,128]{2,1,0:T(8,128)}, f32[8,128,128]{2,1,0:T(8,128)}) custom-call(s32[6,16]{1,0:T(8,128)} %bitcast.24, f32[16,6,128,128]{3,2,1,0:T(8,128)} %blocks_ref.3, f32[4,128,128]{2,1,0:T(8,128)} %get-tuple-element.46.refs_8_.refs_0_.refs_1_.refs_2_, ...), custom_call_target="tpu_custom_call" | custom-call | tf_op jit(solution)/shard_map/operator/pallas_call | solution.py:343
  111.1 0.4 collective-permute-start.32
  111.7 1.3 collective-permute-done.30
  113.1 1.1 add.31
  114.2 1.6 %collective-permute-start.31 = (f32[8,128,128]{2,1,0:T(8,128)S(1)}, f32[8,128,128]{2,1,0:T(8,128)S(1)}, u32[]{:S(2)}, u32[]{:S(2)}) collective-permute-start(f32[8,128,128]{2,1,0:T(8,128)S(1)} %add.31), channel_id=1, source_target_pairs={{0,2},{1,3},{2,0},{3,1},{4,6},{5,7},{6,4},{7,5},{8,10},{9,11},{10,... | collective-permute-start | bytes 1572872 | tf_op jit(solution)/shard_map/ppermute | solution.py:521
  115.8 6.0 %far_part.3.refs_6_ = f32[8,128,128]{2,1,0:T(8,128)} custom-call(s32[2,8]{1,0:T(2,128)} %copy-done.33, s32[2,8]{1,0:T(2,128)} %copy-done.34, s32[2,8]{1,0:T(2,128)} %copy-done.35, s32[2,8]{1,0:T(2,128)} %copy-done.36, f32[8,64,128]{2,1,0:T(8,128)} %bitcast.21, f32[8,64,128]{2,1,0:T(8,128)} %copy-done.5, f32[8,64,128]{2,1,0:T(8,128)} %copy-done.7, ...), custom_call_target="tpu_custom_call" | custom-call | flops 100663296 | bytes 4194304 | tf_op jit(solution)/shard_map/far_part/pallas_call | solution.py:212
  121.8 6.4 %collective-permute-done.31.refs_4_ = f32[8,128,128]{2,1,0:T(8,128)S(1)} collective-permute-done((f32[8,128,128]{2,1,0:T(8,128)S(1)}, f32[8,128,128]{2,1,0:T(8,128)S(1)}, u32[]{:S(2)}, u32[]{:S(2)}) %collective-permute-start.31) | collective-permute-done | bytes 524320 | tf_op jit(solution)/shard_map/ppermute | solution.py:521
  128.2 0.8 copy-done.18
  129.0 3.0 %dots.1 = (f32[8,128]{1,0:T(8,128)}, f32[8,128,128]{2,1,0:T(8,128)}) custom-call(f32[8,128,128]{2,1,0:T(8,128)} %pack.1.refs_8_.refs_0_.refs_1_, f32[4,128,128]{2,1,0:T(8,128)} %get-tuple-element.46.refs_8_.refs_0_.refs_1_.refs_2_, f32[4,128,128]{2,1,0:T(8,128)} %get-tuple-element.47.refs_9_.refs_1_.refs_2_.refs_3_, ...), custom_call_target="tpu_custom_call" | custom-call | flops 1835008 | bytes 2621440 | tf_op jit(solution)/shard_map/dots/pallas_call | solution.py:420
  132.0 2.5 %collective-permute-start.33 = (f32[8,128]{1,0:T(8,128)}, f32[8,128]{1,0:T(8,128)S(1)}, u32[]{:S(2)}, u32[]{:S(2)}) collective-permute-start(f32[8,128]{1,0:T(8,128)} %get-tuple-element.58), channel_id=1, source_target_pairs={{0,4},{4,0},{8,12},{12,8},{16,20},{20,16},{24,28},{28,24},{1,5},{5... | collective-permute-start | bytes 12296 | tf_op jit(solution)/shard_map/ppermute | solution.py:545
  134.5 1.8 %collective-permute-done.33 = f32[8,128]{1,0:T(8,128)S(1)} collective-permute-done((f32[8,128]{1,0:T(8,128)}, f32[8,128]{1,0:T(8,128)S(1)}, u32[]{:S(2)}, u32[]{:S(2)}) %collective-permute-start.33) | collective-permute-done | bytes 4128 | tf_op jit(solution)/shard_map/ppermute | solution.py:545
  136.3 0.7 add.32
  136.9 3.6 %collective-permute-start.34 = (f32[8,128]{1,0:T(8,128)S(1)}, f32[8,128]{1,0:T(8,128)S(1)}, u32[]{:S(2)}, u32[]{:S(2)}) collective-permute-start(f32[8,128]{1,0:T(8,128)S(1)} %add.32), channel_id=1, source_target_pairs={{0,8},{4,12},{8,0},{12,4},{16,24},{20,28},{24,16},{28,20},{1,9},{5... | collective-permute-start | bytes 12296 | tf_op jit(solution)/shard_map/ppermute | solution.py:545
  140.5 1.6 %collective-permute-done.34 = f32[8,128]{1,0:T(8,128)S(1)} collective-permute-done((f32[8,128]{1,0:T(8,128)S(1)}, f32[8,128]{1,0:T(8,128)S(1)}, u32[]{:S(2)}, u32[]{:S(2)}) %collective-permute-start.34) | collective-permute-done | bytes 4128 | tf_op jit(solution)/shard_map/ppermute | solution.py:545
  142.1 2.9 %collective-permute-start.35 = (f32[8,128]{1,0:T(8,128)S(1)}, f32[8,128]{1,0:T(8,128)S(1)}, u32[]{:S(2)}, u32[]{:S(2)}) collective-permute-start(f32[8,128]{1,0:T(8,128)S(1)} %add.33), channel_id=1, source_target_pairs={{0,16},{4,20},{8,24},{12,28},{16,0},{20,4},{24,8},{28,12},{1,17},{... | collective-permute-start | bytes 12296 | tf_op jit(solution)/shard_map/ppermute | solution.py:545
  145.0 1.6 %collective-permute-done.35 = f32[8,128]{1,0:T(8,128)S(1)} collective-permute-done((f32[8,128]{1,0:T(8,128)S(1)}, f32[8,128]{1,0:T(8,128)S(1)}, u32[]{:S(2)}, u32[]{:S(2)}) %collective-permute-start.35) | collective-permute-done | bytes 4128 | tf_op jit(solution)/shard_map/ppermute | solution.py:545
  146.6 0.6 add.34.refs_0_
  147.2 2.8 %finish.1 = (f32[64,2048]{1,0:T(8,128)}, f32[64,2048]{1,0:T(8,128)}) custom-call(f32[8,128]{1,0:T(8,128)} %add.34.refs_0_, f32[8,128,128]{2,1,0:T(8,128)} %pack.1.refs_8_.refs_0_.refs_1_, f32[4,128,128]{2,1,0:T(8,128)} %get-tuple-element.46.refs_8_.refs_0_.refs_1_.refs_2_, f32[4,128,128]{2,1,0:T(8,128)} %get-tuple-element.47.refs_9_.refs_1_.refs_2_.refs_3_, ...), custom_call_target="tpu_custom_call" | custom-call | flops 1048576 | bytes 3670016 | tf_op jit(solution)/shard_map/finish/pallas_call | solution.py:501
  (107 shorter events, 2.6 us)
Async XLA Ops:
  0.6 10.3 %copy-start.37 = (s32[1,8,1]{1,2,0:T(1,128)S(1)}, s32[1,8,1]{1,2,0:T(1,128)}, u32[]{:S(2)}) copy-start(s32[1,8,1]{1,2,0:T(1,128)} %param.11) | copy-start | bytes 100
  0.6 10.3 %copy-start.38 = (s32[1,8,1]{1,2,0:T(1,128)S(1)}, s32[1,8,1]{1,2,0:T(1,128)}, u32[]{:S(2)}) copy-start(s32[1,8,1]{1,2,0:T(1,128)} %param.10) | copy-start | bytes 100
  0.6 15.2 %collective-permute-start.4 = (f32[8,64,128]{2,1,0:T(8,128)}, f32[8,64,128]{2,1,0:T(8,128)S(1)}, u32[]{:S(2)}, u32[]{:S(2)}) collective-permute-start(f32[8,64,128]{2,1,0:T(8,128)} %bitcast.19), channel_id=1, source_target_pairs={{0,2},{1,3},{2,0},{3,1},{4,6},{5,7},{6,4},{7,5},{8,10},{9,11},{10,... | collective-permute-start | bytes 786440 | tf_op jit(solution)/shard_map/ppermute | solution.py:521
  3.7 12.2 %collective-permute-start.3 = (f32[8,64,128]{2,1,0:T(8,128)}, f32[8,64,128]{2,1,0:T(8,128)S(1)}, u32[]{:S(2)}, u32[]{:S(2)}) collective-permute-start(f32[8,64,128]{2,1,0:T(8,128)} %bitcast.15), channel_id=1, source_target_pairs={{0,2},{1,3},{2,0},{3,1},{4,6},{5,7},{6,4},{7,5},{8,10},{9,11},{10,... | collective-permute-start | bytes 786440 | tf_op jit(solution)/shard_map/ppermute | solution.py:521
  3.8 12.1 %copy-start.3 = (f32[1,8,1,128,64]{3,4,2,1,0:T(8,128)S(1)}, f32[1,8,1,128,64]{3,4,2,1,0:T(8,128)}, u32[]{:S(2)}) copy-start(f32[1,8,1,128,64]{3,4,2,1,0:T(8,128)} %param.13) | copy-start | bytes 786436
  5.1 21.1 %collective-permute-start.1 = (f32[4,128,256]{2,1,0:T(8,128)S(1)}, f32[4,128,256]{2,1,0:T(8,128)S(1)}, u32[]{:S(2)}, u32[]{:S(2)}) collective-permute-start(f32[4,128,256]{2,1,0:T(8,128)S(1)} %get-tuple-element.62), channel_id=1, source_target_pairs={{4,0},{8,4},{12,8},{16,12},{20,16},{24,20},{28,24},{5,1},{9,5},{13... | collective-permute-start | bytes 1572872 | tf_op jit(solution)/shard_map/ppermute | solution.py:538
  6.4 25.3 %collective-permute-start = (f32[4,128,256]{2,1,0:T(8,128)S(1)}, f32[4,128,256]{2,1,0:T(8,128)S(1)}, u32[]{:S(2)}, u32[]{:S(2)}) collective-permute-start(f32[4,128,256]{2,1,0:T(8,128)S(1)} %get-tuple-element.63), channel_id=1, source_target_pairs={{0,4},{4,8},{8,12},{12,16},{16,20},{20,24},{24,28},{1,5},{5,9},{9,... | collective-permute-start | bytes 1572872 | tf_op jit(solution)/shard_map/ppermute | solution.py:534
  11.0 8.0 %copy-start.33 = (s32[2,8]{1,0:T(2,128)}, s32[2,8]{1,0:T(2,128)S(1)}, u32[]{:S(2)}) copy-start(s32[2,8]{1,0:T(2,128)S(1)} %pad_add_fusion.refs_0_) | copy-start | bytes 196
  11.0 4.9 %collective-permute-start.2 = (s32[2,8]{1,0:T(2,128)S(1)}, s32[2,8]{1,0:T(2,128)S(1)}, u32[]{:S(2)}, u32[]{:S(2)}) collective-permute-start(s32[2,8]{1,0:T(2,128)S(1)} %pad_add_fusion.refs_0_), channel_id=1, source_target_pairs={{0,2},{1,3},{2,0},{3,1},{4,6},{5,7},{6,4},{7,5},{8,10},{9,11},{10,... | collective-permute-start | bytes 200 | tf_op jit(solution)/shard_map/ppermute | solution.py:521
  15.9 3.2 %copy-start.34 = (s32[2,8]{1,0:T(2,128)}, s32[2,8]{1,0:T(2,128)S(1)}, u32[]{:S(2)}) copy-start(s32[2,8]{1,0:T(2,128)S(1)} %collective-permute-done.2.refs_1_) | copy-start | bytes 196
  15.9 39.6 %copy-start.5 = (f32[8,64,128]{2,1,0:T(8,128)}, f32[8,64,128]{2,1,0:T(8,128)S(1)}, u32[]{:S(2)}) copy-start(f32[8,64,128]{2,1,0:T(8,128)S(1)} %collective-permute-done.4.refs_5_) | copy-start | bytes 786436
  15.9 3.2 %copy-start.6 = (f32[8,64,128]{2,1,0:T(8,128)}, f32[8,64,128]{2,1,0:T(8,128)S(1)}, u32[]{:S(2)}) copy-start(f32[8,64,128]{2,1,0:T(8,128)S(1)} %collective-permute-done.3.refs_5_) | copy-start | bytes 786436
  15.9 3.1 %collective-permute-start.7 = (f32[8,64,128]{2,1,0:T(8,128)S(1)}, f32[8,64,128]{2,1,0:T(8,128)S(1)}, u32[]{:S(2)}, u32[]{:S(2)}) collective-permute-start(f32[8,64,128]{2,1,0:T(8,128)S(1)} %bitcast.18), channel_id=1, source_target_pairs={{0,1},{1,0},{2,3},{3,2},{4,5},{5,4},{6,7},{7,6},{8,9},{9,8},{10,11... | collective-permute-start | bytes 786440 | tf_op jit(solution)/shard_map/ppermute | solution.py:516
  16.0 3.0 %collective-permute-start.8 = (f32[8,64,128]{2,1,0:T(8,128)S(1)}, f32[8,64,128]{2,1,0:T(8,128)S(1)}, u32[]{:S(2)}, u32[]{:S(2)}) collective-permute-start(f32[8,64,128]{2,1,0:T(8,128)S(1)} %collective-permute-done.3.refs_5_), channel_id=1, source_target_pairs={{0,1},{1,0},{2,3},{3,2},{4,5},{5,4},{6,7},{7,6},{8,9},{9,8},{10,11... | collective-permute-start | bytes 786440 | tf_op jit(solution)/shard_map/ppermute | solution.py:516
  16.5 1.4 collective-permute-start.5
  17.9 1.2 copy-start.35
  17.9 1.1 collective-permute-start.6
  26.2 11.7 %copy-start.11 = (f32[4,128,256]{2,1,0:T(8,128)}, f32[4,128,256]{2,1,0:T(8,128)S(1)}, u32[]{:S(2)}) copy-start(f32[4,128,256]{2,1,0:T(8,128)S(1)} %collective-permute-done.1.refs_2_) | copy-start | bytes 1572868
  31.7 6.3 %copy-start.12 = (f32[4,128,256]{2,1,0:T(8,128)}, f32[4,128,256]{2,1,0:T(8,128)S(1)}, u32[]{:S(2)}) copy-start(f32[4,128,256]{2,1,0:T(8,128)S(1)} %collective-permute-done.refs_1_) | copy-start | bytes 1572868
  31.7 6.3 %collective-permute-start.9 = (f32[4,128,256]{2,1,0:T(8,128)S(1)}, f32[4,128,256]{2,1,0:T(8,128)S(1)}, u32[]{:S(2)}, u32[]{:S(2)}) collective-permute-start(f32[4,128,256]{2,1,0:T(8,128)S(1)} %collective-permute-done.refs_1_), channel_id=1, source_target_pairs={{0,1},{1,0},{2,3},{3,2},{4,5},{5,4},{6,7},{7,6},{8,9},{9,8},{10,11... | collective-permute-start | bytes 1572872 | tf_op jit(solution)/shard_map/ppermute | solution.py:516
  31.7 6.3 %collective-permute-start.10 = (f32[4,128,256]{2,1,0:T(8,128)S(1)}, f32[4,128,256]{2,1,0:T(8,128)S(1)}, u32[]{:S(2)}, u32[]{:S(2)}) collective-permute-start(f32[4,128,256]{2,1,0:T(8,128)S(1)} %collective-permute-done.1.refs_2_), channel_id=1, source_target_pairs={{0,1},{1,0},{2,3},{3,2},{4,5},{5,4},{6,7},{7,6},{8,9},{9,8},{10,11... | collective-permute-start | bytes 1572872 | tf_op jit(solution)/shard_map/ppermute | solution.py:516
  32.2 20.5 %all-to-all-start = ((f32[8,2,64,128]{3,2,1,0:T(8,128)}), f32[8,2,64,128]{3,2,1,0:T(8,128)S(1)}, u32[]{:S(2)}, u32[]{:S(2)}) async-start(f32[8,2,64,128]{3,2,1,0:T(8,128)} %coefficients.2), calls=%async_computation | async-start | bytes 1048576 | tf_op jit(solution)/shard_map/all_to_all | solution.py:551
  38.0 1.0 copy-start.14
  38.9 16.6 %copy-start.4 = (f32[1,8,1,128,64]{3,4,2,1,0:T(8,128)S(1)}, f32[1,8,1,128,64]{3,4,2,1,0:T(8,128)}, u32[]{:S(2)}) copy-start(f32[1,8,1,128,64]{3,4,2,1,0:T(8,128)} %param.12) | copy-start | bytes 786436
  48.8 3.8 %collective-permute-start.11 = (f32[8,128,128]{2,1,0:T(8,128)}, f32[8,128,128]{2,1,0:T(8,128)S(1)}, u32[]{:S(2)}, u32[]{:S(2)}) collective-permute-start(f32[8,128,128]{2,1,0:T(8,128)} %get-tuple-element.40), channel_id=1, source_target_pairs={{0,1},{1,0},{2,3},{3,2},{4,5},{5,4},{6,7},{7,6},{8,9},{9,8},{10,11... | collective-permute-start | bytes 1572872 | tf_op jit(solution)/shard_map/ppermute | solution.py:516
  48.9 15.5 %collective-permute-start.13 = (f32[8,128,128]{2,1,0:T(8,128)}, f32[8,128,128]{2,1,0:T(8,128)S(1)}, u32[]{:S(2)}, u32[]{:S(2)}) collective-permute-start(f32[8,128,128]{2,1,0:T(8,128)} %get-tuple-element.42), channel_id=1, source_target_pairs={{0,1},{1,0},{2,3},{3,2},{4,5},{5,4},{6,7},{7,6},{8,9},{9,8},{10,11... | collective-permute-start | bytes 1572872 | tf_op jit(solution)/shard_map/ppermute | solution.py:516
  52.6 4.8 %copy-start.2 = (f32[8,2,64,128]{3,2,1,0:T(8,128)}, f32[8,2,64,128]{3,2,1,0:T(8,128)S(1)}, u32[]{:S(2)}) copy-start(f32[8,2,64,128]{3,2,1,0:T(8,128)S(1)} %all-to-all-done.refs_8_) | copy-start | bytes 1572868
  53.9 12.4 %collective-permute-start.12 = (f32[8,128,128]{2,1,0:T(8,128)S(1)}, f32[8,128,128]{2,1,0:T(8,128)S(1)}, u32[]{:S(2)}, u32[]{:S(2)}) collective-permute-start(f32[8,128,128]{2,1,0:T(8,128)S(1)} %add.30), channel_id=1, source_target_pairs={{0,2},{1,3},{2,0},{3,1},{4,6},{5,7},{6,4},{7,5},{8,10},{9,11},{10,... | collective-permute-start | bytes 1572872 | tf_op jit(solution)/shard_map/ppermute | solution.py:521
  55.5 1.5 %collective-permute-start.14 = (f32[8,64,128]{2,1,0:T(8,128)S(1)}, f32[8,64,128]{2,1,0:T(8,128)S(1)}, u32[]{:S(2)}, u32[]{:S(2)}) collective-permute-start(f32[8,64,128]{2,1,0:T(8,128)S(1)} %bitcast.22), channel_id=1, source_target_pairs={{0,1},{1,0},{2,3},{3,2},{4,5},{5,4},{6,7},{7,6},{8,9},{9,8},{10,11... | collective-permute-start | bytes 786440 | tf_op jit(solution)/shard_map/ppermute | solution.py:516
  55.5 1.9 %collective-permute-start.15 = (f32[8,64,128]{2,1,0:T(8,128)S(1)}, f32[8,64,128]{2,1,0:T(8,128)S(1)}, u32[]{:S(2)}, u32[]{:S(2)}) collective-permute-start(f32[8,64,128]{2,1,0:T(8,128)S(1)} %collective-permute-done.4.refs_5_), channel_id=1, source_target_pairs={{0,1},{1,0},{2,3},{3,2},{4,5},{5,4},{6,7},{7,6},{8,9},{9,8},{10,11... | collective-permute-start | bytes 786440 | tf_op jit(solution)/shard_map/ppermute | solution.py:516
  64.5 1.9 %copy-start.15 = (f32[8,128,128]{2,1,0:T(8,128)}, f32[8,128,128]{2,1,0:T(8,128)S(1)}, u32[]{:S(2)}) copy-start(f32[8,128,128]{2,1,0:T(8,128)S(1)} %collective-permute-done.13.refs_2_) | copy-start | bytes 1572868
  69.5 13.9 %copy-start = (f32[4,128,128]{2,1,0:T(8,128)S(1)}, f32[4,128,128]{2,1,0:T(8,128)}, u32[]{:S(2)}) copy-start(f32[4,128,128]{2,1,0:T(8,128)} %get-tuple-element.47.refs_9_.refs_1_.refs_2_.refs_3_) | copy-start | bytes 786436
  69.6 13.9 %collective-permute-start.18 = (f32[4,128,128]{2,1,0:T(8,128)}, f32[4,128,128]{2,1,0:T(8,128)S(1)}, u32[]{:S(2)}, u32[]{:S(2)}) collective-permute-start(f32[4,128,128]{2,1,0:T(8,128)} %get-tuple-element.46.refs_8_.refs_0_.refs_1_.refs_2_), channel_id=1, source_target_pairs={{0,2},{1,3},{2,0},{3,1},{4,6},{5,7},{6,4},{7,5},{8,10},{9,11},{10,... | collective-permute-start | bytes 786440 | tf_op jit(solution)/shard_map/ppermute | solution.py:521
  71.1 12.9 %collective-permute-start.17 = (f32[4,128,128]{2,1,0:T(8,128)}, f32[4,128,128]{2,1,0:T(8,128)S(1)}, u32[]{:S(2)}, u32[]{:S(2)}) collective-permute-start(f32[4,128,128]{2,1,0:T(8,128)} %get-tuple-element.46.refs_8_.refs_0_.refs_1_.refs_2_), channel_id=1, source_target_pairs={{4,0},{8,4},{12,8},{16,12},{20,16},{24,20},{28,24},{5,1},{9,5},{13... | collective-permute-start | bytes 786440 | tf_op jit(solution)/shard_map/ppermute | solution.py:538
  72.4 11.6 %collective-permute-start.19 = (f32[4,128,128]{2,1,0:T(8,128)}, f32[4,128,128]{2,1,0:T(8,128)S(1)}, u32[]{:S(2)}, u32[]{:S(2)}) collective-permute-start(f32[4,128,128]{2,1,0:T(8,128)} %get-tuple-element.47.refs_9_.refs_1_.refs_2_.refs_3_), channel_id=1, source_target_pairs={{0,2},{1,3},{2,0},{3,1},{4,6},{5,7},{6,4},{7,5},{8,10},{9,11},{10,... | collective-permute-start | bytes 786440 | tf_op jit(solution)/shard_map/ppermute | solution.py:521
  73.0 12.5 %collective-permute-start.16 = (f32[4,128,128]{2,1,0:T(8,128)}, f32[4,128,128]{2,1,0:T(8,128)S(1)}, u32[]{:S(2)}, u32[]{:S(2)}) collective-permute-start(f32[4,128,128]{2,1,0:T(8,128)} %get-tuple-element.47.refs_9_.refs_1_.refs_2_.refs_3_), channel_id=1, source_target_pairs={{0,4},{4,8},{8,12},{12,16},{16,20},{20,24},{24,28},{1,5},{5,9},{9,... | collective-permute-start | bytes 786440 | tf_op jit(solution)/shard_map/ppermute | solution.py:534
  77.6 18.3 %collective-permute-start.20 = (f32[4,128,128]{2,1,0:T(8,128)}, f32[4,128,128]{2,1,0:T(8,128)S(1)}, u32[]{:S(2)}, u32[]{:S(2)}) collective-permute-start(f32[4,128,128]{2,1,0:T(8,128)} %get-tuple-element.46.refs_8_.refs_0_.refs_1_.refs_2_), channel_id=1, source_target_pairs={{0,1},{1,0},{2,3},{3,2},{4,5},{5,4},{6,7},{7,6},{8,9},{9,8},{10,11... | collective-permute-start | bytes 786440 | tf_op jit(solution)/shard_map/ppermute | solution.py:516
  83.5 15.5 %copy-start.19 = (f32[4,128,128]{2,1,0:T(8,128)}, f32[4,128,128]{2,1,0:T(8,128)S(1)}, u32[]{:S(2)}) copy-start(f32[4,128,128]{2,1,0:T(8,128)S(1)} %collective-permute-done.18.refs_2_) | copy-start | bytes 786436
  83.5 12.5 %collective-permute-start.21 = (f32[4,128,128]{2,1,0:T(8,128)S(1)}, f32[4,128,128]{2,1,0:T(8,128)S(1)}, u32[]{:S(2)}, u32[]{:S(2)}) collective-permute-start(f32[4,128,128]{2,1,0:T(8,128)S(1)} %copy-done), channel_id=1, source_target_pairs={{0,1},{1,0},{2,3},{3,2},{4,5},{5,4},{6,7},{7,6},{8,9},{9,8},{10,11... | collective-permute-start | bytes 786440 | tf_op jit(solution)/shard_map/ppermute | solution.py:516
  84.0 14.9 %copy-start.20 = (f32[4,128,128]{2,1,0:T(8,128)}, f32[4,128,128]{2,1,0:T(8,128)S(1)}, u32[]{:S(2)}) copy-start(f32[4,128,128]{2,1,0:T(8,128)S(1)} %collective-permute-done.17.refs_9_) | copy-start | bytes 786436
  84.0 14.9 %copy-start.21 = (f32[4,128,128]{2,1,0:T(8,128)}, f32[4,128,128]{2,1,0:T(8,128)S(1)}, u32[]{:S(2)}) copy-start(f32[4,128,128]{2,1,0:T(8,128)S(1)} %collective-permute-done.19.refs_3_) | copy-start | bytes 786436
  85.5 13.5 %copy-start.22 = (f32[4,128,128]{2,1,0:T(8,128)}, f32[4,128,128]{2,1,0:T(8,128)S(1)}, u32[]{:S(2)}) copy-start(f32[4,128,128]{2,1,0:T(8,128)S(1)} %collective-permute-done.16.refs_8_) | copy-start | bytes 786436
  85.5 11.0 %collective-permute-start.23 = (f32[4,128,128]{2,1,0:T(8,128)S(1)}, f32[4,128,128]{2,1,0:T(8,128)S(1)}, u32[]{:S(2)}, u32[]{:S(2)}) collective-permute-start(f32[4,128,128]{2,1,0:T(8,128)S(1)} %collective-permute-done.19.refs_3_), channel_id=1, source_target_pairs={{0,1},{1,0},{2,3},{3,2},{4,5},{5,4},{6,7},{7,6},{8,9},{9,8},{10,11... | collective-permute-start | bytes 786440 | tf_op jit(solution)/shard_map/ppermute | solution.py:516
  85.5 11.2 %collective-permute-start.25 = (f32[4,128,128]{2,1,0:T(8,128)S(1)}, f32[4,128,128]{2,1,0:T(8,128)S(1)}, u32[]{:S(2)}, u32[]{:S(2)}) collective-permute-start(f32[4,128,128]{2,1,0:T(8,128)S(1)} %collective-permute-done.18.refs_2_), channel_id=1, source_target_pairs={{4,0},{8,4},{12,8},{16,12},{20,16},{24,20},{28,24},{5,1},{9,5},{13... | collective-permute-start | bytes 786440 | tf_op jit(solution)/shard_map/ppermute | solution.py:538
  86.8 10.2 %collective-permute-start.24 = (f32[4,128,128]{2,1,0:T(8,128)S(1)}, f32[4,128,128]{2,1,0:T(8,128)S(1)}, u32[]{:S(2)}, u32[]{:S(2)}) collective-permute-start(f32[4,128,128]{2,1,0:T(8,128)S(1)} %collective-permute-done.16.refs_8_), channel_id=1, source_target_pairs={{0,2},{1,3},{2,0},{3,1},{4,6},{5,7},{6,4},{7,5},{8,10},{9,11},{10,... | collective-permute-start | bytes 786440 | tf_op jit(solution)/shard_map/ppermute | solution.py:521
  87.3 24.4 %all-to-all-start.1 = ((f32[8,2,64,128]{3,2,1,0:T(8,128)}), f32[8,2,64,128]{3,2,1,0:T(8,128)S(1)}, u32[]{:S(2)}, u32[]{:S(2)}) async-start(f32[8,2,64,128]{3,2,1,0:T(8,128)} %coefficients.3), calls=%async_computation.1 | async-start | bytes 1048576 | tf_op jit(solution)/shard_map/all_to_all | solution.py:551
  95.8 3.1 %copy-start.23 = (f32[4,128,128]{2,1,0:T(8,128)}, f32[4,128,128]{2,1,0:T(8,128)S(1)}, u32[]{:S(2)}) copy-start(f32[4,128,128]{2,1,0:T(8,128)S(1)} %collective-permute-done.20.refs_4_) | copy-start | bytes 786436
  95.8 2.4 %collective-permute-start.22 = (f32[4,128,128]{2,1,0:T(8,128)S(1)}, f32[4,128,128]{2,1,0:T(8,128)S(1)}, u32[]{:S(2)}, u32[]{:S(2)}) collective-permute-start(f32[4,128,128]{2,1,0:T(8,128)S(1)} %collective-permute-done.18.refs_2_), channel_id=1, source_target_pairs={{0,1},{1,0},{2,3},{3,2},{4,5},{5,4},{6,7},{7,6},{8,9},{9,8},{10,11... | collective-permute-start | bytes 786440 | tf_op jit(solution)/shard_map/ppermute | solution.py:516
  95.9 3.0 %copy-start.24 = (f32[4,128,128]{2,1,0:T(8,128)}, f32[4,128,128]{2,1,0:T(8,128)S(1)}, u32[]{:S(2)}) copy-start(f32[4,128,128]{2,1,0:T(8,128)S(1)} %collective-permute-done.21.refs_5_) | copy-start | bytes 786436
  95.9 2.3 %collective-permute-start.26 = (f32[4,128,128]{2,1,0:T(8,128)S(1)}, f32[4,128,128]{2,1,0:T(8,128)S(1)}, u32[]{:S(2)}, u32[]{:S(2)}) collective-permute-start(f32[4,128,128]{2,1,0:T(8,128)S(1)} %collective-permute-done.16.refs_8_), channel_id=1, source_target_pairs={{0,1},{1,0},{2,3},{3,2},{4,5},{5,4},{6,7},{7,6},{8,9},{9,8},{10,11... | collective-permute-start | bytes 786440 | tf_op jit(solution)/shard_map/ppermute | solution.py:516
  96.4 2.6 %copy-start.25 = (f32[4,128,128]{2,1,0:T(8,128)}, f32[4,128,128]{2,1,0:T(8,128)S(1)}, u32[]{:S(2)}) copy-start(f32[4,128,128]{2,1,0:T(8,128)S(1)} %collective-permute-done.23.refs_7_) | copy-start | bytes 786436
  96.4 1.8 %collective-permute-start.27 = (f32[4,128,128]{2,1,0:T(8,128)S(1)}, f32[4,128,128]{2,1,0:T(8,128)S(1)}, u32[]{:S(2)}, u32[]{:S(2)}) collective-permute-start(f32[4,128,128]{2,1,0:T(8,128)S(1)} %collective-permute-done.17.refs_9_), channel_id=1, source_target_pairs={{0,1},{1,0},{2,3},{3,2},{4,5},{5,4},{6,7},{7,6},{8,9},{9,8},{10,11... | collective-permute-start | bytes 786440 | tf_op jit(solution)/shard_map/ppermute | solution.py:516
  96.7 2.3 %copy-start.26 = (f32[4,128,128]{2,1,0:T(8,128)}, f32[4,128,128]{2,1,0:T(8,128)S(1)}, u32[]{:S(2)}) copy-start(f32[4,128,128]{2,1,0:T(8,128)S(1)} %collective-permute-done.25.refs_11_) | copy-start | bytes 786436
  96.7 1.9 %collective-permute-start.29 = (f32[4,128,128]{2,1,0:T(8,128)S(1)}, f32[4,128,128]{2,1,0:T(8,128)S(1)}, u32[]{:S(2)}, u32[]{:S(2)}) collective-permute-start(f32[4,128,128]{2,1,0:T(8,128)S(1)} %collective-permute-done.25.refs_11_), channel_id=1, source_target_pairs={{0,1},{1,0},{2,3},{3,2},{4,5},{5,4},{6,7},{7,6},{8,9},{9,8},{10,11... | collective-permute-start | bytes 786440 | tf_op jit(solution)/shard_map/ppermute | solution.py:516
  97.0 2.1 %copy-start.27 = (f32[4,128,128]{2,1,0:T(8,128)}, f32[4,128,128]{2,1,0:T(8,128)S(1)}, u32[]{:S(2)}) copy-start(f32[4,128,128]{2,1,0:T(8,128)S(1)} %collective-permute-done.24.refs_10_) | copy-start | bytes 786436
  97.0 2.0 %collective-permute-start.28 = (f32[4,128,128]{2,1,0:T(8,128)S(1)}, f32[4,128,128]{2,1,0:T(8,128)S(1)}, u32[]{:S(2)}, u32[]{:S(2)}) collective-permute-start(f32[4,128,128]{2,1,0:T(8,128)S(1)} %collective-permute-done.24.refs_10_), channel_id=1, source_target_pairs={{0,1},{1,0},{2,3},{3,2},{4,5},{5,4},{6,7},{7,6},{8,9},{9,8},{10,11... | collective-permute-start | bytes 786440 | tf_op jit(solution)/shard_map/ppermute | solution.py:516
  110.9 2.2 %collective-permute-start.30 = (f32[8,128,128]{2,1,0:T(8,128)}, f32[8,128,128]{2,1,0:T(8,128)S(1)}, u32[]{:S(2)}, u32[]{:S(2)}) collective-permute-start(f32[8,128,128]{2,1,0:T(8,128)} %get-tuple-element.54), channel_id=1, source_target_pairs={{0,1},{1,0},{2,3},{3,2},{4,5},{5,4},{6,7},{7,6},{8,9},{9,8},{10,11... | collective-permute-start | bytes 1572872 | tf_op jit(solution)/shard_map/ppermute | solution.py:516
  111.1 10.7 %collective-permute-start.32 = (f32[8,128,128]{2,1,0:T(8,128)}, f32[8,128,128]{2,1,0:T(8,128)S(1)}, u32[]{:S(2)}, u32[]{:S(2)}) collective-permute-start(f32[8,128,128]{2,1,0:T(8,128)} %get-tuple-element.56), channel_id=1, source_target_pairs={{0,1},{1,0},{2,3},{3,2},{4,5},{5,4},{6,7},{7,6},{8,9},{9,8},{10,11... | collective-permute-start | bytes 1572872 | tf_op jit(solution)/shard_map/ppermute | solution.py:516
  111.7 4.0 %copy-start.1 = (f32[8,2,64,128]{3,2,1,0:T(8,128)}, f32[8,2,64,128]{3,2,1,0:T(8,128)S(1)}, u32[]{:S(2)}) copy-start(f32[8,2,64,128]{3,2,1,0:T(8,128)S(1)} %all-to-all-done.1.refs_8_) | copy-start | bytes 1572868
  114.2 14.0 %collective-permute-start.31 = (f32[8,128,128]{2,1,0:T(8,128)S(1)}, f32[8,128,128]{2,1,0:T(8,128)S(1)}, u32[]{:S(2)}, u32[]{:S(2)}) collective-permute-start(f32[8,128,128]{2,1,0:T(8,128)S(1)} %add.31), channel_id=1, source_target_pairs={{0,2},{1,3},{2,0},{3,1},{4,6},{5,7},{6,4},{7,5},{8,10},{9,11},{10,... | collective-permute-start | bytes 1572872 | tf_op jit(solution)/shard_map/ppermute | solution.py:521
  121.8 6.4 %copy-start.16 = (f32[8,128,128]{2,1,0:T(8,128)}, f32[8,128,128]{2,1,0:T(8,128)S(1)}, u32[]{:S(2)}) copy-start(f32[8,128,128]{2,1,0:T(8,128)S(1)} %collective-permute-done.32.refs_5_) | copy-start | bytes 1572868
  132.0 4.3 %collective-permute-start.33 = (f32[8,128]{1,0:T(8,128)}, f32[8,128]{1,0:T(8,128)S(1)}, u32[]{:S(2)}, u32[]{:S(2)}) collective-permute-start(f32[8,128]{1,0:T(8,128)} %get-tuple-element.58), channel_id=1, source_target_pairs={{0,4},{4,0},{8,12},{12,8},{16,20},{20,16},{24,28},{28,24},{1,5},{5... | collective-permute-start | bytes 12296 | tf_op jit(solution)/shard_map/ppermute | solution.py:545
  136.9 5.2 %collective-permute-start.34 = (f32[8,128]{1,0:T(8,128)S(1)}, f32[8,128]{1,0:T(8,128)S(1)}, u32[]{:S(2)}, u32[]{:S(2)}) collective-permute-start(f32[8,128]{1,0:T(8,128)S(1)} %add.32), channel_id=1, source_target_pairs={{0,8},{4,12},{8,0},{12,4},{16,24},{20,28},{24,16},{28,20},{1,9},{5... | collective-permute-start | bytes 12296 | tf_op jit(solution)/shard_map/ppermute | solution.py:545
  142.1 4.5 %collective-permute-start.35 = (f32[8,128]{1,0:T(8,128)S(1)}, f32[8,128]{1,0:T(8,128)S(1)}, u32[]{:S(2)}, u32[]{:S(2)}) collective-permute-start(f32[8,128]{1,0:T(8,128)S(1)} %add.33), channel_id=1, source_target_pairs={{0,16},{4,20},{8,24},{12,28},{16,0},{20,4},{24,8},{28,12},{1,17},{... | collective-permute-start | bytes 12296 | tf_op jit(solution)/shard_map/ppermute | solution.py:545
  (13 other events, 9.8 us)

commit v4 on v3

--- a/solution.py
+++ b/solution.py
@@ -16,13 +16,15 @@
 EPS = 1e-06
 F32 = jnp.float32
 BF16 = jnp.bfloat16
-VMEM_LIMIT = 54 * 1024 * 1024
+VMEM_LIMIT = 16 * 1024 * 1024
+WIDE_LIMIT = 60 * 1024 * 1024
 
 
 VMEM_SPEC = pl.BlockSpec(memory_space=pltpu.VMEM)
 SMEM_SPEC = pl.BlockSpec(memory_space=pltpu.SMEM)
 ANY_SPEC = pl.BlockSpec(memory_space=pl.ANY)
 PARAMS = pltpu.CompilerParams(vmem_limit_bytes=VMEM_LIMIT)
+WIDE = pltpu.CompilerParams(vmem_limit_bytes=WIDE_LIMIT)
 
 
 def split(value):
@@ -52,6 +54,12 @@
     y, core, ys = place(far_size)
     shift, other = n % ys, n // ys
     return lax.rem(y - shift + ys, ys) * CORES + (1 - core if other else core)
+
+
+def halo_parts(ys):
+    part = REACH // CORES
+    shared = max(1, part // ys)
+    return part, shared, part - ys * shared
 
 
 def begin(pairs, sems, first=0):
@@ -113,10 +121,13 @@
     )(field)
 
 
-def coefficient_kernel(far_size, n_fields, *refs):
+def coefficient_kernel(far_size, n_fields, n_waits, *refs):
+    refs = refs[: 2 * far_size + n_fields] + refs[2 * far_size + n_fields + n_waits :]
     meta, hbm = refs[:far_size], refs[far_size : 2 * far_size + n_fields]
     out, refs = refs[2 * far_size + n_fields], refs[2 * far_size + n_fields + 1 :]
     vmem, (held, high, low, sems) = refs[: far_size + n_fields], refs[far_size + n_fields :]
+    groups = held.shape[0]
+    hbm = [ref.at[pl.ds(0, groups)] for ref in hbm[:far_size]] + list(hbm[far_size:])
     copies = begin(list(zip(hbm, vmem)), sems)
     factors, fields = vmem[:far_size], vmem[far_size:]
     per = sum(f.shape[0] for f in fields) // 2
@@ -146,22 +157,23 @@
             held[t, e] = jnp.concatenate(parts, axis=1)
         return carry
 
-    lax.fori_loop(0, held.shape[0], group, 0)
+    lax.fori_loop(0, held.shape[0], group, 0, unroll=4)
     fetch([(held, out)], sems)
 
 
-def coefficients(meta, factors, fields, far_size):
-    groups = factors[0].shape[0]
+def coefficients(meta, factors, fields, far_size, waits=()):
+    groups = factors[0].shape[0] // 2
     per = sum(f.shape[0] for f in fields) // 2
     packs = REACH // per
     width = LANES // packs
     out = jax.ShapeDtypeStruct((groups, far_size // packs, R, LANES), F32)
     return pl.pallas_call(
-        functools.partial(coefficient_kernel, far_size, len(fields)),
+        functools.partial(coefficient_kernel, far_size, len(fields), len(waits)),
         out_shape=out,
-        in_specs=[SMEM_SPEC] * far_size + [ANY_SPEC] * (far_size + len(fields)),
+        in_specs=[SMEM_SPEC] * far_size + [ANY_SPEC] * (far_size + len(fields) + len(waits)),
         out_specs=ANY_SPEC,
-        scratch_shapes=buffers([*factors, *fields, out])
+        scratch_shapes=[pltpu.VMEM((groups, R, B), F32)] * far_size
+        + buffers([*fields, out])
         + [
             pltpu.VMEM((CL_DEV, B, width), BF16),
             pltpu.VMEM((CL_DEV, B, width), BF16),
@@ -170,14 +182,17 @@
         compiler_params=PARAMS,
         cost_estimate=cost(6 * groups * far_size * R * B * width, 4 * 1024 * 1024),
         name="coefficients",
-    )(*meta, *factors, *fields)
-
-
-def far_kernel(far_size, *refs):
-    meta, hbm = refs[:far_size], refs[far_size : 2 * far_size + 1]
-    out, refs = refs[2 * far_size + 1], refs[2 * far_size + 2 :]
-    vmem, (held, total, sems) = refs[: far_size + 1], refs[far_size + 1 :]
+    )(*meta, *factors, *fields, *waits)
+
+
+def far_kernel(far_size, n_terms, *refs):
+    n = far_size + 1 + n_terms
+    meta, hbm, held = refs[:far_size], refs[far_size : far_size + n], refs[far_size + n]
+    vmem, (total, sems) = refs[far_size + n + 1 : -2], refs[-2:]
+    groups = vmem[0].shape[0]
+    hbm = [ref.at[pl.ds(groups, groups)] for ref in hbm[:far_size]] + list(hbm[far_size:])
     copies = begin(list(zip(hbm, vmem)), sems)
+    terms = vmem[far_size + 1 :]
     factors, coef = vmem[:far_size], vmem[far_size]
     per = held.shape[0] // 2
     packs = REACH // per
@@ -196,30 +211,33 @@
                 total[target] += dot3(split(factors[n][a]), split(here), ((0,), (0,)))
         return carry
 
-    lax.fori_loop(0, coef.shape[0], group, 0)
+    lax.fori_loop(0, coef.shape[0], group, 0, unroll=4)
     for half in range(2):
         for k in range(per):
-            held[half * per + k] = jnp.concatenate(
+            value = jnp.concatenate(
                 [total[cluster_at(half, j, k, per)] for j in range(packs)], axis=1
             )
-    fetch([(held, out)], sems)
-
-
-def far_part(meta, factors, coef, far_size, per):
+            for term in terms:
+                value = value + term[half * per + k]
+            held[half * per + k] = value
+
+
+def far_part(meta, factors, coef, terms, far_size, per):
     groups = coef.shape[0]
     width = LANES * per // REACH
-    out = jax.ShapeDtypeStruct((2 * per, B, LANES), F32)
+    operands = [*factors, coef, *terms]
     return pl.pallas_call(
-        functools.partial(far_kernel, far_size),
-        out_shape=out,
-        in_specs=[SMEM_SPEC] * far_size + [ANY_SPEC] * (far_size + 1),
-        out_specs=ANY_SPEC,
-        scratch_shapes=buffers([*factors, coef, out])
-        + [pltpu.VMEM((CL_DEV, B, width), F32), pltpu.SemaphoreType.DMA((far_size + 1,))],
+        functools.partial(far_kernel, far_size, len(terms)),
+        out_shape=jax.ShapeDtypeStruct((2 * per, B, LANES), F32),
+        in_specs=[SMEM_SPEC] * far_size + [ANY_SPEC] * len(operands),
+        out_specs=VMEM_SPEC,
+        scratch_shapes=[pltpu.VMEM((groups, R, B), F32)] * far_size
+        + buffers([coef, *terms])
+        + [pltpu.VMEM((CL_DEV, B, width), F32), pltpu.SemaphoreType.DMA((len(operands),))],
         compiler_params=PARAMS,
         cost_estimate=cost(6 * groups * far_size * R * B * width, 4 * 1024 * 1024),
         name="far_part",
-    )(*meta, *factors, coef)
+    )(*meta, *operands)
 
 
 def unpack(stage, per, put):
@@ -260,7 +278,7 @@
     pieces, refs = refs[:n_pieces], refs[n_pieces:]
     ys = far_size // CORES
     outs, refs = refs[: 2 * ys], refs[2 * ys :]
-    high, low, own_stage, stage, held, own_sems, in_sems, out_sems = refs
+    blocks, high, low, own_stage, stage, held, own_sems, in_sems, block_sems, out_sems = refs
     slots = cols_ref.shape[0]
     packs = REACH // per
     width = LANES // packs
@@ -271,12 +289,18 @@
         own_pairs = packed_pairs(pieces[: 2 * far_size], far_size, own_stage)
         halo_pairs = packed_pairs(pieces[2 * far_size :], far_size, stage)
     else:
-        part = REACH // CORES
+        part, shared, direct = halo_parts(ys)
         own_pairs = [(pieces[0], own_stage)]
         halo_pairs = []
+        each = (len(pieces) - 1) // CORES
         for n, piece in enumerate(pieces[1:]):
-            c = core if n < 2 else 1 - core
-            halo_pairs.append((piece, stage.at[pl.ds((n % 2) * REACH + c * part, part)]))
+            turn, side = divmod(n % each, 2)
+            first = side * REACH + (core if n < each else 1 - core) * part
+            if turn < ys:
+                first, count = first + lax.rem(y - turn + ys, ys) * shared, shared
+            else:
+                first, count = first + ys * shared, direct
+            halo_pairs.append((piece, stage.at[pl.ds(first, count)]))
     own_copies = begin(own_pairs, own_sems)
     halo_copies = begin(halo_pairs, in_sems)
 
@@ -287,8 +311,16 @@
     else:
         for c in range(CL_DEV):
             high[REACH + c], low[REACH + c] = split(own_stage[c])
+    def block_copies(entry):
+        half, k = entry // per, entry % per
+        at = [cluster_at(half, j, k, per) for j in range(packs)]
+        return [pltpu.make_async_copy(blocks_ref.at[c], blocks.at[c], block_sems.at[c]) for c in at]
+
     for copy in halo_copies:
         copy.wait()
+    for entry in range(2 * per):
+        for copy in block_copies(entry):
+            copy.start()
     if last:
         unpack(stage, per, store_split(high, low, 0, REACH + CL_DEV))
     else:
@@ -296,41 +328,41 @@
             at = c if c < REACH else CL_DEV + c
             high[at], low[at] = split(stage[c])
 
-    def out_copies(entry):
+    def out_copies(half):
+        rows = pl.ds(half * per, per)
         copies = []
         for n, out in enumerate(outs):
             taker = core if n < ys else 1 - core
             owner = lax.rem(y + n % ys, ys) * CORES + taker
             copies.append(
-                pltpu.make_async_copy(held.at[owner, entry], out.at[entry], out_sems.at[n, entry])
+                pltpu.make_async_copy(held.at[owner, rows], out.at[rows], out_sems.at[n, half])
             )
         return copies
 
     def step(entry, carry):
         half, k = entry // per, entry % per
+        for copy in block_copies(entry):
+            copy.wait()
         images = []
         for j in range(packs):
             cluster = cluster_at(half, j, k, per)
             at = [cols_ref[s, cluster] - base for s in range(slots)]
             right = tuple(jnp.concatenate([ref[p] for p in at], axis=0) for ref in (high, low))
-            left = split(jnp.concatenate([blocks_ref[cluster, s] for s in range(slots)], axis=1))
+            left = split(jnp.concatenate([blocks[cluster, s] for s in range(slots)], axis=1))
             images.append(dot3(left, right))
         for owner in range(far_size):
             held[owner, entry] = jnp.concatenate(
                 [im[:, owner * width : (owner + 1) * width] for im in images], axis=1
             )
-        for copy in out_copies(entry):
+        return carry
+
+    for half in range(2):
+        lax.fori_loop(half * per, (half + 1) * per, step, 0, unroll=2)
+        for copy in out_copies(half):
             copy.start()
-        return carry
-
-    lax.fori_loop(0, 2 * per, step, 0, unroll=2)
-
-    def drain(entry, carry):
-        for copy in out_copies(entry):
+    for half in range(2):
+        for copy in out_copies(half):
             copy.wait()
-        return carry
-
-    lax.fori_loop(0, 2 * per, drain, 0)
 
 
 def operator(blocks, pieces, cols, far_size, per, width, last):
@@ -343,18 +375,20 @@
     outs = pl.pallas_call(
         functools.partial(operator_kernel, far_size, per, last, len(pieces)),
         out_shape=[jax.ShapeDtypeStruct((2 * per, B, LANES), F32)] * (2 * ys),
-        in_specs=[SMEM_SPEC, VMEM_SPEC] + [ANY_SPEC] * len(pieces),
+        in_specs=[SMEM_SPEC] + [ANY_SPEC] * (1 + len(pieces)),
         out_specs=[ANY_SPEC] * (2 * ys),
-        scratch_shapes=[
+        scratch_shapes=buffers([blocks])
+        + [
             pltpu.VMEM((CL_DEV + 2 * REACH, B, width), BF16),
             pltpu.VMEM((CL_DEV + 2 * REACH, B, width), BF16),
             *stages,
             pltpu.VMEM((far_size, 2 * per, B, LANES), F32),
             pltpu.SemaphoreType.DMA((n_own,)),
             pltpu.SemaphoreType.DMA((len(pieces) - n_own,)),
-            pltpu.SemaphoreType.DMA((2 * ys, 2 * per)),
+            pltpu.SemaphoreType.DMA((CL_DEV,)),
+            pltpu.SemaphoreType.DMA((2 * ys, 2)),
         ],
-        compiler_params=PARAMS,
+        compiler_params=WIDE,
         cost_estimate=cost(0, 0),
         name="operator",
     )(cols, blocks, *pieces)
@@ -362,15 +396,18 @@
 
 
 def add_kernel(n, *refs):
-    hbm, outs, vmem, (first, second, sems) = refs[:n], refs[n : n + 2], refs[n + 2 : -3], refs[-3:]
-    fetch(list(zip(hbm, vmem)), sems)
-    total = vmem[0][...]
-    for part in vmem[1:]:
-        total = total + part[...]
-    per = total.shape[0] // 2
-    first[...] = total[:per]
-    second[...] = total[per:]
-    fetch([(first, outs[0]), (second, outs[1])], sems)
+    parts, outs, (first, second, sems) = refs[:n], refs[n : n + 2], refs[n + 2 :]
+    per = first.shape[0]
+    copies = []
+    for half, held in enumerate((first, second)):
+        rows = slice(half * per, (half + 1) * per)
+        total = parts[0][rows]
+        for part in parts[1:]:
+            total = total + part[rows]
+        held[...] = total
+        copies += begin([(held, outs[half])], sems, half)
+    for copy in copies:
+        copy.wait()
 
 
 def add_halves(parts):
@@ -379,52 +416,75 @@
     return pl.pallas_call(
         functools.partial(add_kernel, len(parts)),
         out_shape=[half] * 2,
-        in_specs=[ANY_SPEC] * len(parts),
+        in_specs=[VMEM_SPEC] * len(parts),
         out_specs=[ANY_SPEC] * 2,
-        scratch_shapes=buffers(list(parts) + [half] * 2) + [pltpu.SemaphoreType.DMA((len(parts),))],
+        scratch_shapes=buffers([half] * 2) + [pltpu.SemaphoreType.DMA((2,))],
         compiler_params=PARAMS,
         cost_estimate=cost(4 * parts[0].size, 20 * parts[0].size),
         name="add_halves",
     )(*parts)
 
 
-def dots_kernel(packs, n, *refs):
-    hbm, (out, image_out), vmem = refs[:n], refs[n : n + 2], refs[n + 2 : 2 * n + 2]
-    held, image_held, sems = refs[2 * n + 2 :]
-    fetch(list(zip(hbm, vmem)), sems)
-    b_ref, gl_ref, gr_ref, *parts = vmem
-    image = parts[0][...]
-    for part in parts[1:]:
-        image = image + part[...]
-    image_held[...] = image
-    (image_copy,) = begin([(image_held, image_out)], sems)
-    vectors = (b_ref[...], jnp.concatenate([gl_ref[...], gr_ref[...]], axis=0), image)
+PRODUCTS = ((0, 0), (0, 1), (0, 2), (1, 1), (1, 2), (2, 2))
+
+
+def products(vectors, packs, chosen):
     width = LANES // packs
     rows = []
-    for left, right in ((0, 0), (0, 1), (0, 2), (1, 1), (1, 2), (2, 2)):
-        total = jnp.sum(vectors[left] * vectors[right], axis=0)
+    for pair in PRODUCTS:
+        if pair not in chosen:
+            rows.append(jnp.zeros((1, LANES), F32))
+            continue
+        total = jnp.sum(vectors[pair[0]] * vectors[pair[1]], axis=0)
         total = jnp.sum(total, axis=0, keepdims=True)
         folded = total
         for g in range(1, packs):
             folded = folded + pltpu.roll(total, g * width, 1)
         rows.append(folded)
     rows.append(jnp.zeros((2, LANES), F32))
-    held[...] = jnp.concatenate(rows, axis=0)
-    fetch([(held, out)], sems, 1)
-    image_copy.wait()
-
-
-def dots(b_own, g_own, parts, packs):
-    operands = (b_own, *g_own, *parts)
+    return jnp.concatenate(rows, axis=0)
+
+
+def early_kernel(packs, b_ref, gl_ref, gr_ref, out_ref):
+    first = jnp.concatenate([gl_ref[...], gr_ref[...]], axis=0)
+    out_ref[...] = products((b_ref[...], first), packs, ((0, 0), (0, 1), (1, 1)))
+
+
+def early_dots(b_own, g_own, packs):
+    return pl.pallas_call(
+        functools.partial(early_kernel, packs),
+        out_shape=jax.ShapeDtypeStruct((8, LANES), F32),
+        in_specs=[VMEM_SPEC] * 3,
+        out_specs=VMEM_SPEC,
+        compiler_params=PARAMS,
+        cost_estimate=cost(6 * b_own.size, 8 * b_own.size),
+        name="early_dots",
+    )(b_own, *g_own)
+
+
+def dots_kernel(packs, b_ref, gl_ref, gr_ref, early_ref, *refs):
+    parts, (out, image_ref, held, sems) = refs[:-4], refs[-4:]
+    image = parts[0][...]
+    for part in parts[1:]:
+        image = image + part[...]
+    image_ref[...] = image
+    first = jnp.concatenate([gl_ref[...], gr_ref[...]], axis=0)
+    late = products((b_ref[...], first, image), packs, ((0, 2), (1, 2), (2, 2)))
+    held[...] = early_ref[...] + late
+    fetch([(held, out)], sems)
+
+
+def dots(b_own, g_own, early, parts, packs):
+    operands = (b_own, *g_own, early, *parts)
     outs = [jax.ShapeDtypeStruct((8, LANES), F32), jax.ShapeDtypeStruct(b_own.shape, F32)]
     return pl.pallas_call(
-        functools.partial(dots_kernel, packs, len(operands)),
+        functools.partial(dots_kernel, packs),
         out_shape=outs,
-        in_specs=[ANY_SPEC] * len(operands),
-        out_specs=[ANY_SPEC] * 2,
-        scratch_shapes=buffers([*operands, *outs]) + [pltpu.SemaphoreType.DMA((len(operands),))],
+        in_specs=[VMEM_SPEC] * len(operands),
+        out_specs=[ANY_SPEC, VMEM_SPEC],
+        scratch_shapes=buffers(outs[:1]) + [pltpu.SemaphoreType.DMA((1,))],
         compiler_params=PARAMS,
-        cost_estimate=cost(14 * b_own.size, 20 * b_own.size),
+        cost_estimate=cost(8 * b_own.size, 20 * b_own.size),
         name="dots",
     )(*operands)
 
@@ -444,10 +504,10 @@
 
 
 def finish_kernel(packs, *refs):
-    hbm, outs, vmem, (solution_ref, residual_ref, sems) = refs[:5], refs[5:7], refs[7:12], refs[12:]
-    fetch(list(zip(hbm, vmem)), sems)
-    dots_ref, b_ref, gl_ref, gr_ref, image_ref = vmem
-    bb, b1, b2, s11, s12, s22 = [dots_ref[i : i + 1, :] for i in range(6)]
+    mine_ref, other_ref, b_ref, gl_ref, gr_ref, image_ref = refs[:6]
+    outs, (solution_ref, residual_ref, sems) = refs[6:8], refs[8:]
+    total = mine_ref[...] + other_ref[...]
+    bb, b1, b2, s11, s12, s22 = [total[i : i + 1, :] for i in range(6)]
     square = bb + EPS
     rhs_length = jnp.sqrt(square)
     upper_left = (0.5 * bb + b1) / square
@@ -495,22 +555,40 @@
     fetch([(solution_ref, outs[0]), (residual_ref, outs[1])], sems)
 
 
-def finish(total, b_own, g_own, image, packs):
-    operands = (total, b_own, *g_own, image)
+def finish(totals, b_own, g_own, image, packs):
+    operands = (*totals, b_own, *g_own, image)
     out = jax.ShapeDtypeStruct((LANES // packs, CL_DEV * B), F32)
     return pl.pallas_call(
         functools.partial(finish_kernel, packs),
         out_shape=[out] * 2,
-        in_specs=[ANY_SPEC] * len(operands),
+        in_specs=[VMEM_SPEC] * len(operands),
         out_specs=[ANY_SPEC] * 2,
-        scratch_shapes=buffers([*operands, out, out])
-        + [pltpu.SemaphoreType.DMA((len(operands),))],
+        scratch_shapes=buffers([out, out]) + [pltpu.SemaphoreType.DMA((2,))],
         compiler_params=PARAMS,
         cost_estimate=cost(8 * b_own.size, 28 * b_own.size),
         name="finish",
     )(*operands)
 
 
+def hold_kernel(*refs):
+    del refs
+
+
+def hold(values):
+    return list(
+        pl.pallas_call(
+            hold_kernel,
+            out_shape=[jax.ShapeDtypeStruct(v.shape, v.dtype) for v in values],
+            in_specs=[ANY_SPEC] * len(values),
+            out_specs=[ANY_SPEC] * len(values),
+            input_output_aliases={n: n for n in range(len(values))},
+            compiler_params=PARAMS,
+            cost_estimate=cost(4 * 10**10, 0),
+            name="hold",
+        )(*values)
+    )
+
+
 def swap_cores(value):
     size = lax.axis_size("far")
     return lax.ppermute(value, "far", [(i, i ^ 1) for i in range(size)])
@@ -541,10 +619,12 @@
 def sum_rows(value):
     size = lax.axis_size("rows")
     step = 1
-    while step < size:
-        value = value + lax.ppermute(value, "rows", [(i, i ^ step) for i in range(size)])
+    while True:
+        other = lax.ppermute(value, "rows", [(i, i ^ step) for i in range(size)])
         step *= 2
-    return value
+        if step >= size:
+            return value, other
+        value = value + other
 
 
 def exchange(coef):
@@ -552,11 +632,11 @@
 
 
 def sum_far(keeps, sends, coef):
-    terms = [keeps[0]]
+    others = []
     for shift in range(1, len(keeps)):
         got, coef = lax.optimization_barrier((swap_cores(sends[shift]), coef))
-        terms.append(along_y(keeps[shift] + got, shift))
-    return terms + [swap_cores(sends[0])], coef
+        others.append(along_y(keeps[shift] + got, shift))
+    return [keeps[0], swap_cores(sends[0])], others, coef
 
 
 def shards(right_side, near_blocks, near_cols, far_src, far_tgt, far_left, far_right):
@@ -570,37 +650,42 @@
     own = right_side.reshape(CL_DEV, B, width)
     groups = far_left.shape[1]
 
-    part = REACH // CORES
-    tail = lax.dynamic_slice_in_dim(own, CL_DEV - REACH + core * part, part, 0)
-    head = lax.dynamic_slice_in_dim(own, core * part, part, 0)
-    from_left, from_right = to_next(tail), to_previous(head)
-    gathered = [
-        item
-        for value in (
-            jnp.stack([far_src.reshape(-1), far_tgt.reshape(-1)]),
-            far_right.reshape(groups, B, R).transpose(0, 2, 1),
-            far_left.reshape(groups, B, R).transpose(0, 2, 1),
-        )
-        for item in along_all_y(value)
-    ]
+    part, shared, direct = halo_parts(ys)
+    at = core * part
+    turn = at + lax.axis_index("far") // CORES * shared
+
+    def cut(first, count):
+        return lax.dynamic_slice_in_dim(own, first, count, 0)
+
+    ends = [to_next(cut(CL_DEV - REACH + turn, shared)), to_previous(cut(turn, shared))]
+    meta = along_all_y(jnp.stack([far_src.reshape(-1), far_tgt.reshape(-1)]))
+    factors = [f.reshape(groups, B, R).transpose(0, 2, 1) for f in (far_right, far_left)]
+    factors = along_all_y(jnp.concatenate(factors, axis=0))
     b_own = pack(own, far_size, per)
-    gathered = after(gathered, b_own)
-    meta, rights, lefts = [
-        part_ + [swap_cores(item) for item in part_]
-        for part_ in (gathered[:ys], gathered[ys : 2 * ys], gathered[2 * ys :])
-    ]
-    coef = coefficients(meta, rights, [b_own], far_size)
-    pieces = after([from_left, from_right], coef)
+    arrived = hold(ends + meta[1:])
+    near, ends, meta = own, arrived[:2], meta[:1] + arrived[2:]
+    pieces = list(ends)
+    for s in range(1, ys):
+        pieces += [along_y(item, s) for item in ends]
+    if direct:
+        first = at + ys * shared
+        pieces += [
+            to_next(lax.dynamic_slice_in_dim(near, CL_DEV - REACH + first, direct, 0)),
+            to_previous(lax.dynamic_slice_in_dim(near, first, direct, 0)),
+        ]
+    meta, factors = [items + [swap_cores(item) for item in items] for items in (meta, factors)]
+    coef = coefficients(meta, factors, [b_own], far_size)
+    pieces = after(pieces, coef)
     pieces += [swap_cores(item) for item in pieces]
     coef = exchange(coef)
     keeps, sends = operator(near_blocks, [own] + pieces, cols, far_size, per, width, False)
-    terms, coef = sum_far(keeps, sends, coef)
-    g_own = add_halves(terms + [far_part(meta, lefts, coef, far_size, per)])
+    terms, others, coef = sum_far(keeps, sends, coef)
+    g_own = add_halves([far_part(meta, factors, coef, terms, far_size, per)] + others)
 
     head, tail = g_own
     from_left, from_right = to_next(tail), to_previous(head)
     heads, tails = along_all_y(head), along_all_y(tail)
-    coef = coefficients(meta, rights, g_own, far_size)
+    coef = coefficients(meta, factors, g_own, far_size)
     arrived = after([from_left, from_right] + heads[1:] + tails[1:], coef)
     from_left, from_right = arrived[:2]
     heads, tails = heads[:1] + arrived[2 : 1 + ys], tails[:1] + arrived[1 + ys :]
@@ -612,9 +697,10 @@
     halos += [swap_cores(item) for item in halos]
     coef = exchange(coef)
     keeps, sends = operator(near_blocks, owns + halos, cols, far_size, per, width, True)
-    terms, coef = sum_far(keeps, sends, coef)
-    far = far_part(meta, lefts, coef, far_size, per)
-    part_dots, image = dots(b_own, g_own, terms + [far], packs)
+    terms, others, coef = sum_far(keeps, sends, coef)
+    base = far_part(meta, factors, coef, terms, far_size, per)
+    early = early_dots(b_own, g_own, packs)
+    part_dots, image = dots(b_own, g_own, early, [base] + others, packs)
     answer, residual = finish(sum_rows(part_dots), b_own, g_own, image, packs)
     return answer.T, residual.T
 

time: 151 us -> 143 us (0.947)
  Pallas kernels: 55 us -> 36.5 us
  waiting for transfers between devices: 30.8 us -> 46.4 us
  starting transfers between devices: 52 us -> 47.6 us
    ppermute x8 -> x9, waiting for transfers between devices: 8.55 us -> 25.6 us  [along_y(): lax.ppermute(value, 'far', [(i, (i + CORES * shift) % size) for i in rang...]
    pallas_call x3 -> x5, Pallas kernels: 14.9 us -> 7.08 us  [the longest x2 6.51 us: far_part(): pl.pallas_call(functools.partial(far_kernel, far_size, len(terms)), out_s...]
    pallas_call x2, Pallas kernels: 11.6 us -> 6.54 us  [coefficients(): pl.pallas_call(functools.partial(coefficient_kernel, far_size, len(fields...]
    all_to_all x2, waiting for transfers between devices: 3.47 us -> 0.38 us  [exchange(): return lax.all_to_all(coef, 'rows', split_axis=0, concat_axis=0, tiled=True)]
    ppermute x3, starting transfers between devices: 8.98 us -> 6.57 us  [sum_rows(): other = lax.ppermute(value, 'rows', [(i, i ^ step) for i in range(size)])]
    pallas_call x1, Pallas kernels: 2.38 us -> 0.11 us  [add_halves(): pl.pallas_call(functools.partial(add_kernel, len(parts)), out_shape=[half...]
    pallas_call x1, Pallas kernels: 2.63 us -> 0.41 us  [pack(): pl.pallas_call(functools.partial(pack_kernel, far_size), out_shape=out, i...]
    ppermute x2, starting transfers between devices: 9.13 us -> 7.34 us  [to_next(): lax.ppermute(value, 'rows', [(i, i + 1) for i in range(lax.axis_size('row...]
  transfers between devices with their start and end apart: 38 -> 39, of which waited for: 19 -> 23; matrix products, arithmetic and copies ran while one was open for 2% -> 2% of each run, Pallas kernels for 31% -> 24%
where the time goes in v4:
time: 143 us
  starting transfers between devices  47.6 us (33%)
  waiting for transfers between devices  46.4 us (32%)
  Pallas kernels  36.5 us (26%)
  local copies, waits for them, and re-layouts  7.35 us (5%)
  other arithmetic  3.44 us (2%)
    ppermute x9, waiting for transfers between devices, along_y(): lax.ppermute(value, 'far', [(i, (i + CORES * shift) % size) for i in rang...  25.6 us
    pallas_call x2, Pallas kernels, operator(): pl.pallas_call(functools.partial(operator_kernel, far_size, per, last, le...  21 us
    all_to_all x2, starting transfers between devices, exchange(): return lax.all_to_all(coef, 'rows', split_axis=0, concat_axis=0, tiled=True)  15.7 us
    ppermute x9, starting transfers between devices, along_y(): lax.ppermute(value, 'far', [(i, (i + CORES * shift) % size) for i in rang...  10.3 us
    ppermute x20, waiting for transfers between devices, swap_cores(): return lax.ppermute(value, 'far', [(i, i ^ 1) for i in range(size)])  8.39 us
    ppermute x2, starting transfers between devices, to_next(): lax.ppermute(value, 'rows', [(i, i + 1) for i in range(lax.axis_size('row...  7.34 us
    ppermute x2, waiting for transfers between devices, to_next(): lax.ppermute(value, 'rows', [(i, i + 1) for i in range(lax.axis_size('row...  6.84 us
    ppermute x3, starting transfers between devices, sum_rows(): other = lax.ppermute(value, 'rows', [(i, i ^ step) for i in range(size)])  6.57 us
  transfers between devices with their start and end apart: 39, of which 23 were waited for; matrix products, arithmetic and copies ran while one was open for 2% of the time, Pallas kernels for 24%

profile of v4, /device:TPU:0, one launch (start us, length us, event | category | flops | bytes accessed | tf_op | source)
XLA Modules:
  0.0 142.5 jit_solution(1241138356636953111)
XLA Ops:
  0.7 1.1 pad_maximum_fusion.refs_4_
  1.7 3.0 %collective-permute-start.5 = (f32[16,64,128]{2,1,0:T(8,128)S(1)}, f32[16,64,128]{2,1,0:T(8,128)}, u32[]{:S(2)}, u32[]{:S(2)}) collective-permute-start(f32[16,64,128]{2,1,0:T(8,128)S(1)} %pad_maximum_fusion.refs_4_), channel_id=1, source_target_pairs={{0,2},{1,3},{2,0},{3,1},{4,6},{5,7},{6,4},{7,5},{8,10},{9,11},{10,... | collective-permute-start | bytes 1572872 | tf_op jit(solution)/shard_map/ppermute | solution.py:599
  4.8 1.1 constant_dynamic-slice_fusion
  5.8 3.4 %collective-permute-start = (f32[2,128,256]{2,1,0:T(8,128)S(1)}, f32[2,128,256]{2,1,0:T(8,128)S(1)}, u32[]{:S(2)}, u32[]{:S(2)}) collective-permute-start(f32[2,128,256]{2,1,0:T(8,128)S(1)} %get-tuple-element.61), channel_id=1, source_target_pairs={{0,4},{4,8},{8,12},{12,16},{16,20},{20,24},{24,28},{1,5},{5,9},{9,... | collective-permute-start | bytes 786440 | tf_op jit(solution)/shard_map/ppermute | solution.py:612
  9.2 1.3 collective-permute-start.1
  10.7 0.6 collective-permute-start.2
  11.2 5.6 %collective-permute-done.5.refs_5_ = f32[16,64,128]{2,1,0:T(8,128)} collective-permute-done((f32[16,64,128]{2,1,0:T(8,128)S(1)}, f32[16,64,128]{2,1,0:T(8,128)}, u32[]{:S(2)}, u32[]{:S(2)}) %collective-permute-start.5) | collective-permute-done | bytes 524320 | tf_op jit(solution)/shard_map/ppermute | solution.py:599
  16.8 3.3 %collective-permute-done.refs_0_ = f32[2,128,256]{2,1,0:T(8,128)S(1)} collective-permute-done((f32[2,128,256]{2,1,0:T(8,128)S(1)}, f32[2,128,256]{2,1,0:T(8,128)S(1)}, u32[]{:S(2)}, u32[]{:S(2)}) %collective-permute-start) | collective-permute-done | bytes 262176 | tf_op jit(solution)/shard_map/ppermute | solution.py:612
  20.1 0.6 collective-permute-start.8
  20.7 1.5 %collective-permute-start.9 = (f32[2,128,256]{2,1,0:T(8,128)S(1)}, f32[2,128,256]{2,1,0:T(8,128)S(1)}, u32[]{:S(2)}, u32[]{:S(2)}) collective-permute-start(f32[2,128,256]{2,1,0:T(8,128)S(1)} %get-tuple-element.35.refs_2_), channel_id=1, source_target_pairs={{0,2},{1,3},{2,0},{3,1},{4,6},{5,7},{6,4},{7,5},{8,10},{9,11},{10,... | collective-permute-start | bytes 786440 | tf_op jit(solution)/shard_map/ppermute | solution.py:599
  22.2 1.1 collective-permute-done.3.refs_2_
  23.5 0.4 pack.1.refs_8_.b_ref.refs_2_
  24.0 0.5 collective-permute-done.4.refs_3_
  24.5 3.7 %coefficients.2 = f32[8,2,64,128]{3,2,1,0:T(8,128)} custom-call(s32[2,8]{1,0:T(2,128)S(1)} %pad_add_fusion.refs_0_, s32[2,8]{1,0:T(2,128)S(1)} %get-tuple-element.31.refs_1_, s32[2,8]{1,0:T(2,128)S(1)} %collective-permute-done.3.refs_2_, s32[2,8]{1,0:T(2,128)S(1)} %collective-permute-done.4.refs_3_, f32[16,64,128]{2,1,0:T(8,128)S(1)} %pad_maximum_fusion.refs_4_, ...), custom_call_target="tpu_custom_call" | custom-call | flops 100663296 | bytes 4194304 | tf_op jit(solution)/shard_map/coefficients/pallas_call | solution.py:170
  28.2 0.8 copy-done.1
  29.0 0.8 copy-done.3
  29.7 6.7 %all-to-all-start = ((f32[8,2,64,128]{3,2,1,0:T(8,128)}), f32[8,2,64,128]{3,2,1,0:T(8,128)S(1)}, u32[]{:S(2)}, u32[]{:S(2)}) async-start(f32[8,2,64,128]{3,2,1,0:T(8,128)} %coefficients.2), calls=%async_computation | async-start | bytes 1048576 | tf_op jit(solution)/shard_map/all_to_all | solution.py:631
  36.6 0.5 collective-permute-start.11
  37.2 0.4 collective-permute-start.13
  37.6 0.5 collective-permute-done.10.refs_5_
  38.1 0.4 collective-permute-done.11.refs_6_
  38.5 0.4 collective-permute-done.12.refs_7_
  38.9 0.4 collective-permute-done.13.refs_8_
  39.2 0.7 copy-done.26
  40.0 10.2 %operator.2 = (f32[8,128,128]{2,1,0:T(8,128)}, f32[8,128,128]{2,1,0:T(8,128)}, f32[8,128,128]{2,1,0:T(8,128)}, f32[8,128,128]{2,1,0:T(8,128)}) custom-call(s32[6,16]{1,0:T(8,128)} %bitcast.17, f32[16,6,128,128]{3,2,1,0:T(8,128)} %blocks_ref.3, f32[16,128,256]{2,1,0:T(8,128)} %bitcast.13, f32[2,128,256]{2,1,0:T(8,128)} %copy-done.14, ...), custom_call_target="tpu_custom_call" | custom-call | tf_op jit(solution)/shard_map/operator/pallas_call | solution.py:375
  50.4 0.4 collective-permute-start.15
  50.8 1.7 %collective-permute-done.14 = f32[8,128,128]{2,1,0:T(8,128)} collective-permute-done((f32[8,128,128]{2,1,0:T(8,128)}, f32[8,128,128]{2,1,0:T(8,128)}, u32[]{:S(2)}, u32[]{:S(2)}) %collective-permute-start.14) | collective-permute-done | bytes 524320 | tf_op jit(solution)/shard_map/ppermute | solution.py:594
  52.5 1.3 add.32
  53.8 0.6 collective-permute-start.16
  54.4 1.0 copy-done.13
  55.4 3.1 %far_part.2.refs_0_ = f32[8,128,128]{2,1,0:T(8,128)S(1)} custom-call(s32[2,8]{1,0:T(2,128)S(1)} %pad_add_fusion.refs_0_, s32[2,8]{1,0:T(2,128)S(1)} %get-tuple-element.31.refs_1_, s32[2,8]{1,0:T(2,128)S(1)} %collective-permute-done.3.refs_2_, s32[2,8]{1,0:T(2,128)S(1)} %collective-permute-done.4.refs_3_, f32[16,64,128]{2,1,0:T(8,128)S(1)} %pad_maximum_fusion.refs_4_, ...), custom_call_target="tpu_custom_call" | custom-call | flops 100663296 | bytes 4194304 | tf_op jit(solution)/shard_map/far_part/pallas_call | solution.py:229
  58.6 9.2 %collective-permute-done.16.refs_1_ = f32[8,128,128]{2,1,0:T(8,128)S(1)} collective-permute-done((f32[8,128,128]{2,1,0:T(8,128)S(1)}, f32[8,128,128]{2,1,0:T(8,128)S(1)}, u32[]{:S(2)}, u32[]{:S(2)}) %collective-permute-start.16) | collective-permute-done | bytes 524320 | tf_op jit(solution)/shard_map/ppermute | solution.py:599
  68.0 3.9 %collective-permute-start.17 = (f32[4,128,128]{2,1,0:T(8,128)S(1)}, f32[4,128,128]{2,1,0:T(8,128)S(1)}, u32[]{:S(2)}, u32[]{:S(2)}) collective-permute-start(f32[4,128,128]{2,1,0:T(8,128)S(1)} %get-tuple-element.45.gr_ref.refs_9_.refs_1_.refs_4_), channel_id=1, source_target_pairs={{0,4},{4,8},{8,12},{12,16},{16,20},{20,24},{24,28},{1,5},{5,9},{9,... | collective-permute-start | bytes 786440 | tf_op jit(solution)/shard_map/ppermute | solution.py:612
  71.9 1.3 collective-permute-start.18
  73.2 0.6 collective-permute-start.19
  73.8 1.5 %collective-permute-start.20 = (f32[4,128,128]{2,1,0:T(8,128)S(1)}, f32[4,128,128]{2,1,0:T(8,128)S(1)}, u32[]{:S(2)}, u32[]{:S(2)}) collective-permute-start(f32[4,128,128]{2,1,0:T(8,128)S(1)} %get-tuple-element.45.gr_ref.refs_9_.refs_1_.refs_4_), channel_id=1, source_target_pairs={{0,2},{1,3},{2,0},{3,1},{4,6},{5,7},{6,4},{7,5},{8,10},{9,11},{10,... | collective-permute-start | bytes 786440 | tf_op jit(solution)/shard_map/ppermute | solution.py:599
  75.3 2.9 %coefficients.3 = f32[8,2,64,128]{3,2,1,0:T(8,128)S(1)} custom-call(s32[2,8]{1,0:T(2,128)S(1)} %pad_add_fusion.refs_0_, s32[2,8]{1,0:T(2,128)S(1)} %get-tuple-element.31.refs_1_, s32[2,8]{1,0:T(2,128)S(1)} %collective-permute-done.3.refs_2_, s32[2,8]{1,0:T(2,128)S(1)} %collective-permute-done.4.refs_3_, f32[16,64,128]{2,1,0:T(8,128)S(1)} %pad_maximum_fusion.refs_4_, ...), custom_call_target="tpu_custom_call" | custom-call | flops 100663296 | bytes 4194304 | tf_op jit(solution)/shard_map/coefficients/pallas_call | solution.py:170
  78.2 0.8 copy-done.11
  79.0 3.5 %collective-permute-done.17.refs_8_ = f32[4,128,128]{2,1,0:T(8,128)S(1)} collective-permute-done((f32[4,128,128]{2,1,0:T(8,128)S(1)}, f32[4,128,128]{2,1,0:T(8,128)S(1)}, u32[]{:S(2)}, u32[]{:S(2)}) %collective-permute-start.17) | collective-permute-done | bytes 262176 | tf_op jit(solution)/shard_map/ppermute | solution.py:612
  82.6 3.5 %collective-permute-done.20.refs_3_ = f32[4,128,128]{2,1,0:T(8,128)S(1)} collective-permute-done((f32[4,128,128]{2,1,0:T(8,128)S(1)}, f32[4,128,128]{2,1,0:T(8,128)S(1)}, u32[]{:S(2)}, u32[]{:S(2)}) %collective-permute-start.20) | collective-permute-done | bytes 262176 | tf_op jit(solution)/shard_map/ppermute | solution.py:599
  86.1 0.5 collective-permute-start.25
  86.8 1.3 collective-permute-start.26
  88.2 9.0 %all-to-all-start.1 = ((f32[8,2,64,128]{3,2,1,0:T(8,128)}), f32[8,2,64,128]{3,2,1,0:T(8,128)S(1)}, u32[]{:S(2)}, u32[]{:S(2)}) async-start(f32[8,2,64,128]{3,2,1,0:T(8,128)} %copy-done.11), calls=%async_computation.1 | async-start | bytes 1048576 | tf_op jit(solution)/shard_map/all_to_all | solution.py:631
  98.6 0.9 collective-permute-done.24.refs_7_
  99.4 0.5 collective-permute-done.28.refs_13_
  99.9 0.4 collective-permute-done.29.refs_14_
  100.3 0.4 collective-permute-done.30.refs_15_
  100.7 10.7 %operator.3 = (f32[8,128,128]{2,1,0:T(8,128)}, f32[8,128,128]{2,1,0:T(8,128)}, f32[8,128,128]{2,1,0:T(8,128)}, f32[8,128,128]{2,1,0:T(8,128)}) custom-call(s32[6,16]{1,0:T(8,128)} %bitcast.18, f32[16,6,128,128]{3,2,1,0:T(8,128)} %blocks_ref.3, f32[4,128,128]{2,1,0:T(8,128)} %copy-done.5, f32[4,128,128]{2,1,0:T(8,128)} %copy-done.8, ...), custom_call_target="tpu_custom_call" | custom-call | tf_op jit(solution)/shard_map/operator/pallas_call | solution.py:375
  112.0 0.4 all-to-all-done.1.refs_8_
  112.4 1.2 collective-permute-done.31
  113.6 1.1 add.33
  114.7 1.4 collective-permute-start.33
  116.1 0.9 copy-done.6
  117.1 0.9 copy-done.9
  118.3 3.4 %far_part.3.refs_0_ = f32[8,128,128]{2,1,0:T(8,128)S(1)} custom-call(s32[2,8]{1,0:T(2,128)S(1)} %pad_add_fusion.refs_0_, s32[2,8]{1,0:T(2,128)S(1)} %get-tuple-element.31.refs_1_, s32[2,8]{1,0:T(2,128)S(1)} %collective-permute-done.3.refs_2_, s32[2,8]{1,0:T(2,128)S(1)} %collective-permute-done.4.refs_3_, f32[16,64,128]{2,1,0:T(8,128)S(1)} %pad_maximum_fusion.refs_4_, ...), custom_call_target="tpu_custom_call" | custom-call | flops 100663296 | bytes 4194304 | tf_op jit(solution)/shard_map/far_part/pallas_call | solution.py:229
  121.7 7.2 %collective-permute-done.33.refs_1_ = f32[8,128,128]{2,1,0:T(8,128)S(1)} collective-permute-done((f32[8,128,128]{2,1,0:T(8,128)S(1)}, f32[8,128,128]{2,1,0:T(8,128)S(1)}, u32[]{:S(2)}, u32[]{:S(2)}) %collective-permute-start.33) | collective-permute-done | bytes 524320 | tf_op jit(solution)/shard_map/ppermute | solution.py:599
  128.9 0.3 dots.1
  129.2 1.9 %collective-permute-start.34 = (f32[8,128]{1,0:T(8,128)S(1)}, f32[8,128]{1,0:T(8,128)S(1)}, u32[]{:S(2)}, u32[]{:S(2)}) collective-permute-start(f32[8,128]{1,0:T(8,128)S(1)} %get-tuple-element.56), channel_id=1, source_target_pairs={{0,4},{4,0},{8,12},{12,8},{16,20},{20,16},{24,28},{28,24},{1,5},{5... | collective-permute-start | bytes 12296 | tf_op jit(solution)/shard_map/ppermute | solution.py:623
  131.1 1.7 %collective-permute-done.34 = f32[8,128]{1,0:T(8,128)S(1)} collective-permute-done((f32[8,128]{1,0:T(8,128)S(1)}, f32[8,128]{1,0:T(8,128)S(1)}, u32[]{:S(2)}, u32[]{:S(2)}) %collective-permute-start.34) | collective-permute-done | bytes 4128 | tf_op jit(solution)/shard_map/ppermute | solution.py:623
  132.9 1.9 %collective-permute-start.35 = (f32[8,128]{1,0:T(8,128)S(1)}, f32[8,128]{1,0:T(8,128)S(1)}, u32[]{:S(2)}, u32[]{:S(2)}) collective-permute-start(f32[8,128]{1,0:T(8,128)S(1)} %add.34), channel_id=1, source_target_pairs={{0,8},{4,12},{8,0},{12,4},{16,24},{20,28},{24,16},{28,20},{1,9},{5... | collective-permute-start | bytes 12296 | tf_op jit(solution)/shard_map/ppermute | solution.py:623
  134.7 1.7 %collective-permute-done.35 = f32[8,128]{1,0:T(8,128)S(1)} collective-permute-done((f32[8,128]{1,0:T(8,128)S(1)}, f32[8,128]{1,0:T(8,128)S(1)}, u32[]{:S(2)}, u32[]{:S(2)}) %collective-permute-start.35) | collective-permute-done | bytes 4128 | tf_op jit(solution)/shard_map/ppermute | solution.py:623
  136.5 2.8 %collective-permute-start.36 = (f32[8,128]{1,0:T(8,128)S(1)}, f32[8,128]{1,0:T(8,128)S(1)}, u32[]{:S(2)}, u32[]{:S(2)}) collective-permute-start(f32[8,128]{1,0:T(8,128)S(1)} %add.35.refs_0_), channel_id=1, source_target_pairs={{0,16},{4,20},{8,24},{12,28},{16,0},{20,4},{24,8},{28,12},{1,17},{... | collective-permute-start | bytes 12296 | tf_op jit(solution)/shard_map/ppermute | solution.py:623
  139.2 1.7 %collective-permute-done.36.refs_1_ = f32[8,128]{1,0:T(8,128)S(1)} collective-permute-done((f32[8,128]{1,0:T(8,128)S(1)}, f32[8,128]{1,0:T(8,128)S(1)}, u32[]{:S(2)}, u32[]{:S(2)}) %collective-permute-start.36) | collective-permute-done | bytes 4128 | tf_op jit(solution)/shard_map/ppermute | solution.py:623
  141.0 1.4 finish.1
  (91 shorter events, 3.4 us)
Async XLA Ops:
  0.6 10.0 %copy-start.28 = (s32[1,8,1]{1,2,0:T(1,128)S(1)}, s32[1,8,1]{1,2,0:T(1,128)}, u32[]{:S(2)}) copy-start(s32[1,8,1]{1,2,0:T(1,128)} %param.10) | copy-start | bytes 100
  0.6 10.0 %copy-start.27 = (s32[1,8,1]{1,2,0:T(1,128)S(1)}, s32[1,8,1]{1,2,0:T(1,128)}, u32[]{:S(2)}) copy-start(s32[1,8,1]{1,2,0:T(1,128)} %param.11) | copy-start | bytes 100
  1.7 15.1 %collective-permute-start.5 = (f32[16,64,128]{2,1,0:T(8,128)S(1)}, f32[16,64,128]{2,1,0:T(8,128)}, u32[]{:S(2)}, u32[]{:S(2)}) collective-permute-start(f32[16,64,128]{2,1,0:T(8,128)S(1)} %pad_maximum_fusion.refs_4_), channel_id=1, source_target_pairs={{0,2},{1,3},{2,0},{3,1},{4,6},{5,7},{6,4},{7,5},{8,10},{9,11},{10,... | collective-permute-start | bytes 1572872 | tf_op jit(solution)/shard_map/ppermute | solution.py:599
  5.8 14.3 %collective-permute-start = (f32[2,128,256]{2,1,0:T(8,128)S(1)}, f32[2,128,256]{2,1,0:T(8,128)S(1)}, u32[]{:S(2)}, u32[]{:S(2)}) collective-permute-start(f32[2,128,256]{2,1,0:T(8,128)S(1)} %get-tuple-element.61), channel_id=1, source_target_pairs={{0,4},{4,8},{8,12},{12,16},{16,20},{20,24},{24,28},{1,5},{5,9},{9,... | collective-permute-start | bytes 786440 | tf_op jit(solution)/shard_map/ppermute | solution.py:612
  9.2 10.9 %collective-permute-start.1 = (f32[2,128,256]{2,1,0:T(8,128)S(1)}, f32[2,128,256]{2,1,0:T(8,128)S(1)}, u32[]{:S(2)}, u32[]{:S(2)}) collective-permute-start(f32[2,128,256]{2,1,0:T(8,128)S(1)} %get-tuple-element.60), channel_id=1, source_target_pairs={{4,0},{8,4},{12,8},{16,12},{20,16},{24,20},{28,24},{5,1},{9,5},{13... | collective-permute-start | bytes 786440 | tf_op jit(solution)/shard_map/ppermute | solution.py:616
  10.5 13.9 %collective-permute-start.6 = (f32[16,64,128]{2,1,0:T(8,128)S(1)}, f32[16,64,128]{2,1,0:T(8,128)S(1)}, u32[]{:S(2)}, u32[]{:S(2)}) collective-permute-start(f32[16,64,128]{2,1,0:T(8,128)S(1)} %pad_maximum_fusion.refs_4_), channel_id=1, source_target_pairs={{0,1},{1,0},{2,3},{3,2},{4,5},{5,4},{6,7},{7,6},{8,9},{9,8},{10,11... | collective-permute-start | bytes 1572872 | tf_op jit(solution)/shard_map/ppermute | solution.py:594
  10.7 12.9 %copy-start = (f32[2048,256]{1,0:T(8,128)S(1)}, f32[2048,256]{1,0:T(8,128)}, u32[]{:S(2)}) copy-start(f32[2048,256]{1,0:T(8,128)} %param.7) | copy-start | bytes 6291460
  10.7 6.1 %collective-permute-start.2 = (s32[2,8]{1,0:T(2,128)S(1)}, s32[2,8]{1,0:T(2,128)S(1)}, u32[]{:S(2)}, u32[]{:S(2)}) collective-permute-start(s32[2,8]{1,0:T(2,128)S(1)} %pad_add_fusion.refs_0_), channel_id=1, source_target_pairs={{0,2},{1,3},{2,0},{3,1},{4,6},{5,7},{6,4},{7,5},{8,10},{9,11},{10,... | collective-permute-start | bytes 200 | tf_op jit(solution)/shard_map/ppermute | solution.py:599
  16.8 7.7 %collective-permute-start.7 = (f32[16,64,128]{2,1,0:T(8,128)}, f32[16,64,128]{2,1,0:T(8,128)S(1)}, u32[]{:S(2)}, u32[]{:S(2)}) collective-permute-start(f32[16,64,128]{2,1,0:T(8,128)} %collective-permute-done.5.refs_5_), channel_id=1, source_target_pairs={{0,1},{1,0},{2,3},{3,2},{4,5},{5,4},{6,7},{7,6},{8,9},{9,8},{10,11... | collective-permute-start | bytes 1572872 | tf_op jit(solution)/shard_map/ppermute | solution.py:594
  20.1 16.4 %copy-start.14 = (f32[2,128,256]{2,1,0:T(8,128)}, f32[2,128,256]{2,1,0:T(8,128)S(1)}, u32[]{:S(2)}) copy-start(f32[2,128,256]{2,1,0:T(8,128)S(1)} %get-tuple-element.34.refs_1_) | copy-start | bytes 786436
  20.1 16.5 %copy-start.15 = (f32[2,128,256]{2,1,0:T(8,128)}, f32[2,128,256]{2,1,0:T(8,128)S(1)}, u32[]{:S(2)}) copy-start(f32[2,128,256]{2,1,0:T(8,128)S(1)} %get-tuple-element.35.refs_2_) | copy-start | bytes 786436
  20.1 16.3 %collective-permute-start.8 = (f32[2,128,256]{2,1,0:T(8,128)S(1)}, f32[2,128,256]{2,1,0:T(8,128)S(1)}, u32[]{:S(2)}, u32[]{:S(2)}) collective-permute-start(f32[2,128,256]{2,1,0:T(8,128)S(1)} %get-tuple-element.34.refs_1_), channel_id=1, source_target_pairs={{0,2},{1,3},{2,0},{3,1},{4,6},{5,7},{6,4},{7,5},{8,10},{9,11},{10,... | collective-permute-start | bytes 786440 | tf_op jit(solution)/shard_map/ppermute | solution.py:599
  20.7 15.8 %collective-permute-start.9 = (f32[2,128,256]{2,1,0:T(8,128)S(1)}, f32[2,128,256]{2,1,0:T(8,128)S(1)}, u32[]{:S(2)}, u32[]{:S(2)}) collective-permute-start(f32[2,128,256]{2,1,0:T(8,128)S(1)} %get-tuple-element.35.refs_2_), channel_id=1, source_target_pairs={{0,2},{1,3},{2,0},{3,1},{4,6},{5,7},{6,4},{7,5},{8,10},{9,11},{10,... | collective-permute-start | bytes 786440 | tf_op jit(solution)/shard_map/ppermute | solution.py:599
  22.2 1.1 collective-permute-start.3
  23.4 1.1 collective-permute-start.4
  29.7 22.8 %all-to-all-start = ((f32[8,2,64,128]{3,2,1,0:T(8,128)}), f32[8,2,64,128]{3,2,1,0:T(8,128)S(1)}, u32[]{:S(2)}, u32[]{:S(2)}) async-start(f32[8,2,64,128]{3,2,1,0:T(8,128)} %coefficients.2), calls=%async_computation | async-start | bytes 1048576 | tf_op jit(solution)/shard_map/all_to_all | solution.py:631
  36.5 3.5 %copy-start.19 = (f32[2,128,256]{2,1,0:T(8,128)}, f32[2,128,256]{2,1,0:T(8,128)S(1)}, u32[]{:S(2)}) copy-start(f32[2,128,256]{2,1,0:T(8,128)S(1)} %collective-permute-done.8.refs_3_) | copy-start | bytes 786436
  36.5 3.4 %copy-start.20 = (f32[2,128,256]{2,1,0:T(8,128)}, f32[2,128,256]{2,1,0:T(8,128)S(1)}, u32[]{:S(2)}) copy-start(f32[2,128,256]{2,1,0:T(8,128)S(1)} %collective-permute-done.9.refs_4_) | copy-start | bytes 786436
  36.5 1.6 %collective-permute-start.10 = (f32[2,128,256]{2,1,0:T(8,128)S(1)}, f32[2,128,256]{2,1,0:T(8,128)S(1)}, u32[]{:S(2)}, u32[]{:S(2)}) collective-permute-start(f32[2,128,256]{2,1,0:T(8,128)S(1)} %get-tuple-element.34.refs_1_), channel_id=1, source_target_pairs={{0,1},{1,0},{2,3},{3,2},{4,5},{5,4},{6,7},{7,6},{8,9},{9,8},{10,11... | collective-permute-start | bytes 786440 | tf_op jit(solution)/shard_map/ppermute | solution.py:594
  36.6 1.9 %collective-permute-start.11 = (f32[2,128,256]{2,1,0:T(8,128)S(1)}, f32[2,128,256]{2,1,0:T(8,128)S(1)}, u32[]{:S(2)}, u32[]{:S(2)}) collective-permute-start(f32[2,128,256]{2,1,0:T(8,128)S(1)} %get-tuple-element.35.refs_2_), channel_id=1, source_target_pairs={{0,1},{1,0},{2,3},{3,2},{4,5},{5,4},{6,7},{7,6},{8,9},{9,8},{10,11... | collective-permute-start | bytes 786440 | tf_op jit(solution)/shard_map/ppermute | solution.py:594
  37.1 1.8 %collective-permute-start.12 = (f32[2,128,256]{2,1,0:T(8,128)S(1)}, f32[2,128,256]{2,1,0:T(8,128)S(1)}, u32[]{:S(2)}, u32[]{:S(2)}) collective-permute-start(f32[2,128,256]{2,1,0:T(8,128)S(1)} %collective-permute-done.8.refs_3_), channel_id=1, source_target_pairs={{0,1},{1,0},{2,3},{3,2},{4,5},{5,4},{6,7},{7,6},{8,9},{9,8},{10,11... | collective-permute-start | bytes 786440 | tf_op jit(solution)/shard_map/ppermute | solution.py:594
  37.2 2.1 %collective-permute-start.13 = (f32[2,128,256]{2,1,0:T(8,128)S(1)}, f32[2,128,256]{2,1,0:T(8,128)S(1)}, u32[]{:S(2)}, u32[]{:S(2)}) collective-permute-start(f32[2,128,256]{2,1,0:T(8,128)S(1)} %collective-permute-done.9.refs_4_), channel_id=1, source_target_pairs={{0,1},{1,0},{2,3},{3,2},{4,5},{5,4},{6,7},{7,6},{8,9},{9,8},{10,11... | collective-permute-start | bytes 786440 | tf_op jit(solution)/shard_map/ppermute | solution.py:594
  38.1 1.8 %copy-start.23 = (f32[2,128,256]{2,1,0:T(8,128)}, f32[2,128,256]{2,1,0:T(8,128)S(1)}, u32[]{:S(2)}) copy-start(f32[2,128,256]{2,1,0:T(8,128)S(1)} %collective-permute-done.10.refs_5_) | copy-start | bytes 786436
  38.5 1.5 %copy-start.24 = (f32[2,128,256]{2,1,0:T(8,128)}, f32[2,128,256]{2,1,0:T(8,128)S(1)}, u32[]{:S(2)}) copy-start(f32[2,128,256]{2,1,0:T(8,128)S(1)} %collective-permute-done.11.refs_6_) | copy-start | bytes 786436
  38.9 1.1 copy-start.25
  39.9 14.4 %copy-start.2 = (f32[16,64,128]{2,1,0:T(8,128)S(1)}, f32[16,64,128]{2,1,0:T(8,128)}, u32[]{:S(2)}) copy-start(f32[16,64,128]{2,1,0:T(8,128)} %copy-done.1) | copy-start | bytes 1572868
  40.0 14.4 %copy-start.4 = (f32[16,64,128]{2,1,0:T(8,128)S(1)}, f32[16,64,128]{2,1,0:T(8,128)}, u32[]{:S(2)}) copy-start(f32[16,64,128]{2,1,0:T(8,128)} %copy-done.3) | copy-start | bytes 1572868
  50.2 2.3 %collective-permute-start.14 = (f32[8,128,128]{2,1,0:T(8,128)}, f32[8,128,128]{2,1,0:T(8,128)}, u32[]{:S(2)}, u32[]{:S(2)}) collective-permute-start(f32[8,128,128]{2,1,0:T(8,128)} %get-tuple-element.38), channel_id=1, source_target_pairs={{0,1},{1,0},{2,3},{3,2},{4,5},{5,4},{6,7},{7,6},{8,9},{9,8},{10,11... | collective-permute-start | bytes 1572872 | tf_op jit(solution)/shard_map/ppermute | solution.py:594
  50.4 4.0 %collective-permute-start.15 = (f32[8,128,128]{2,1,0:T(8,128)}, f32[8,128,128]{2,1,0:T(8,128)S(1)}, u32[]{:S(2)}, u32[]{:S(2)}) collective-permute-start(f32[8,128,128]{2,1,0:T(8,128)} %get-tuple-element.41), channel_id=1, source_target_pairs={{0,1},{1,0},{2,3},{3,2},{4,5},{5,4},{6,7},{7,6},{8,9},{9,8},{10,11... | collective-permute-start | bytes 1572872 | tf_op jit(solution)/shard_map/ppermute | solution.py:594
  53.8 14.0 %collective-permute-start.16 = (f32[8,128,128]{2,1,0:T(8,128)S(1)}, f32[8,128,128]{2,1,0:T(8,128)S(1)}, u32[]{:S(2)}, u32[]{:S(2)}) collective-permute-start(f32[8,128,128]{2,1,0:T(8,128)S(1)} %add.32), channel_id=1, source_target_pairs={{0,2},{1,3},{2,0},{3,1},{4,6},{5,7},{6,4},{7,5},{8,10},{9,11},{10,... | collective-permute-start | bytes 1572872 | tf_op jit(solution)/shard_map/ppermute | solution.py:599
  54.4 1.0 copy-start.13
  68.0 32.7 %copy-start.5 = (f32[4,128,128]{2,1,0:T(8,128)}, f32[4,128,128]{2,1,0:T(8,128)S(1)}, u32[]{:S(2)}) copy-start(f32[4,128,128]{2,1,0:T(8,128)S(1)} %get-tuple-element.44.gl_ref.refs_8_.refs_0_.refs_3_) | copy-start | bytes 786436
  68.0 32.7 %copy-start.8 = (f32[4,128,128]{2,1,0:T(8,128)}, f32[4,128,128]{2,1,0:T(8,128)S(1)}, u32[]{:S(2)}) copy-start(f32[4,128,128]{2,1,0:T(8,128)S(1)} %get-tuple-element.45.gr_ref.refs_9_.refs_1_.refs_4_) | copy-start | bytes 786436
  68.0 14.6 %collective-permute-start.17 = (f32[4,128,128]{2,1,0:T(8,128)S(1)}, f32[4,128,128]{2,1,0:T(8,128)S(1)}, u32[]{:S(2)}, u32[]{:S(2)}) collective-permute-start(f32[4,128,128]{2,1,0:T(8,128)S(1)} %get-tuple-element.45.gr_ref.refs_9_.refs_1_.refs_4_), channel_id=1, source_target_pairs={{0,4},{4,8},{8,12},{12,16},{16,20},{20,24},{24,28},{1,5},{5,9},{9,... | collective-permute-start | bytes 786440 | tf_op jit(solution)/shard_map/ppermute | solution.py:612
  71.9 10.6 %collective-permute-start.18 = (f32[4,128,128]{2,1,0:T(8,128)S(1)}, f32[4,128,128]{2,1,0:T(8,128)S(1)}, u32[]{:S(2)}, u32[]{:S(2)}) collective-permute-start(f32[4,128,128]{2,1,0:T(8,128)S(1)} %get-tuple-element.44.gl_ref.refs_8_.refs_0_.refs_3_), channel_id=1, source_target_pairs={{4,0},{8,4},{12,8},{16,12},{20,16},{24,20},{28,24},{5,1},{9,5},{13... | collective-permute-start | bytes 786440 | tf_op jit(solution)/shard_map/ppermute | solution.py:616
  73.2 9.4 %collective-permute-start.19 = (f32[4,128,128]{2,1,0:T(8,128)S(1)}, f32[4,128,128]{2,1,0:T(8,128)}, u32[]{:S(2)}, u32[]{:S(2)}) collective-permute-start(f32[4,128,128]{2,1,0:T(8,128)S(1)} %get-tuple-element.44.gl_ref.refs_8_.refs_0_.refs_3_), channel_id=1, source_target_pairs={{0,2},{1,3},{2,0},{3,1},{4,6},{5,7},{6,4},{7,5},{8,10},{9,11},{10,... | collective-permute-start | bytes 786440 | tf_op jit(solution)/shard_map/ppermute | solution.py:599
  73.8 12.3 %collective-permute-start.20 = (f32[4,128,128]{2,1,0:T(8,128)S(1)}, f32[4,128,128]{2,1,0:T(8,128)S(1)}, u32[]{:S(2)}, u32[]{:S(2)}) collective-permute-start(f32[4,128,128]{2,1,0:T(8,128)S(1)} %get-tuple-element.45.gr_ref.refs_9_.refs_1_.refs_4_), channel_id=1, source_target_pairs={{0,2},{1,3},{2,0},{3,1},{4,6},{5,7},{6,4},{7,5},{8,10},{9,11},{10,... | collective-permute-start | bytes 786440 | tf_op jit(solution)/shard_map/ppermute | solution.py:599
  75.3 21.9 %collective-permute-start.21 = (f32[4,128,128]{2,1,0:T(8,128)S(1)}, f32[4,128,128]{2,1,0:T(8,128)}, u32[]{:S(2)}, u32[]{:S(2)}) collective-permute-start(f32[4,128,128]{2,1,0:T(8,128)S(1)} %get-tuple-element.44.gl_ref.refs_8_.refs_0_.refs_3_), channel_id=1, source_target_pairs={{0,1},{1,0},{2,3},{3,2},{4,5},{5,4},{6,7},{7,6},{8,9},{9,8},{10,11... | collective-permute-start | bytes 786440 | tf_op jit(solution)/shard_map/ppermute | solution.py:594
  78.2 0.8 copy-start.11
  82.5 18.2 %copy-start.16 = (f32[4,128,128]{2,1,0:T(8,128)}, f32[4,128,128]{2,1,0:T(8,128)S(1)}, u32[]{:S(2)}) copy-start(f32[4,128,128]{2,1,0:T(8,128)S(1)} %collective-permute-done.17.refs_8_) | copy-start | bytes 786436
  82.5 15.0 %collective-permute-start.22 = (f32[4,128,128]{2,1,0:T(8,128)S(1)}, f32[4,128,128]{2,1,0:T(8,128)}, u32[]{:S(2)}, u32[]{:S(2)}) collective-permute-start(f32[4,128,128]{2,1,0:T(8,128)S(1)} %get-tuple-element.45.gr_ref.refs_9_.refs_1_.refs_4_), channel_id=1, source_target_pairs={{0,1},{1,0},{2,3},{3,2},{4,5},{5,4},{6,7},{7,6},{8,9},{9,8},{10,11... | collective-permute-start | bytes 786440 | tf_op jit(solution)/shard_map/ppermute | solution.py:594
  82.5 3.6 %copy-start.17 = (f32[4,128,128]{2,1,0:T(8,128)}, f32[4,128,128]{2,1,0:T(8,128)S(1)}, u32[]{:S(2)}) copy-start(f32[4,128,128]{2,1,0:T(8,128)S(1)} %collective-permute-done.18.refs_9_) | copy-start | bytes 786436
  86.1 11.7 %collective-permute-start.25 = (f32[4,128,128]{2,1,0:T(8,128)S(1)}, f32[4,128,128]{2,1,0:T(8,128)}, u32[]{:S(2)}, u32[]{:S(2)}) collective-permute-start(f32[4,128,128]{2,1,0:T(8,128)S(1)} %collective-permute-done.17.refs_8_), channel_id=1, source_target_pairs={{0,2},{1,3},{2,0},{3,1},{4,6},{5,7},{6,4},{7,5},{8,10},{9,11},{10,... | collective-permute-start | bytes 786440 | tf_op jit(solution)/shard_map/ppermute | solution.py:599
  86.8 11.2 %collective-permute-start.26 = (f32[4,128,128]{2,1,0:T(8,128)}, f32[4,128,128]{2,1,0:T(8,128)}, u32[]{:S(2)}, u32[]{:S(2)}) collective-permute-start(f32[4,128,128]{2,1,0:T(8,128)} %collective-permute-done.19.refs_2_), channel_id=1, source_target_pairs={{4,0},{8,4},{12,8},{16,12},{20,16},{24,20},{28,24},{5,1},{9,5},{13... | collective-permute-start | bytes 786440 | tf_op jit(solution)/shard_map/ppermute | solution.py:616
  88.1 10.2 %collective-permute-start.23 = (f32[4,128,128]{2,1,0:T(8,128)}, f32[4,128,128]{2,1,0:T(8,128)}, u32[]{:S(2)}, u32[]{:S(2)}) collective-permute-start(f32[4,128,128]{2,1,0:T(8,128)} %collective-permute-done.19.refs_2_), channel_id=1, source_target_pairs={{0,1},{1,0},{2,3},{3,2},{4,5},{5,4},{6,7},{7,6},{8,9},{9,8},{10,11... | collective-permute-start | bytes 786440 | tf_op jit(solution)/shard_map/ppermute | solution.py:594
  88.2 24.2 %all-to-all-start.1 = ((f32[8,2,64,128]{3,2,1,0:T(8,128)}), f32[8,2,64,128]{3,2,1,0:T(8,128)S(1)}, u32[]{:S(2)}, u32[]{:S(2)}) async-start(f32[8,2,64,128]{3,2,1,0:T(8,128)} %copy-done.11), calls=%async_computation.1 | async-start | bytes 1048576 | tf_op jit(solution)/shard_map/all_to_all | solution.py:631
  97.2 2.2 %collective-permute-start.27 = (f32[4,128,128]{2,1,0:T(8,128)S(1)}, f32[4,128,128]{2,1,0:T(8,128)S(1)}, u32[]{:S(2)}, u32[]{:S(2)}) collective-permute-start(f32[4,128,128]{2,1,0:T(8,128)S(1)} %collective-permute-done.17.refs_8_), channel_id=1, source_target_pairs={{0,1},{1,0},{2,3},{3,2},{4,5},{5,4},{6,7},{7,6},{8,9},{9,8},{10,11... | collective-permute-start | bytes 786440 | tf_op jit(solution)/shard_map/ppermute | solution.py:594
  97.5 1.9 %collective-permute-start.24 = (f32[4,128,128]{2,1,0:T(8,128)}, f32[4,128,128]{2,1,0:T(8,128)S(1)}, u32[]{:S(2)}, u32[]{:S(2)}) collective-permute-start(f32[4,128,128]{2,1,0:T(8,128)} %copy-done.18), channel_id=1, source_target_pairs={{0,1},{1,0},{2,3},{3,2},{4,5},{5,4},{6,7},{7,6},{8,9},{9,8},{10,11... | collective-permute-start | bytes 786440 | tf_op jit(solution)/shard_map/ppermute | solution.py:594
  97.8 2.1 %collective-permute-start.28 = (f32[4,128,128]{2,1,0:T(8,128)}, f32[4,128,128]{2,1,0:T(8,128)}, u32[]{:S(2)}, u32[]{:S(2)}) collective-permute-start(f32[4,128,128]{2,1,0:T(8,128)} %copy-done.17), channel_id=1, source_target_pairs={{0,1},{1,0},{2,3},{3,2},{4,5},{5,4},{6,7},{7,6},{8,9},{9,8},{10,11... | collective-permute-start | bytes 786440 | tf_op jit(solution)/shard_map/ppermute | solution.py:594
  98.1 2.3 %collective-permute-start.29 = (f32[4,128,128]{2,1,0:T(8,128)}, f32[4,128,128]{2,1,0:T(8,128)}, u32[]{:S(2)}, u32[]{:S(2)}) collective-permute-start(f32[4,128,128]{2,1,0:T(8,128)} %collective-permute-done.25.refs_10_), channel_id=1, source_target_pairs={{0,1},{1,0},{2,3},{3,2},{4,5},{5,4},{6,7},{7,6},{8,9},{9,8},{10,11... | collective-permute-start | bytes 786440 | tf_op jit(solution)/shard_map/ppermute | solution.py:594
  98.3 2.3 %collective-permute-start.30 = (f32[4,128,128]{2,1,0:T(8,128)}, f32[4,128,128]{2,1,0:T(8,128)}, u32[]{:S(2)}, u32[]{:S(2)}) collective-permute-start(f32[4,128,128]{2,1,0:T(8,128)} %collective-permute-done.26.refs_11_), channel_id=1, source_target_pairs={{0,1},{1,0},{2,3},{3,2},{4,5},{5,4},{6,7},{7,6},{8,9},{9,8},{10,11... | collective-permute-start | bytes 786440 | tf_op jit(solution)/shard_map/ppermute | solution.py:594
  99.4 1.3 copy-start.22
  99.4 1.3 copy-start.21
  111.4 2.2 %collective-permute-start.31 = (f32[8,128,128]{2,1,0:T(8,128)}, f32[8,128,128]{2,1,0:T(8,128)S(1)}, u32[]{:S(2)}, u32[]{:S(2)}) collective-permute-start(f32[8,128,128]{2,1,0:T(8,128)} %get-tuple-element.50), channel_id=1, source_target_pairs={{0,1},{1,0},{2,3},{3,2},{4,5},{5,4},{6,7},{7,6},{8,9},{9,8},{10,11... | collective-permute-start | bytes 1572872 | tf_op jit(solution)/shard_map/ppermute | solution.py:594
  111.7 6.5 %collective-permute-start.32 = (f32[8,128,128]{2,1,0:T(8,128)}, f32[8,128,128]{2,1,0:T(8,128)}, u32[]{:S(2)}, u32[]{:S(2)}) collective-permute-start(f32[8,128,128]{2,1,0:T(8,128)} %get-tuple-element.53), channel_id=1, source_target_pairs={{0,1},{1,0},{2,3},{3,2},{4,5},{5,4},{6,7},{7,6},{8,9},{9,8},{10,11... | collective-permute-start | bytes 1572872 | tf_op jit(solution)/shard_map/ppermute | solution.py:594
  112.4 5.9 %copy-start.12 = (f32[8,128,128]{2,1,0:T(8,128)S(1)}, f32[8,128,128]{2,1,0:T(8,128)}, u32[]{:S(2)}) copy-start(f32[8,128,128]{2,1,0:T(8,128)} %get-tuple-element.52.refs_9_) | copy-start | bytes 1572868
  114.7 14.1 %collective-permute-start.33 = (f32[8,128,128]{2,1,0:T(8,128)S(1)}, f32[8,128,128]{2,1,0:T(8,128)S(1)}, u32[]{:S(2)}, u32[]{:S(2)}) collective-permute-start(f32[8,128,128]{2,1,0:T(8,128)S(1)} %add.33), channel_id=1, source_target_pairs={{0,2},{1,3},{2,0},{3,1},{4,6},{5,7},{6,4},{7,5},{8,10},{9,11},{10,... | collective-permute-start | bytes 1572872 | tf_op jit(solution)/shard_map/ppermute | solution.py:599
  116.1 0.9 copy-start.6
  117.1 0.9 copy-start.9
  118.3 10.6 %copy-start.7 = (f32[4,128,128]{2,1,0:T(8,128)S(1)}, f32[4,128,128]{2,1,0:T(8,128)}, u32[]{:S(2)}) copy-start(f32[4,128,128]{2,1,0:T(8,128)} %copy-done.5) | copy-start | bytes 786436
  118.3 10.6 %copy-start.10 = (f32[4,128,128]{2,1,0:T(8,128)S(1)}, f32[4,128,128]{2,1,0:T(8,128)}, u32[]{:S(2)}) copy-start(f32[4,128,128]{2,1,0:T(8,128)} %copy-done.8) | copy-start | bytes 786436
  129.2 3.7 %collective-permute-start.34 = (f32[8,128]{1,0:T(8,128)S(1)}, f32[8,128]{1,0:T(8,128)S(1)}, u32[]{:S(2)}, u32[]{:S(2)}) collective-permute-start(f32[8,128]{1,0:T(8,128)S(1)} %get-tuple-element.56), channel_id=1, source_target_pairs={{0,4},{4,0},{8,12},{12,8},{16,20},{20,16},{24,28},{28,24},{1,5},{5... | collective-permute-start | bytes 12296 | tf_op jit(solution)/shard_map/ppermute | solution.py:623
  132.9 3.6 %collective-permute-start.35 = (f32[8,128]{1,0:T(8,128)S(1)}, f32[8,128]{1,0:T(8,128)S(1)}, u32[]{:S(2)}, u32[]{:S(2)}) collective-permute-start(f32[8,128]{1,0:T(8,128)S(1)} %add.34), channel_id=1, source_target_pairs={{0,8},{4,12},{8,0},{12,4},{16,24},{20,28},{24,16},{28,20},{1,9},{5... | collective-permute-start | bytes 12296 | tf_op jit(solution)/shard_map/ppermute | solution.py:623
  136.5 4.5 %collective-permute-start.36 = (f32[8,128]{1,0:T(8,128)S(1)}, f32[8,128]{1,0:T(8,128)S(1)}, u32[]{:S(2)}, u32[]{:S(2)}) collective-permute-start(f32[8,128]{1,0:T(8,128)S(1)} %add.35.refs_0_), channel_id=1, source_target_pairs={{0,16},{4,20},{8,24},{12,28},{16,0},{20,4},{24,8},{28,12},{1,17},{... | collective-permute-start | bytes 12296 | tf_op jit(solution)/shard_map/ppermute | solution.py:623
  (4 other events, 3.0 us)

commit v5 on v4

--- a/solution.py
+++ b/solution.py
@@ -304,23 +304,23 @@
     own_copies = begin(own_pairs, own_sems)
     halo_copies = begin(halo_pairs, in_sems)
 
+    def block_copies(entry):
+        half, k = entry // per, entry % per
+        at = [cluster_at(half, j, k, per) for j in range(packs)]
+        return [pltpu.make_async_copy(blocks_ref.at[c], blocks.at[c], block_sems.at[c]) for c in at]
+
     for copy in own_copies:
         copy.wait()
+    for entry in range(2 * per):
+        for copy in block_copies(entry):
+            copy.start()
     if last:
         unpack(own_stage, per, store_split(high, low, REACH, 2 * REACH))
     else:
         for c in range(CL_DEV):
             high[REACH + c], low[REACH + c] = split(own_stage[c])
-    def block_copies(entry):
-        half, k = entry // per, entry % per
-        at = [cluster_at(half, j, k, per) for j in range(packs)]
-        return [pltpu.make_async_copy(blocks_ref.at[c], blocks.at[c], block_sems.at[c]) for c in at]
-
     for copy in halo_copies:
         copy.wait()
-    for entry in range(2 * per):
-        for copy in block_copies(entry):
-            copy.start()
     if last:
         unpack(stage, per, store_split(high, low, 0, REACH + CL_DEV))
     else:
@@ -328,14 +328,16 @@
             at = c if c < REACH else CL_DEV + c
             high[at], low[at] = split(stage[c])
 
-    def out_copies(half):
-        rows = pl.ds(half * per, per)
+    chunk = max(1, per // 2)
+
+    def out_copies(part):
+        rows = pl.ds(part * chunk, chunk)
         copies = []
         for n, out in enumerate(outs):
             taker = core if n < ys else 1 - core
             owner = lax.rem(y + n % ys, ys) * CORES + taker
             copies.append(
-                pltpu.make_async_copy(held.at[owner, rows], out.at[rows], out_sems.at[n, half])
+                pltpu.make_async_copy(held.at[owner, rows], out.at[rows], out_sems.at[n, part])
             )
         return copies
 
@@ -356,12 +358,13 @@
             )
         return carry
 
-    for half in range(2):
-        lax.fori_loop(half * per, (half + 1) * per, step, 0, unroll=2)
-        for copy in out_copies(half):
+    parts = 2 * per // chunk
+    for part in range(parts):
+        lax.fori_loop(part * chunk, (part + 1) * chunk, step, 0, unroll=True)
+        for copy in out_copies(part):
             copy.start()
-    for half in range(2):
-        for copy in out_copies(half):
+    for part in range(parts):
+        for copy in out_copies(part):
             copy.wait()
 
 
@@ -386,7 +389,7 @@
             pltpu.SemaphoreType.DMA((n_own,)),
             pltpu.SemaphoreType.DMA((len(pieces) - n_own,)),
             pltpu.SemaphoreType.DMA((CL_DEV,)),
-            pltpu.SemaphoreType.DMA((2 * ys, 2)),
+            pltpu.SemaphoreType.DMA((2 * ys, 2 * per // max(1, per // 2))),
         ],
         compiler_params=WIDE,
         cost_estimate=cost(0, 0),
@@ -650,29 +653,21 @@
     own = right_side.reshape(CL_DEV, B, width)
     groups = far_left.shape[1]
 
-    part, shared, direct = halo_parts(ys)
-    at = core * part
-    turn = at + lax.axis_index("far") // CORES * shared
-
-    def cut(first, count):
-        return lax.dynamic_slice_in_dim(own, first, count, 0)
-
-    ends = [to_next(cut(CL_DEV - REACH + turn, shared)), to_previous(cut(turn, shared))]
+    factors = [f.reshape(groups, B, R).transpose(0, 2, 1) for f in (far_right, far_left)]
+    part, shared, _ = halo_parts(ys)
+    first = core * part + lax.axis_index("far") // CORES * shared
+    ends = [
+        to_next(lax.dynamic_slice_in_dim(own, CL_DEV - REACH + first, shared, 0)),
+        to_previous(lax.dynamic_slice_in_dim(own, first, shared, 0)),
+    ]
     meta = along_all_y(jnp.stack([far_src.reshape(-1), far_tgt.reshape(-1)]))
-    factors = [f.reshape(groups, B, R).transpose(0, 2, 1) for f in (far_right, far_left)]
     factors = along_all_y(jnp.concatenate(factors, axis=0))
     b_own = pack(own, far_size, per)
     arrived = hold(ends + meta[1:])
-    near, ends, meta = own, arrived[:2], meta[:1] + arrived[2:]
+    ends, meta = arrived[:2], meta[:1] + arrived[2:]
     pieces = list(ends)
     for s in range(1, ys):
         pieces += [along_y(item, s) for item in ends]
-    if direct:
-        first = at + ys * shared
-        pieces += [
-            to_next(lax.dynamic_slice_in_dim(near, CL_DEV - REACH + first, direct, 0)),
-            to_previous(lax.dynamic_slice_in_dim(near, first, direct, 0)),
-        ]
     meta, factors = [items + [swap_cores(item) for item in items] for items in (meta, factors)]
     coef = coefficients(meta, factors, [b_own], far_size)
     pieces = after(pieces, coef)

time: 143 us -> 143 us (level)
  no operation moved by 1% of the time
where the time goes in v5:
time: 143 us; the launch traced here: 142 us
  starting transfers between devices  47.6 us (33%)
  waiting for transfers between devices  46.4 us (32%)
  Pallas kernels  35.8 us (25%)
  local copies, waits for them, and re-layouts  7.35 us (5%)
  other arithmetic  3.44 us (2%)
    ppermute x9, waiting for transfers between devices, along_y(): lax.ppermute(value, 'far', [(i, (i + CORES * shift) % size) for i in rang...  25.6 us
    pallas_call x2, Pallas kernels, operator(): pl.pallas_call(functools.partial(operator_kernel, far_size, per, last, le...  20.2 us
    all_to_all x2, starting transfers between devices, exchange(): return lax.all_to_all(coef, 'rows', split_axis=0, concat_axis=0, tiled=True)  15.7 us
    ppermute x9, starting transfers between devices, along_y(): lax.ppermute(value, 'far', [(i, (i + CORES * shift) % size) for i in rang...  10.3 us
    ppermute x20, waiting for transfers between devices, swap_cores(): return lax.ppermute(value, 'far', [(i, i ^ 1) for i in range(size)])  7.98 us
    ppermute x2, starting transfers between devices, to_next(): lax.ppermute(value, 'rows', [(i, i + 1) for i in range(lax.axis_size('row...  7.34 us
    ppermute x2, waiting for transfers between devices, to_next(): lax.ppermute(value, 'rows', [(i, i + 1) for i in range(lax.axis_size('row...  6.84 us
    ppermute x3, starting transfers between devices, sum_rows(): other = lax.ppermute(value, 'rows', [(i, i ^ step) for i in range(size)])  6.57 us
  transfers between devices with their start and end apart: 39, of which 23 were waited for; matrix products, arithmetic and copies ran while one was open for 2% of the time, Pallas kernels for 24%

profile of v5, /device:TPU:0, one launch (start us, length us, event | category | flops | bytes accessed | tf_op | source)
XLA Modules:
  0.0 141.8 jit_solution(10616423926766482762)
XLA Ops:
  0.7 1.1 pad_maximum_fusion.refs_4_
  1.7 3.0 %collective-permute-start.5 = (f32[16,64,128]{2,1,0:T(8,128)S(1)}, f32[16,64,128]{2,1,0:T(8,128)}, u32[]{:S(2)}, u32[]{:S(2)}) collective-permute-start(f32[16,64,128]{2,1,0:T(8,128)S(1)} %pad_maximum_fusion.refs_4_), channel_id=1, source_target_pairs={{0,2},{1,3},{2,0},{3,1},{4,6},{5,7},{6,4},{7,5},{8,10},{9,11},{10,... | collective-permute-start | bytes 1572872 | tf_op jit(solution)/shard_map/ppermute | solution.py:602
  4.8 1.1 constant_dynamic-slice_fusion
  5.8 3.4 %collective-permute-start = (f32[2,128,256]{2,1,0:T(8,128)S(1)}, f32[2,128,256]{2,1,0:T(8,128)S(1)}, u32[]{:S(2)}, u32[]{:S(2)}) collective-permute-start(f32[2,128,256]{2,1,0:T(8,128)S(1)} %get-tuple-element.61), channel_id=1, source_target_pairs={{0,4},{4,8},{8,12},{12,16},{16,20},{20,24},{24,28},{1,5},{5,9},{9,... | collective-permute-start | bytes 786440 | tf_op jit(solution)/shard_map/ppermute | solution.py:615
  9.2 1.3 collective-permute-start.1
  10.7 0.6 collective-permute-start.2
  11.2 5.6 %collective-permute-done.5.refs_5_ = f32[16,64,128]{2,1,0:T(8,128)} collective-permute-done((f32[16,64,128]{2,1,0:T(8,128)S(1)}, f32[16,64,128]{2,1,0:T(8,128)}, u32[]{:S(2)}, u32[]{:S(2)}) %collective-permute-start.5) | collective-permute-done | bytes 524320 | tf_op jit(solution)/shard_map/ppermute | solution.py:602
  16.8 3.3 %collective-permute-done.refs_0_ = f32[2,128,256]{2,1,0:T(8,128)S(1)} collective-permute-done((f32[2,128,256]{2,1,0:T(8,128)S(1)}, f32[2,128,256]{2,1,0:T(8,128)S(1)}, u32[]{:S(2)}, u32[]{:S(2)}) %collective-permute-start) | collective-permute-done | bytes 262176 | tf_op jit(solution)/shard_map/ppermute | solution.py:615
  20.1 0.6 collective-permute-start.8
  20.7 1.5 %collective-permute-start.9 = (f32[2,128,256]{2,1,0:T(8,128)S(1)}, f32[2,128,256]{2,1,0:T(8,128)S(1)}, u32[]{:S(2)}, u32[]{:S(2)}) collective-permute-start(f32[2,128,256]{2,1,0:T(8,128)S(1)} %get-tuple-element.35.refs_2_), channel_id=1, source_target_pairs={{0,2},{1,3},{2,0},{3,1},{4,6},{5,7},{6,4},{7,5},{8,10},{9,11},{10,... | collective-permute-start | bytes 786440 | tf_op jit(solution)/shard_map/ppermute | solution.py:602
  22.2 1.1 collective-permute-done.3.refs_2_
  23.5 0.4 pack.1.refs_8_.b_ref.refs_2_
  24.0 0.5 collective-permute-done.4.refs_3_
  24.5 3.7 %coefficients.2 = f32[8,2,64,128]{3,2,1,0:T(8,128)} custom-call(s32[2,8]{1,0:T(2,128)S(1)} %pad_add_fusion.refs_0_, s32[2,8]{1,0:T(2,128)S(1)} %get-tuple-element.31.refs_1_, s32[2,8]{1,0:T(2,128)S(1)} %collective-permute-done.3.refs_2_, s32[2,8]{1,0:T(2,128)S(1)} %collective-permute-done.4.refs_3_, f32[16,64,128]{2,1,0:T(8,128)S(1)} %pad_maximum_fusion.refs_4_, ...), custom_call_target="tpu_custom_call" | custom-call | flops 100663296 | bytes 4194304 | tf_op jit(solution)/shard_map/coefficients/pallas_call | solution.py:170
  28.2 0.8 copy-done.1
  29.0 0.8 copy-done.3
  29.7 6.7 %all-to-all-start = ((f32[8,2,64,128]{3,2,1,0:T(8,128)}), f32[8,2,64,128]{3,2,1,0:T(8,128)S(1)}, u32[]{:S(2)}, u32[]{:S(2)}) async-start(f32[8,2,64,128]{3,2,1,0:T(8,128)} %coefficients.2), calls=%async_computation | async-start | bytes 1048576 | tf_op jit(solution)/shard_map/all_to_all | solution.py:634
  36.6 0.5 collective-permute-start.11
  37.2 0.4 collective-permute-start.13
  37.6 0.5 collective-permute-done.10.refs_5_
  38.1 0.4 collective-permute-done.11.refs_6_
  38.5 0.4 collective-permute-done.12.refs_7_
  38.9 0.4 collective-permute-done.13.refs_8_
  39.2 0.7 copy-done.26
  40.0 9.9 %operator.2 = (f32[8,128,128]{2,1,0:T(8,128)}, f32[8,128,128]{2,1,0:T(8,128)}, f32[8,128,128]{2,1,0:T(8,128)}, f32[8,128,128]{2,1,0:T(8,128)}) custom-call(s32[6,16]{1,0:T(8,128)} %bitcast.17, f32[16,6,128,128]{3,2,1,0:T(8,128)} %blocks_ref.3, f32[16,128,256]{2,1,0:T(8,128)} %bitcast.13, f32[2,128,256]{2,1,0:T(8,128)} %copy-done.14, ...), custom_call_target="tpu_custom_call" | custom-call | tf_op jit(solution)/shard_map/operator/pallas_call | solution.py:378
  50.1 0.4 collective-permute-start.15
  50.5 1.7 %collective-permute-done.14 = f32[8,128,128]{2,1,0:T(8,128)} collective-permute-done((f32[8,128,128]{2,1,0:T(8,128)}, f32[8,128,128]{2,1,0:T(8,128)}, u32[]{:S(2)}, u32[]{:S(2)}) %collective-permute-start.14) | collective-permute-done | bytes 524320 | tf_op jit(solution)/shard_map/ppermute | solution.py:597
  52.2 1.3 add.32
  53.5 0.6 collective-permute-start.16
  54.1 1.0 copy-done.13
  55.1 3.1 %far_part.2.refs_0_ = f32[8,128,128]{2,1,0:T(8,128)S(1)} custom-call(s32[2,8]{1,0:T(2,128)S(1)} %pad_add_fusion.refs_0_, s32[2,8]{1,0:T(2,128)S(1)} %get-tuple-element.31.refs_1_, s32[2,8]{1,0:T(2,128)S(1)} %collective-permute-done.3.refs_2_, s32[2,8]{1,0:T(2,128)S(1)} %collective-permute-done.4.refs_3_, f32[16,64,128]{2,1,0:T(8,128)S(1)} %pad_maximum_fusion.refs_4_, ...), custom_call_target="tpu_custom_call" | custom-call | flops 100663296 | bytes 4194304 | tf_op jit(solution)/shard_map/far_part/pallas_call | solution.py:229
  58.3 9.3 %collective-permute-done.16.refs_1_ = f32[8,128,128]{2,1,0:T(8,128)S(1)} collective-permute-done((f32[8,128,128]{2,1,0:T(8,128)S(1)}, f32[8,128,128]{2,1,0:T(8,128)S(1)}, u32[]{:S(2)}, u32[]{:S(2)}) %collective-permute-start.16) | collective-permute-done | bytes 524320 | tf_op jit(solution)/shard_map/ppermute | solution.py:602
  67.7 3.9 %collective-permute-start.17 = (f32[4,128,128]{2,1,0:T(8,128)S(1)}, f32[4,128,128]{2,1,0:T(8,128)S(1)}, u32[]{:S(2)}, u32[]{:S(2)}) collective-permute-start(f32[4,128,128]{2,1,0:T(8,128)S(1)} %get-tuple-element.45.gr_ref.refs_9_.refs_1_.refs_4_), channel_id=1, source_target_pairs={{0,4},{4,8},{8,12},{12,16},{16,20},{20,24},{24,28},{1,5},{5,9},{9,... | collective-permute-start | bytes 786440 | tf_op jit(solution)/shard_map/ppermute | solution.py:615
  71.6 1.3 collective-permute-start.18
  72.9 0.6 collective-permute-start.19
  73.5 1.5 %collective-permute-start.20 = (f32[4,128,128]{2,1,0:T(8,128)S(1)}, f32[4,128,128]{2,1,0:T(8,128)S(1)}, u32[]{:S(2)}, u32[]{:S(2)}) collective-permute-start(f32[4,128,128]{2,1,0:T(8,128)S(1)} %get-tuple-element.45.gr_ref.refs_9_.refs_1_.refs_4_), channel_id=1, source_target_pairs={{0,2},{1,3},{2,0},{3,1},{4,6},{5,7},{6,4},{7,5},{8,10},{9,11},{10,... | collective-permute-start | bytes 786440 | tf_op jit(solution)/shard_map/ppermute | solution.py:602
  75.0 2.9 %coefficients.3 = f32[8,2,64,128]{3,2,1,0:T(8,128)S(1)} custom-call(s32[2,8]{1,0:T(2,128)S(1)} %pad_add_fusion.refs_0_, s32[2,8]{1,0:T(2,128)S(1)} %get-tuple-element.31.refs_1_, s32[2,8]{1,0:T(2,128)S(1)} %collective-permute-done.3.refs_2_, s32[2,8]{1,0:T(2,128)S(1)} %collective-permute-done.4.refs_3_, f32[16,64,128]{2,1,0:T(8,128)S(1)} %pad_maximum_fusion.refs_4_, ...), custom_call_target="tpu_custom_call" | custom-call | flops 100663296 | bytes 4194304 | tf_op jit(solution)/shard_map/coefficients/pallas_call | solution.py:170
  77.9 0.8 copy-done.11
  78.7 3.5 %collective-permute-done.17.refs_8_ = f32[4,128,128]{2,1,0:T(8,128)S(1)} collective-permute-done((f32[4,128,128]{2,1,0:T(8,128)S(1)}, f32[4,128,128]{2,1,0:T(8,128)S(1)}, u32[]{:S(2)}, u32[]{:S(2)}) %collective-permute-start.17) | collective-permute-done | bytes 262176 | tf_op jit(solution)/shard_map/ppermute | solution.py:615
  82.3 3.5 %collective-permute-done.20.refs_3_ = f32[4,128,128]{2,1,0:T(8,128)S(1)} collective-permute-done((f32[4,128,128]{2,1,0:T(8,128)S(1)}, f32[4,128,128]{2,1,0:T(8,128)S(1)}, u32[]{:S(2)}, u32[]{:S(2)}) %collective-permute-start.20) | collective-permute-done | bytes 262176 | tf_op jit(solution)/shard_map/ppermute | solution.py:602
  85.8 0.5 collective-permute-start.25
  86.5 1.3 collective-permute-start.26
  87.9 9.0 %all-to-all-start.1 = ((f32[8,2,64,128]{3,2,1,0:T(8,128)}), f32[8,2,64,128]{3,2,1,0:T(8,128)S(1)}, u32[]{:S(2)}, u32[]{:S(2)}) async-start(f32[8,2,64,128]{3,2,1,0:T(8,128)} %copy-done.11), calls=%async_computation.1 | async-start | bytes 1048576 | tf_op jit(solution)/shard_map/all_to_all | solution.py:634
  98.3 0.9 collective-permute-done.24.refs_7_
  99.1 0.5 collective-permute-done.28.refs_13_
  99.6 0.4 collective-permute-done.29.refs_14_
  100.0 0.4 collective-permute-done.30.refs_15_
  100.4 10.3 %operator.3 = (f32[8,128,128]{2,1,0:T(8,128)}, f32[8,128,128]{2,1,0:T(8,128)}, f32[8,128,128]{2,1,0:T(8,128)}, f32[8,128,128]{2,1,0:T(8,128)}) custom-call(s32[6,16]{1,0:T(8,128)} %bitcast.18, f32[16,6,128,128]{3,2,1,0:T(8,128)} %blocks_ref.3, f32[4,128,128]{2,1,0:T(8,128)} %copy-done.5, f32[4,128,128]{2,1,0:T(8,128)} %copy-done.8, ...), custom_call_target="tpu_custom_call" | custom-call | tf_op jit(solution)/shard_map/operator/pallas_call | solution.py:378
  111.3 0.8 all-to-all-done.1.refs_8_
  112.1 0.8 collective-permute-done.31
  112.9 1.1 add.33
  114.0 1.4 collective-permute-start.33
  115.4 0.9 copy-done.6
  116.3 0.9 copy-done.9
  117.6 3.4 %far_part.3.refs_0_ = f32[8,128,128]{2,1,0:T(8,128)S(1)} custom-call(s32[2,8]{1,0:T(2,128)S(1)} %pad_add_fusion.refs_0_, s32[2,8]{1,0:T(2,128)S(1)} %get-tuple-element.31.refs_1_, s32[2,8]{1,0:T(2,128)S(1)} %collective-permute-done.3.refs_2_, s32[2,8]{1,0:T(2,128)S(1)} %collective-permute-done.4.refs_3_, f32[16,64,128]{2,1,0:T(8,128)S(1)} %pad_maximum_fusion.refs_4_, ...), custom_call_target="tpu_custom_call" | custom-call | flops 100663296 | bytes 4194304 | tf_op jit(solution)/shard_map/far_part/pallas_call | solution.py:229
  120.9 7.2 %collective-permute-done.33.refs_1_ = f32[8,128,128]{2,1,0:T(8,128)S(1)} collective-permute-done((f32[8,128,128]{2,1,0:T(8,128)S(1)}, f32[8,128,128]{2,1,0:T(8,128)S(1)}, u32[]{:S(2)}, u32[]{:S(2)}) %collective-permute-start.33) | collective-permute-done | bytes 524320 | tf_op jit(solution)/shard_map/ppermute | solution.py:602
  128.1 0.3 dots.1
  128.4 1.9 %collective-permute-start.34 = (f32[8,128]{1,0:T(8,128)S(1)}, f32[8,128]{1,0:T(8,128)S(1)}, u32[]{:S(2)}, u32[]{:S(2)}) collective-permute-start(f32[8,128]{1,0:T(8,128)S(1)} %get-tuple-element.56), channel_id=1, source_target_pairs={{0,4},{4,0},{8,12},{12,8},{16,20},{20,16},{24,28},{28,24},{1,5},{5... | collective-permute-start | bytes 12296 | tf_op jit(solution)/shard_map/ppermute | solution.py:626
  130.4 1.7 %collective-permute-done.34 = f32[8,128]{1,0:T(8,128)S(1)} collective-permute-done((f32[8,128]{1,0:T(8,128)S(1)}, f32[8,128]{1,0:T(8,128)S(1)}, u32[]{:S(2)}, u32[]{:S(2)}) %collective-permute-start.34) | collective-permute-done | bytes 4128 | tf_op jit(solution)/shard_map/ppermute | solution.py:626
  132.1 1.9 %collective-permute-start.35 = (f32[8,128]{1,0:T(8,128)S(1)}, f32[8,128]{1,0:T(8,128)S(1)}, u32[]{:S(2)}, u32[]{:S(2)}) collective-permute-start(f32[8,128]{1,0:T(8,128)S(1)} %add.34), channel_id=1, source_target_pairs={{0,8},{4,12},{8,0},{12,4},{16,24},{20,28},{24,16},{28,20},{1,9},{5... | collective-permute-start | bytes 12296 | tf_op jit(solution)/shard_map/ppermute | solution.py:626
  134.0 1.7 %collective-permute-done.35 = f32[8,128]{1,0:T(8,128)S(1)} collective-permute-done((f32[8,128]{1,0:T(8,128)S(1)}, f32[8,128]{1,0:T(8,128)S(1)}, u32[]{:S(2)}, u32[]{:S(2)}) %collective-permute-start.35) | collective-permute-done | bytes 4128 | tf_op jit(solution)/shard_map/ppermute | solution.py:626
  135.7 2.8 %collective-permute-start.36 = (f32[8,128]{1,0:T(8,128)S(1)}, f32[8,128]{1,0:T(8,128)S(1)}, u32[]{:S(2)}, u32[]{:S(2)}) collective-permute-start(f32[8,128]{1,0:T(8,128)S(1)} %add.35.refs_0_), channel_id=1, source_target_pairs={{0,16},{4,20},{8,24},{12,28},{16,0},{20,4},{24,8},{28,12},{1,17},{... | collective-permute-start | bytes 12296 | tf_op jit(solution)/shard_map/ppermute | solution.py:626
  138.5 1.7 %collective-permute-done.36.refs_1_ = f32[8,128]{1,0:T(8,128)S(1)} collective-permute-done((f32[8,128]{1,0:T(8,128)S(1)}, f32[8,128]{1,0:T(8,128)S(1)}, u32[]{:S(2)}, u32[]{:S(2)}) %collective-permute-start.36) | collective-permute-done | bytes 4128 | tf_op jit(solution)/shard_map/ppermute | solution.py:626
  140.2 1.4 finish.1
  (91 shorter events, 3.4 us)
Async XLA Ops:
  0.6 10.0 %copy-start.28 = (s32[1,8,1]{1,2,0:T(1,128)S(1)}, s32[1,8,1]{1,2,0:T(1,128)}, u32[]{:S(2)}) copy-start(s32[1,8,1]{1,2,0:T(1,128)} %param.10) | copy-start | bytes 100
  0.6 10.0 %copy-start.27 = (s32[1,8,1]{1,2,0:T(1,128)S(1)}, s32[1,8,1]{1,2,0:T(1,128)}, u32[]{:S(2)}) copy-start(s32[1,8,1]{1,2,0:T(1,128)} %param.11) | copy-start | bytes 100
  1.7 15.1 %collective-permute-start.5 = (f32[16,64,128]{2,1,0:T(8,128)S(1)}, f32[16,64,128]{2,1,0:T(8,128)}, u32[]{:S(2)}, u32[]{:S(2)}) collective-permute-start(f32[16,64,128]{2,1,0:T(8,128)S(1)} %pad_maximum_fusion.refs_4_), channel_id=1, source_target_pairs={{0,2},{1,3},{2,0},{3,1},{4,6},{5,7},{6,4},{7,5},{8,10},{9,11},{10,... | collective-permute-start | bytes 1572872 | tf_op jit(solution)/shard_map/ppermute | solution.py:602
  5.8 14.3 %collective-permute-start = (f32[2,128,256]{2,1,0:T(8,128)S(1)}, f32[2,128,256]{2,1,0:T(8,128)S(1)}, u32[]{:S(2)}, u32[]{:S(2)}) collective-permute-start(f32[2,128,256]{2,1,0:T(8,128)S(1)} %get-tuple-element.61), channel_id=1, source_target_pairs={{0,4},{4,8},{8,12},{12,16},{16,20},{20,24},{24,28},{1,5},{5,9},{9,... | collective-permute-start | bytes 786440 | tf_op jit(solution)/shard_map/ppermute | solution.py:615
  9.2 10.9 %collective-permute-start.1 = (f32[2,128,256]{2,1,0:T(8,128)S(1)}, f32[2,128,256]{2,1,0:T(8,128)S(1)}, u32[]{:S(2)}, u32[]{:S(2)}) collective-permute-start(f32[2,128,256]{2,1,0:T(8,128)S(1)} %get-tuple-element.60), channel_id=1, source_target_pairs={{4,0},{8,4},{12,8},{16,12},{20,16},{24,20},{28,24},{5,1},{9,5},{13... | collective-permute-start | bytes 786440 | tf_op jit(solution)/shard_map/ppermute | solution.py:619
  10.5 13.9 %collective-permute-start.6 = (f32[16,64,128]{2,1,0:T(8,128)S(1)}, f32[16,64,128]{2,1,0:T(8,128)S(1)}, u32[]{:S(2)}, u32[]{:S(2)}) collective-permute-start(f32[16,64,128]{2,1,0:T(8,128)S(1)} %pad_maximum_fusion.refs_4_), channel_id=1, source_target_pairs={{0,1},{1,0},{2,3},{3,2},{4,5},{5,4},{6,7},{7,6},{8,9},{9,8},{10,11... | collective-permute-start | bytes 1572872 | tf_op jit(solution)/shard_map/ppermute | solution.py:597
  10.7 12.9 %copy-start = (f32[2048,256]{1,0:T(8,128)S(1)}, f32[2048,256]{1,0:T(8,128)}, u32[]{:S(2)}) copy-start(f32[2048,256]{1,0:T(8,128)} %param.7) | copy-start | bytes 6291460
  10.7 6.1 %collective-permute-start.2 = (s32[2,8]{1,0:T(2,128)S(1)}, s32[2,8]{1,0:T(2,128)S(1)}, u32[]{:S(2)}, u32[]{:S(2)}) collective-permute-start(s32[2,8]{1,0:T(2,128)S(1)} %pad_add_fusion.refs_0_), channel_id=1, source_target_pairs={{0,2},{1,3},{2,0},{3,1},{4,6},{5,7},{6,4},{7,5},{8,10},{9,11},{10,... | collective-permute-start | bytes 200 | tf_op jit(solution)/shard_map/ppermute | solution.py:602
  16.8 7.7 %collective-permute-start.7 = (f32[16,64,128]{2,1,0:T(8,128)}, f32[16,64,128]{2,1,0:T(8,128)S(1)}, u32[]{:S(2)}, u32[]{:S(2)}) collective-permute-start(f32[16,64,128]{2,1,0:T(8,128)} %collective-permute-done.5.refs_5_), channel_id=1, source_target_pairs={{0,1},{1,0},{2,3},{3,2},{4,5},{5,4},{6,7},{7,6},{8,9},{9,8},{10,11... | collective-permute-start | bytes 1572872 | tf_op jit(solution)/shard_map/ppermute | solution.py:597
  20.1 16.4 %copy-start.14 = (f32[2,128,256]{2,1,0:T(8,128)}, f32[2,128,256]{2,1,0:T(8,128)S(1)}, u32[]{:S(2)}) copy-start(f32[2,128,256]{2,1,0:T(8,128)S(1)} %get-tuple-element.34.refs_1_) | copy-start | bytes 786436
  20.1 16.5 %copy-start.15 = (f32[2,128,256]{2,1,0:T(8,128)}, f32[2,128,256]{2,1,0:T(8,128)S(1)}, u32[]{:S(2)}) copy-start(f32[2,128,256]{2,1,0:T(8,128)S(1)} %get-tuple-element.35.refs_2_) | copy-start | bytes 786436
  20.1 16.3 %collective-permute-start.8 = (f32[2,128,256]{2,1,0:T(8,128)S(1)}, f32[2,128,256]{2,1,0:T(8,128)S(1)}, u32[]{:S(2)}, u32[]{:S(2)}) collective-permute-start(f32[2,128,256]{2,1,0:T(8,128)S(1)} %get-tuple-element.34.refs_1_), channel_id=1, source_target_pairs={{0,2},{1,3},{2,0},{3,1},{4,6},{5,7},{6,4},{7,5},{8,10},{9,11},{10,... | collective-permute-start | bytes 786440 | tf_op jit(solution)/shard_map/ppermute | solution.py:602
  20.7 15.8 %collective-permute-start.9 = (f32[2,128,256]{2,1,0:T(8,128)S(1)}, f32[2,128,256]{2,1,0:T(8,128)S(1)}, u32[]{:S(2)}, u32[]{:S(2)}) collective-permute-start(f32[2,128,256]{2,1,0:T(8,128)S(1)} %get-tuple-element.35.refs_2_), channel_id=1, source_target_pairs={{0,2},{1,3},{2,0},{3,1},{4,6},{5,7},{6,4},{7,5},{8,10},{9,11},{10,... | collective-permute-start | bytes 786440 | tf_op jit(solution)/shard_map/ppermute | solution.py:602
  22.2 1.1 collective-permute-start.3
  23.4 1.1 collective-permute-start.4
  29.7 22.5 %all-to-all-start = ((f32[8,2,64,128]{3,2,1,0:T(8,128)}), f32[8,2,64,128]{3,2,1,0:T(8,128)S(1)}, u32[]{:S(2)}, u32[]{:S(2)}) async-start(f32[8,2,64,128]{3,2,1,0:T(8,128)} %coefficients.2), calls=%async_computation | async-start | bytes 1048576 | tf_op jit(solution)/shard_map/all_to_all | solution.py:634
  36.5 3.5 %copy-start.19 = (f32[2,128,256]{2,1,0:T(8,128)}, f32[2,128,256]{2,1,0:T(8,128)S(1)}, u32[]{:S(2)}) copy-start(f32[2,128,256]{2,1,0:T(8,128)S(1)} %collective-permute-done.8.refs_3_) | copy-start | bytes 786436
  36.5 3.4 %copy-start.20 = (f32[2,128,256]{2,1,0:T(8,128)}, f32[2,128,256]{2,1,0:T(8,128)S(1)}, u32[]{:S(2)}) copy-start(f32[2,128,256]{2,1,0:T(8,128)S(1)} %collective-permute-done.9.refs_4_) | copy-start | bytes 786436
  36.5 1.6 %collective-permute-start.10 = (f32[2,128,256]{2,1,0:T(8,128)S(1)}, f32[2,128,256]{2,1,0:T(8,128)S(1)}, u32[]{:S(2)}, u32[]{:S(2)}) collective-permute-start(f32[2,128,256]{2,1,0:T(8,128)S(1)} %get-tuple-element.34.refs_1_), channel_id=1, source_target_pairs={{0,1},{1,0},{2,3},{3,2},{4,5},{5,4},{6,7},{7,6},{8,9},{9,8},{10,11... | collective-permute-start | bytes 786440 | tf_op jit(solution)/shard_map/ppermute | solution.py:597
  36.6 1.9 %collective-permute-start.11 = (f32[2,128,256]{2,1,0:T(8,128)S(1)}, f32[2,128,256]{2,1,0:T(8,128)S(1)}, u32[]{:S(2)}, u32[]{:S(2)}) collective-permute-start(f32[2,128,256]{2,1,0:T(8,128)S(1)} %get-tuple-element.35.refs_2_), channel_id=1, source_target_pairs={{0,1},{1,0},{2,3},{3,2},{4,5},{5,4},{6,7},{7,6},{8,9},{9,8},{10,11... | collective-permute-start | bytes 786440 | tf_op jit(solution)/shard_map/ppermute | solution.py:597
  37.1 1.8 %collective-permute-start.12 = (f32[2,128,256]{2,1,0:T(8,128)S(1)}, f32[2,128,256]{2,1,0:T(8,128)S(1)}, u32[]{:S(2)}, u32[]{:S(2)}) collective-permute-start(f32[2,128,256]{2,1,0:T(8,128)S(1)} %collective-permute-done.8.refs_3_), channel_id=1, source_target_pairs={{0,1},{1,0},{2,3},{3,2},{4,5},{5,4},{6,7},{7,6},{8,9},{9,8},{10,11... | collective-permute-start | bytes 786440 | tf_op jit(solution)/shard_map/ppermute | solution.py:597
  37.2 2.1 %collective-permute-start.13 = (f32[2,128,256]{2,1,0:T(8,128)S(1)}, f32[2,128,256]{2,1,0:T(8,128)S(1)}, u32[]{:S(2)}, u32[]{:S(2)}) collective-permute-start(f32[2,128,256]{2,1,0:T(8,128)S(1)} %collective-permute-done.9.refs_4_), channel_id=1, source_target_pairs={{0,1},{1,0},{2,3},{3,2},{4,5},{5,4},{6,7},{7,6},{8,9},{9,8},{10,11... | collective-permute-start | bytes 786440 | tf_op jit(solution)/shard_map/ppermute | solution.py:597
  38.1 1.8 %copy-start.23 = (f32[2,128,256]{2,1,0:T(8,128)}, f32[2,128,256]{2,1,0:T(8,128)S(1)}, u32[]{:S(2)}) copy-start(f32[2,128,256]{2,1,0:T(8,128)S(1)} %collective-permute-done.10.refs_5_) | copy-start | bytes 786436
  38.5 1.5 %copy-start.24 = (f32[2,128,256]{2,1,0:T(8,128)}, f32[2,128,256]{2,1,0:T(8,128)S(1)}, u32[]{:S(2)}) copy-start(f32[2,128,256]{2,1,0:T(8,128)S(1)} %collective-permute-done.11.refs_6_) | copy-start | bytes 786436
  38.9 1.1 copy-start.25
  39.9 14.1 %copy-start.2 = (f32[16,64,128]{2,1,0:T(8,128)S(1)}, f32[16,64,128]{2,1,0:T(8,128)}, u32[]{:S(2)}) copy-start(f32[16,64,128]{2,1,0:T(8,128)} %copy-done.1) | copy-start | bytes 1572868
  40.0 14.1 %copy-start.4 = (f32[16,64,128]{2,1,0:T(8,128)S(1)}, f32[16,64,128]{2,1,0:T(8,128)}, u32[]{:S(2)}) copy-start(f32[16,64,128]{2,1,0:T(8,128)} %copy-done.3) | copy-start | bytes 1572868
  49.9 2.3 %collective-permute-start.14 = (f32[8,128,128]{2,1,0:T(8,128)}, f32[8,128,128]{2,1,0:T(8,128)}, u32[]{:S(2)}, u32[]{:S(2)}) collective-permute-start(f32[8,128,128]{2,1,0:T(8,128)} %get-tuple-element.38), channel_id=1, source_target_pairs={{0,1},{1,0},{2,3},{3,2},{4,5},{5,4},{6,7},{7,6},{8,9},{9,8},{10,11... | collective-permute-start | bytes 1572872 | tf_op jit(solution)/shard_map/ppermute | solution.py:597
  50.1 4.0 %collective-permute-start.15 = (f32[8,128,128]{2,1,0:T(8,128)}, f32[8,128,128]{2,1,0:T(8,128)S(1)}, u32[]{:S(2)}, u32[]{:S(2)}) collective-permute-start(f32[8,128,128]{2,1,0:T(8,128)} %get-tuple-element.41), channel_id=1, source_target_pairs={{0,1},{1,0},{2,3},{3,2},{4,5},{5,4},{6,7},{7,6},{8,9},{9,8},{10,11... | collective-permute-start | bytes 1572872 | tf_op jit(solution)/shard_map/ppermute | solution.py:597
  53.5 14.0 %collective-permute-start.16 = (f32[8,128,128]{2,1,0:T(8,128)S(1)}, f32[8,128,128]{2,1,0:T(8,128)S(1)}, u32[]{:S(2)}, u32[]{:S(2)}) collective-permute-start(f32[8,128,128]{2,1,0:T(8,128)S(1)} %add.32), channel_id=1, source_target_pairs={{0,2},{1,3},{2,0},{3,1},{4,6},{5,7},{6,4},{7,5},{8,10},{9,11},{10,... | collective-permute-start | bytes 1572872 | tf_op jit(solution)/shard_map/ppermute | solution.py:602
  54.1 1.0 copy-start.13
  67.6 32.7 %copy-start.5 = (f32[4,128,128]{2,1,0:T(8,128)}, f32[4,128,128]{2,1,0:T(8,128)S(1)}, u32[]{:S(2)}) copy-start(f32[4,128,128]{2,1,0:T(8,128)S(1)} %get-tuple-element.44.gl_ref.refs_8_.refs_0_.refs_3_) | copy-start | bytes 786436
  67.6 32.7 %copy-start.8 = (f32[4,128,128]{2,1,0:T(8,128)}, f32[4,128,128]{2,1,0:T(8,128)S(1)}, u32[]{:S(2)}) copy-start(f32[4,128,128]{2,1,0:T(8,128)S(1)} %get-tuple-element.45.gr_ref.refs_9_.refs_1_.refs_4_) | copy-start | bytes 786436
  67.7 14.6 %collective-permute-start.17 = (f32[4,128,128]{2,1,0:T(8,128)S(1)}, f32[4,128,128]{2,1,0:T(8,128)S(1)}, u32[]{:S(2)}, u32[]{:S(2)}) collective-permute-start(f32[4,128,128]{2,1,0:T(8,128)S(1)} %get-tuple-element.45.gr_ref.refs_9_.refs_1_.refs_4_), channel_id=1, source_target_pairs={{0,4},{4,8},{8,12},{12,16},{16,20},{20,24},{24,28},{1,5},{5,9},{9,... | collective-permute-start | bytes 786440 | tf_op jit(solution)/shard_map/ppermute | solution.py:615
  71.6 10.6 %collective-permute-start.18 = (f32[4,128,128]{2,1,0:T(8,128)S(1)}, f32[4,128,128]{2,1,0:T(8,128)S(1)}, u32[]{:S(2)}, u32[]{:S(2)}) collective-permute-start(f32[4,128,128]{2,1,0:T(8,128)S(1)} %get-tuple-element.44.gl_ref.refs_8_.refs_0_.refs_3_), channel_id=1, source_target_pairs={{4,0},{8,4},{12,8},{16,12},{20,16},{24,20},{28,24},{5,1},{9,5},{13... | collective-permute-start | bytes 786440 | tf_op jit(solution)/shard_map/ppermute | solution.py:619
  72.9 9.4 %collective-permute-start.19 = (f32[4,128,128]{2,1,0:T(8,128)S(1)}, f32[4,128,128]{2,1,0:T(8,128)}, u32[]{:S(2)}, u32[]{:S(2)}) collective-permute-start(f32[4,128,128]{2,1,0:T(8,128)S(1)} %get-tuple-element.44.gl_ref.refs_8_.refs_0_.refs_3_), channel_id=1, source_target_pairs={{0,2},{1,3},{2,0},{3,1},{4,6},{5,7},{6,4},{7,5},{8,10},{9,11},{10,... | collective-permute-start | bytes 786440 | tf_op jit(solution)/shard_map/ppermute | solution.py:602
  73.5 12.3 %collective-permute-start.20 = (f32[4,128,128]{2,1,0:T(8,128)S(1)}, f32[4,128,128]{2,1,0:T(8,128)S(1)}, u32[]{:S(2)}, u32[]{:S(2)}) collective-permute-start(f32[4,128,128]{2,1,0:T(8,128)S(1)} %get-tuple-element.45.gr_ref.refs_9_.refs_1_.refs_4_), channel_id=1, source_target_pairs={{0,2},{1,3},{2,0},{3,1},{4,6},{5,7},{6,4},{7,5},{8,10},{9,11},{10,... | collective-permute-start | bytes 786440 | tf_op jit(solution)/shard_map/ppermute | solution.py:602
  75.0 21.9 %collective-permute-start.21 = (f32[4,128,128]{2,1,0:T(8,128)S(1)}, f32[4,128,128]{2,1,0:T(8,128)}, u32[]{:S(2)}, u32[]{:S(2)}) collective-permute-start(f32[4,128,128]{2,1,0:T(8,128)S(1)} %get-tuple-element.44.gl_ref.refs_8_.refs_0_.refs_3_), channel_id=1, source_target_pairs={{0,1},{1,0},{2,3},{3,2},{4,5},{5,4},{6,7},{7,6},{8,9},{9,8},{10,11... | collective-permute-start | bytes 786440 | tf_op jit(solution)/shard_map/ppermute | solution.py:597
  77.9 0.8 copy-start.11
  82.2 18.2 %copy-start.16 = (f32[4,128,128]{2,1,0:T(8,128)}, f32[4,128,128]{2,1,0:T(8,128)S(1)}, u32[]{:S(2)}) copy-start(f32[4,128,128]{2,1,0:T(8,128)S(1)} %collective-permute-done.17.refs_8_) | copy-start | bytes 786436
  82.2 15.0 %collective-permute-start.22 = (f32[4,128,128]{2,1,0:T(8,128)S(1)}, f32[4,128,128]{2,1,0:T(8,128)}, u32[]{:S(2)}, u32[]{:S(2)}) collective-permute-start(f32[4,128,128]{2,1,0:T(8,128)S(1)} %get-tuple-element.45.gr_ref.refs_9_.refs_1_.refs_4_), channel_id=1, source_target_pairs={{0,1},{1,0},{2,3},{3,2},{4,5},{5,4},{6,7},{7,6},{8,9},{9,8},{10,11... | collective-permute-start | bytes 786440 | tf_op jit(solution)/shard_map/ppermute | solution.py:597
  82.2 3.6 %copy-start.17 = (f32[4,128,128]{2,1,0:T(8,128)}, f32[4,128,128]{2,1,0:T(8,128)S(1)}, u32[]{:S(2)}) copy-start(f32[4,128,128]{2,1,0:T(8,128)S(1)} %collective-permute-done.18.refs_9_) | copy-start | bytes 786436
  85.8 11.7 %collective-permute-start.25 = (f32[4,128,128]{2,1,0:T(8,128)S(1)}, f32[4,128,128]{2,1,0:T(8,128)}, u32[]{:S(2)}, u32[]{:S(2)}) collective-permute-start(f32[4,128,128]{2,1,0:T(8,128)S(1)} %collective-permute-done.17.refs_8_), channel_id=1, source_target_pairs={{0,2},{1,3},{2,0},{3,1},{4,6},{5,7},{6,4},{7,5},{8,10},{9,11},{10,... | collective-permute-start | bytes 786440 | tf_op jit(solution)/shard_map/ppermute | solution.py:602
  86.5 11.2 %collective-permute-start.26 = (f32[4,128,128]{2,1,0:T(8,128)}, f32[4,128,128]{2,1,0:T(8,128)}, u32[]{:S(2)}, u32[]{:S(2)}) collective-permute-start(f32[4,128,128]{2,1,0:T(8,128)} %collective-permute-done.19.refs_2_), channel_id=1, source_target_pairs={{4,0},{8,4},{12,8},{16,12},{20,16},{24,20},{28,24},{5,1},{9,5},{13... | collective-permute-start | bytes 786440 | tf_op jit(solution)/shard_map/ppermute | solution.py:619
  87.8 10.2 %collective-permute-start.23 = (f32[4,128,128]{2,1,0:T(8,128)}, f32[4,128,128]{2,1,0:T(8,128)}, u32[]{:S(2)}, u32[]{:S(2)}) collective-permute-start(f32[4,128,128]{2,1,0:T(8,128)} %collective-permute-done.19.refs_2_), channel_id=1, source_target_pairs={{0,1},{1,0},{2,3},{3,2},{4,5},{5,4},{6,7},{7,6},{8,9},{9,8},{10,11... | collective-permute-start | bytes 786440 | tf_op jit(solution)/shard_map/ppermute | solution.py:597
  87.9 24.2 %all-to-all-start.1 = ((f32[8,2,64,128]{3,2,1,0:T(8,128)}), f32[8,2,64,128]{3,2,1,0:T(8,128)S(1)}, u32[]{:S(2)}, u32[]{:S(2)}) async-start(f32[8,2,64,128]{3,2,1,0:T(8,128)} %copy-done.11), calls=%async_computation.1 | async-start | bytes 1048576 | tf_op jit(solution)/shard_map/all_to_all | solution.py:634
  96.9 2.2 %collective-permute-start.27 = (f32[4,128,128]{2,1,0:T(8,128)S(1)}, f32[4,128,128]{2,1,0:T(8,128)S(1)}, u32[]{:S(2)}, u32[]{:S(2)}) collective-permute-start(f32[4,128,128]{2,1,0:T(8,128)S(1)} %collective-permute-done.17.refs_8_), channel_id=1, source_target_pairs={{0,1},{1,0},{2,3},{3,2},{4,5},{5,4},{6,7},{7,6},{8,9},{9,8},{10,11... | collective-permute-start | bytes 786440 | tf_op jit(solution)/shard_map/ppermute | solution.py:597
  97.2 1.9 %collective-permute-start.24 = (f32[4,128,128]{2,1,0:T(8,128)}, f32[4,128,128]{2,1,0:T(8,128)S(1)}, u32[]{:S(2)}, u32[]{:S(2)}) collective-permute-start(f32[4,128,128]{2,1,0:T(8,128)} %copy-done.18), channel_id=1, source_target_pairs={{0,1},{1,0},{2,3},{3,2},{4,5},{5,4},{6,7},{7,6},{8,9},{9,8},{10,11... | collective-permute-start | bytes 786440 | tf_op jit(solution)/shard_map/ppermute | solution.py:597
  97.5 2.1 %collective-permute-start.28 = (f32[4,128,128]{2,1,0:T(8,128)}, f32[4,128,128]{2,1,0:T(8,128)}, u32[]{:S(2)}, u32[]{:S(2)}) collective-permute-start(f32[4,128,128]{2,1,0:T(8,128)} %copy-done.17), channel_id=1, source_target_pairs={{0,1},{1,0},{2,3},{3,2},{4,5},{5,4},{6,7},{7,6},{8,9},{9,8},{10,11... | collective-permute-start | bytes 786440 | tf_op jit(solution)/shard_map/ppermute | solution.py:597
  97.7 2.3 %collective-permute-start.29 = (f32[4,128,128]{2,1,0:T(8,128)}, f32[4,128,128]{2,1,0:T(8,128)}, u32[]{:S(2)}, u32[]{:S(2)}) collective-permute-start(f32[4,128,128]{2,1,0:T(8,128)} %collective-permute-done.25.refs_10_), channel_id=1, source_target_pairs={{0,1},{1,0},{2,3},{3,2},{4,5},{5,4},{6,7},{7,6},{8,9},{9,8},{10,11... | collective-permute-start | bytes 786440 | tf_op jit(solution)/shard_map/ppermute | solution.py:597
  98.0 2.3 %collective-permute-start.30 = (f32[4,128,128]{2,1,0:T(8,128)}, f32[4,128,128]{2,1,0:T(8,128)}, u32[]{:S(2)}, u32[]{:S(2)}) collective-permute-start(f32[4,128,128]{2,1,0:T(8,128)} %collective-permute-done.26.refs_11_), channel_id=1, source_target_pairs={{0,1},{1,0},{2,3},{3,2},{4,5},{5,4},{6,7},{7,6},{8,9},{9,8},{10,11... | collective-permute-start | bytes 786440 | tf_op jit(solution)/shard_map/ppermute | solution.py:597
  99.1 1.3 copy-start.22
  99.1 1.3 copy-start.21
  110.7 2.2 %collective-permute-start.31 = (f32[8,128,128]{2,1,0:T(8,128)}, f32[8,128,128]{2,1,0:T(8,128)S(1)}, u32[]{:S(2)}, u32[]{:S(2)}) collective-permute-start(f32[8,128,128]{2,1,0:T(8,128)} %get-tuple-element.50), channel_id=1, source_target_pairs={{0,1},{1,0},{2,3},{3,2},{4,5},{5,4},{6,7},{7,6},{8,9},{9,8},{10,11... | collective-permute-start | bytes 1572872 | tf_op jit(solution)/shard_map/ppermute | solution.py:597
  111.0 6.5 %collective-permute-start.32 = (f32[8,128,128]{2,1,0:T(8,128)}, f32[8,128,128]{2,1,0:T(8,128)}, u32[]{:S(2)}, u32[]{:S(2)}) collective-permute-start(f32[8,128,128]{2,1,0:T(8,128)} %get-tuple-element.53), channel_id=1, source_target_pairs={{0,1},{1,0},{2,3},{3,2},{4,5},{5,4},{6,7},{7,6},{8,9},{9,8},{10,11... | collective-permute-start | bytes 1572872 | tf_op jit(solution)/shard_map/ppermute | solution.py:597
  112.1 5.5 %copy-start.12 = (f32[8,128,128]{2,1,0:T(8,128)S(1)}, f32[8,128,128]{2,1,0:T(8,128)}, u32[]{:S(2)}) copy-start(f32[8,128,128]{2,1,0:T(8,128)} %get-tuple-element.52.refs_9_) | copy-start | bytes 1572868
  114.0 14.1 %collective-permute-start.33 = (f32[8,128,128]{2,1,0:T(8,128)S(1)}, f32[8,128,128]{2,1,0:T(8,128)S(1)}, u32[]{:S(2)}, u32[]{:S(2)}) collective-permute-start(f32[8,128,128]{2,1,0:T(8,128)S(1)} %add.33), channel_id=1, source_target_pairs={{0,2},{1,3},{2,0},{3,1},{4,6},{5,7},{6,4},{7,5},{8,10},{9,11},{10,... | collective-permute-start | bytes 1572872 | tf_op jit(solution)/shard_map/ppermute | solution.py:602
  115.4 0.9 copy-start.6
  116.3 0.9 copy-start.9
  117.6 10.6 %copy-start.7 = (f32[4,128,128]{2,1,0:T(8,128)S(1)}, f32[4,128,128]{2,1,0:T(8,128)}, u32[]{:S(2)}) copy-start(f32[4,128,128]{2,1,0:T(8,128)} %copy-done.5) | copy-start | bytes 786436
  117.6 10.6 %copy-start.10 = (f32[4,128,128]{2,1,0:T(8,128)S(1)}, f32[4,128,128]{2,1,0:T(8,128)}, u32[]{:S(2)}) copy-start(f32[4,128,128]{2,1,0:T(8,128)} %copy-done.8) | copy-start | bytes 786436
  128.4 3.7 %collective-permute-start.34 = (f32[8,128]{1,0:T(8,128)S(1)}, f32[8,128]{1,0:T(8,128)S(1)}, u32[]{:S(2)}, u32[]{:S(2)}) collective-permute-start(f32[8,128]{1,0:T(8,128)S(1)} %get-tuple-element.56), channel_id=1, source_target_pairs={{0,4},{4,0},{8,12},{12,8},{16,20},{20,16},{24,28},{28,24},{1,5},{5... | collective-permute-start | bytes 12296 | tf_op jit(solution)/shard_map/ppermute | solution.py:626
  132.1 3.6 %collective-permute-start.35 = (f32[8,128]{1,0:T(8,128)S(1)}, f32[8,128]{1,0:T(8,128)S(1)}, u32[]{:S(2)}, u32[]{:S(2)}) collective-permute-start(f32[8,128]{1,0:T(8,128)S(1)} %add.34), channel_id=1, source_target_pairs={{0,8},{4,12},{8,0},{12,4},{16,24},{20,28},{24,16},{28,20},{1,9},{5... | collective-permute-start | bytes 12296 | tf_op jit(solution)/shard_map/ppermute | solution.py:626
  135.7 4.5 %collective-permute-start.36 = (f32[8,128]{1,0:T(8,128)S(1)}, f32[8,128]{1,0:T(8,128)S(1)}, u32[]{:S(2)}, u32[]{:S(2)}) collective-permute-start(f32[8,128]{1,0:T(8,128)S(1)} %add.35.refs_0_), channel_id=1, source_target_pairs={{0,16},{4,20},{8,24},{12,28},{16,0},{20,4},{24,8},{28,12},{1,17},{... | collective-permute-start | bytes 12296 | tf_op jit(solution)/shard_map/ppermute | solution.py:626
  (4 other events, 3.0 us)

commit v6 on v5

--- a/solution.py
+++ b/solution.py
@@ -398,33 +398,30 @@
     return outs[:ys], outs[ys:]
 
 
-def add_kernel(n, *refs):
-    parts, outs, (first, second, sems) = refs[:n], refs[n : n + 2], refs[n + 2 :]
-    per = first.shape[0]
-    copies = []
-    for half, held in enumerate((first, second)):
-        rows = slice(half * per, (half + 1) * per)
-        total = parts[0][rows]
-        for part in parts[1:]:
-            total = total + part[rows]
-        held[...] = total
-        copies += begin([(held, outs[half])], sems, half)
-    for copy in copies:
-        copy.wait()
-
-
-def add_halves(parts):
-    shape = parts[0].shape
-    half = jax.ShapeDtypeStruct((shape[0] // 2,) + shape[1:], F32)
+def add_kernel(half, n_whole, *refs):
+    parts, (out, held, sems) = refs[:-3], refs[-3:]
+    per = held.shape[0]
+    total = parts[0][half * per : (half + 1) * per]
+    for part in parts[1:n_whole]:
+        total = total + part[half * per : (half + 1) * per]
+    for part in parts[n_whole:]:
+        total = total + part[...]
+    held[...] = total
+    fetch([(held, out)], sems)
+
+
+def add_half(half, wholes, halves):
+    out = jax.ShapeDtypeStruct(halves[0].shape, F32)
+    parts = list(wholes) + list(halves)
     return pl.pallas_call(
-        functools.partial(add_kernel, len(parts)),
-        out_shape=[half] * 2,
+        functools.partial(add_kernel, half, len(wholes)),
+        out_shape=out,
         in_specs=[VMEM_SPEC] * len(parts),
-        out_specs=[ANY_SPEC] * 2,
-        scratch_shapes=buffers([half] * 2) + [pltpu.SemaphoreType.DMA((2,))],
+        out_specs=ANY_SPEC,
+        scratch_shapes=buffers([out]) + [pltpu.SemaphoreType.DMA((1,))],
         compiler_params=PARAMS,
-        cost_estimate=cost(4 * parts[0].size, 20 * parts[0].size),
-        name="add_halves",
+        cost_estimate=cost(0, 0),
+        name="add_half",
     )(*parts)
 
 
@@ -634,11 +631,14 @@
     return lax.all_to_all(coef, "rows", split_axis=0, concat_axis=0, tiled=True)
 
 
-def sum_far(keeps, sends, coef):
-    others = []
-    for shift in range(1, len(keeps)):
-        got, coef = lax.optimization_barrier((swap_cores(sends[shift]), coef))
-        others.append(along_y(keeps[shift] + got, shift))
+def sum_far(keeps, sends, coef, pieces):
+    others = [[] for _ in range(pieces)]
+    size = keeps[0].shape[0] // pieces
+    for turn in range(1, len(keeps)):
+        got, coef = lax.optimization_barrier((swap_cores(sends[turn]), coef))
+        for n in range(pieces):
+            rows = slice(n * size, (n + 1) * size)
+            others[n].append(along_y(keeps[turn][rows] + got[rows], turn))
     return [keeps[0], swap_cores(sends[0])], others, coef
 
 
@@ -674,8 +674,9 @@
     pieces += [swap_cores(item) for item in pieces]
     coef = exchange(coef)
     keeps, sends = operator(near_blocks, [own] + pieces, cols, far_size, per, width, False)
-    terms, others, coef = sum_far(keeps, sends, coef)
-    g_own = add_halves([far_part(meta, factors, coef, terms, far_size, per)] + others)
+    terms, others, coef = sum_far(keeps, sends, coef, 2)
+    base = far_part(meta, factors, coef, terms, far_size, per)
+    g_own = [add_half(half, [base], others[half]) for half in range(2)]
 
     head, tail = g_own
     from_left, from_right = to_next(tail), to_previous(head)
@@ -692,7 +693,7 @@
     halos += [swap_cores(item) for item in halos]
     coef = exchange(coef)
     keeps, sends = operator(near_blocks, owns + halos, cols, far_size, per, width, True)
-    terms, others, coef = sum_far(keeps, sends, coef)
+    terms, (others,), coef = sum_far(keeps, sends, coef, 1)
     base = far_part(meta, factors, coef, terms, far_size, per)
     early = early_dots(b_own, g_own, packs)
     part_dots, image = dots(b_own, g_own, early, [base] + others, packs)

time: 143 us -> 133 us (0.930)
  waiting for transfers between devices: 46.4 us -> 37.4 us
    ppermute x9 -> x10, waiting for transfers between devices: 25.6 us -> 18.5 us  [along_y(): lax.ppermute(value, 'far', [(i, (i + CORES * shift) % size) for i in rang...]
    ppermute x2, waiting for transfers between devices: 6.84 us -> 3.31 us  [to_next(): lax.ppermute(value, 'rows', [(i, i + 1) for i in range(lax.axis_size('row...]
    ppermute x3, waiting for transfers between devices: 0.01 us -> 1.64 us  [to_previous(): lax.ppermute(value, 'rows', [(i + 1, i) for i in range(lax.axis_size('row...]
    ppermute x9 -> x10, starting transfers between devices: 10.3 us -> 11.8 us  [along_y(): lax.ppermute(value, 'far', [(i, (i + CORES * shift) % size) for i in rang...]
  transfers between devices with their start and end apart: 39 -> 40, of which waited for: 23 -> 24; matrix products, arithmetic and copies ran while one was open for 2% -> 3% of each run, Pallas kernels for 24% -> 25%
where the time goes in v6:
time: 133 us
  starting transfers between devices  48.4 us (36%)
  waiting for transfers between devices  37.4 us (28%)
  Pallas kernels  35.1 us (26%)
  local copies, waits for them, and re-layouts  7.16 us (5%)
  other arithmetic  3.43 us (3%)
    pallas_call x2, Pallas kernels, operator(): pl.pallas_call(functools.partial(operator_kernel, far_size, per, last, le...  19.5 us
    ppermute x10, waiting for transfers between devices, along_y(): lax.ppermute(value, 'far', [(i, (i + CORES * shift) % size) for i in rang...  18.5 us
    all_to_all x2, starting transfers between devices, exchange(): return lax.all_to_all(coef, 'rows', split_axis=0, concat_axis=0, tiled=True)  14.4 us
    ppermute x10, starting transfers between devices, along_y(): lax.ppermute(value, 'far', [(i, (i + CORES * shift) % size) for i in rang...  11.8 us
    ppermute x20, waiting for transfers between devices, swap_cores(): return lax.ppermute(value, 'far', [(i, i ^ 1) for i in range(size)])  7.64 us
    ppermute x2, starting transfers between devices, to_next(): lax.ppermute(value, 'rows', [(i, i + 1) for i in range(lax.axis_size('row...  7.35 us
    ppermute x3, starting transfers between devices, sum_rows(): other = lax.ppermute(value, 'rows', [(i, i ^ step) for i in range(size)])  6.57 us
    pallas_call x2, Pallas kernels, coefficients(): pl.pallas_call(functools.partial(coefficient_kernel, far_size, len(fields...  6.54 us
  transfers between devices with their start and end apart: 40, of which 24 were waited for; matrix products, arithmetic and copies ran while one was open for 3% of the time, Pallas kernels for 25%

profile of v6, /device:TPU:0, one launch (start us, length us, event | category | flops | bytes accessed | tf_op | source)
XLA Modules:
  0.0 132.7 jit_solution(6850760647610272222)
XLA Ops:
  0.7 1.1 pad_maximum_fusion.refs_4_
  1.7 3.0 %collective-permute-start.5 = (f32[16,64,128]{2,1,0:T(8,128)S(1)}, f32[16,64,128]{2,1,0:T(8,128)}, u32[]{:S(2)}, u32[]{:S(2)}) collective-permute-start(f32[16,64,128]{2,1,0:T(8,128)S(1)} %pad_maximum_fusion.refs_4_), channel_id=1, source_target_pairs={{0,2},{1,3},{2,0},{3,1},{4,6},{5,7},{6,4},{7,5},{8,10},{9,11},{10,... | collective-permute-start | bytes 1572872 | tf_op jit(solution)/shard_map/ppermute | solution.py:599
  4.8 1.1 constant_dynamic-slice_fusion
  5.8 3.4 %collective-permute-start = (f32[2,128,256]{2,1,0:T(8,128)S(1)}, f32[2,128,256]{2,1,0:T(8,128)S(1)}, u32[]{:S(2)}, u32[]{:S(2)}) collective-permute-start(f32[2,128,256]{2,1,0:T(8,128)S(1)} %get-tuple-element.57), channel_id=1, source_target_pairs={{0,4},{4,8},{8,12},{12,16},{16,20},{20,24},{24,28},{1,5},{5,9},{9,... | collective-permute-start | bytes 786440 | tf_op jit(solution)/shard_map/ppermute | solution.py:612
  9.2 1.3 collective-permute-start.1
  10.7 0.6 collective-permute-start.2
  11.2 5.6 %collective-permute-done.5.refs_5_ = f32[16,64,128]{2,1,0:T(8,128)} collective-permute-done((f32[16,64,128]{2,1,0:T(8,128)S(1)}, f32[16,64,128]{2,1,0:T(8,128)}, u32[]{:S(2)}, u32[]{:S(2)}) %collective-permute-start.5) | collective-permute-done | bytes 524320 | tf_op jit(solution)/shard_map/ppermute | solution.py:599
  16.8 3.3 %collective-permute-done.refs_0_ = f32[2,128,256]{2,1,0:T(8,128)S(1)} collective-permute-done((f32[2,128,256]{2,1,0:T(8,128)S(1)}, f32[2,128,256]{2,1,0:T(8,128)S(1)}, u32[]{:S(2)}, u32[]{:S(2)}) %collective-permute-start) | collective-permute-done | bytes 262176 | tf_op jit(solution)/shard_map/ppermute | solution.py:612
  20.1 0.6 collective-permute-start.8
  20.7 1.5 %collective-permute-start.9 = (f32[2,128,256]{2,1,0:T(8,128)S(1)}, f32[2,128,256]{2,1,0:T(8,128)S(1)}, u32[]{:S(2)}, u32[]{:S(2)}) collective-permute-start(f32[2,128,256]{2,1,0:T(8,128)S(1)} %get-tuple-element.33.refs_2_), channel_id=1, source_target_pairs={{0,2},{1,3},{2,0},{3,1},{4,6},{5,7},{6,4},{7,5},{8,10},{9,11},{10,... | collective-permute-start | bytes 786440 | tf_op jit(solution)/shard_map/ppermute | solution.py:599
  22.2 1.1 collective-permute-done.3.refs_2_
  23.5 0.4 pack.1.refs_8_.b_ref.refs_2_
  24.0 0.5 collective-permute-done.4.refs_3_
  24.5 3.6 %coefficients.2 = f32[8,2,64,128]{3,2,1,0:T(8,128)} custom-call(s32[2,8]{1,0:T(2,128)S(1)} %pad_add_fusion.refs_0_, s32[2,8]{1,0:T(2,128)S(1)} %get-tuple-element.29.refs_1_, s32[2,8]{1,0:T(2,128)S(1)} %collective-permute-done.3.refs_2_, s32[2,8]{1,0:T(2,128)S(1)} %collective-permute-done.4.refs_3_, f32[16,64,128]{2,1,0:T(8,128)S(1)} %pad_maximum_fusion.refs_4_, ...), custom_call_target="tpu_custom_call" | custom-call | flops 100663296 | bytes 4194304 | tf_op jit(solution)/shard_map/coefficients/pallas_call | solution.py:170
  28.2 0.8 copy-done.7
  29.0 0.8 copy-done.9
  29.7 6.7 %all-to-all-start = ((f32[8,2,64,128]{3,2,1,0:T(8,128)}), f32[8,2,64,128]{3,2,1,0:T(8,128)S(1)}, u32[]{:S(2)}, u32[]{:S(2)}) async-start(f32[8,2,64,128]{3,2,1,0:T(8,128)} %coefficients.2), calls=%async_computation | async-start | bytes 1048576 | tf_op jit(solution)/shard_map/all_to_all | solution.py:631
  36.6 0.5 collective-permute-start.11
  37.2 0.4 collective-permute-start.13
  37.6 0.5 collective-permute-done.10.refs_5_
  38.1 0.4 collective-permute-done.11.refs_6_
  38.5 0.4 collective-permute-done.12.refs_7_
  39.2 0.7 copy-done.26
  40.0 9.6 %operator.2 = (f32[8,128,128]{2,1,0:T(8,128)}, f32[8,128,128]{2,1,0:T(8,128)}, f32[8,128,128]{2,1,0:T(8,128)}, f32[8,128,128]{2,1,0:T(8,128)}) custom-call(s32[6,16]{1,0:T(8,128)} %bitcast.17, f32[16,6,128,128]{3,2,1,0:T(8,128)} %blocks_ref.3, f32[16,128,256]{2,1,0:T(8,128)} %bitcast.13, f32[2,128,256]{2,1,0:T(8,128)} %copy-done.14, ...), custom_call_target="tpu_custom_call" | custom-call | tf_op jit(solution)/shard_map/operator/pallas_call | solution.py:378
  50.1 1.7 %collective-permute-done.14 = f32[8,128,128]{2,1,0:T(8,128)} collective-permute-done((f32[8,128,128]{2,1,0:T(8,128)}, f32[8,128,128]{2,1,0:T(8,128)}, u32[]{:S(2)}, u32[]{:S(2)}) %collective-permute-start.14) | collective-permute-done | bytes 524320 | tf_op jit(solution)/shard_map/ppermute | solution.py:594
  51.9 1.2 slice_add_fusion
  53.1 0.6 collective-permute-start.17
  53.7 1.5 %collective-permute-start.16 = (f32[4,128,128]{2,1,0:T(8,128)S(1)}, f32[4,128,128]{2,1,0:T(8,128)S(1)}, u32[]{:S(2)}, u32[]{:S(2)}) collective-permute-start(f32[4,128,128]{2,1,0:T(8,128)S(1)} %get-tuple-element.59), channel_id=1, source_target_pairs={{0,2},{1,3},{2,0},{3,1},{4,6},{5,7},{6,4},{7,5},{8,10},{9,11},{10,... | collective-permute-start | bytes 786440 | tf_op jit(solution)/shard_map/ppermute | solution.py:599
  55.2 1.0 copy-done.13
  56.3 3.1 %far_part.2.refs_0_ = f32[8,128,128]{2,1,0:T(8,128)S(1)} custom-call(s32[2,8]{1,0:T(2,128)S(1)} %pad_add_fusion.refs_0_, s32[2,8]{1,0:T(2,128)S(1)} %get-tuple-element.29.refs_1_, s32[2,8]{1,0:T(2,128)S(1)} %collective-permute-done.3.refs_2_, s32[2,8]{1,0:T(2,128)S(1)} %collective-permute-done.4.refs_3_, f32[16,64,128]{2,1,0:T(8,128)S(1)} %pad_maximum_fusion.refs_4_, ...), custom_call_target="tpu_custom_call" | custom-call | flops 100663296 | bytes 4194304 | tf_op jit(solution)/shard_map/far_part/pallas_call | solution.py:229
  59.4 2.9 %collective-permute-done.17.refs_1_ = f32[4,128,128]{2,1,0:T(8,128)S(1)} collective-permute-done((f32[4,128,128]{2,1,0:T(8,128)S(1)}, f32[4,128,128]{2,1,0:T(8,128)S(1)}, u32[]{:S(2)}, u32[]{:S(2)}) %collective-permute-start.17) | collective-permute-done | bytes 262176 | tf_op jit(solution)/shard_map/ppermute | solution.py:599
  62.4 3.9 %collective-permute-start.18 = (f32[4,128,128]{2,1,0:T(8,128)S(1)}, f32[4,128,128]{2,1,0:T(8,128)S(1)}, u32[]{:S(2)}, u32[]{:S(2)}) collective-permute-start(f32[4,128,128]{2,1,0:T(8,128)S(1)} %add_half.3.gr_ref.refs_9_.refs_1_.refs_4_), channel_id=1, source_target_pairs={{0,4},{4,8},{8,12},{12,16},{16,20},{20,24},{24,28},{1,5},{5,9},{9,... | collective-permute-start | bytes 786440 | tf_op jit(solution)/shard_map/ppermute | solution.py:612
  66.4 0.5 collective-permute-start.21
  67.2 1.3 collective-permute-start.19
  68.5 1.4 %collective-permute-start.20 = (f32[4,128,128]{2,1,0:T(8,128)S(1)}, f32[4,128,128]{2,1,0:T(8,128)}, u32[]{:S(2)}, u32[]{:S(2)}) collective-permute-start(f32[4,128,128]{2,1,0:T(8,128)S(1)} %add_half.2.gl_ref.refs_8_.refs_0_.refs_3_), channel_id=1, source_target_pairs={{0,2},{1,3},{2,0},{3,1},{4,6},{5,7},{6,4},{7,5},{8,10},{9,11},{10,... | collective-permute-start | bytes 786440 | tf_op jit(solution)/shard_map/ppermute | solution.py:599
  69.9 2.9 %coefficients.3 = f32[8,2,64,128]{3,2,1,0:T(8,128)S(1)} custom-call(s32[2,8]{1,0:T(2,128)S(1)} %pad_add_fusion.refs_0_, s32[2,8]{1,0:T(2,128)S(1)} %get-tuple-element.29.refs_1_, s32[2,8]{1,0:T(2,128)S(1)} %collective-permute-done.3.refs_2_, s32[2,8]{1,0:T(2,128)S(1)} %collective-permute-done.4.refs_3_, f32[16,64,128]{2,1,0:T(8,128)S(1)} %pad_maximum_fusion.refs_4_, ...), custom_call_target="tpu_custom_call" | custom-call | flops 100663296 | bytes 4194304 | tf_op jit(solution)/shard_map/coefficients/pallas_call | solution.py:170
  72.8 0.8 copy-done.11
  73.6 0.5 collective-permute-start.22
  74.1 1.1 collective-permute-done.21.refs_3_
  75.3 1.6 %collective-permute-done.19.refs_9_ = f32[4,128,128]{2,1,0:T(8,128)S(1)} collective-permute-done((f32[4,128,128]{2,1,0:T(8,128)S(1)}, f32[4,128,128]{2,1,0:T(8,128)S(1)}, u32[]{:S(2)}, u32[]{:S(2)}) %collective-permute-start.19) | collective-permute-done | bytes 262176 | tf_op jit(solution)/shard_map/ppermute | solution.py:616
  76.9 1.7 %collective-permute-done.20.refs_2_ = f32[4,128,128]{2,1,0:T(8,128)} collective-permute-done((f32[4,128,128]{2,1,0:T(8,128)S(1)}, f32[4,128,128]{2,1,0:T(8,128)}, u32[]{:S(2)}, u32[]{:S(2)}) %collective-permute-start.20) | collective-permute-done | bytes 262176 | tf_op jit(solution)/shard_map/ppermute | solution.py:599
  78.6 0.5 collective-permute-start.26
  79.1 1.3 collective-permute-start.27
  80.5 7.7 %all-to-all-start.1 = ((f32[8,2,64,128]{3,2,1,0:T(8,128)}), f32[8,2,64,128]{3,2,1,0:T(8,128)S(1)}, u32[]{:S(2)}, u32[]{:S(2)}) async-start(f32[8,2,64,128]{3,2,1,0:T(8,128)} %copy-done.11), calls=%async_computation.1 | async-start | bytes 1048576 | tf_op jit(solution)/shard_map/all_to_all | solution.py:631
  89.5 0.9 collective-permute-done.25.refs_7_
  90.4 0.5 collective-permute-done.29.refs_13_
  90.9 0.4 collective-permute-done.30.refs_14_
  91.2 0.4 collective-permute-done.31.refs_15_
  91.6 10.0 %operator.3 = (f32[8,128,128]{2,1,0:T(8,128)}, f32[8,128,128]{2,1,0:T(8,128)}, f32[8,128,128]{2,1,0:T(8,128)}, f32[8,128,128]{2,1,0:T(8,128)}) custom-call(s32[6,16]{1,0:T(8,128)} %bitcast.18, f32[16,6,128,128]{3,2,1,0:T(8,128)} %blocks_ref.3, f32[4,128,128]{2,1,0:T(8,128)} %copy-done.4, f32[4,128,128]{2,1,0:T(8,128)} %copy-done.1, ...), custom_call_target="tpu_custom_call" | custom-call | tf_op jit(solution)/shard_map/operator/pallas_call | solution.py:378
  102.2 1.1 all-to-all-done.1.refs_8_
  103.3 0.5 collective-permute-done.32
  103.8 1.1 add.37
  104.9 1.6 %collective-permute-start.34 = (f32[8,128,128]{2,1,0:T(8,128)S(1)}, f32[8,128,128]{2,1,0:T(8,128)S(1)}, u32[]{:S(2)}, u32[]{:S(2)}) collective-permute-start(f32[8,128,128]{2,1,0:T(8,128)S(1)} %add.37), channel_id=1, source_target_pairs={{0,2},{1,3},{2,0},{3,1},{4,6},{5,7},{6,4},{7,5},{8,10},{9,11},{10,... | collective-permute-start | bytes 1572872 | tf_op jit(solution)/shard_map/ppermute | solution.py:599
  106.5 0.9 copy-done.2
  107.4 0.9 copy-done.5
  108.7 3.4 %far_part.3.refs_0_ = f32[8,128,128]{2,1,0:T(8,128)S(1)} custom-call(s32[2,8]{1,0:T(2,128)S(1)} %pad_add_fusion.refs_0_, s32[2,8]{1,0:T(2,128)S(1)} %get-tuple-element.29.refs_1_, s32[2,8]{1,0:T(2,128)S(1)} %collective-permute-done.3.refs_2_, s32[2,8]{1,0:T(2,128)S(1)} %collective-permute-done.4.refs_3_, f32[16,64,128]{2,1,0:T(8,128)S(1)} %pad_maximum_fusion.refs_4_, ...), custom_call_target="tpu_custom_call" | custom-call | flops 100663296 | bytes 4194304 | tf_op jit(solution)/shard_map/far_part/pallas_call | solution.py:229
  112.0 7.0 %collective-permute-done.34.refs_1_ = f32[8,128,128]{2,1,0:T(8,128)S(1)} collective-permute-done((f32[8,128,128]{2,1,0:T(8,128)S(1)}, f32[8,128,128]{2,1,0:T(8,128)S(1)}, u32[]{:S(2)}, u32[]{:S(2)}) %collective-permute-start.34) | collective-permute-done | bytes 524320 | tf_op jit(solution)/shard_map/ppermute | solution.py:599
  119.3 1.9 %collective-permute-start.35 = (f32[8,128]{1,0:T(8,128)S(1)}, f32[8,128]{1,0:T(8,128)S(1)}, u32[]{:S(2)}, u32[]{:S(2)}) collective-permute-start(f32[8,128]{1,0:T(8,128)S(1)} %get-tuple-element.52), channel_id=1, source_target_pairs={{0,4},{4,0},{8,12},{12,8},{16,20},{20,16},{24,28},{28,24},{1,5},{5... | collective-permute-start | bytes 12296 | tf_op jit(solution)/shard_map/ppermute | solution.py:623
  121.3 1.7 %collective-permute-done.35 = f32[8,128]{1,0:T(8,128)S(1)} collective-permute-done((f32[8,128]{1,0:T(8,128)S(1)}, f32[8,128]{1,0:T(8,128)S(1)}, u32[]{:S(2)}, u32[]{:S(2)}) %collective-permute-start.35) | collective-permute-done | bytes 4128 | tf_op jit(solution)/shard_map/ppermute | solution.py:623
  123.0 1.9 %collective-permute-start.36 = (f32[8,128]{1,0:T(8,128)S(1)}, f32[8,128]{1,0:T(8,128)S(1)}, u32[]{:S(2)}, u32[]{:S(2)}) collective-permute-start(f32[8,128]{1,0:T(8,128)S(1)} %add.38), channel_id=1, source_target_pairs={{0,8},{4,12},{8,0},{12,4},{16,24},{20,28},{24,16},{28,20},{1,9},{5... | collective-permute-start | bytes 12296 | tf_op jit(solution)/shard_map/ppermute | solution.py:623
  124.9 1.7 %collective-permute-done.36 = f32[8,128]{1,0:T(8,128)S(1)} collective-permute-done((f32[8,128]{1,0:T(8,128)S(1)}, f32[8,128]{1,0:T(8,128)S(1)}, u32[]{:S(2)}, u32[]{:S(2)}) %collective-permute-start.36) | collective-permute-done | bytes 4128 | tf_op jit(solution)/shard_map/ppermute | solution.py:623
  126.6 2.8 %collective-permute-start.37 = (f32[8,128]{1,0:T(8,128)S(1)}, f32[8,128]{1,0:T(8,128)S(1)}, u32[]{:S(2)}, u32[]{:S(2)}) collective-permute-start(f32[8,128]{1,0:T(8,128)S(1)} %add.39.refs_0_), channel_id=1, source_target_pairs={{0,16},{4,20},{8,24},{12,28},{16,0},{20,4},{24,8},{28,12},{1,17},{... | collective-permute-start | bytes 12296 | tf_op jit(solution)/shard_map/ppermute | solution.py:623
  129.4 1.7 %collective-permute-done.37.refs_1_ = f32[8,128]{1,0:T(8,128)S(1)} collective-permute-done((f32[8,128]{1,0:T(8,128)S(1)}, f32[8,128]{1,0:T(8,128)S(1)}, u32[]{:S(2)}, u32[]{:S(2)}) %collective-permute-start.37) | collective-permute-done | bytes 4128 | tf_op jit(solution)/shard_map/ppermute | solution.py:623
  131.1 1.4 %finish.1 = (f32[64,2048]{1,0:T(8,128)}, f32[64,2048]{1,0:T(8,128)}) custom-call(f32[8,128]{1,0:T(8,128)S(1)} %add.39.refs_0_, f32[8,128]{1,0:T(8,128)S(1)} %collective-permute-done.37.refs_1_, f32[8,128,128]{2,1,0:T(8,128)S(1)} %pack.1.refs_8_.b_ref.refs_2_, f32[4,128,128]{2,1,0:T(8,128)S(1)} %copy-done.6, f32[4,128,128]{2,1,0:T(8,128)S(1)} %copy-done.3, ...), custom_call_target="tpu_custom_call" | custom-call | flops 1048576 | bytes 3670016 | tf_op jit(solution)/shard_map/finish/pallas_call | solution.py:561
  (94 shorter events, 4.4 us)
Async XLA Ops:
  0.6 10.0 %copy-start.28 = (s32[1,8,1]{1,2,0:T(1,128)S(1)}, s32[1,8,1]{1,2,0:T(1,128)}, u32[]{:S(2)}) copy-start(s32[1,8,1]{1,2,0:T(1,128)} %param.10) | copy-start | bytes 100
  0.6 10.0 %copy-start.27 = (s32[1,8,1]{1,2,0:T(1,128)S(1)}, s32[1,8,1]{1,2,0:T(1,128)}, u32[]{:S(2)}) copy-start(s32[1,8,1]{1,2,0:T(1,128)} %param.11) | copy-start | bytes 100
  1.7 15.1 %collective-permute-start.5 = (f32[16,64,128]{2,1,0:T(8,128)S(1)}, f32[16,64,128]{2,1,0:T(8,128)}, u32[]{:S(2)}, u32[]{:S(2)}) collective-permute-start(f32[16,64,128]{2,1,0:T(8,128)S(1)} %pad_maximum_fusion.refs_4_), channel_id=1, source_target_pairs={{0,2},{1,3},{2,0},{3,1},{4,6},{5,7},{6,4},{7,5},{8,10},{9,11},{10,... | collective-permute-start | bytes 1572872 | tf_op jit(solution)/shard_map/ppermute | solution.py:599
  5.8 14.3 %collective-permute-start = (f32[2,128,256]{2,1,0:T(8,128)S(1)}, f32[2,128,256]{2,1,0:T(8,128)S(1)}, u32[]{:S(2)}, u32[]{:S(2)}) collective-permute-start(f32[2,128,256]{2,1,0:T(8,128)S(1)} %get-tuple-element.57), channel_id=1, source_target_pairs={{0,4},{4,8},{8,12},{12,16},{16,20},{20,24},{24,28},{1,5},{5,9},{9,... | collective-permute-start | bytes 786440 | tf_op jit(solution)/shard_map/ppermute | solution.py:612
  9.2 10.9 %collective-permute-start.1 = (f32[2,128,256]{2,1,0:T(8,128)S(1)}, f32[2,128,256]{2,1,0:T(8,128)S(1)}, u32[]{:S(2)}, u32[]{:S(2)}) collective-permute-start(f32[2,128,256]{2,1,0:T(8,128)S(1)} %get-tuple-element.56), channel_id=1, source_target_pairs={{4,0},{8,4},{12,8},{16,12},{20,16},{24,20},{28,24},{5,1},{9,5},{13... | collective-permute-start | bytes 786440 | tf_op jit(solution)/shard_map/ppermute | solution.py:616
  10.5 13.9 %collective-permute-start.6 = (f32[16,64,128]{2,1,0:T(8,128)S(1)}, f32[16,64,128]{2,1,0:T(8,128)S(1)}, u32[]{:S(2)}, u32[]{:S(2)}) collective-permute-start(f32[16,64,128]{2,1,0:T(8,128)S(1)} %pad_maximum_fusion.refs_4_), channel_id=1, source_target_pairs={{0,1},{1,0},{2,3},{3,2},{4,5},{5,4},{6,7},{7,6},{8,9},{9,8},{10,11... | collective-permute-start | bytes 1572872 | tf_op jit(solution)/shard_map/ppermute | solution.py:594
  10.7 12.9 %copy-start = (f32[2048,256]{1,0:T(8,128)S(1)}, f32[2048,256]{1,0:T(8,128)}, u32[]{:S(2)}) copy-start(f32[2048,256]{1,0:T(8,128)} %param.7) | copy-start | bytes 6291460
  10.7 6.1 %collective-permute-start.2 = (s32[2,8]{1,0:T(2,128)S(1)}, s32[2,8]{1,0:T(2,128)S(1)}, u32[]{:S(2)}, u32[]{:S(2)}) collective-permute-start(s32[2,8]{1,0:T(2,128)S(1)} %pad_add_fusion.refs_0_), channel_id=1, source_target_pairs={{0,2},{1,3},{2,0},{3,1},{4,6},{5,7},{6,4},{7,5},{8,10},{9,11},{10,... | collective-permute-start | bytes 200 | tf_op jit(solution)/shard_map/ppermute | solution.py:599
  16.8 7.7 %collective-permute-start.7 = (f32[16,64,128]{2,1,0:T(8,128)}, f32[16,64,128]{2,1,0:T(8,128)S(1)}, u32[]{:S(2)}, u32[]{:S(2)}) collective-permute-start(f32[16,64,128]{2,1,0:T(8,128)} %collective-permute-done.5.refs_5_), channel_id=1, source_target_pairs={{0,1},{1,0},{2,3},{3,2},{4,5},{5,4},{6,7},{7,6},{8,9},{9,8},{10,11... | collective-permute-start | bytes 1572872 | tf_op jit(solution)/shard_map/ppermute | solution.py:594
  20.1 16.4 %copy-start.14 = (f32[2,128,256]{2,1,0:T(8,128)}, f32[2,128,256]{2,1,0:T(8,128)S(1)}, u32[]{:S(2)}) copy-start(f32[2,128,256]{2,1,0:T(8,128)S(1)} %get-tuple-element.32.refs_1_) | copy-start | bytes 786436
  20.1 16.4 %copy-start.15 = (f32[2,128,256]{2,1,0:T(8,128)}, f32[2,128,256]{2,1,0:T(8,128)S(1)}, u32[]{:S(2)}) copy-start(f32[2,128,256]{2,1,0:T(8,128)S(1)} %get-tuple-element.33.refs_2_) | copy-start | bytes 786436
  20.1 16.3 %collective-permute-start.8 = (f32[2,128,256]{2,1,0:T(8,128)S(1)}, f32[2,128,256]{2,1,0:T(8,128)S(1)}, u32[]{:S(2)}, u32[]{:S(2)}) collective-permute-start(f32[2,128,256]{2,1,0:T(8,128)S(1)} %get-tuple-element.32.refs_1_), channel_id=1, source_target_pairs={{0,2},{1,3},{2,0},{3,1},{4,6},{5,7},{6,4},{7,5},{8,10},{9,11},{10,... | collective-permute-start | bytes 786440 | tf_op jit(solution)/shard_map/ppermute | solution.py:599
  20.7 15.8 %collective-permute-start.9 = (f32[2,128,256]{2,1,0:T(8,128)S(1)}, f32[2,128,256]{2,1,0:T(8,128)S(1)}, u32[]{:S(2)}, u32[]{:S(2)}) collective-permute-start(f32[2,128,256]{2,1,0:T(8,128)S(1)} %get-tuple-element.33.refs_2_), channel_id=1, source_target_pairs={{0,2},{1,3},{2,0},{3,1},{4,6},{5,7},{6,4},{7,5},{8,10},{9,11},{10,... | collective-permute-start | bytes 786440 | tf_op jit(solution)/shard_map/ppermute | solution.py:599
  22.2 1.1 collective-permute-start.3
  23.4 1.1 collective-permute-start.4
  29.7 22.1 %all-to-all-start = ((f32[8,2,64,128]{3,2,1,0:T(8,128)}), f32[8,2,64,128]{3,2,1,0:T(8,128)S(1)}, u32[]{:S(2)}, u32[]{:S(2)}) async-start(f32[8,2,64,128]{3,2,1,0:T(8,128)} %coefficients.2), calls=%async_computation | async-start | bytes 1048576 | tf_op jit(solution)/shard_map/all_to_all | solution.py:631
  36.5 3.5 %copy-start.19 = (f32[2,128,256]{2,1,0:T(8,128)}, f32[2,128,256]{2,1,0:T(8,128)S(1)}, u32[]{:S(2)}) copy-start(f32[2,128,256]{2,1,0:T(8,128)S(1)} %collective-permute-done.8.refs_3_) | copy-start | bytes 786436
  36.5 3.4 %copy-start.20 = (f32[2,128,256]{2,1,0:T(8,128)}, f32[2,128,256]{2,1,0:T(8,128)S(1)}, u32[]{:S(2)}) copy-start(f32[2,128,256]{2,1,0:T(8,128)S(1)} %collective-permute-done.9.refs_4_) | copy-start | bytes 786436
  36.5 1.6 %collective-permute-start.10 = (f32[2,128,256]{2,1,0:T(8,128)S(1)}, f32[2,128,256]{2,1,0:T(8,128)S(1)}, u32[]{:S(2)}, u32[]{:S(2)}) collective-permute-start(f32[2,128,256]{2,1,0:T(8,128)S(1)} %get-tuple-element.32.refs_1_), channel_id=1, source_target_pairs={{0,1},{1,0},{2,3},{3,2},{4,5},{5,4},{6,7},{7,6},{8,9},{9,8},{10,11... | collective-permute-start | bytes 786440 | tf_op jit(solution)/shard_map/ppermute | solution.py:594
  36.6 1.9 %collective-permute-start.11 = (f32[2,128,256]{2,1,0:T(8,128)S(1)}, f32[2,128,256]{2,1,0:T(8,128)S(1)}, u32[]{:S(2)}, u32[]{:S(2)}) collective-permute-start(f32[2,128,256]{2,1,0:T(8,128)S(1)} %get-tuple-element.33.refs_2_), channel_id=1, source_target_pairs={{0,1},{1,0},{2,3},{3,2},{4,5},{5,4},{6,7},{7,6},{8,9},{9,8},{10,11... | collective-permute-start | bytes 786440 | tf_op jit(solution)/shard_map/ppermute | solution.py:594
  37.1 1.8 %collective-permute-start.12 = (f32[2,128,256]{2,1,0:T(8,128)S(1)}, f32[2,128,256]{2,1,0:T(8,128)S(1)}, u32[]{:S(2)}, u32[]{:S(2)}) collective-permute-start(f32[2,128,256]{2,1,0:T(8,128)S(1)} %collective-permute-done.8.refs_3_), channel_id=1, source_target_pairs={{0,1},{1,0},{2,3},{3,2},{4,5},{5,4},{6,7},{7,6},{8,9},{9,8},{10,11... | collective-permute-start | bytes 786440 | tf_op jit(solution)/shard_map/ppermute | solution.py:594
  37.2 2.1 %collective-permute-start.13 = (f32[2,128,256]{2,1,0:T(8,128)S(1)}, f32[2,128,256]{2,1,0:T(8,128)S(1)}, u32[]{:S(2)}, u32[]{:S(2)}) collective-permute-start(f32[2,128,256]{2,1,0:T(8,128)S(1)} %collective-permute-done.9.refs_4_), channel_id=1, source_target_pairs={{0,1},{1,0},{2,3},{3,2},{4,5},{5,4},{6,7},{7,6},{8,9},{9,8},{10,11... | collective-permute-start | bytes 786440 | tf_op jit(solution)/shard_map/ppermute | solution.py:594
  38.1 1.8 %copy-start.23 = (f32[2,128,256]{2,1,0:T(8,128)}, f32[2,128,256]{2,1,0:T(8,128)S(1)}, u32[]{:S(2)}) copy-start(f32[2,128,256]{2,1,0:T(8,128)S(1)} %collective-permute-done.10.refs_5_) | copy-start | bytes 786436
  38.5 1.5 %copy-start.24 = (f32[2,128,256]{2,1,0:T(8,128)}, f32[2,128,256]{2,1,0:T(8,128)S(1)}, u32[]{:S(2)}) copy-start(f32[2,128,256]{2,1,0:T(8,128)S(1)} %collective-permute-done.11.refs_6_) | copy-start | bytes 786436
  38.8 1.1 copy-start.25
  39.9 15.3 %copy-start.8 = (f32[16,64,128]{2,1,0:T(8,128)S(1)}, f32[16,64,128]{2,1,0:T(8,128)}, u32[]{:S(2)}) copy-start(f32[16,64,128]{2,1,0:T(8,128)} %copy-done.7) | copy-start | bytes 1572868
  40.0 15.3 %copy-start.10 = (f32[16,64,128]{2,1,0:T(8,128)S(1)}, f32[16,64,128]{2,1,0:T(8,128)}, u32[]{:S(2)}) copy-start(f32[16,64,128]{2,1,0:T(8,128)} %copy-done.9) | copy-start | bytes 1572868
  49.5 2.3 %collective-permute-start.14 = (f32[8,128,128]{2,1,0:T(8,128)}, f32[8,128,128]{2,1,0:T(8,128)}, u32[]{:S(2)}, u32[]{:S(2)}) collective-permute-start(f32[8,128,128]{2,1,0:T(8,128)} %get-tuple-element.36), channel_id=1, source_target_pairs={{0,1},{1,0},{2,3},{3,2},{4,5},{5,4},{6,7},{7,6},{8,9},{9,8},{10,11... | collective-permute-start | bytes 1572872 | tf_op jit(solution)/shard_map/ppermute | solution.py:594
  49.7 5.5 %collective-permute-start.15 = (f32[8,128,128]{2,1,0:T(8,128)}, f32[8,128,128]{2,1,0:T(8,128)S(1)}, u32[]{:S(2)}, u32[]{:S(2)}) collective-permute-start(f32[8,128,128]{2,1,0:T(8,128)} %get-tuple-element.39), channel_id=1, source_target_pairs={{0,1},{1,0},{2,3},{3,2},{4,5},{5,4},{6,7},{7,6},{8,9},{9,8},{10,11... | collective-permute-start | bytes 1572872 | tf_op jit(solution)/shard_map/ppermute | solution.py:594
  53.1 9.2 %collective-permute-start.17 = (f32[4,128,128]{2,1,0:T(8,128)S(1)}, f32[4,128,128]{2,1,0:T(8,128)S(1)}, u32[]{:S(2)}, u32[]{:S(2)}) collective-permute-start(f32[4,128,128]{2,1,0:T(8,128)S(1)} %get-tuple-element.58), channel_id=1, source_target_pairs={{0,2},{1,3},{2,0},{3,1},{4,6},{5,7},{6,4},{7,5},{8,10},{9,11},{10,... | collective-permute-start | bytes 786440 | tf_op jit(solution)/shard_map/ppermute | solution.py:599
  53.7 13.5 %collective-permute-start.16 = (f32[4,128,128]{2,1,0:T(8,128)S(1)}, f32[4,128,128]{2,1,0:T(8,128)S(1)}, u32[]{:S(2)}, u32[]{:S(2)}) collective-permute-start(f32[4,128,128]{2,1,0:T(8,128)S(1)} %get-tuple-element.59), channel_id=1, source_target_pairs={{0,2},{1,3},{2,0},{3,1},{4,6},{5,7},{6,4},{7,5},{8,10},{9,11},{10,... | collective-permute-start | bytes 786440 | tf_op jit(solution)/shard_map/ppermute | solution.py:599
  55.2 1.0 copy-start.13
  62.4 29.2 %copy-start.1 = (f32[4,128,128]{2,1,0:T(8,128)}, f32[4,128,128]{2,1,0:T(8,128)S(1)}, u32[]{:S(2)}) copy-start(f32[4,128,128]{2,1,0:T(8,128)S(1)} %add_half.3.gr_ref.refs_9_.refs_1_.refs_4_) | copy-start | bytes 786436
  62.4 11.2 %collective-permute-start.18 = (f32[4,128,128]{2,1,0:T(8,128)S(1)}, f32[4,128,128]{2,1,0:T(8,128)S(1)}, u32[]{:S(2)}, u32[]{:S(2)}) collective-permute-start(f32[4,128,128]{2,1,0:T(8,128)S(1)} %add_half.3.gr_ref.refs_9_.refs_1_.refs_4_), channel_id=1, source_target_pairs={{0,4},{4,8},{8,12},{12,16},{16,20},{20,24},{24,28},{1,5},{5,9},{9,... | collective-permute-start | bytes 786440 | tf_op jit(solution)/shard_map/ppermute | solution.py:612
  66.4 8.9 %collective-permute-start.21 = (f32[4,128,128]{2,1,0:T(8,128)S(1)}, f32[4,128,128]{2,1,0:T(8,128)S(1)}, u32[]{:S(2)}, u32[]{:S(2)}) collective-permute-start(f32[4,128,128]{2,1,0:T(8,128)S(1)} %add_half.3.gr_ref.refs_9_.refs_1_.refs_4_), channel_id=1, source_target_pairs={{0,2},{1,3},{2,0},{3,1},{4,6},{5,7},{6,4},{7,5},{8,10},{9,11},{10,... | collective-permute-start | bytes 786440 | tf_op jit(solution)/shard_map/ppermute | solution.py:599
  67.2 24.4 %copy-start.4 = (f32[4,128,128]{2,1,0:T(8,128)}, f32[4,128,128]{2,1,0:T(8,128)S(1)}, u32[]{:S(2)}) copy-start(f32[4,128,128]{2,1,0:T(8,128)S(1)} %add_half.2.gl_ref.refs_8_.refs_0_.refs_3_) | copy-start | bytes 786436
  67.2 9.7 %collective-permute-start.19 = (f32[4,128,128]{2,1,0:T(8,128)S(1)}, f32[4,128,128]{2,1,0:T(8,128)S(1)}, u32[]{:S(2)}, u32[]{:S(2)}) collective-permute-start(f32[4,128,128]{2,1,0:T(8,128)S(1)} %add_half.2.gl_ref.refs_8_.refs_0_.refs_3_), channel_id=1, source_target_pairs={{4,0},{8,4},{12,8},{16,12},{20,16},{24,20},{28,24},{5,1},{9,5},{13... | collective-permute-start | bytes 786440 | tf_op jit(solution)/shard_map/ppermute | solution.py:616
  68.5 10.0 %collective-permute-start.20 = (f32[4,128,128]{2,1,0:T(8,128)S(1)}, f32[4,128,128]{2,1,0:T(8,128)}, u32[]{:S(2)}, u32[]{:S(2)}) collective-permute-start(f32[4,128,128]{2,1,0:T(8,128)S(1)} %add_half.2.gl_ref.refs_8_.refs_0_.refs_3_), channel_id=1, source_target_pairs={{0,2},{1,3},{2,0},{3,1},{4,6},{5,7},{6,4},{7,5},{8,10},{9,11},{10,... | collective-permute-start | bytes 786440 | tf_op jit(solution)/shard_map/ppermute | solution.py:599
  69.9 18.3 %collective-permute-start.23 = (f32[4,128,128]{2,1,0:T(8,128)S(1)}, f32[4,128,128]{2,1,0:T(8,128)}, u32[]{:S(2)}, u32[]{:S(2)}) collective-permute-start(f32[4,128,128]{2,1,0:T(8,128)S(1)} %add_half.3.gr_ref.refs_9_.refs_1_.refs_4_), channel_id=1, source_target_pairs={{0,1},{1,0},{2,3},{3,2},{4,5},{5,4},{6,7},{7,6},{8,9},{9,8},{10,11... | collective-permute-start | bytes 786440 | tf_op jit(solution)/shard_map/ppermute | solution.py:594
  73.6 18.0 %copy-start.16 = (f32[4,128,128]{2,1,0:T(8,128)}, f32[4,128,128]{2,1,0:T(8,128)S(1)}, u32[]{:S(2)}) copy-start(f32[4,128,128]{2,1,0:T(8,128)S(1)} %collective-permute-done.18.refs_8_) | copy-start | bytes 786436
  73.6 14.9 %collective-permute-start.22 = (f32[4,128,128]{2,1,0:T(8,128)S(1)}, f32[4,128,128]{2,1,0:T(8,128)}, u32[]{:S(2)}, u32[]{:S(2)}) collective-permute-start(f32[4,128,128]{2,1,0:T(8,128)S(1)} %add_half.2.gl_ref.refs_8_.refs_0_.refs_3_), channel_id=1, source_target_pairs={{0,1},{1,0},{2,3},{3,2},{4,5},{5,4},{6,7},{7,6},{8,9},{9,8},{10,11... | collective-permute-start | bytes 786440 | tf_op jit(solution)/shard_map/ppermute | solution.py:594
  75.3 3.3 %copy-start.17 = (f32[4,128,128]{2,1,0:T(8,128)}, f32[4,128,128]{2,1,0:T(8,128)S(1)}, u32[]{:S(2)}) copy-start(f32[4,128,128]{2,1,0:T(8,128)S(1)} %collective-permute-done.21.refs_3_) | copy-start | bytes 786436
  76.9 2.2 %copy-start.18 = (f32[4,128,128]{2,1,0:T(8,128)}, f32[4,128,128]{2,1,0:T(8,128)S(1)}, u32[]{:S(2)}) copy-start(f32[4,128,128]{2,1,0:T(8,128)S(1)} %collective-permute-done.19.refs_9_) | copy-start | bytes 786436
  78.6 10.2 %collective-permute-start.26 = (f32[4,128,128]{2,1,0:T(8,128)S(1)}, f32[4,128,128]{2,1,0:T(8,128)}, u32[]{:S(2)}, u32[]{:S(2)}) collective-permute-start(f32[4,128,128]{2,1,0:T(8,128)S(1)} %collective-permute-done.18.refs_8_), channel_id=1, source_target_pairs={{0,2},{1,3},{2,0},{3,1},{4,6},{5,7},{6,4},{7,5},{8,10},{9,11},{10,... | collective-permute-start | bytes 786440 | tf_op jit(solution)/shard_map/ppermute | solution.py:599
  79.1 9.9 %collective-permute-start.27 = (f32[4,128,128]{2,1,0:T(8,128)}, f32[4,128,128]{2,1,0:T(8,128)}, u32[]{:S(2)}, u32[]{:S(2)}) collective-permute-start(f32[4,128,128]{2,1,0:T(8,128)} %collective-permute-done.20.refs_2_), channel_id=1, source_target_pairs={{4,0},{8,4},{12,8},{16,12},{20,16},{24,20},{28,24},{5,1},{9,5},{13... | collective-permute-start | bytes 786440 | tf_op jit(solution)/shard_map/ppermute | solution.py:616
  80.4 8.9 %collective-permute-start.24 = (f32[4,128,128]{2,1,0:T(8,128)}, f32[4,128,128]{2,1,0:T(8,128)}, u32[]{:S(2)}, u32[]{:S(2)}) collective-permute-start(f32[4,128,128]{2,1,0:T(8,128)} %collective-permute-done.20.refs_2_), channel_id=1, source_target_pairs={{0,1},{1,0},{2,3},{3,2},{4,5},{5,4},{6,7},{7,6},{8,9},{9,8},{10,11... | collective-permute-start | bytes 786440 | tf_op jit(solution)/shard_map/ppermute | solution.py:594
  80.5 22.9 %all-to-all-start.1 = ((f32[8,2,64,128]{3,2,1,0:T(8,128)}), f32[8,2,64,128]{3,2,1,0:T(8,128)S(1)}, u32[]{:S(2)}, u32[]{:S(2)}) async-start(f32[8,2,64,128]{3,2,1,0:T(8,128)} %copy-done.11), calls=%async_computation.1 | async-start | bytes 1048576 | tf_op jit(solution)/shard_map/all_to_all | solution.py:631
  88.2 2.2 %collective-permute-start.28 = (f32[4,128,128]{2,1,0:T(8,128)S(1)}, f32[4,128,128]{2,1,0:T(8,128)S(1)}, u32[]{:S(2)}, u32[]{:S(2)}) collective-permute-start(f32[4,128,128]{2,1,0:T(8,128)S(1)} %collective-permute-done.18.refs_8_), channel_id=1, source_target_pairs={{0,1},{1,0},{2,3},{3,2},{4,5},{5,4},{6,7},{7,6},{8,9},{9,8},{10,11... | collective-permute-start | bytes 786440 | tf_op jit(solution)/shard_map/ppermute | solution.py:594
  88.5 1.9 %collective-permute-start.25 = (f32[4,128,128]{2,1,0:T(8,128)}, f32[4,128,128]{2,1,0:T(8,128)S(1)}, u32[]{:S(2)}, u32[]{:S(2)}) collective-permute-start(f32[4,128,128]{2,1,0:T(8,128)} %copy-done.17), channel_id=1, source_target_pairs={{0,1},{1,0},{2,3},{3,2},{4,5},{5,4},{6,7},{7,6},{8,9},{9,8},{10,11... | collective-permute-start | bytes 786440 | tf_op jit(solution)/shard_map/ppermute | solution.py:594
  88.7 2.1 %collective-permute-start.29 = (f32[4,128,128]{2,1,0:T(8,128)}, f32[4,128,128]{2,1,0:T(8,128)}, u32[]{:S(2)}, u32[]{:S(2)}) collective-permute-start(f32[4,128,128]{2,1,0:T(8,128)} %copy-done.18), channel_id=1, source_target_pairs={{0,1},{1,0},{2,3},{3,2},{4,5},{5,4},{6,7},{7,6},{8,9},{9,8},{10,11... | collective-permute-start | bytes 786440 | tf_op jit(solution)/shard_map/ppermute | solution.py:594
  89.0 2.3 %collective-permute-start.30 = (f32[4,128,128]{2,1,0:T(8,128)}, f32[4,128,128]{2,1,0:T(8,128)}, u32[]{:S(2)}, u32[]{:S(2)}) collective-permute-start(f32[4,128,128]{2,1,0:T(8,128)} %collective-permute-done.26.refs_10_), channel_id=1, source_target_pairs={{0,1},{1,0},{2,3},{3,2},{4,5},{5,4},{6,7},{7,6},{8,9},{9,8},{10,11... | collective-permute-start | bytes 786440 | tf_op jit(solution)/shard_map/ppermute | solution.py:594
  89.3 2.3 %collective-permute-start.31 = (f32[4,128,128]{2,1,0:T(8,128)}, f32[4,128,128]{2,1,0:T(8,128)}, u32[]{:S(2)}, u32[]{:S(2)}) collective-permute-start(f32[4,128,128]{2,1,0:T(8,128)} %collective-permute-done.27.refs_11_), channel_id=1, source_target_pairs={{0,1},{1,0},{2,3},{3,2},{4,5},{5,4},{6,7},{7,6},{8,9},{9,8},{10,11... | collective-permute-start | bytes 786440 | tf_op jit(solution)/shard_map/ppermute | solution.py:594
  90.4 1.3 copy-start.22
  90.4 1.3 copy-start.21
  101.6 2.2 %collective-permute-start.32 = (f32[8,128,128]{2,1,0:T(8,128)}, f32[8,128,128]{2,1,0:T(8,128)S(1)}, u32[]{:S(2)}, u32[]{:S(2)}) collective-permute-start(f32[8,128,128]{2,1,0:T(8,128)} %get-tuple-element.46), channel_id=1, source_target_pairs={{0,1},{1,0},{2,3},{3,2},{4,5},{5,4},{6,7},{7,6},{8,9},{9,8},{10,11... | collective-permute-start | bytes 1572872 | tf_op jit(solution)/shard_map/ppermute | solution.py:594
  101.9 6.7 %collective-permute-start.33 = (f32[8,128,128]{2,1,0:T(8,128)}, f32[8,128,128]{2,1,0:T(8,128)}, u32[]{:S(2)}, u32[]{:S(2)}) collective-permute-start(f32[8,128,128]{2,1,0:T(8,128)} %get-tuple-element.49), channel_id=1, source_target_pairs={{0,1},{1,0},{2,3},{3,2},{4,5},{5,4},{6,7},{7,6},{8,9},{9,8},{10,11... | collective-permute-start | bytes 1572872 | tf_op jit(solution)/shard_map/ppermute | solution.py:594
  103.3 5.3 %copy-start.12 = (f32[8,128,128]{2,1,0:T(8,128)S(1)}, f32[8,128,128]{2,1,0:T(8,128)}, u32[]{:S(2)}) copy-start(f32[8,128,128]{2,1,0:T(8,128)} %get-tuple-element.48.refs_9_) | copy-start | bytes 1572868
  104.9 14.1 %collective-permute-start.34 = (f32[8,128,128]{2,1,0:T(8,128)S(1)}, f32[8,128,128]{2,1,0:T(8,128)S(1)}, u32[]{:S(2)}, u32[]{:S(2)}) collective-permute-start(f32[8,128,128]{2,1,0:T(8,128)S(1)} %add.37), channel_id=1, source_target_pairs={{0,2},{1,3},{2,0},{3,1},{4,6},{5,7},{6,4},{7,5},{8,10},{9,11},{10,... | collective-permute-start | bytes 1572872 | tf_op jit(solution)/shard_map/ppermute | solution.py:599
  106.5 0.9 copy-start.2
  108.6 10.4 %copy-start.3 = (f32[4,128,128]{2,1,0:T(8,128)S(1)}, f32[4,128,128]{2,1,0:T(8,128)}, u32[]{:S(2)}) copy-start(f32[4,128,128]{2,1,0:T(8,128)} %copy-done.1) | copy-start | bytes 786436
  108.7 10.4 %copy-start.6 = (f32[4,128,128]{2,1,0:T(8,128)S(1)}, f32[4,128,128]{2,1,0:T(8,128)}, u32[]{:S(2)}) copy-start(f32[4,128,128]{2,1,0:T(8,128)} %copy-done.4) | copy-start | bytes 786436
  119.3 3.7 %collective-permute-start.35 = (f32[8,128]{1,0:T(8,128)S(1)}, f32[8,128]{1,0:T(8,128)S(1)}, u32[]{:S(2)}, u32[]{:S(2)}) collective-permute-start(f32[8,128]{1,0:T(8,128)S(1)} %get-tuple-element.52), channel_id=1, source_target_pairs={{0,4},{4,0},{8,12},{12,8},{16,20},{20,16},{24,28},{28,24},{1,5},{5... | collective-permute-start | bytes 12296 | tf_op jit(solution)/shard_map/ppermute | solution.py:623
  123.0 3.6 %collective-permute-start.36 = (f32[8,128]{1,0:T(8,128)S(1)}, f32[8,128]{1,0:T(8,128)S(1)}, u32[]{:S(2)}, u32[]{:S(2)}) collective-permute-start(f32[8,128]{1,0:T(8,128)S(1)} %add.38), channel_id=1, source_target_pairs={{0,8},{4,12},{8,0},{12,4},{16,24},{20,28},{24,16},{28,20},{1,9},{5... | collective-permute-start | bytes 12296 | tf_op jit(solution)/shard_map/ppermute | solution.py:623
  126.6 4.5 %collective-permute-start.37 = (f32[8,128]{1,0:T(8,128)S(1)}, f32[8,128]{1,0:T(8,128)S(1)}, u32[]{:S(2)}, u32[]{:S(2)}) collective-permute-start(f32[8,128]{1,0:T(8,128)S(1)} %add.39.refs_0_), channel_id=1, source_target_pairs={{0,16},{4,20},{8,24},{12,28},{16,0},{20,4},{24,8},{28,12},{1,17},{... | collective-permute-start | bytes 12296 | tf_op jit(solution)/shard_map/ppermute | solution.py:623
  (5 other events, 4.0 us)

commit v7 on v6

--- a/solution.py
+++ b/solution.py
@@ -126,8 +126,6 @@
     meta, hbm = refs[:far_size], refs[far_size : 2 * far_size + n_fields]
     out, refs = refs[2 * far_size + n_fields], refs[2 * far_size + n_fields + 1 :]
     vmem, (held, high, low, sems) = refs[: far_size + n_fields], refs[far_size + n_fields :]
-    groups = held.shape[0]
-    hbm = [ref.at[pl.ds(0, groups)] for ref in hbm[:far_size]] + list(hbm[far_size:])
     copies = begin(list(zip(hbm, vmem)), sems)
     factors, fields = vmem[:far_size], vmem[far_size:]
     per = sum(f.shape[0] for f in fields) // 2
@@ -162,7 +160,7 @@
 
 
 def coefficients(meta, factors, fields, far_size, waits=()):
-    groups = factors[0].shape[0] // 2
+    groups = factors[0].shape[0]
     per = sum(f.shape[0] for f in fields) // 2
     packs = REACH // per
     width = LANES // packs
@@ -189,8 +187,6 @@
     n = far_size + 1 + n_terms
     meta, hbm, held = refs[:far_size], refs[far_size : far_size + n], refs[far_size + n]
     vmem, (total, sems) = refs[far_size + n + 1 : -2], refs[-2:]
-    groups = vmem[0].shape[0]
-    hbm = [ref.at[pl.ds(groups, groups)] for ref in hbm[:far_size]] + list(hbm[far_size:])
     copies = begin(list(zip(hbm, vmem)), sems)
     terms = vmem[far_size + 1 :]
     factors, coef = vmem[:far_size], vmem[far_size]
@@ -661,27 +657,30 @@
         to_previous(lax.dynamic_slice_in_dim(own, first, shared, 0)),
     ]
     meta = along_all_y(jnp.stack([far_src.reshape(-1), far_tgt.reshape(-1)]))
-    factors = along_all_y(jnp.concatenate(factors, axis=0))
+    rights, lefts = [along_all_y(item) for item in factors]
     b_own = pack(own, far_size, per)
-    arrived = hold(ends + meta[1:])
-    ends, meta = arrived[:2], meta[:1] + arrived[2:]
-    pieces = list(ends)
+    second, *arrived = hold(ends[1:] + meta[1:])
+    first, *held = hold(ends[:1] + lefts[1:])
+    meta, lefts = meta[:1] + arrived, lefts[:1] + held
+    pieces = [first, second]
     for s in range(1, ys):
-        pieces += [along_y(item, s) for item in ends]
-    meta, factors = [items + [swap_cores(item) for item in items] for items in (meta, factors)]
-    coef = coefficients(meta, factors, [b_own], far_size)
+        pieces += [along_y(item, s) for item in (first, second)]
+    meta, rights, lefts = [
+        items + [swap_cores(item) for item in items] for items in (meta, rights, lefts)
+    ]
+    coef = coefficients(meta, rights, [b_own], far_size)
     pieces = after(pieces, coef)
     pieces += [swap_cores(item) for item in pieces]
     coef = exchange(coef)
     keeps, sends = operator(near_blocks, [own] + pieces, cols, far_size, per, width, False)
     terms, others, coef = sum_far(keeps, sends, coef, 2)
-    base = far_part(meta, factors, coef, terms, far_size, per)
+    base = far_part(meta, lefts, coef, terms, far_size, per)
     g_own = [add_half(half, [base], others[half]) for half in range(2)]
 
     head, tail = g_own
     from_left, from_right = to_next(tail), to_previous(head)
     heads, tails = along_all_y(head), along_all_y(tail)
-    coef = coefficients(meta, factors, g_own, far_size)
+    coef = coefficients(meta, rights, g_own, far_size)
     arrived = after([from_left, from_right] + heads[1:] + tails[1:], coef)
     from_left, from_right = arrived[:2]
     heads, tails = heads[:1] + arrived[2 : 1 + ys], tails[:1] + arrived[1 + ys :]
@@ -694,7 +693,7 @@
     coef = exchange(coef)
     keeps, sends = operator(near_blocks, owns + halos, cols, far_size, per, width, True)
     terms, (others,), coef = sum_far(keeps, sends, coef, 1)
-    base = far_part(meta, factors, coef, terms, far_size, per)
+    base = far_part(meta, lefts, coef, terms, far_size, per)
     early = early_dots(b_own, g_own, packs)
     part_dots, image = dots(b_own, g_own, early, [base] + others, packs)
     answer, residual = finish(sum_rows(part_dots), b_own, g_own, image, packs)

time: 133 us -> 133 us (level)
  local copies, waits for them, and re-layouts: 7.16 us -> 9.41 us
  Pallas kernels: 35.1 us -> 33.1 us
  waiting for transfers between devices: 37.4 us -> 35.9 us
    all_to_all x2, starting transfers between devices: 14.4 us -> 10.7 us  [exchange(): return lax.all_to_all(coef, 'rows', split_axis=0, concat_axis=0, tiled=True)]
    ppermute x2, starting transfers between devices: 7.35 us -> 10.2 us  [to_next(): lax.ppermute(value, 'rows', [(i, i + 1) for i in range(lax.axis_size('row...]
    ppermute x10 -> x11, waiting for transfers between devices: 18.5 us -> 21.2 us  [along_y(): lax.ppermute(value, 'far', [(i, (i + CORES * shift) % size) for i in rang...]
    ppermute x2, waiting for transfers between devices: 3.31 us -> 0.82 us  [to_next(): lax.ppermute(value, 'rows', [(i, i + 1) for i in range(lax.axis_size('row...]
    unnamed x58 -> x56, local copies, waits for them, and re-layouts: 6.09 us -> 8.34 us
    pallas_call x2, Pallas kernels: 6.51 us -> 4.87 us  [far_part(): pl.pallas_call(functools.partial(far_kernel, far_size, len(terms)), out_s...]
    ppermute x10 -> x11, starting transfers between devices: 11.8 us -> 12.9 us  [along_y(): lax.ppermute(value, 'far', [(i, (i + CORES * shift) % size) for i in rang...]
    ppermute x20 -> x22, starting transfers between devices: 4.38 us -> 5.07 us  [swap_cores(): return lax.ppermute(value, 'far', [(i, i ^ 1) for i in range(size)])]
  transfers between devices with their start and end apart: 40 -> 43, of which waited for: 24 -> 23; matrix products, arithmetic and copies ran while one was open for 3% -> 2% of each run, Pallas kernels for 25% -> 24%
where the time goes in v7:
time: 133 us; the launch traced here: 132 us
  starting transfers between devices  49.2 us (37%)
  waiting for transfers between devices  35.9 us (27%)
  Pallas kernels  33.1 us (25%)
  local copies, waits for them, and re-layouts  9.41 us (7%)
  other arithmetic  3.19 us (2%)
    ppermute x11, waiting for transfers between devices, along_y(): lax.ppermute(value, 'far', [(i, (i + CORES * shift) % size) for i in rang...  21.2 us
    pallas_call x2, Pallas kernels, operator(): pl.pallas_call(functools.partial(operator_kernel, far_size, per, last, le...  19.5 us
    ppermute x11, starting transfers between devices, along_y(): lax.ppermute(value, 'far', [(i, (i + CORES * shift) % size) for i in rang...  12.9 us
    all_to_all x2, starting transfers between devices, exchange(): return lax.all_to_all(coef, 'rows', split_axis=0, concat_axis=0, tiled=True)  10.7 us
    ppermute x2, starting transfers between devices, to_next(): lax.ppermute(value, 'rows', [(i, i + 1) for i in range(lax.axis_size('row...  10.2 us
    unnamed x56, local copies, waits for them, and re-layouts  8.34 us
    ppermute x22, waiting for transfers between devices, swap_cores(): return lax.ppermute(value, 'far', [(i, i ^ 1) for i in range(size)])  7.76 us
    ppermute x3, starting transfers between devices, sum_rows(): other = lax.ppermute(value, 'rows', [(i, i ^ step) for i in range(size)])  6.46 us
  transfers between devices with their start and end apart: 43, of which 23 were waited for; matrix products, arithmetic and copies ran while one was open for 2% of the time, Pallas kernels for 24%

profile of v7, /device:TPU:0, one launch (start us, length us, event | category | flops | bytes accessed | tf_op | source)
XLA Modules:
  0.0 132.0 jit_solution(15094004532669672831)
XLA Ops:
  0.7 1.1 constant_dynamic-slice_fusion
  1.7 5.6 %collective-permute-start.4 = (f32[2,128,256]{2,1,0:T(8,128)S(1)}, f32[2,128,256]{2,1,0:T(8,128)}, u32[]{:S(2)}, u32[]{:S(2)}) collective-permute-start(f32[2,128,256]{2,1,0:T(8,128)S(1)} %get-tuple-element.58), channel_id=1, source_target_pairs={{0,4},{4,8},{8,12},{12,16},{16,20},{20,24},{24,28},{1,5},{5,9},{9,... | collective-permute-start | bytes 786440 | tf_op jit(solution)/shard_map/ppermute | solution.py:608
  7.3 1.5 %collective-permute-start.5 = (f32[8,64,128]{2,1,0:T(8,128)}, f32[8,64,128]{2,1,0:T(8,128)S(1)}, u32[]{:S(2)}, u32[]{:S(2)}) collective-permute-start(f32[8,64,128]{2,1,0:T(8,128)} %bitcast.15), channel_id=1, source_target_pairs={{0,2},{1,3},{2,0},{3,1},{4,6},{5,7},{6,4},{7,5},{8,10},{9,11},{10,... | collective-permute-start | bytes 786440 | tf_op jit(solution)/shard_map/ppermute | solution.py:595
  8.8 0.5 collective-permute-start.10
  9.3 1.3 collective-permute-start
  10.6 0.7 pad_add_fusion.refs_0_
  11.3 0.8 collective-permute-done.4.refs_0_
  12.1 1.5 %collective-permute-start.1 = (s32[2,8]{1,0:T(2,128)S(1)}, s32[2,8]{1,0:T(2,128)S(1)}, u32[]{:S(2)}, u32[]{:S(2)}) collective-permute-start(s32[2,8]{1,0:T(2,128)S(1)} %pad_add_fusion.refs_0_), channel_id=1, source_target_pairs={{0,2},{1,3},{2,0},{3,1},{4,6},{5,7},{6,4},{7,5},{8,10},{9,11},{10,... | collective-permute-start | bytes 200 | tf_op jit(solution)/shard_map/ppermute | solution.py:595
  13.6 3.1 %collective-permute-done.5.refs_1_ = f32[8,64,128]{2,1,0:T(8,128)S(1)} collective-permute-done((f32[8,64,128]{2,1,0:T(8,128)}, f32[8,64,128]{2,1,0:T(8,128)S(1)}, u32[]{:S(2)}, u32[]{:S(2)}) %collective-permute-start.5) | collective-permute-done | bytes 262176 | tf_op jit(solution)/shard_map/ppermute | solution.py:595
  16.7 1.5 %collective-permute-start.8 = (f32[2,128,256]{2,1,0:T(8,128)}, f32[2,128,256]{2,1,0:T(8,128)}, u32[]{:S(2)}, u32[]{:S(2)}) collective-permute-start(f32[2,128,256]{2,1,0:T(8,128)} %get-tuple-element.34.refs_1_), channel_id=1, source_target_pairs={{0,2},{1,3},{2,0},{3,1},{4,6},{5,7},{6,4},{7,5},{8,10},{9,11},{10,... | collective-permute-start | bytes 786440 | tf_op jit(solution)/shard_map/ppermute | solution.py:595
  18.3 4.1 %collective-permute-done.10.refs_5_ = f32[8,64,128]{2,1,0:T(8,128)S(1)} collective-permute-done((f32[8,64,128]{2,1,0:T(8,128)}, f32[8,64,128]{2,1,0:T(8,128)S(1)}, u32[]{:S(2)}, u32[]{:S(2)}) %collective-permute-start.10) | collective-permute-done | bytes 262176 | tf_op jit(solution)/shard_map/ppermute | solution.py:595
  22.4 1.6 %collective-permute-start.9 = (f32[2,128,256]{2,1,0:T(8,128)}, f32[2,128,256]{2,1,0:T(8,128)}, u32[]{:S(2)}, u32[]{:S(2)}) collective-permute-start(f32[2,128,256]{2,1,0:T(8,128)} %get-tuple-element.35.refs_2_), channel_id=1, source_target_pairs={{0,2},{1,3},{2,0},{3,1},{4,6},{5,7},{6,4},{7,5},{8,10},{9,11},{10,... | collective-permute-start | bytes 786440 | tf_op jit(solution)/shard_map/ppermute | solution.py:595
  24.2 0.4 pack.1.refs_8_.b_ref.refs_2_
  24.6 0.5 collective-permute-done.2.refs_2_
  25.3 0.9 collective-permute-done.3.refs_3_
  26.3 3.1 %coefficients.2 = f32[8,2,64,128]{3,2,1,0:T(8,128)} custom-call(s32[2,8]{1,0:T(2,128)S(1)} %pad_add_fusion.refs_0_, s32[2,8]{1,0:T(2,128)S(1)} %get-tuple-element.30.refs_1_, s32[2,8]{1,0:T(2,128)S(1)} %collective-permute-done.2.refs_2_, s32[2,8]{1,0:T(2,128)S(1)} %collective-permute-done.3.refs_3_, f32[8,64,128]{2,1,0:T(8,128)S(1)} %bitcast.21, ...), custom_call_target="tpu_custom_call" | custom-call | flops 100663296 | bytes 4194304 | tf_op jit(solution)/shard_map/coefficients/pallas_call | solution.py:168
  29.4 0.7 copy-done.9
  30.1 0.7 copy-done.11
  30.8 4.2 %all-to-all-start = ((f32[8,2,64,128]{3,2,1,0:T(8,128)}), f32[8,2,64,128]{3,2,1,0:T(8,128)S(1)}, u32[]{:S(2)}, u32[]{:S(2)}) async-start(f32[8,2,64,128]{3,2,1,0:T(8,128)} %coefficients.2), calls=%async_computation | async-start | bytes 1048576 | tf_op jit(solution)/shard_map/all_to_all | solution.py:627
  35.1 0.5 collective-permute-start.14
  35.7 0.4 collective-permute-start.16
  36.1 0.7 collective-permute-done.13.refs_5_
  38.3 0.4 copy-done.27
  38.7 9.5 %operator.2 = (f32[8,128,128]{2,1,0:T(8,128)}, f32[8,128,128]{2,1,0:T(8,128)}, f32[8,128,128]{2,1,0:T(8,128)}, f32[8,128,128]{2,1,0:T(8,128)}) custom-call(s32[6,16]{1,0:T(8,128)} %bitcast.23, f32[16,6,128,128]{3,2,1,0:T(8,128)} %blocks_ref.3, f32[16,128,256]{2,1,0:T(8,128)} %bitcast.13, f32[2,128,256]{2,1,0:T(8,128)} %get-tuple-element.34.refs_1_, ...), custom_call_target="tpu_custom_call" | custom-call | tf_op jit(solution)/shard_map/operator/pallas_call | solution.py:374
  49.3 1.2 collective-permute-done.17
  50.6 1.2 slice_add_fusion
  51.8 0.6 collective-permute-start.20
  52.4 1.5 %collective-permute-start.19 = (f32[4,128,128]{2,1,0:T(8,128)S(1)}, f32[4,128,128]{2,1,0:T(8,128)S(1)}, u32[]{:S(2)}, u32[]{:S(2)}) collective-permute-start(f32[4,128,128]{2,1,0:T(8,128)S(1)} %get-tuple-element.61), channel_id=1, source_target_pairs={{0,2},{1,3},{2,0},{3,1},{4,6},{5,7},{6,4},{7,5},{8,10},{9,11},{10,... | collective-permute-start | bytes 786440 | tf_op jit(solution)/shard_map/ppermute | solution.py:595
  53.9 0.8 copy-done.15
  54.7 1.0 copy-done.13
  55.8 1.0 copy-done.16
  56.8 2.4 %far_part.2.refs_0_ = f32[8,128,128]{2,1,0:T(8,128)S(1)} custom-call(s32[2,8]{1,0:T(2,128)S(1)} %pad_add_fusion.refs_0_, s32[2,8]{1,0:T(2,128)S(1)} %get-tuple-element.30.refs_1_, s32[2,8]{1,0:T(2,128)S(1)} %collective-permute-done.2.refs_2_, s32[2,8]{1,0:T(2,128)S(1)} %collective-permute-done.3.refs_3_, f32[8,64,128]{2,1,0:T(8,128)S(1)} %bitcast.17, ...), custom_call_target="tpu_custom_call" | custom-call | flops 100663296 | bytes 4194304 | tf_op jit(solution)/shard_map/far_part/pallas_call | solution.py:225
  59.3 1.8 %collective-permute-done.20.refs_1_ = f32[4,128,128]{2,1,0:T(8,128)S(1)} collective-permute-done((f32[4,128,128]{2,1,0:T(8,128)S(1)}, f32[4,128,128]{2,1,0:T(8,128)S(1)}, u32[]{:S(2)}, u32[]{:S(2)}) %collective-permute-start.20) | collective-permute-done | bytes 262176 | tf_op jit(solution)/shard_map/ppermute | solution.py:595
  61.1 4.6 %collective-permute-start.21 = (f32[4,128,128]{2,1,0:T(8,128)S(1)}, f32[4,128,128]{2,1,0:T(8,128)}, u32[]{:S(2)}, u32[]{:S(2)}) collective-permute-start(f32[4,128,128]{2,1,0:T(8,128)S(1)} %add_half.3.gr_ref.refs_9_.refs_1_.refs_4_), channel_id=1, source_target_pairs={{0,4},{4,8},{8,12},{12,16},{16,20},{20,24},{24,28},{1,5},{5,9},{9,... | collective-permute-start | bytes 786440 | tf_op jit(solution)/shard_map/ppermute | solution.py:608
  65.8 0.5 collective-permute-start.24
  66.3 1.3 collective-permute-start.22
  67.6 1.6 %collective-permute-start.23 = (f32[4,128,128]{2,1,0:T(8,128)S(1)}, f32[4,128,128]{2,1,0:T(8,128)}, u32[]{:S(2)}, u32[]{:S(2)}) collective-permute-start(f32[4,128,128]{2,1,0:T(8,128)S(1)} %add_half.2.gl_ref.refs_8_.refs_0_.refs_3_), channel_id=1, source_target_pairs={{0,2},{1,3},{2,0},{3,1},{4,6},{5,7},{6,4},{7,5},{8,10},{9,11},{10,... | collective-permute-start | bytes 786440 | tf_op jit(solution)/shard_map/ppermute | solution.py:595
  69.3 3.1 %coefficients.3 = f32[8,2,64,128]{3,2,1,0:T(8,128)} custom-call(s32[2,8]{1,0:T(2,128)S(1)} %pad_add_fusion.refs_0_, s32[2,8]{1,0:T(2,128)S(1)} %get-tuple-element.30.refs_1_, s32[2,8]{1,0:T(2,128)S(1)} %collective-permute-done.2.refs_2_, s32[2,8]{1,0:T(2,128)S(1)} %collective-permute-done.3.refs_3_, f32[8,64,128]{2,1,0:T(8,128)S(1)} %bitcast.22, ...), custom_call_target="tpu_custom_call" | custom-call | flops 100663296 | bytes 4194304 | tf_op jit(solution)/shard_map/coefficients/pallas_call | solution.py:168
  72.4 0.6 collective-permute-start.25
  73.0 2.1 %collective-permute-done.24.refs_3_ = f32[4,128,128]{2,1,0:T(8,128)} collective-permute-done((f32[4,128,128]{2,1,0:T(8,128)S(1)}, f32[4,128,128]{2,1,0:T(8,128)}, u32[]{:S(2)}, u32[]{:S(2)}) %collective-permute-start.24) | collective-permute-done | bytes 262176 | tf_op jit(solution)/shard_map/ppermute | solution.py:595
  75.1 0.6 collective-permute-done.22.refs_9_
  75.7 2.2 %collective-permute-done.23.refs_2_ = f32[4,128,128]{2,1,0:T(8,128)} collective-permute-done((f32[4,128,128]{2,1,0:T(8,128)S(1)}, f32[4,128,128]{2,1,0:T(8,128)}, u32[]{:S(2)}, u32[]{:S(2)}) %collective-permute-start.23) | collective-permute-done | bytes 262176 | tf_op jit(solution)/shard_map/ppermute | solution.py:595
  77.9 0.5 collective-permute-start.29
  78.4 1.3 collective-permute-start.30
  79.8 6.5 %all-to-all-start.1 = ((f32[8,2,64,128]{3,2,1,0:T(8,128)}), f32[8,2,64,128]{3,2,1,0:T(8,128)S(1)}, u32[]{:S(2)}, u32[]{:S(2)}) async-start(f32[8,2,64,128]{3,2,1,0:T(8,128)} %coefficients.3), calls=%async_computation.1 | async-start | bytes 1048576 | tf_op jit(solution)/shard_map/all_to_all | solution.py:627
  87.6 0.9 collective-permute-done.28.refs_7_
  88.5 0.7 collective-permute-done.32.refs_13_
  89.2 0.7 copy-done.22
  89.9 0.7 copy-done.23
  90.7 10.0 %operator.3 = (f32[8,128,128]{2,1,0:T(8,128)}, f32[8,128,128]{2,1,0:T(8,128)}, f32[8,128,128]{2,1,0:T(8,128)}, f32[8,128,128]{2,1,0:T(8,128)}) custom-call(s32[6,16]{1,0:T(8,128)} %bitcast.24, f32[16,6,128,128]{3,2,1,0:T(8,128)} %blocks_ref.3, f32[4,128,128]{2,1,0:T(8,128)} %copy-done.4, f32[4,128,128]{2,1,0:T(8,128)} %copy-done.1, ...), custom_call_target="tpu_custom_call" | custom-call | tf_op jit(solution)/shard_map/operator/pallas_call | solution.py:374
  101.4 1.6 %collective-permute-done.35 = f32[8,128,128]{2,1,0:T(8,128)} collective-permute-done((f32[8,128,128]{2,1,0:T(8,128)}, f32[8,128,128]{2,1,0:T(8,128)}, u32[]{:S(2)}, u32[]{:S(2)}) %collective-permute-start.35) | collective-permute-done | bytes 524320 | tf_op jit(solution)/shard_map/ppermute | solution.py:590
  103.0 1.3 add.37
  104.2 1.6 %collective-permute-start.37 = (f32[8,128,128]{2,1,0:T(8,128)S(1)}, f32[8,128,128]{2,1,0:T(8,128)S(1)}, u32[]{:S(2)}, u32[]{:S(2)}) collective-permute-start(f32[8,128,128]{2,1,0:T(8,128)S(1)} %add.37), channel_id=1, source_target_pairs={{0,2},{1,3},{2,0},{3,1},{4,6},{5,7},{6,4},{7,5},{8,10},{9,11},{10,... | collective-permute-start | bytes 1572872 | tf_op jit(solution)/shard_map/ppermute | solution.py:595
  105.8 0.9 copy-done.2
  106.8 0.9 copy-done.5
  108.0 2.4 %far_part.3.refs_0_ = f32[8,128,128]{2,1,0:T(8,128)S(1)} custom-call(s32[2,8]{1,0:T(2,128)S(1)} %pad_add_fusion.refs_0_, s32[2,8]{1,0:T(2,128)S(1)} %get-tuple-element.30.refs_1_, s32[2,8]{1,0:T(2,128)S(1)} %collective-permute-done.2.refs_2_, s32[2,8]{1,0:T(2,128)S(1)} %collective-permute-done.3.refs_3_, f32[8,64,128]{2,1,0:T(8,128)S(1)} %bitcast.18, ...), custom_call_target="tpu_custom_call" | custom-call | flops 100663296 | bytes 4194304 | tf_op jit(solution)/shard_map/far_part/pallas_call | solution.py:225
  110.4 7.8 %collective-permute-done.37.refs_1_ = f32[8,128,128]{2,1,0:T(8,128)S(1)} collective-permute-done((f32[8,128,128]{2,1,0:T(8,128)S(1)}, f32[8,128,128]{2,1,0:T(8,128)S(1)}, u32[]{:S(2)}, u32[]{:S(2)}) %collective-permute-start.37) | collective-permute-done | bytes 524320 | tf_op jit(solution)/shard_map/ppermute | solution.py:595
  118.6 1.6 %collective-permute-start.38 = (f32[8,128]{1,0:T(8,128)S(1)}, f32[8,128]{1,0:T(8,128)S(1)}, u32[]{:S(2)}, u32[]{:S(2)}) collective-permute-start(f32[8,128]{1,0:T(8,128)S(1)} %get-tuple-element.54), channel_id=1, source_target_pairs={{0,4},{4,0},{8,12},{12,8},{16,20},{20,16},{24,28},{28,24},{1,5},{5... | collective-permute-start | bytes 12296 | tf_op jit(solution)/shard_map/ppermute | solution.py:619
  120.2 2.0 %collective-permute-done.38 = f32[8,128]{1,0:T(8,128)S(1)} collective-permute-done((f32[8,128]{1,0:T(8,128)S(1)}, f32[8,128]{1,0:T(8,128)S(1)}, u32[]{:S(2)}, u32[]{:S(2)}) %collective-permute-start.38) | collective-permute-done | bytes 4128 | tf_op jit(solution)/shard_map/ppermute | solution.py:619
  122.3 2.0 %collective-permute-start.39 = (f32[8,128]{1,0:T(8,128)S(1)}, f32[8,128]{1,0:T(8,128)S(1)}, u32[]{:S(2)}, u32[]{:S(2)}) collective-permute-start(f32[8,128]{1,0:T(8,128)S(1)} %add.38), channel_id=1, source_target_pairs={{0,8},{4,12},{8,0},{12,4},{16,24},{20,28},{24,16},{28,20},{1,9},{5... | collective-permute-start | bytes 12296 | tf_op jit(solution)/shard_map/ppermute | solution.py:619
  124.2 1.7 %collective-permute-done.39 = f32[8,128]{1,0:T(8,128)S(1)} collective-permute-done((f32[8,128]{1,0:T(8,128)S(1)}, f32[8,128]{1,0:T(8,128)S(1)}, u32[]{:S(2)}, u32[]{:S(2)}) %collective-permute-start.39) | collective-permute-done | bytes 4128 | tf_op jit(solution)/shard_map/ppermute | solution.py:619
  125.9 2.9 %collective-permute-start.40 = (f32[8,128]{1,0:T(8,128)S(1)}, f32[8,128]{1,0:T(8,128)S(1)}, u32[]{:S(2)}, u32[]{:S(2)}) collective-permute-start(f32[8,128]{1,0:T(8,128)S(1)} %add.39.refs_0_), channel_id=1, source_target_pairs={{0,16},{4,20},{8,24},{12,28},{16,0},{20,4},{24,8},{28,12},{1,17},{... | collective-permute-start | bytes 12296 | tf_op jit(solution)/shard_map/ppermute | solution.py:619
  128.7 1.6 %collective-permute-done.40.refs_1_ = f32[8,128]{1,0:T(8,128)S(1)} collective-permute-done((f32[8,128]{1,0:T(8,128)S(1)}, f32[8,128]{1,0:T(8,128)S(1)}, u32[]{:S(2)}, u32[]{:S(2)}) %collective-permute-start.40) | collective-permute-done | bytes 4128 | tf_op jit(solution)/shard_map/ppermute | solution.py:619
  130.4 1.4 %finish.1 = (f32[64,2048]{1,0:T(8,128)}, f32[64,2048]{1,0:T(8,128)}) custom-call(f32[8,128]{1,0:T(8,128)S(1)} %add.39.refs_0_, f32[8,128]{1,0:T(8,128)S(1)} %collective-permute-done.40.refs_1_, f32[8,128,128]{2,1,0:T(8,128)S(1)} %pack.1.refs_8_.b_ref.refs_2_, f32[4,128,128]{2,1,0:T(8,128)S(1)} %copy-done.6, f32[4,128,128]{2,1,0:T(8,128)S(1)} %copy-done.3, ...), custom_call_target="tpu_custom_call" | custom-call | flops 1048576 | bytes 3670016 | tf_op jit(solution)/shard_map/finish/pallas_call | solution.py:557
  (98 shorter events, 6.0 us)
Async XLA Ops:
  1.7 10.4 %collective-permute-start.4 = (f32[2,128,256]{2,1,0:T(8,128)S(1)}, f32[2,128,256]{2,1,0:T(8,128)}, u32[]{:S(2)}, u32[]{:S(2)}) collective-permute-start(f32[2,128,256]{2,1,0:T(8,128)S(1)} %get-tuple-element.58), channel_id=1, source_target_pairs={{0,4},{4,8},{8,12},{12,16},{16,20},{20,24},{24,28},{1,5},{5,9},{9,... | collective-permute-start | bytes 786440 | tf_op jit(solution)/shard_map/ppermute | solution.py:608
  7.3 9.4 %collective-permute-start.5 = (f32[8,64,128]{2,1,0:T(8,128)}, f32[8,64,128]{2,1,0:T(8,128)S(1)}, u32[]{:S(2)}, u32[]{:S(2)}) collective-permute-start(f32[8,64,128]{2,1,0:T(8,128)} %bitcast.15), channel_id=1, source_target_pairs={{0,2},{1,3},{2,0},{3,1},{4,6},{5,7},{6,4},{7,5},{8,10},{9,11},{10,... | collective-permute-start | bytes 786440 | tf_op jit(solution)/shard_map/ppermute | solution.py:595
  8.8 13.5 %collective-permute-start.10 = (f32[8,64,128]{2,1,0:T(8,128)}, f32[8,64,128]{2,1,0:T(8,128)S(1)}, u32[]{:S(2)}, u32[]{:S(2)}) collective-permute-start(f32[8,64,128]{2,1,0:T(8,128)} %bitcast.19), channel_id=1, source_target_pairs={{0,2},{1,3},{2,0},{3,1},{4,6},{5,7},{6,4},{7,5},{8,10},{9,11},{10,... | collective-permute-start | bytes 786440 | tf_op jit(solution)/shard_map/ppermute | solution.py:595
  9.3 16.0 %collective-permute-start.11 = (f32[8,64,128]{2,1,0:T(8,128)}, f32[8,64,128]{2,1,0:T(8,128)S(1)}, u32[]{:S(2)}, u32[]{:S(2)}) collective-permute-start(f32[8,64,128]{2,1,0:T(8,128)} %bitcast.20), channel_id=1, source_target_pairs={{0,1},{1,0},{2,3},{3,2},{4,5},{5,4},{6,7},{7,6},{8,9},{9,8},{10,11... | collective-permute-start | bytes 786440 | tf_op jit(solution)/shard_map/ppermute | solution.py:590
  9.3 13.1 %collective-permute-start = (f32[2,128,256]{2,1,0:T(8,128)S(1)}, f32[2,128,256]{2,1,0:T(8,128)}, u32[]{:S(2)}, u32[]{:S(2)}) collective-permute-start(f32[2,128,256]{2,1,0:T(8,128)S(1)} %get-tuple-element.59), channel_id=1, source_target_pairs={{4,0},{8,4},{12,8},{16,12},{20,16},{24,20},{28,24},{5,1},{9,5},{13... | collective-permute-start | bytes 786440 | tf_op jit(solution)/shard_map/ppermute | solution.py:612
  12.1 10.3 %collective-permute-start.1 = (s32[2,8]{1,0:T(2,128)S(1)}, s32[2,8]{1,0:T(2,128)S(1)}, u32[]{:S(2)}, u32[]{:S(2)}) collective-permute-start(s32[2,8]{1,0:T(2,128)S(1)} %pad_add_fusion.refs_0_), channel_id=1, source_target_pairs={{0,2},{1,3},{2,0},{3,1},{4,6},{5,7},{6,4},{7,5},{8,10},{9,11},{10,... | collective-permute-start | bytes 200 | tf_op jit(solution)/shard_map/ppermute | solution.py:595
  16.7 7.5 %copy-start = (f32[2048,256]{1,0:T(8,128)S(1)}, f32[2048,256]{1,0:T(8,128)}, u32[]{:S(2)}) copy-start(f32[2048,256]{1,0:T(8,128)} %param.7) | copy-start | bytes 6291460
  16.7 18.3 %collective-permute-start.8 = (f32[2,128,256]{2,1,0:T(8,128)}, f32[2,128,256]{2,1,0:T(8,128)}, u32[]{:S(2)}, u32[]{:S(2)}) collective-permute-start(f32[2,128,256]{2,1,0:T(8,128)} %get-tuple-element.34.refs_1_), channel_id=1, source_target_pairs={{0,2},{1,3},{2,0},{3,1},{4,6},{5,7},{6,4},{7,5},{8,10},{9,11},{10,... | collective-permute-start | bytes 786440 | tf_op jit(solution)/shard_map/ppermute | solution.py:595
  22.4 3.9 %collective-permute-start.12 = (f32[8,64,128]{2,1,0:T(8,128)S(1)}, f32[8,64,128]{2,1,0:T(8,128)S(1)}, u32[]{:S(2)}, u32[]{:S(2)}) collective-permute-start(f32[8,64,128]{2,1,0:T(8,128)S(1)} %collective-permute-done.10.refs_5_), channel_id=1, source_target_pairs={{0,1},{1,0},{2,3},{3,2},{4,5},{5,4},{6,7},{7,6},{8,9},{9,8},{10,11... | collective-permute-start | bytes 786440 | tf_op jit(solution)/shard_map/ppermute | solution.py:590
  22.4 3.9 %copy-start.8 = (f32[1,8,1,128,64]{3,4,2,1,0:T(8,128)S(1)}, f32[1,8,1,128,64]{3,4,2,1,0:T(8,128)}, u32[]{:S(2)}) copy-start(f32[1,8,1,128,64]{3,4,2,1,0:T(8,128)} %param.13) | copy-start | bytes 786436
  22.4 12.6 %collective-permute-start.9 = (f32[2,128,256]{2,1,0:T(8,128)}, f32[2,128,256]{2,1,0:T(8,128)}, u32[]{:S(2)}, u32[]{:S(2)}) collective-permute-start(f32[2,128,256]{2,1,0:T(8,128)} %get-tuple-element.35.refs_2_), channel_id=1, source_target_pairs={{0,2},{1,3},{2,0},{3,1},{4,6},{5,7},{6,4},{7,5},{8,10},{9,11},{10,... | collective-permute-start | bytes 786440 | tf_op jit(solution)/shard_map/ppermute | solution.py:595
  24.0 1.1 collective-permute-start.2
  25.1 1.1 collective-permute-start.3
  30.8 19.8 %all-to-all-start = ((f32[8,2,64,128]{3,2,1,0:T(8,128)}), f32[8,2,64,128]{3,2,1,0:T(8,128)S(1)}, u32[]{:S(2)}, u32[]{:S(2)}) async-start(f32[8,2,64,128]{3,2,1,0:T(8,128)} %coefficients.2), calls=%async_computation | async-start | bytes 1048576 | tf_op jit(solution)/shard_map/all_to_all | solution.py:627
  35.0 1.8 %collective-permute-start.13 = (f32[2,128,256]{2,1,0:T(8,128)}, f32[2,128,256]{2,1,0:T(8,128)S(1)}, u32[]{:S(2)}, u32[]{:S(2)}) collective-permute-start(f32[2,128,256]{2,1,0:T(8,128)} %get-tuple-element.34.refs_1_), channel_id=1, source_target_pairs={{0,1},{1,0},{2,3},{3,2},{4,5},{5,4},{6,7},{7,6},{8,9},{9,8},{10,11... | collective-permute-start | bytes 786440 | tf_op jit(solution)/shard_map/ppermute | solution.py:590
  35.1 2.1 %collective-permute-start.14 = (f32[2,128,256]{2,1,0:T(8,128)}, f32[2,128,256]{2,1,0:T(8,128)S(1)}, u32[]{:S(2)}, u32[]{:S(2)}) collective-permute-start(f32[2,128,256]{2,1,0:T(8,128)} %get-tuple-element.35.refs_2_), channel_id=1, source_target_pairs={{0,1},{1,0},{2,3},{3,2},{4,5},{5,4},{6,7},{7,6},{8,9},{9,8},{10,11... | collective-permute-start | bytes 786440 | tf_op jit(solution)/shard_map/ppermute | solution.py:590
  35.6 2.0 %collective-permute-start.15 = (f32[2,128,256]{2,1,0:T(8,128)}, f32[2,128,256]{2,1,0:T(8,128)S(1)}, u32[]{:S(2)}, u32[]{:S(2)}) collective-permute-start(f32[2,128,256]{2,1,0:T(8,128)} %collective-permute-done.8.refs_3_), channel_id=1, source_target_pairs={{0,1},{1,0},{2,3},{3,2},{4,5},{5,4},{6,7},{7,6},{8,9},{9,8},{10,11... | collective-permute-start | bytes 786440 | tf_op jit(solution)/shard_map/ppermute | solution.py:590
  35.7 2.3 %collective-permute-start.16 = (f32[2,128,256]{2,1,0:T(8,128)}, f32[2,128,256]{2,1,0:T(8,128)S(1)}, u32[]{:S(2)}, u32[]{:S(2)}) collective-permute-start(f32[2,128,256]{2,1,0:T(8,128)} %collective-permute-done.9.refs_4_), channel_id=1, source_target_pairs={{0,1},{1,0},{2,3},{3,2},{4,5},{5,4},{6,7},{7,6},{8,9},{9,8},{10,11... | collective-permute-start | bytes 786440 | tf_op jit(solution)/shard_map/ppermute | solution.py:590
  36.9 1.1 copy-start.24
  38.7 10.1 %copy-start.7 = (f32[1,8,1,128,64]{3,4,2,1,0:T(8,128)S(1)}, f32[1,8,1,128,64]{3,4,2,1,0:T(8,128)}, u32[]{:S(2)}) copy-start(f32[1,8,1,128,64]{3,4,2,1,0:T(8,128)} %param.12) | copy-start | bytes 786436
  48.2 2.3 %collective-permute-start.17 = (f32[8,128,128]{2,1,0:T(8,128)}, f32[8,128,128]{2,1,0:T(8,128)}, u32[]{:S(2)}, u32[]{:S(2)}) collective-permute-start(f32[8,128,128]{2,1,0:T(8,128)} %get-tuple-element.38), channel_id=1, source_target_pairs={{0,1},{1,0},{2,3},{3,2},{4,5},{5,4},{6,7},{7,6},{8,9},{9,8},{10,11... | collective-permute-start | bytes 1572872 | tf_op jit(solution)/shard_map/ppermute | solution.py:590
  48.4 5.5 %collective-permute-start.18 = (f32[8,128,128]{2,1,0:T(8,128)}, f32[8,128,128]{2,1,0:T(8,128)S(1)}, u32[]{:S(2)}, u32[]{:S(2)}) collective-permute-start(f32[8,128,128]{2,1,0:T(8,128)} %get-tuple-element.41), channel_id=1, source_target_pairs={{0,1},{1,0},{2,3},{3,2},{4,5},{5,4},{6,7},{7,6},{8,9},{9,8},{10,11... | collective-permute-start | bytes 1572872 | tf_op jit(solution)/shard_map/ppermute | solution.py:590
  48.8 5.1 %collective-permute-start.6 = (f32[8,64,128]{2,1,0:T(8,128)S(1)}, f32[8,64,128]{2,1,0:T(8,128)S(1)}, u32[]{:S(2)}, u32[]{:S(2)}) collective-permute-start(f32[8,64,128]{2,1,0:T(8,128)S(1)} %bitcast.16), channel_id=1, source_target_pairs={{0,1},{1,0},{2,3},{3,2},{4,5},{5,4},{6,7},{7,6},{8,9},{9,8},{10,11... | collective-permute-start | bytes 786440 | tf_op jit(solution)/shard_map/ppermute | solution.py:590
  49.0 5.0 %collective-permute-start.7 = (f32[8,64,128]{2,1,0:T(8,128)S(1)}, f32[8,64,128]{2,1,0:T(8,128)S(1)}, u32[]{:S(2)}, u32[]{:S(2)}) collective-permute-start(f32[8,64,128]{2,1,0:T(8,128)S(1)} %get-tuple-element.31.refs_5_), channel_id=1, source_target_pairs={{0,1},{1,0},{2,3},{3,2},{4,5},{5,4},{6,7},{7,6},{8,9},{9,8},{10,11... | collective-permute-start | bytes 786440 | tf_op jit(solution)/shard_map/ppermute | solution.py:590
  51.8 9.2 %collective-permute-start.20 = (f32[4,128,128]{2,1,0:T(8,128)S(1)}, f32[4,128,128]{2,1,0:T(8,128)S(1)}, u32[]{:S(2)}, u32[]{:S(2)}) collective-permute-start(f32[4,128,128]{2,1,0:T(8,128)S(1)} %get-tuple-element.60), channel_id=1, source_target_pairs={{0,2},{1,3},{2,0},{3,1},{4,6},{5,7},{6,4},{7,5},{8,10},{9,11},{10,... | collective-permute-start | bytes 786440 | tf_op jit(solution)/shard_map/ppermute | solution.py:595
  52.4 13.9 %collective-permute-start.19 = (f32[4,128,128]{2,1,0:T(8,128)S(1)}, f32[4,128,128]{2,1,0:T(8,128)S(1)}, u32[]{:S(2)}, u32[]{:S(2)}) collective-permute-start(f32[4,128,128]{2,1,0:T(8,128)S(1)} %get-tuple-element.61), channel_id=1, source_target_pairs={{0,2},{1,3},{2,0},{3,1},{4,6},{5,7},{6,4},{7,5},{8,10},{9,11},{10,... | collective-permute-start | bytes 786440 | tf_op jit(solution)/shard_map/ppermute | solution.py:595
  53.9 0.8 copy-start.15
  54.7 1.0 copy-start.13
  55.8 1.0 copy-start.16
  56.8 12.4 %copy-start.10 = (f32[8,64,128]{2,1,0:T(8,128)S(1)}, f32[8,64,128]{2,1,0:T(8,128)}, u32[]{:S(2)}) copy-start(f32[8,64,128]{2,1,0:T(8,128)} %copy-done.9) | copy-start | bytes 786436
  56.8 12.4 %copy-start.12 = (f32[8,64,128]{2,1,0:T(8,128)S(1)}, f32[8,64,128]{2,1,0:T(8,128)}, u32[]{:S(2)}) copy-start(f32[8,64,128]{2,1,0:T(8,128)} %copy-done.11) | copy-start | bytes 786436
  61.1 29.5 %copy-start.1 = (f32[4,128,128]{2,1,0:T(8,128)}, f32[4,128,128]{2,1,0:T(8,128)S(1)}, u32[]{:S(2)}) copy-start(f32[4,128,128]{2,1,0:T(8,128)S(1)} %add_half.3.gr_ref.refs_9_.refs_1_.refs_4_) | copy-start | bytes 786436
  61.1 11.3 %collective-permute-start.21 = (f32[4,128,128]{2,1,0:T(8,128)S(1)}, f32[4,128,128]{2,1,0:T(8,128)}, u32[]{:S(2)}, u32[]{:S(2)}) collective-permute-start(f32[4,128,128]{2,1,0:T(8,128)S(1)} %add_half.3.gr_ref.refs_9_.refs_1_.refs_4_), channel_id=1, source_target_pairs={{0,4},{4,8},{8,12},{12,16},{16,20},{20,24},{24,28},{1,5},{5,9},{9,... | collective-permute-start | bytes 786440 | tf_op jit(solution)/shard_map/ppermute | solution.py:608
  65.8 9.3 %collective-permute-start.24 = (f32[4,128,128]{2,1,0:T(8,128)S(1)}, f32[4,128,128]{2,1,0:T(8,128)}, u32[]{:S(2)}, u32[]{:S(2)}) collective-permute-start(f32[4,128,128]{2,1,0:T(8,128)S(1)} %add_half.3.gr_ref.refs_9_.refs_1_.refs_4_), channel_id=1, source_target_pairs={{0,2},{1,3},{2,0},{3,1},{4,6},{5,7},{6,4},{7,5},{8,10},{9,11},{10,... | collective-permute-start | bytes 786440 | tf_op jit(solution)/shard_map/ppermute | solution.py:595
  66.3 24.3 %copy-start.4 = (f32[4,128,128]{2,1,0:T(8,128)}, f32[4,128,128]{2,1,0:T(8,128)S(1)}, u32[]{:S(2)}) copy-start(f32[4,128,128]{2,1,0:T(8,128)S(1)} %add_half.2.gl_ref.refs_8_.refs_0_.refs_3_) | copy-start | bytes 786436
  66.3 9.4 %collective-permute-start.22 = (f32[4,128,128]{2,1,0:T(8,128)S(1)}, f32[4,128,128]{2,1,0:T(8,128)}, u32[]{:S(2)}, u32[]{:S(2)}) collective-permute-start(f32[4,128,128]{2,1,0:T(8,128)S(1)} %add_half.2.gl_ref.refs_8_.refs_0_.refs_3_), channel_id=1, source_target_pairs={{4,0},{8,4},{12,8},{16,12},{20,16},{24,20},{28,24},{5,1},{9,5},{13... | collective-permute-start | bytes 786440 | tf_op jit(solution)/shard_map/ppermute | solution.py:612
  67.6 10.2 %collective-permute-start.23 = (f32[4,128,128]{2,1,0:T(8,128)S(1)}, f32[4,128,128]{2,1,0:T(8,128)}, u32[]{:S(2)}, u32[]{:S(2)}) collective-permute-start(f32[4,128,128]{2,1,0:T(8,128)S(1)} %add_half.2.gl_ref.refs_8_.refs_0_.refs_3_), channel_id=1, source_target_pairs={{0,2},{1,3},{2,0},{3,1},{4,6},{5,7},{6,4},{7,5},{8,10},{9,11},{10,... | collective-permute-start | bytes 786440 | tf_op jit(solution)/shard_map/ppermute | solution.py:595
  69.2 17.0 %collective-permute-start.26 = (f32[4,128,128]{2,1,0:T(8,128)S(1)}, f32[4,128,128]{2,1,0:T(8,128)}, u32[]{:S(2)}, u32[]{:S(2)}) collective-permute-start(f32[4,128,128]{2,1,0:T(8,128)S(1)} %add_half.3.gr_ref.refs_9_.refs_1_.refs_4_), channel_id=1, source_target_pairs={{0,1},{1,0},{2,3},{3,2},{4,5},{5,4},{6,7},{7,6},{8,9},{9,8},{10,11... | collective-permute-start | bytes 786440 | tf_op jit(solution)/shard_map/ppermute | solution.py:590
  72.4 14.1 %collective-permute-start.25 = (f32[4,128,128]{2,1,0:T(8,128)S(1)}, f32[4,128,128]{2,1,0:T(8,128)S(1)}, u32[]{:S(2)}, u32[]{:S(2)}) collective-permute-start(f32[4,128,128]{2,1,0:T(8,128)S(1)} %add_half.2.gl_ref.refs_8_.refs_0_.refs_3_), channel_id=1, source_target_pairs={{0,1},{1,0},{2,3},{3,2},{4,5},{5,4},{6,7},{7,6},{8,9},{9,8},{10,11... | collective-permute-start | bytes 786440 | tf_op jit(solution)/shard_map/ppermute | solution.py:590
  77.9 9.0 %collective-permute-start.29 = (f32[4,128,128]{2,1,0:T(8,128)}, f32[4,128,128]{2,1,0:T(8,128)S(1)}, u32[]{:S(2)}, u32[]{:S(2)}) collective-permute-start(f32[4,128,128]{2,1,0:T(8,128)} %collective-permute-done.21.refs_8_), channel_id=1, source_target_pairs={{0,2},{1,3},{2,0},{3,1},{4,6},{5,7},{6,4},{7,5},{8,10},{9,11},{10,... | collective-permute-start | bytes 786440 | tf_op jit(solution)/shard_map/ppermute | solution.py:595
  78.4 8.6 %collective-permute-start.30 = (f32[4,128,128]{2,1,0:T(8,128)}, f32[4,128,128]{2,1,0:T(8,128)S(1)}, u32[]{:S(2)}, u32[]{:S(2)}) collective-permute-start(f32[4,128,128]{2,1,0:T(8,128)} %collective-permute-done.23.refs_2_), channel_id=1, source_target_pairs={{4,0},{8,4},{12,8},{16,12},{20,16},{24,20},{28,24},{5,1},{9,5},{13... | collective-permute-start | bytes 786440 | tf_op jit(solution)/shard_map/ppermute | solution.py:612
  79.7 7.7 %collective-permute-start.27 = (f32[4,128,128]{2,1,0:T(8,128)}, f32[4,128,128]{2,1,0:T(8,128)}, u32[]{:S(2)}, u32[]{:S(2)}) collective-permute-start(f32[4,128,128]{2,1,0:T(8,128)} %collective-permute-done.23.refs_2_), channel_id=1, source_target_pairs={{0,1},{1,0},{2,3},{3,2},{4,5},{5,4},{6,7},{7,6},{8,9},{9,8},{10,11... | collective-permute-start | bytes 786440 | tf_op jit(solution)/shard_map/ppermute | solution.py:590
  79.8 21.6 %all-to-all-start.1 = ((f32[8,2,64,128]{3,2,1,0:T(8,128)}), f32[8,2,64,128]{3,2,1,0:T(8,128)S(1)}, u32[]{:S(2)}, u32[]{:S(2)}) async-start(f32[8,2,64,128]{3,2,1,0:T(8,128)} %coefficients.3), calls=%async_computation.1 | async-start | bytes 1048576 | tf_op jit(solution)/shard_map/all_to_all | solution.py:627
  86.3 2.2 %collective-permute-start.31 = (f32[4,128,128]{2,1,0:T(8,128)}, f32[4,128,128]{2,1,0:T(8,128)S(1)}, u32[]{:S(2)}, u32[]{:S(2)}) collective-permute-start(f32[4,128,128]{2,1,0:T(8,128)} %collective-permute-done.21.refs_8_), channel_id=1, source_target_pairs={{0,1},{1,0},{2,3},{3,2},{4,5},{5,4},{6,7},{7,6},{8,9},{9,8},{10,11... | collective-permute-start | bytes 786440 | tf_op jit(solution)/shard_map/ppermute | solution.py:590
  86.5 4.1 %copy-start.17 = (f32[4,128,128]{2,1,0:T(8,128)}, f32[4,128,128]{2,1,0:T(8,128)S(1)}, u32[]{:S(2)}) copy-start(f32[4,128,128]{2,1,0:T(8,128)S(1)} %collective-permute-done.25.refs_4_) | copy-start | bytes 786436
  86.5 1.9 %collective-permute-start.28 = (f32[4,128,128]{2,1,0:T(8,128)}, f32[4,128,128]{2,1,0:T(8,128)S(1)}, u32[]{:S(2)}, u32[]{:S(2)}) collective-permute-start(f32[4,128,128]{2,1,0:T(8,128)} %collective-permute-done.24.refs_3_), channel_id=1, source_target_pairs={{0,1},{1,0},{2,3},{3,2},{4,5},{5,4},{6,7},{7,6},{8,9},{9,8},{10,11... | collective-permute-start | bytes 786440 | tf_op jit(solution)/shard_map/ppermute | solution.py:590
  86.8 3.8 %copy-start.18 = (f32[4,128,128]{2,1,0:T(8,128)}, f32[4,128,128]{2,1,0:T(8,128)S(1)}, u32[]{:S(2)}) copy-start(f32[4,128,128]{2,1,0:T(8,128)S(1)} %collective-permute-done.29.refs_10_) | copy-start | bytes 786436
  86.8 2.3 %collective-permute-start.32 = (f32[4,128,128]{2,1,0:T(8,128)}, f32[4,128,128]{2,1,0:T(8,128)S(1)}, u32[]{:S(2)}, u32[]{:S(2)}) collective-permute-start(f32[4,128,128]{2,1,0:T(8,128)} %collective-permute-done.22.refs_9_), channel_id=1, source_target_pairs={{0,1},{1,0},{2,3},{3,2},{4,5},{5,4},{6,7},{7,6},{8,9},{9,8},{10,11... | collective-permute-start | bytes 786440 | tf_op jit(solution)/shard_map/ppermute | solution.py:590
  87.1 3.6 %copy-start.19 = (f32[4,128,128]{2,1,0:T(8,128)}, f32[4,128,128]{2,1,0:T(8,128)S(1)}, u32[]{:S(2)}) copy-start(f32[4,128,128]{2,1,0:T(8,128)S(1)} %collective-permute-done.30.refs_11_) | copy-start | bytes 786436
  87.1 2.1 %collective-permute-start.33 = (f32[4,128,128]{2,1,0:T(8,128)S(1)}, f32[4,128,128]{2,1,0:T(8,128)S(1)}, u32[]{:S(2)}, u32[]{:S(2)}) collective-permute-start(f32[4,128,128]{2,1,0:T(8,128)S(1)} %collective-permute-done.29.refs_10_), channel_id=1, source_target_pairs={{0,1},{1,0},{2,3},{3,2},{4,5},{5,4},{6,7},{7,6},{8,9},{9,8},{10,11... | collective-permute-start | bytes 786440 | tf_op jit(solution)/shard_map/ppermute | solution.py:590
  87.4 3.3 %collective-permute-start.34 = (f32[4,128,128]{2,1,0:T(8,128)S(1)}, f32[4,128,128]{2,1,0:T(8,128)}, u32[]{:S(2)}, u32[]{:S(2)}) collective-permute-start(f32[4,128,128]{2,1,0:T(8,128)S(1)} %collective-permute-done.30.refs_11_), channel_id=1, source_target_pairs={{0,1},{1,0},{2,3},{3,2},{4,5},{5,4},{6,7},{7,6},{8,9},{9,8},{10,11... | collective-permute-start | bytes 786440 | tf_op jit(solution)/shard_map/ppermute | solution.py:590
  88.4 2.2 %copy-start.21 = (f32[4,128,128]{2,1,0:T(8,128)}, f32[4,128,128]{2,1,0:T(8,128)S(1)}, u32[]{:S(2)}) copy-start(f32[4,128,128]{2,1,0:T(8,128)S(1)} %collective-permute-done.28.refs_7_) | copy-start | bytes 786436
  88.4 2.2 %copy-start.20 = (f32[4,128,128]{2,1,0:T(8,128)}, f32[4,128,128]{2,1,0:T(8,128)S(1)}, u32[]{:S(2)}) copy-start(f32[4,128,128]{2,1,0:T(8,128)S(1)} %collective-permute-done.31.refs_12_) | copy-start | bytes 786436
  100.6 7.3 %copy-start.14 = (f32[8,128,128]{2,1,0:T(8,128)S(1)}, f32[8,128,128]{2,1,0:T(8,128)}, u32[]{:S(2)}) copy-start(f32[8,128,128]{2,1,0:T(8,128)} %get-tuple-element.50.refs_9_) | copy-start | bytes 1572868
  100.7 2.3 %collective-permute-start.35 = (f32[8,128,128]{2,1,0:T(8,128)}, f32[8,128,128]{2,1,0:T(8,128)}, u32[]{:S(2)}, u32[]{:S(2)}) collective-permute-start(f32[8,128,128]{2,1,0:T(8,128)} %get-tuple-element.48), channel_id=1, source_target_pairs={{0,1},{1,0},{2,3},{3,2},{4,5},{5,4},{6,7},{7,6},{8,9},{9,8},{10,11... | collective-permute-start | bytes 1572872 | tf_op jit(solution)/shard_map/ppermute | solution.py:590
  100.9 7.1 %collective-permute-start.36 = (f32[8,128,128]{2,1,0:T(8,128)}, f32[8,128,128]{2,1,0:T(8,128)S(1)}, u32[]{:S(2)}, u32[]{:S(2)}) collective-permute-start(f32[8,128,128]{2,1,0:T(8,128)} %get-tuple-element.51), channel_id=1, source_target_pairs={{0,1},{1,0},{2,3},{3,2},{4,5},{5,4},{6,7},{7,6},{8,9},{9,8},{10,11... | collective-permute-start | bytes 1572872 | tf_op jit(solution)/shard_map/ppermute | solution.py:590
  104.2 14.0 %collective-permute-start.37 = (f32[8,128,128]{2,1,0:T(8,128)S(1)}, f32[8,128,128]{2,1,0:T(8,128)S(1)}, u32[]{:S(2)}, u32[]{:S(2)}) collective-permute-start(f32[8,128,128]{2,1,0:T(8,128)S(1)} %add.37), channel_id=1, source_target_pairs={{0,2},{1,3},{2,0},{3,1},{4,6},{5,7},{6,4},{7,5},{8,10},{9,11},{10,... | collective-permute-start | bytes 1572872 | tf_op jit(solution)/shard_map/ppermute | solution.py:595
  105.8 0.9 copy-start.2
  106.8 0.9 copy-start.5
  107.7 10.5 %copy-start.3 = (f32[4,128,128]{2,1,0:T(8,128)S(1)}, f32[4,128,128]{2,1,0:T(8,128)}, u32[]{:S(2)}) copy-start(f32[4,128,128]{2,1,0:T(8,128)} %copy-done.1) | copy-start | bytes 786436
  107.7 10.5 %copy-start.6 = (f32[4,128,128]{2,1,0:T(8,128)S(1)}, f32[4,128,128]{2,1,0:T(8,128)}, u32[]{:S(2)}) copy-start(f32[4,128,128]{2,1,0:T(8,128)} %copy-done.4) | copy-start | bytes 786436
  118.6 3.7 %collective-permute-start.38 = (f32[8,128]{1,0:T(8,128)S(1)}, f32[8,128]{1,0:T(8,128)S(1)}, u32[]{:S(2)}, u32[]{:S(2)}) collective-permute-start(f32[8,128]{1,0:T(8,128)S(1)} %get-tuple-element.54), channel_id=1, source_target_pairs={{0,4},{4,0},{8,12},{12,8},{16,20},{20,16},{24,28},{28,24},{1,5},{5... | collective-permute-start | bytes 12296 | tf_op jit(solution)/shard_map/ppermute | solution.py:619
  122.3 3.6 %collective-permute-start.39 = (f32[8,128]{1,0:T(8,128)S(1)}, f32[8,128]{1,0:T(8,128)S(1)}, u32[]{:S(2)}, u32[]{:S(2)}) collective-permute-start(f32[8,128]{1,0:T(8,128)S(1)} %add.38), channel_id=1, source_target_pairs={{0,8},{4,12},{8,0},{12,4},{16,24},{20,28},{24,16},{28,20},{1,9},{5... | collective-permute-start | bytes 12296 | tf_op jit(solution)/shard_map/ppermute | solution.py:619
  125.9 4.5 %collective-permute-start.40 = (f32[8,128]{1,0:T(8,128)S(1)}, f32[8,128]{1,0:T(8,128)S(1)}, u32[]{:S(2)}, u32[]{:S(2)}) collective-permute-start(f32[8,128]{1,0:T(8,128)S(1)} %add.39.refs_0_), channel_id=1, source_target_pairs={{0,16},{4,20},{8,24},{12,28},{16,0},{20,4},{24,8},{28,12},{1,17},{... | collective-permute-start | bytes 12296 | tf_op jit(solution)/shard_map/ppermute | solution.py:619
  (7 other events, 5.0 us)

commit v8 on v7

--- a/solution.py
+++ b/solution.py
@@ -686,7 +686,7 @@
     heads, tails = heads[:1] + arrived[2 : 1 + ys], tails[:1] + arrived[1 + ys :]
     halos = [from_left, from_right]
     for s in range(1, ys):
-        halos += [along_y(from_left, s), to_previous(heads[s])]
+        halos += [to_next(tails[s]), along_y(from_right, s)]
     owns = [item for pair in zip(heads, tails) for item in pair]
     owns += [swap_cores(item) for item in owns]
     halos += [swap_cores(item) for item in halos]

time: 133 us -> 132 us (level)
    ppermute x2 -> x3, starting transfers between devices: 10.2 us -> 13.4 us  [to_next(): lax.ppermute(value, 'rows', [(i, i + 1) for i in range(lax.axis_size('row...]
    all_to_all x2, starting transfers between devices: 10.7 us -> 8.75 us  [exchange(): return lax.all_to_all(coef, 'rows', split_axis=0, concat_axis=0, tiled=True)]
    ppermute x3 -> x2, starting transfers between devices: 3.85 us -> 2.57 us  [to_previous(): lax.ppermute(value, 'rows', [(i + 1, i) for i in range(lax.axis_size('row...]
  transfers between devices with their start and end apart: 43 -> 43, of which waited for: 23 -> 24; matrix products, arithmetic and copies ran while one was open for 2% -> 2% of each run, Pallas kernels for 24% -> 24%
where the time goes in v8:
time: 132 us
  starting transfers between devices  49.8 us (38%)
  waiting for transfers between devices  35.6 us (27%)
  Pallas kernels  33.1 us (25%)
  local copies, waits for them, and re-layouts  8.82 us (7%)
  other arithmetic  3.19 us (2%)
    ppermute x11, waiting for transfers between devices, along_y(): lax.ppermute(value, 'far', [(i, (i + CORES * shift) % size) for i in rang...  22.1 us
    pallas_call x2, Pallas kernels, operator(): pl.pallas_call(functools.partial(operator_kernel, far_size, per, last, le...  19.5 us
    ppermute x3, starting transfers between devices, to_next(): lax.ppermute(value, 'rows', [(i, i + 1) for i in range(lax.axis_size('row...  13.4 us
    ppermute x11, starting transfers between devices, along_y(): lax.ppermute(value, 'far', [(i, (i + CORES * shift) % size) for i in rang...  13 us
    all_to_all x2, starting transfers between devices, exchange(): return lax.all_to_all(coef, 'rows', split_axis=0, concat_axis=0, tiled=True)  8.75 us
    unnamed x56, local copies, waits for them, and re-layouts  7.75 us
    ppermute x3, starting transfers between devices, sum_rows(): other = lax.ppermute(value, 'rows', [(i, i ^ step) for i in range(size)])  7.02 us
    ppermute x22, waiting for transfers between devices, swap_cores(): return lax.ppermute(value, 'far', [(i, i ^ 1) for i in range(size)])  6.76 us
  transfers between devices with their start and end apart: 43, of which 24 were waited for; matrix products, arithmetic and copies ran while one was open for 2% of the time, Pallas kernels for 24%

profile of v8, /device:TPU:0, one launch (start us, length us, event | category | flops | bytes accessed | tf_op | source)
XLA Modules:
  0.0 131.6 jit_solution(13207680324411685211)
XLA Ops:
  0.7 1.1 constant_dynamic-slice_fusion
  1.7 5.6 %collective-permute-start.4 = (f32[2,128,256]{2,1,0:T(8,128)S(1)}, f32[2,128,256]{2,1,0:T(8,128)}, u32[]{:S(2)}, u32[]{:S(2)}) collective-permute-start(f32[2,128,256]{2,1,0:T(8,128)S(1)} %get-tuple-element.58), channel_id=1, source_target_pairs={{0,4},{4,8},{8,12},{12,16},{16,20},{20,24},{24,28},{1,5},{5,9},{9,... | collective-permute-start | bytes 786440 | tf_op jit(solution)/shard_map/ppermute | solution.py:608
  7.3 1.5 %collective-permute-start.5 = (f32[8,64,128]{2,1,0:T(8,128)}, f32[8,64,128]{2,1,0:T(8,128)S(1)}, u32[]{:S(2)}, u32[]{:S(2)}) collective-permute-start(f32[8,64,128]{2,1,0:T(8,128)} %bitcast.15), channel_id=1, source_target_pairs={{0,2},{1,3},{2,0},{3,1},{4,6},{5,7},{6,4},{7,5},{8,10},{9,11},{10,... | collective-permute-start | bytes 786440 | tf_op jit(solution)/shard_map/ppermute | solution.py:595
  8.8 0.5 collective-permute-start.10
  9.3 1.3 collective-permute-start
  10.6 0.7 pad_add_fusion.refs_0_
  11.3 0.8 collective-permute-done.4.refs_0_
  12.1 1.5 %collective-permute-start.1 = (s32[2,8]{1,0:T(2,128)S(1)}, s32[2,8]{1,0:T(2,128)S(1)}, u32[]{:S(2)}, u32[]{:S(2)}) collective-permute-start(s32[2,8]{1,0:T(2,128)S(1)} %pad_add_fusion.refs_0_), channel_id=1, source_target_pairs={{0,2},{1,3},{2,0},{3,1},{4,6},{5,7},{6,4},{7,5},{8,10},{9,11},{10,... | collective-permute-start | bytes 200 | tf_op jit(solution)/shard_map/ppermute | solution.py:595
  13.6 3.1 %collective-permute-done.5.refs_1_ = f32[8,64,128]{2,1,0:T(8,128)S(1)} collective-permute-done((f32[8,64,128]{2,1,0:T(8,128)}, f32[8,64,128]{2,1,0:T(8,128)S(1)}, u32[]{:S(2)}, u32[]{:S(2)}) %collective-permute-start.5) | collective-permute-done | bytes 262176 | tf_op jit(solution)/shard_map/ppermute | solution.py:595
  16.7 1.5 %collective-permute-start.8 = (f32[2,128,256]{2,1,0:T(8,128)}, f32[2,128,256]{2,1,0:T(8,128)}, u32[]{:S(2)}, u32[]{:S(2)}) collective-permute-start(f32[2,128,256]{2,1,0:T(8,128)} %get-tuple-element.34.refs_1_), channel_id=1, source_target_pairs={{0,2},{1,3},{2,0},{3,1},{4,6},{5,7},{6,4},{7,5},{8,10},{9,11},{10,... | collective-permute-start | bytes 786440 | tf_op jit(solution)/shard_map/ppermute | solution.py:595
  18.3 4.1 %collective-permute-done.10.refs_5_ = f32[8,64,128]{2,1,0:T(8,128)S(1)} collective-permute-done((f32[8,64,128]{2,1,0:T(8,128)}, f32[8,64,128]{2,1,0:T(8,128)S(1)}, u32[]{:S(2)}, u32[]{:S(2)}) %collective-permute-start.10) | collective-permute-done | bytes 262176 | tf_op jit(solution)/shard_map/ppermute | solution.py:595
  22.4 1.6 %collective-permute-start.9 = (f32[2,128,256]{2,1,0:T(8,128)}, f32[2,128,256]{2,1,0:T(8,128)}, u32[]{:S(2)}, u32[]{:S(2)}) collective-permute-start(f32[2,128,256]{2,1,0:T(8,128)} %get-tuple-element.35.refs_2_), channel_id=1, source_target_pairs={{0,2},{1,3},{2,0},{3,1},{4,6},{5,7},{6,4},{7,5},{8,10},{9,11},{10,... | collective-permute-start | bytes 786440 | tf_op jit(solution)/shard_map/ppermute | solution.py:595
  24.6 0.5 collective-permute-done.2.refs_2_
  25.3 0.9 collective-permute-done.3.refs_3_
  26.3 3.1 %coefficients.2 = f32[8,2,64,128]{3,2,1,0:T(8,128)} custom-call(s32[2,8]{1,0:T(2,128)S(1)} %pad_add_fusion.refs_0_, s32[2,8]{1,0:T(2,128)S(1)} %get-tuple-element.30.refs_1_, s32[2,8]{1,0:T(2,128)S(1)} %collective-permute-done.2.refs_2_, s32[2,8]{1,0:T(2,128)S(1)} %collective-permute-done.3.refs_3_, f32[8,64,128]{2,1,0:T(8,128)S(1)} %bitcast.21, ...), custom_call_target="tpu_custom_call" | custom-call | flops 100663296 | bytes 4194304 | tf_op jit(solution)/shard_map/coefficients/pallas_call | solution.py:168
  29.4 0.7 copy-done.9
  30.1 0.7 copy-done.11
  30.8 4.2 %all-to-all-start = ((f32[8,2,64,128]{3,2,1,0:T(8,128)}), f32[8,2,64,128]{3,2,1,0:T(8,128)S(1)}, u32[]{:S(2)}, u32[]{:S(2)}) async-start(f32[8,2,64,128]{3,2,1,0:T(8,128)} %coefficients.2), calls=%async_computation | async-start | bytes 1048576 | tf_op jit(solution)/shard_map/all_to_all | solution.py:627
  35.1 0.5 collective-permute-start.14
  35.7 0.4 collective-permute-start.16
  36.1 0.7 collective-permute-done.13.refs_5_
  38.7 9.5 %operator.2 = (f32[8,128,128]{2,1,0:T(8,128)}, f32[8,128,128]{2,1,0:T(8,128)}, f32[8,128,128]{2,1,0:T(8,128)}, f32[8,128,128]{2,1,0:T(8,128)}) custom-call(s32[6,16]{1,0:T(8,128)} %bitcast.23, f32[16,6,128,128]{3,2,1,0:T(8,128)} %blocks_ref.3, f32[16,128,256]{2,1,0:T(8,128)} %bitcast.13, f32[2,128,256]{2,1,0:T(8,128)} %get-tuple-element.34.refs_1_, ...), custom_call_target="tpu_custom_call" | custom-call | tf_op jit(solution)/shard_map/operator/pallas_call | solution.py:374
  49.3 1.2 collective-permute-done.17
  50.6 1.2 slice_add_fusion
  51.8 0.6 collective-permute-start.20
  52.4 1.5 %collective-permute-start.19 = (f32[4,128,128]{2,1,0:T(8,128)S(1)}, f32[4,128,128]{2,1,0:T(8,128)S(1)}, u32[]{:S(2)}, u32[]{:S(2)}) collective-permute-start(f32[4,128,128]{2,1,0:T(8,128)S(1)} %get-tuple-element.61), channel_id=1, source_target_pairs={{0,2},{1,3},{2,0},{3,1},{4,6},{5,7},{6,4},{7,5},{8,10},{9,11},{10,... | collective-permute-start | bytes 786440 | tf_op jit(solution)/shard_map/ppermute | solution.py:595
  53.9 0.8 copy-done.15
  54.7 1.0 copy-done.13
  55.8 1.0 copy-done.16
  56.8 2.4 %far_part.2.refs_0_ = f32[8,128,128]{2,1,0:T(8,128)S(1)} custom-call(s32[2,8]{1,0:T(2,128)S(1)} %pad_add_fusion.refs_0_, s32[2,8]{1,0:T(2,128)S(1)} %get-tuple-element.30.refs_1_, s32[2,8]{1,0:T(2,128)S(1)} %collective-permute-done.2.refs_2_, s32[2,8]{1,0:T(2,128)S(1)} %collective-permute-done.3.refs_3_, f32[8,64,128]{2,1,0:T(8,128)S(1)} %bitcast.17, ...), custom_call_target="tpu_custom_call" | custom-call | flops 100663296 | bytes 4194304 | tf_op jit(solution)/shard_map/far_part/pallas_call | solution.py:225
  59.3 1.8 %collective-permute-done.20.refs_1_ = f32[4,128,128]{2,1,0:T(8,128)S(1)} collective-permute-done((f32[4,128,128]{2,1,0:T(8,128)S(1)}, f32[4,128,128]{2,1,0:T(8,128)S(1)}, u32[]{:S(2)}, u32[]{:S(2)}) %collective-permute-start.20) | collective-permute-done | bytes 262176 | tf_op jit(solution)/shard_map/ppermute | solution.py:595
  61.1 4.6 %collective-permute-start.21 = (f32[4,128,128]{2,1,0:T(8,128)S(1)}, f32[4,128,128]{2,1,0:T(8,128)}, u32[]{:S(2)}, u32[]{:S(2)}) collective-permute-start(f32[4,128,128]{2,1,0:T(8,128)S(1)} %add_half.3.gr_ref.refs_9_.refs_1_.refs_4_), channel_id=1, source_target_pairs={{0,4},{4,8},{8,12},{12,16},{16,20},{20,24},{24,28},{1,5},{5,9},{9,... | collective-permute-start | bytes 786440 | tf_op jit(solution)/shard_map/ppermute | solution.py:608
  65.8 0.5 collective-permute-start.24
  66.3 1.3 collective-permute-start.22
  67.6 1.6 %collective-permute-start.23 = (f32[4,128,128]{2,1,0:T(8,128)S(1)}, f32[4,128,128]{2,1,0:T(8,128)}, u32[]{:S(2)}, u32[]{:S(2)}) collective-permute-start(f32[4,128,128]{2,1,0:T(8,128)S(1)} %add_half.2.gl_ref.refs_8_.refs_0_.refs_3_), channel_id=1, source_target_pairs={{0,2},{1,3},{2,0},{3,1},{4,6},{5,7},{6,4},{7,5},{8,10},{9,11},{10,... | collective-permute-start | bytes 786440 | tf_op jit(solution)/shard_map/ppermute | solution.py:595
  69.3 3.1 %coefficients.3 = f32[8,2,64,128]{3,2,1,0:T(8,128)} custom-call(s32[2,8]{1,0:T(2,128)S(1)} %pad_add_fusion.refs_0_, s32[2,8]{1,0:T(2,128)S(1)} %get-tuple-element.30.refs_1_, s32[2,8]{1,0:T(2,128)S(1)} %collective-permute-done.2.refs_2_, s32[2,8]{1,0:T(2,128)S(1)} %collective-permute-done.3.refs_3_, f32[8,64,128]{2,1,0:T(8,128)S(1)} %bitcast.22, ...), custom_call_target="tpu_custom_call" | custom-call | flops 100663296 | bytes 4194304 | tf_op jit(solution)/shard_map/coefficients/pallas_call | solution.py:168
  72.4 0.6 collective-permute-start.25
  73.0 2.1 %collective-permute-done.24.refs_3_ = f32[4,128,128]{2,1,0:T(8,128)} collective-permute-done((f32[4,128,128]{2,1,0:T(8,128)S(1)}, f32[4,128,128]{2,1,0:T(8,128)}, u32[]{:S(2)}, u32[]{:S(2)}) %collective-permute-start.24) | collective-permute-done | bytes 262176 | tf_op jit(solution)/shard_map/ppermute | solution.py:595
  75.1 0.6 collective-permute-done.22.refs_9_
  75.7 2.2 %collective-permute-done.23.refs_2_ = f32[4,128,128]{2,1,0:T(8,128)} collective-permute-done((f32[4,128,128]{2,1,0:T(8,128)S(1)}, f32[4,128,128]{2,1,0:T(8,128)}, u32[]{:S(2)}, u32[]{:S(2)}) %collective-permute-start.23) | collective-permute-done | bytes 262176 | tf_op jit(solution)/shard_map/ppermute | solution.py:595
  77.9 3.2 %collective-permute-start.29 = (f32[4,128,128]{2,1,0:T(8,128)}, f32[4,128,128]{2,1,0:T(8,128)S(1)}, u32[]{:S(2)}, u32[]{:S(2)}) collective-permute-start(f32[4,128,128]{2,1,0:T(8,128)} %collective-permute-done.24.refs_3_), channel_id=1, source_target_pairs={{0,4},{4,8},{8,12},{12,16},{16,20},{20,24},{24,28},{1,5},{5,9},{9,... | collective-permute-start | bytes 786440 | tf_op jit(solution)/shard_map/ppermute | solution.py:608
  81.1 0.6 collective-permute-start.30
  81.7 4.5 %all-to-all-start.1 = ((f32[8,2,64,128]{3,2,1,0:T(8,128)}), f32[8,2,64,128]{3,2,1,0:T(8,128)S(1)}, u32[]{:S(2)}, u32[]{:S(2)}) async-start(f32[8,2,64,128]{3,2,1,0:T(8,128)} %coefficients.3), calls=%async_computation.1 | async-start | bytes 1048576 | tf_op jit(solution)/shard_map/all_to_all | solution.py:627
  87.0 0.8 collective-permute-done.30.refs_11_
  87.9 0.5 collective-permute-start.34
  88.4 0.4 collective-permute-done.31.refs_12_
  88.8 0.6 collective-permute-done.33.refs_14_
  89.5 0.7 copy-done.23
  90.3 10.0 %operator.3 = (f32[8,128,128]{2,1,0:T(8,128)}, f32[8,128,128]{2,1,0:T(8,128)}, f32[8,128,128]{2,1,0:T(8,128)}, f32[8,128,128]{2,1,0:T(8,128)}) custom-call(s32[6,16]{1,0:T(8,128)} %bitcast.24, f32[16,6,128,128]{3,2,1,0:T(8,128)} %blocks_ref.3, f32[4,128,128]{2,1,0:T(8,128)} %copy-done.4, f32[4,128,128]{2,1,0:T(8,128)} %copy-done.1, ...), custom_call_target="tpu_custom_call" | custom-call | tf_op jit(solution)/shard_map/operator/pallas_call | solution.py:374
  100.8 0.5 all-to-all-done.1.refs_8_
  101.4 1.2 collective-permute-done.35
  102.6 1.3 add.37
  103.8 1.6 %collective-permute-start.37 = (f32[8,128,128]{2,1,0:T(8,128)S(1)}, f32[8,128,128]{2,1,0:T(8,128)S(1)}, u32[]{:S(2)}, u32[]{:S(2)}) collective-permute-start(f32[8,128,128]{2,1,0:T(8,128)S(1)} %add.37), channel_id=1, source_target_pairs={{0,2},{1,3},{2,0},{3,1},{4,6},{5,7},{6,4},{7,5},{8,10},{9,11},{10,... | collective-permute-start | bytes 1572872 | tf_op jit(solution)/shard_map/ppermute | solution.py:595
  105.4 0.9 copy-done.2
  106.4 0.9 copy-done.5
  107.6 2.4 %far_part.3.refs_0_ = f32[8,128,128]{2,1,0:T(8,128)S(1)} custom-call(s32[2,8]{1,0:T(2,128)S(1)} %pad_add_fusion.refs_0_, s32[2,8]{1,0:T(2,128)S(1)} %get-tuple-element.30.refs_1_, s32[2,8]{1,0:T(2,128)S(1)} %collective-permute-done.2.refs_2_, s32[2,8]{1,0:T(2,128)S(1)} %collective-permute-done.3.refs_3_, f32[8,64,128]{2,1,0:T(8,128)S(1)} %bitcast.18, ...), custom_call_target="tpu_custom_call" | custom-call | flops 100663296 | bytes 4194304 | tf_op jit(solution)/shard_map/far_part/pallas_call | solution.py:225
  110.0 7.9 %collective-permute-done.37.refs_1_ = f32[8,128,128]{2,1,0:T(8,128)S(1)} collective-permute-done((f32[8,128,128]{2,1,0:T(8,128)S(1)}, f32[8,128,128]{2,1,0:T(8,128)S(1)}, u32[]{:S(2)}, u32[]{:S(2)}) %collective-permute-start.37) | collective-permute-done | bytes 524320 | tf_op jit(solution)/shard_map/ppermute | solution.py:595
  118.3 2.1 %collective-permute-start.38 = (f32[8,128]{1,0:T(8,128)S(1)}, f32[8,128]{1,0:T(8,128)S(1)}, u32[]{:S(2)}, u32[]{:S(2)}) collective-permute-start(f32[8,128]{1,0:T(8,128)S(1)} %get-tuple-element.54), channel_id=1, source_target_pairs={{0,4},{4,0},{8,12},{12,8},{16,20},{20,16},{24,28},{28,24},{1,5},{5... | collective-permute-start | bytes 12296 | tf_op jit(solution)/shard_map/ppermute | solution.py:619
  120.4 1.6 %collective-permute-done.38 = f32[8,128]{1,0:T(8,128)S(1)} collective-permute-done((f32[8,128]{1,0:T(8,128)S(1)}, f32[8,128]{1,0:T(8,128)S(1)}, u32[]{:S(2)}, u32[]{:S(2)}) %collective-permute-start.38) | collective-permute-done | bytes 4128 | tf_op jit(solution)/shard_map/ppermute | solution.py:619
  121.9 2.0 %collective-permute-start.39 = (f32[8,128]{1,0:T(8,128)S(1)}, f32[8,128]{1,0:T(8,128)S(1)}, u32[]{:S(2)}, u32[]{:S(2)}) collective-permute-start(f32[8,128]{1,0:T(8,128)S(1)} %add.38), channel_id=1, source_target_pairs={{0,8},{4,12},{8,0},{12,4},{16,24},{20,28},{24,16},{28,20},{1,9},{5... | collective-permute-start | bytes 12296 | tf_op jit(solution)/shard_map/ppermute | solution.py:619
  124.0 1.6 %collective-permute-done.39 = f32[8,128]{1,0:T(8,128)S(1)} collective-permute-done((f32[8,128]{1,0:T(8,128)S(1)}, f32[8,128]{1,0:T(8,128)S(1)}, u32[]{:S(2)}, u32[]{:S(2)}) %collective-permute-start.39) | collective-permute-done | bytes 4128 | tf_op jit(solution)/shard_map/ppermute | solution.py:619
  125.6 2.9 %collective-permute-start.40 = (f32[8,128]{1,0:T(8,128)S(1)}, f32[8,128]{1,0:T(8,128)S(1)}, u32[]{:S(2)}, u32[]{:S(2)}) collective-permute-start(f32[8,128]{1,0:T(8,128)S(1)} %add.39.refs_0_), channel_id=1, source_target_pairs={{0,16},{4,20},{8,24},{12,28},{16,0},{20,4},{24,8},{28,12},{1,17},{... | collective-permute-start | bytes 12296 | tf_op jit(solution)/shard_map/ppermute | solution.py:619
  128.5 1.6 %collective-permute-done.40.refs_1_ = f32[8,128]{1,0:T(8,128)S(1)} collective-permute-done((f32[8,128]{1,0:T(8,128)S(1)}, f32[8,128]{1,0:T(8,128)S(1)}, u32[]{:S(2)}, u32[]{:S(2)}) %collective-permute-start.40) | collective-permute-done | bytes 4128 | tf_op jit(solution)/shard_map/ppermute | solution.py:619
  130.1 1.4 %finish.1 = (f32[64,2048]{1,0:T(8,128)}, f32[64,2048]{1,0:T(8,128)}) custom-call(f32[8,128]{1,0:T(8,128)S(1)} %add.39.refs_0_, f32[8,128]{1,0:T(8,128)S(1)} %collective-permute-done.40.refs_1_, f32[8,128,128]{2,1,0:T(8,128)S(1)} %pack.1.refs_8_.b_ref.refs_2_, f32[4,128,128]{2,1,0:T(8,128)S(1)} %copy-done.6, f32[4,128,128]{2,1,0:T(8,128)S(1)} %copy-done.3, ...), custom_call_target="tpu_custom_call" | custom-call | flops 1048576 | bytes 3670016 | tf_op jit(solution)/shard_map/finish/pallas_call | solution.py:557
  (98 shorter events, 6.3 us)
Async XLA Ops:
  1.7 10.4 %collective-permute-start.4 = (f32[2,128,256]{2,1,0:T(8,128)S(1)}, f32[2,128,256]{2,1,0:T(8,128)}, u32[]{:S(2)}, u32[]{:S(2)}) collective-permute-start(f32[2,128,256]{2,1,0:T(8,128)S(1)} %get-tuple-element.58), channel_id=1, source_target_pairs={{0,4},{4,8},{8,12},{12,16},{16,20},{20,24},{24,28},{1,5},{5,9},{9,... | collective-permute-start | bytes 786440 | tf_op jit(solution)/shard_map/ppermute | solution.py:608
  7.3 9.4 %collective-permute-start.5 = (f32[8,64,128]{2,1,0:T(8,128)}, f32[8,64,128]{2,1,0:T(8,128)S(1)}, u32[]{:S(2)}, u32[]{:S(2)}) collective-permute-start(f32[8,64,128]{2,1,0:T(8,128)} %bitcast.15), channel_id=1, source_target_pairs={{0,2},{1,3},{2,0},{3,1},{4,6},{5,7},{6,4},{7,5},{8,10},{9,11},{10,... | collective-permute-start | bytes 786440 | tf_op jit(solution)/shard_map/ppermute | solution.py:595
  8.8 13.5 %collective-permute-start.10 = (f32[8,64,128]{2,1,0:T(8,128)}, f32[8,64,128]{2,1,0:T(8,128)S(1)}, u32[]{:S(2)}, u32[]{:S(2)}) collective-permute-start(f32[8,64,128]{2,1,0:T(8,128)} %bitcast.19), channel_id=1, source_target_pairs={{0,2},{1,3},{2,0},{3,1},{4,6},{5,7},{6,4},{7,5},{8,10},{9,11},{10,... | collective-permute-start | bytes 786440 | tf_op jit(solution)/shard_map/ppermute | solution.py:595
  9.3 16.0 %collective-permute-start.11 = (f32[8,64,128]{2,1,0:T(8,128)}, f32[8,64,128]{2,1,0:T(8,128)S(1)}, u32[]{:S(2)}, u32[]{:S(2)}) collective-permute-start(f32[8,64,128]{2,1,0:T(8,128)} %bitcast.20), channel_id=1, source_target_pairs={{0,1},{1,0},{2,3},{3,2},{4,5},{5,4},{6,7},{7,6},{8,9},{9,8},{10,11... | collective-permute-start | bytes 786440 | tf_op jit(solution)/shard_map/ppermute | solution.py:590
  9.3 13.1 %collective-permute-start = (f32[2,128,256]{2,1,0:T(8,128)S(1)}, f32[2,128,256]{2,1,0:T(8,128)}, u32[]{:S(2)}, u32[]{:S(2)}) collective-permute-start(f32[2,128,256]{2,1,0:T(8,128)S(1)} %get-tuple-element.59), channel_id=1, source_target_pairs={{4,0},{8,4},{12,8},{16,12},{20,16},{24,20},{28,24},{5,1},{9,5},{13... | collective-permute-start | bytes 786440 | tf_op jit(solution)/shard_map/ppermute | solution.py:612
  12.1 10.3 %collective-permute-start.1 = (s32[2,8]{1,0:T(2,128)S(1)}, s32[2,8]{1,0:T(2,128)S(1)}, u32[]{:S(2)}, u32[]{:S(2)}) collective-permute-start(s32[2,8]{1,0:T(2,128)S(1)} %pad_add_fusion.refs_0_), channel_id=1, source_target_pairs={{0,2},{1,3},{2,0},{3,1},{4,6},{5,7},{6,4},{7,5},{8,10},{9,11},{10,... | collective-permute-start | bytes 200 | tf_op jit(solution)/shard_map/ppermute | solution.py:595
  16.7 7.5 %copy-start = (f32[2048,256]{1,0:T(8,128)S(1)}, f32[2048,256]{1,0:T(8,128)}, u32[]{:S(2)}) copy-start(f32[2048,256]{1,0:T(8,128)} %param.7) | copy-start | bytes 6291460
  16.7 18.3 %collective-permute-start.8 = (f32[2,128,256]{2,1,0:T(8,128)}, f32[2,128,256]{2,1,0:T(8,128)}, u32[]{:S(2)}, u32[]{:S(2)}) collective-permute-start(f32[2,128,256]{2,1,0:T(8,128)} %get-tuple-element.34.refs_1_), channel_id=1, source_target_pairs={{0,2},{1,3},{2,0},{3,1},{4,6},{5,7},{6,4},{7,5},{8,10},{9,11},{10,... | collective-permute-start | bytes 786440 | tf_op jit(solution)/shard_map/ppermute | solution.py:595
  22.4 3.9 %collective-permute-start.12 = (f32[8,64,128]{2,1,0:T(8,128)S(1)}, f32[8,64,128]{2,1,0:T(8,128)S(1)}, u32[]{:S(2)}, u32[]{:S(2)}) collective-permute-start(f32[8,64,128]{2,1,0:T(8,128)S(1)} %collective-permute-done.10.refs_5_), channel_id=1, source_target_pairs={{0,1},{1,0},{2,3},{3,2},{4,5},{5,4},{6,7},{7,6},{8,9},{9,8},{10,11... | collective-permute-start | bytes 786440 | tf_op jit(solution)/shard_map/ppermute | solution.py:590
  22.4 3.9 %copy-start.8 = (f32[1,8,1,128,64]{3,4,2,1,0:T(8,128)S(1)}, f32[1,8,1,128,64]{3,4,2,1,0:T(8,128)}, u32[]{:S(2)}) copy-start(f32[1,8,1,128,64]{3,4,2,1,0:T(8,128)} %param.13) | copy-start | bytes 786436
  22.4 12.6 %collective-permute-start.9 = (f32[2,128,256]{2,1,0:T(8,128)}, f32[2,128,256]{2,1,0:T(8,128)}, u32[]{:S(2)}, u32[]{:S(2)}) collective-permute-start(f32[2,128,256]{2,1,0:T(8,128)} %get-tuple-element.35.refs_2_), channel_id=1, source_target_pairs={{0,2},{1,3},{2,0},{3,1},{4,6},{5,7},{6,4},{7,5},{8,10},{9,11},{10,... | collective-permute-start | bytes 786440 | tf_op jit(solution)/shard_map/ppermute | solution.py:595
  24.0 1.1 collective-permute-start.2
  25.1 1.1 collective-permute-start.3
  30.8 19.8 %all-to-all-start = ((f32[8,2,64,128]{3,2,1,0:T(8,128)}), f32[8,2,64,128]{3,2,1,0:T(8,128)S(1)}, u32[]{:S(2)}, u32[]{:S(2)}) async-start(f32[8,2,64,128]{3,2,1,0:T(8,128)} %coefficients.2), calls=%async_computation | async-start | bytes 1048576 | tf_op jit(solution)/shard_map/all_to_all | solution.py:627
  35.0 1.8 %collective-permute-start.13 = (f32[2,128,256]{2,1,0:T(8,128)}, f32[2,128,256]{2,1,0:T(8,128)S(1)}, u32[]{:S(2)}, u32[]{:S(2)}) collective-permute-start(f32[2,128,256]{2,1,0:T(8,128)} %get-tuple-element.34.refs_1_), channel_id=1, source_target_pairs={{0,1},{1,0},{2,3},{3,2},{4,5},{5,4},{6,7},{7,6},{8,9},{9,8},{10,11... | collective-permute-start | bytes 786440 | tf_op jit(solution)/shard_map/ppermute | solution.py:590
  35.1 2.1 %collective-permute-start.14 = (f32[2,128,256]{2,1,0:T(8,128)}, f32[2,128,256]{2,1,0:T(8,128)S(1)}, u32[]{:S(2)}, u32[]{:S(2)}) collective-permute-start(f32[2,128,256]{2,1,0:T(8,128)} %get-tuple-element.35.refs_2_), channel_id=1, source_target_pairs={{0,1},{1,0},{2,3},{3,2},{4,5},{5,4},{6,7},{7,6},{8,9},{9,8},{10,11... | collective-permute-start | bytes 786440 | tf_op jit(solution)/shard_map/ppermute | solution.py:590
  35.6 2.0 %collective-permute-start.15 = (f32[2,128,256]{2,1,0:T(8,128)}, f32[2,128,256]{2,1,0:T(8,128)S(1)}, u32[]{:S(2)}, u32[]{:S(2)}) collective-permute-start(f32[2,128,256]{2,1,0:T(8,128)} %collective-permute-done.8.refs_3_), channel_id=1, source_target_pairs={{0,1},{1,0},{2,3},{3,2},{4,5},{5,4},{6,7},{7,6},{8,9},{9,8},{10,11... | collective-permute-start | bytes 786440 | tf_op jit(solution)/shard_map/ppermute | solution.py:590
  35.7 2.3 %collective-permute-start.16 = (f32[2,128,256]{2,1,0:T(8,128)}, f32[2,128,256]{2,1,0:T(8,128)S(1)}, u32[]{:S(2)}, u32[]{:S(2)}) collective-permute-start(f32[2,128,256]{2,1,0:T(8,128)} %collective-permute-done.9.refs_4_), channel_id=1, source_target_pairs={{0,1},{1,0},{2,3},{3,2},{4,5},{5,4},{6,7},{7,6},{8,9},{9,8},{10,11... | collective-permute-start | bytes 786440 | tf_op jit(solution)/shard_map/ppermute | solution.py:590
  36.9 1.1 copy-start.24
  38.7 10.1 %copy-start.7 = (f32[1,8,1,128,64]{3,4,2,1,0:T(8,128)S(1)}, f32[1,8,1,128,64]{3,4,2,1,0:T(8,128)}, u32[]{:S(2)}) copy-start(f32[1,8,1,128,64]{3,4,2,1,0:T(8,128)} %param.12) | copy-start | bytes 786436
  48.2 2.3 %collective-permute-start.17 = (f32[8,128,128]{2,1,0:T(8,128)}, f32[8,128,128]{2,1,0:T(8,128)}, u32[]{:S(2)}, u32[]{:S(2)}) collective-permute-start(f32[8,128,128]{2,1,0:T(8,128)} %get-tuple-element.38), channel_id=1, source_target_pairs={{0,1},{1,0},{2,3},{3,2},{4,5},{5,4},{6,7},{7,6},{8,9},{9,8},{10,11... | collective-permute-start | bytes 1572872 | tf_op jit(solution)/shard_map/ppermute | solution.py:590
  48.4 5.5 %collective-permute-start.18 = (f32[8,128,128]{2,1,0:T(8,128)}, f32[8,128,128]{2,1,0:T(8,128)S(1)}, u32[]{:S(2)}, u32[]{:S(2)}) collective-permute-start(f32[8,128,128]{2,1,0:T(8,128)} %get-tuple-element.41), channel_id=1, source_target_pairs={{0,1},{1,0},{2,3},{3,2},{4,5},{5,4},{6,7},{7,6},{8,9},{9,8},{10,11... | collective-permute-start | bytes 1572872 | tf_op jit(solution)/shard_map/ppermute | solution.py:590
  48.8 5.1 %collective-permute-start.6 = (f32[8,64,128]{2,1,0:T(8,128)S(1)}, f32[8,64,128]{2,1,0:T(8,128)S(1)}, u32[]{:S(2)}, u32[]{:S(2)}) collective-permute-start(f32[8,64,128]{2,1,0:T(8,128)S(1)} %bitcast.16), channel_id=1, source_target_pairs={{0,1},{1,0},{2,3},{3,2},{4,5},{5,4},{6,7},{7,6},{8,9},{9,8},{10,11... | collective-permute-start | bytes 786440 | tf_op jit(solution)/shard_map/ppermute | solution.py:590
  49.0 5.0 %collective-permute-start.7 = (f32[8,64,128]{2,1,0:T(8,128)S(1)}, f32[8,64,128]{2,1,0:T(8,128)S(1)}, u32[]{:S(2)}, u32[]{:S(2)}) collective-permute-start(f32[8,64,128]{2,1,0:T(8,128)S(1)} %get-tuple-element.31.refs_5_), channel_id=1, source_target_pairs={{0,1},{1,0},{2,3},{3,2},{4,5},{5,4},{6,7},{7,6},{8,9},{9,8},{10,11... | collective-permute-start | bytes 786440 | tf_op jit(solution)/shard_map/ppermute | solution.py:590
  51.8 9.2 %collective-permute-start.20 = (f32[4,128,128]{2,1,0:T(8,128)S(1)}, f32[4,128,128]{2,1,0:T(8,128)S(1)}, u32[]{:S(2)}, u32[]{:S(2)}) collective-permute-start(f32[4,128,128]{2,1,0:T(8,128)S(1)} %get-tuple-element.60), channel_id=1, source_target_pairs={{0,2},{1,3},{2,0},{3,1},{4,6},{5,7},{6,4},{7,5},{8,10},{9,11},{10,... | collective-permute-start | bytes 786440 | tf_op jit(solution)/shard_map/ppermute | solution.py:595
  52.4 13.9 %collective-permute-start.19 = (f32[4,128,128]{2,1,0:T(8,128)S(1)}, f32[4,128,128]{2,1,0:T(8,128)S(1)}, u32[]{:S(2)}, u32[]{:S(2)}) collective-permute-start(f32[4,128,128]{2,1,0:T(8,128)S(1)} %get-tuple-element.61), channel_id=1, source_target_pairs={{0,2},{1,3},{2,0},{3,1},{4,6},{5,7},{6,4},{7,5},{8,10},{9,11},{10,... | collective-permute-start | bytes 786440 | tf_op jit(solution)/shard_map/ppermute | solution.py:595
  53.9 0.8 copy-start.15
  54.7 1.0 copy-start.13
  55.8 1.0 copy-start.16
  56.8 12.4 %copy-start.10 = (f32[8,64,128]{2,1,0:T(8,128)S(1)}, f32[8,64,128]{2,1,0:T(8,128)}, u32[]{:S(2)}) copy-start(f32[8,64,128]{2,1,0:T(8,128)} %copy-done.9) | copy-start | bytes 786436
  56.8 12.4 %copy-start.12 = (f32[8,64,128]{2,1,0:T(8,128)S(1)}, f32[8,64,128]{2,1,0:T(8,128)}, u32[]{:S(2)}) copy-start(f32[8,64,128]{2,1,0:T(8,128)} %copy-done.11) | copy-start | bytes 786436
  61.1 29.1 %copy-start.1 = (f32[4,128,128]{2,1,0:T(8,128)}, f32[4,128,128]{2,1,0:T(8,128)S(1)}, u32[]{:S(2)}) copy-start(f32[4,128,128]{2,1,0:T(8,128)S(1)} %add_half.3.gr_ref.refs_9_.refs_1_.refs_4_) | copy-start | bytes 786436
  61.1 11.3 %collective-permute-start.21 = (f32[4,128,128]{2,1,0:T(8,128)S(1)}, f32[4,128,128]{2,1,0:T(8,128)}, u32[]{:S(2)}, u32[]{:S(2)}) collective-permute-start(f32[4,128,128]{2,1,0:T(8,128)S(1)} %add_half.3.gr_ref.refs_9_.refs_1_.refs_4_), channel_id=1, source_target_pairs={{0,4},{4,8},{8,12},{12,16},{16,20},{20,24},{24,28},{1,5},{5,9},{9,... | collective-permute-start | bytes 786440 | tf_op jit(solution)/shard_map/ppermute | solution.py:608
  65.8 9.3 %collective-permute-start.24 = (f32[4,128,128]{2,1,0:T(8,128)S(1)}, f32[4,128,128]{2,1,0:T(8,128)}, u32[]{:S(2)}, u32[]{:S(2)}) collective-permute-start(f32[4,128,128]{2,1,0:T(8,128)S(1)} %add_half.3.gr_ref.refs_9_.refs_1_.refs_4_), channel_id=1, source_target_pairs={{0,2},{1,3},{2,0},{3,1},{4,6},{5,7},{6,4},{7,5},{8,10},{9,11},{10,... | collective-permute-start | bytes 786440 | tf_op jit(solution)/shard_map/ppermute | solution.py:595
  66.3 23.9 %copy-start.4 = (f32[4,128,128]{2,1,0:T(8,128)}, f32[4,128,128]{2,1,0:T(8,128)S(1)}, u32[]{:S(2)}) copy-start(f32[4,128,128]{2,1,0:T(8,128)S(1)} %add_half.2.gl_ref.refs_8_.refs_0_.refs_3_) | copy-start | bytes 786436
  66.3 9.4 %collective-permute-start.22 = (f32[4,128,128]{2,1,0:T(8,128)S(1)}, f32[4,128,128]{2,1,0:T(8,128)}, u32[]{:S(2)}, u32[]{:S(2)}) collective-permute-start(f32[4,128,128]{2,1,0:T(8,128)S(1)} %add_half.2.gl_ref.refs_8_.refs_0_.refs_3_), channel_id=1, source_target_pairs={{4,0},{8,4},{12,8},{16,12},{20,16},{24,20},{28,24},{5,1},{9,5},{13... | collective-permute-start | bytes 786440 | tf_op jit(solution)/shard_map/ppermute | solution.py:612
  67.6 10.2 %collective-permute-start.23 = (f32[4,128,128]{2,1,0:T(8,128)S(1)}, f32[4,128,128]{2,1,0:T(8,128)}, u32[]{:S(2)}, u32[]{:S(2)}) collective-permute-start(f32[4,128,128]{2,1,0:T(8,128)S(1)} %add_half.2.gl_ref.refs_8_.refs_0_.refs_3_), channel_id=1, source_target_pairs={{0,2},{1,3},{2,0},{3,1},{4,6},{5,7},{6,4},{7,5},{8,10},{9,11},{10,... | collective-permute-start | bytes 786440 | tf_op jit(solution)/shard_map/ppermute | solution.py:595
  69.2 17.0 %collective-permute-start.26 = (f32[4,128,128]{2,1,0:T(8,128)S(1)}, f32[4,128,128]{2,1,0:T(8,128)}, u32[]{:S(2)}, u32[]{:S(2)}) collective-permute-start(f32[4,128,128]{2,1,0:T(8,128)S(1)} %add_half.3.gr_ref.refs_9_.refs_1_.refs_4_), channel_id=1, source_target_pairs={{0,1},{1,0},{2,3},{3,2},{4,5},{5,4},{6,7},{7,6},{8,9},{9,8},{10,11... | collective-permute-start | bytes 786440 | tf_op jit(solution)/shard_map/ppermute | solution.py:590
  72.4 14.1 %collective-permute-start.25 = (f32[4,128,128]{2,1,0:T(8,128)S(1)}, f32[4,128,128]{2,1,0:T(8,128)S(1)}, u32[]{:S(2)}, u32[]{:S(2)}) collective-permute-start(f32[4,128,128]{2,1,0:T(8,128)S(1)} %add_half.2.gl_ref.refs_8_.refs_0_.refs_3_), channel_id=1, source_target_pairs={{0,1},{1,0},{2,3},{3,2},{4,5},{5,4},{6,7},{7,6},{8,9},{9,8},{10,11... | collective-permute-start | bytes 786440 | tf_op jit(solution)/shard_map/ppermute | solution.py:590
  77.9 8.9 %collective-permute-start.29 = (f32[4,128,128]{2,1,0:T(8,128)}, f32[4,128,128]{2,1,0:T(8,128)S(1)}, u32[]{:S(2)}, u32[]{:S(2)}) collective-permute-start(f32[4,128,128]{2,1,0:T(8,128)} %collective-permute-done.24.refs_3_), channel_id=1, source_target_pairs={{0,4},{4,8},{8,12},{12,16},{16,20},{20,24},{24,28},{1,5},{5,9},{9,... | collective-permute-start | bytes 786440 | tf_op jit(solution)/shard_map/ppermute | solution.py:608
  81.1 6.7 %collective-permute-start.30 = (f32[4,128,128]{2,1,0:T(8,128)}, f32[4,128,128]{2,1,0:T(8,128)S(1)}, u32[]{:S(2)}, u32[]{:S(2)}) collective-permute-start(f32[4,128,128]{2,1,0:T(8,128)} %collective-permute-done.22.refs_9_), channel_id=1, source_target_pairs={{0,2},{1,3},{2,0},{3,1},{4,6},{5,7},{6,4},{7,5},{8,10},{9,11},{10,... | collective-permute-start | bytes 786440 | tf_op jit(solution)/shard_map/ppermute | solution.py:595
  81.7 6.2 %collective-permute-start.27 = (f32[4,128,128]{2,1,0:T(8,128)}, f32[4,128,128]{2,1,0:T(8,128)}, u32[]{:S(2)}, u32[]{:S(2)}) collective-permute-start(f32[4,128,128]{2,1,0:T(8,128)} %collective-permute-done.23.refs_2_), channel_id=1, source_target_pairs={{0,1},{1,0},{2,3},{3,2},{4,5},{5,4},{6,7},{7,6},{8,9},{9,8},{10,11... | collective-permute-start | bytes 786440 | tf_op jit(solution)/shard_map/ppermute | solution.py:590
  81.7 19.7 %all-to-all-start.1 = ((f32[8,2,64,128]{3,2,1,0:T(8,128)}), f32[8,2,64,128]{3,2,1,0:T(8,128)S(1)}, u32[]{:S(2)}, u32[]{:S(2)}) async-start(f32[8,2,64,128]{3,2,1,0:T(8,128)} %coefficients.3), calls=%async_computation.1 | async-start | bytes 1048576 | tf_op jit(solution)/shard_map/all_to_all | solution.py:627
  86.2 2.1 %collective-permute-start.28 = (f32[4,128,128]{2,1,0:T(8,128)}, f32[4,128,128]{2,1,0:T(8,128)S(1)}, u32[]{:S(2)}, u32[]{:S(2)}) collective-permute-start(f32[4,128,128]{2,1,0:T(8,128)} %collective-permute-done.24.refs_3_), channel_id=1, source_target_pairs={{0,1},{1,0},{2,3},{3,2},{4,5},{5,4},{6,7},{7,6},{8,9},{9,8},{10,11... | collective-permute-start | bytes 786440 | tf_op jit(solution)/shard_map/ppermute | solution.py:590
  86.5 3.7 %copy-start.17 = (f32[4,128,128]{2,1,0:T(8,128)}, f32[4,128,128]{2,1,0:T(8,128)S(1)}, u32[]{:S(2)}) copy-start(f32[4,128,128]{2,1,0:T(8,128)S(1)} %collective-permute-done.25.refs_4_) | copy-start | bytes 786436
  86.5 2.3 %collective-permute-start.32 = (f32[4,128,128]{2,1,0:T(8,128)}, f32[4,128,128]{2,1,0:T(8,128)S(1)}, u32[]{:S(2)}, u32[]{:S(2)}) collective-permute-start(f32[4,128,128]{2,1,0:T(8,128)} %collective-permute-done.22.refs_9_), channel_id=1, source_target_pairs={{0,1},{1,0},{2,3},{3,2},{4,5},{5,4},{6,7},{7,6},{8,9},{9,8},{10,11... | collective-permute-start | bytes 786440 | tf_op jit(solution)/shard_map/ppermute | solution.py:590
  86.8 3.4 %copy-start.18 = (f32[4,128,128]{2,1,0:T(8,128)}, f32[4,128,128]{2,1,0:T(8,128)S(1)}, u32[]{:S(2)}) copy-start(f32[4,128,128]{2,1,0:T(8,128)S(1)} %collective-permute-done.29.refs_10_) | copy-start | bytes 786436
  86.8 2.0 %collective-permute-start.31 = (f32[4,128,128]{2,1,0:T(8,128)}, f32[4,128,128]{2,1,0:T(8,128)S(1)}, u32[]{:S(2)}, u32[]{:S(2)}) collective-permute-start(f32[4,128,128]{2,1,0:T(8,128)} %collective-permute-done.21.refs_8_), channel_id=1, source_target_pairs={{0,1},{1,0},{2,3},{3,2},{4,5},{5,4},{6,7},{7,6},{8,9},{9,8},{10,11... | collective-permute-start | bytes 786440 | tf_op jit(solution)/shard_map/ppermute | solution.py:590
  87.8 2.4 %copy-start.19 = (f32[4,128,128]{2,1,0:T(8,128)}, f32[4,128,128]{2,1,0:T(8,128)S(1)}, u32[]{:S(2)}) copy-start(f32[4,128,128]{2,1,0:T(8,128)S(1)} %collective-permute-done.30.refs_11_) | copy-start | bytes 786436
  87.8 1.5 %collective-permute-start.33 = (f32[4,128,128]{2,1,0:T(8,128)S(1)}, f32[4,128,128]{2,1,0:T(8,128)S(1)}, u32[]{:S(2)}, u32[]{:S(2)}) collective-permute-start(f32[4,128,128]{2,1,0:T(8,128)S(1)} %collective-permute-done.29.refs_10_), channel_id=1, source_target_pairs={{0,1},{1,0},{2,3},{3,2},{4,5},{5,4},{6,7},{7,6},{8,9},{9,8},{10,11... | collective-permute-start | bytes 786440 | tf_op jit(solution)/shard_map/ppermute | solution.py:590
  87.9 2.4 %collective-permute-start.34 = (f32[4,128,128]{2,1,0:T(8,128)S(1)}, f32[4,128,128]{2,1,0:T(8,128)}, u32[]{:S(2)}, u32[]{:S(2)}) collective-permute-start(f32[4,128,128]{2,1,0:T(8,128)S(1)} %collective-permute-done.30.refs_11_), channel_id=1, source_target_pairs={{0,1},{1,0},{2,3},{3,2},{4,5},{5,4},{6,7},{7,6},{8,9},{9,8},{10,11... | collective-permute-start | bytes 786440 | tf_op jit(solution)/shard_map/ppermute | solution.py:590
  88.4 1.9 %copy-start.20 = (f32[4,128,128]{2,1,0:T(8,128)}, f32[4,128,128]{2,1,0:T(8,128)S(1)}, u32[]{:S(2)}) copy-start(f32[4,128,128]{2,1,0:T(8,128)S(1)} %collective-permute-done.28.refs_7_) | copy-start | bytes 786436
  88.8 1.5 %copy-start.21 = (f32[4,128,128]{2,1,0:T(8,128)}, f32[4,128,128]{2,1,0:T(8,128)S(1)}, u32[]{:S(2)}) copy-start(f32[4,128,128]{2,1,0:T(8,128)S(1)} %collective-permute-done.32.refs_13_) | copy-start | bytes 786436
  100.2 7.3 %copy-start.14 = (f32[8,128,128]{2,1,0:T(8,128)S(1)}, f32[8,128,128]{2,1,0:T(8,128)}, u32[]{:S(2)}) copy-start(f32[8,128,128]{2,1,0:T(8,128)} %get-tuple-element.50.refs_9_) | copy-start | bytes 1572868
  100.3 2.3 %collective-permute-start.35 = (f32[8,128,128]{2,1,0:T(8,128)}, f32[8,128,128]{2,1,0:T(8,128)}, u32[]{:S(2)}, u32[]{:S(2)}) collective-permute-start(f32[8,128,128]{2,1,0:T(8,128)} %get-tuple-element.48), channel_id=1, source_target_pairs={{0,1},{1,0},{2,3},{3,2},{4,5},{5,4},{6,7},{7,6},{8,9},{9,8},{10,11... | collective-permute-start | bytes 1572872 | tf_op jit(solution)/shard_map/ppermute | solution.py:590
  100.5 7.0 %collective-permute-start.36 = (f32[8,128,128]{2,1,0:T(8,128)}, f32[8,128,128]{2,1,0:T(8,128)S(1)}, u32[]{:S(2)}, u32[]{:S(2)}) collective-permute-start(f32[8,128,128]{2,1,0:T(8,128)} %get-tuple-element.51), channel_id=1, source_target_pairs={{0,1},{1,0},{2,3},{3,2},{4,5},{5,4},{6,7},{7,6},{8,9},{9,8},{10,11... | collective-permute-start | bytes 1572872 | tf_op jit(solution)/shard_map/ppermute | solution.py:590
  103.8 14.1 %collective-permute-start.37 = (f32[8,128,128]{2,1,0:T(8,128)S(1)}, f32[8,128,128]{2,1,0:T(8,128)S(1)}, u32[]{:S(2)}, u32[]{:S(2)}) collective-permute-start(f32[8,128,128]{2,1,0:T(8,128)S(1)} %add.37), channel_id=1, source_target_pairs={{0,2},{1,3},{2,0},{3,1},{4,6},{5,7},{6,4},{7,5},{8,10},{9,11},{10,... | collective-permute-start | bytes 1572872 | tf_op jit(solution)/shard_map/ppermute | solution.py:595
  105.4 0.9 copy-start.2
  106.4 0.9 copy-start.5
  107.3 10.6 %copy-start.3 = (f32[4,128,128]{2,1,0:T(8,128)S(1)}, f32[4,128,128]{2,1,0:T(8,128)}, u32[]{:S(2)}) copy-start(f32[4,128,128]{2,1,0:T(8,128)} %copy-done.1) | copy-start | bytes 786436
  107.3 10.6 %copy-start.6 = (f32[4,128,128]{2,1,0:T(8,128)S(1)}, f32[4,128,128]{2,1,0:T(8,128)}, u32[]{:S(2)}) copy-start(f32[4,128,128]{2,1,0:T(8,128)} %copy-done.4) | copy-start | bytes 786436
  118.3 3.7 %collective-permute-start.38 = (f32[8,128]{1,0:T(8,128)S(1)}, f32[8,128]{1,0:T(8,128)S(1)}, u32[]{:S(2)}, u32[]{:S(2)}) collective-permute-start(f32[8,128]{1,0:T(8,128)S(1)} %get-tuple-element.54), channel_id=1, source_target_pairs={{0,4},{4,0},{8,12},{12,8},{16,20},{20,16},{24,28},{28,24},{1,5},{5... | collective-permute-start | bytes 12296 | tf_op jit(solution)/shard_map/ppermute | solution.py:619
  121.9 3.6 %collective-permute-start.39 = (f32[8,128]{1,0:T(8,128)S(1)}, f32[8,128]{1,0:T(8,128)S(1)}, u32[]{:S(2)}, u32[]{:S(2)}) collective-permute-start(f32[8,128]{1,0:T(8,128)S(1)} %add.38), channel_id=1, source_target_pairs={{0,8},{4,12},{8,0},{12,4},{16,24},{20,28},{24,16},{28,20},{1,9},{5... | collective-permute-start | bytes 12296 | tf_op jit(solution)/shard_map/ppermute | solution.py:619
  125.6 4.5 %collective-permute-start.40 = (f32[8,128]{1,0:T(8,128)S(1)}, f32[8,128]{1,0:T(8,128)S(1)}, u32[]{:S(2)}, u32[]{:S(2)}) collective-permute-start(f32[8,128]{1,0:T(8,128)S(1)} %add.39.refs_0_), channel_id=1, source_target_pairs={{0,16},{4,20},{8,24},{12,28},{16,0},{20,4},{24,8},{28,12},{1,17},{... | collective-permute-start | bytes 12296 | tf_op jit(solution)/shard_map/ppermute | solution.py:619
  (7 other events, 5.0 us)
